TPU v7x, 32 devices: a whole 2x2x4 slice. The times are simulated.
32 devices in a mesh: rep: 8 (over z, y), shard: 4 (over x, core).
Axes of the slice: x: 2, y: 2, z: 4, core: 2. Of those that a mesh axis runs over, the one named last changes fastest.
Arguments:
- q_grad: float32 [8, 1152, 1152], P('rep', None, 'shard'), may hold values from -6 to 6
- o_grad: float32 [8, 1152, 1152], P('rep', None, 'shard'), may hold values from -6 to 6
- q_error: float32 [8, 1152, 1152], P('rep', None, 'shard'), may hold values from -4 to 4
- o_error: float32 [8, 1152, 1152], P('rep', None, 'shard'), may hold values from -4 to 4
- q_basis: float32 [1152, 32], P('shard'), may hold values from -6 to 6
- o_basis: float32 [1152, 32], P('shard'), may hold values from -6 to 6
- q_moment: float32 [1152, 1152], P('rep', 'shard'), may hold values from -6 to 6
- o_moment: float32 [1152, 1152], P('rep', 'shard'), may hold values from -6 to 6
- q_weight: float32 [1152, 1152], P('rep', 'shard'), may hold values from -0.1875 to 0.1875
- o_weight: float32 [1152, 1152], P('rep', 'shard'), may hold values from -0.1875 to 0.1875
- norm_grads: float32 [8, 4, 2304], P('rep', 'shard'), may hold values from -5 to 5
- norm_moment: float32 [2304], P(('rep', 'shard')), may hold values from -6 to 6
- norm_weight: float32 [2304], P(('rep', 'shard')), may hold values from 0.5 to 1.5
Outputs:
- q_weight_new: float32 [1152, 1152], P(None, 'shard')
- o_weight_new: float32 [1152, 1152], P(None, 'shard')
- q_moment_new: float32 [1152, 1152], P('rep', 'shard')
- o_moment_new: float32 [1152, 1152], P('rep', 'shard')
- q_error_new: float32 [8, 1152, 1152], P('rep', None, 'shard')
- o_error_new: float32 [8, 1152, 1152], P('rep', None, 'shard')
- norm_weight_new: float32 [2304], replicated
- norm_moment_new: float32 [2304], P(('rep', 'shard'))
All inputs are finite; a program needn't handle non-finite values.
Results may differ from a plain program's by a relative error of at most 0.0003.
Values sent between devices are 32-bit elements; how exact they have to be, the bound alone decides.
No kernel may reach another device: no remote copies, remote signals or barrier semaphores. Data moves between devices by JAX's collectives and lax.ppermute only.
A program may use at most 64 MiB of HBM per device.

v0:
```python
import jax
import jax.numpy as jnp
from jax import lax
from jax.sharding import PartitionSpec as P

ROUNDS = 2


highest = lax.Precision.HIGHEST
decay_rate = 0.9
step_size = 0.1


def unwhiten(lower, factor):
    return jax.scipy.linalg.solve_triangular(lower, factor.T, lower=True).T


def product(left, right):
    return jnp.dot(left, right, precision=highest)


def per_device(
    q_grad,
    o_grad,
    q_error,
    o_error,
    q_basis,
    o_basis,
    q_moment,
    o_moment,
    q_weight,
    o_weight,
    norm_grads,
    norm_moment,
    norm_weight,
):
    corr_q = q_grad[0] + q_error[0]
    corr_o = o_grad[0] + o_error[0]
    basis_q = q_basis
    basis_o = o_basis
    normal_q = None
    normal_o = None
    for sweep in range(ROUNDS):
        part_q = product(corr_q, basis_q)
        part_o = product(corr_o, basis_o)
        left_q, left_o = lax.psum((part_q, part_o), ("rep", "shard"))
        gram_q = product(left_q.T, left_q)
        gram_o = product(left_o.T, left_o)
        lower_q = jnp.linalg.cholesky(gram_q)
        lower_o = jnp.linalg.cholesky(gram_o)
        reduce_q = product(corr_q.T, left_q)
        reduce_o = product(corr_o.T, left_o)
        summed_q, summed_o = lax.psum((reduce_q, reduce_o), "rep")
        basis_q = unwhiten(lower_q, summed_q)
        basis_o = unwhiten(lower_o, summed_o)
        if sweep == ROUNDS - 1:
            normal_q = unwhiten(lower_q, left_q)
            normal_o = unwhiten(lower_o, left_o)
    decoded_q = product(normal_q, basis_q.T)
    decoded_o = product(normal_o, basis_o.T)
    q_error_new = (corr_q - decoded_q)[None]
    o_error_new = (corr_o - decoded_o)[None]
    row_count = q_moment.shape[0]
    start = lax.axis_index("rep") * row_count
    slice_q = lax.dynamic_slice_in_dim(decoded_q, start, row_count, 0)
    slice_o = lax.dynamic_slice_in_dim(decoded_o, start, row_count, 0)
    q_moment_new = decay_rate * q_moment + slice_q
    o_moment_new = decay_rate * o_moment + slice_o
    weight_q = q_weight - step_size * q_moment_new
    weight_o = o_weight - step_size * o_moment_new
    q_weight_new, o_weight_new = (
        lax.all_gather(weight_q, "rep", axis=0, tiled=True),
        lax.all_gather(weight_o, "rep", axis=0, tiled=True),
    )
    flat_grads = norm_grads.reshape(-1)
    norm_sum = lax.psum_scatter(flat_grads, ("rep", "shard"), scatter_dimension=0, tiled=True)
    norm_moment_new = decay_rate * norm_moment + norm_sum
    gain_share = norm_weight - step_size * norm_moment_new
    norm_weight_new = lax.all_gather(gain_share, ("rep", "shard"), axis=0, tiled=True)
    return (
        q_weight_new,
        o_weight_new,
        q_moment_new,
        o_moment_new,
        q_error_new,
        o_error_new,
        norm_weight_new,
        norm_moment_new,
    )


def solution(mesh):
    return jax.shard_map(
        per_device,
        mesh=mesh,
        in_specs=(
            P("rep", None, "shard"),
            P("rep", None, "shard"),
            P("rep", None, "shard"),
            P("rep", None, "shard"),
            P("shard", None),
            P("shard", None),
            P("rep", "shard"),
            P("rep", "shard"),
            P("rep", "shard"),
            P("rep", "shard"),
            P("rep", "shard", None),
            P(("rep", "shard")),
            P(("rep", "shard")),
        ),
        out_specs=(
            P(None, "shard"),
            P(None, "shard"),
            P("rep", "shard"),
            P("rep", "shard"),
            P("rep", None, "shard"),
            P("rep", None, "shard"),
            P(),
            P(("rep", "shard")),
        ),
        check_vma=False,
    )
```

profile of v0, /device:TPU:0, one launch (start us, length us, event | category | flops | bytes accessed | tf_op | source)
XLA Modules:
  0.0 561.3 jit_solution(7325687698584000244)
XLA Ops:
  7.2 2.0 add.54
  9.2 1.6 fusion.15
  11.0 0.7 copy-done.8
  11.6 1.6 fusion.6
  13.3 129.5 %all-reduce.13.cloned.1.call-done = (f32[1152,32]{0,1:T(8,128)}, f32[1152,32]{0,1:T(8,128)}) async-done(((f32[1152,32]{0,1:T(8,128)}, f32[1152,32]{0,1:T(8,128)}), (f32[1152,32]{0,1:T(8,128)}, f32[1152,32]{0,1:T(8,128)})) %all-reduce.13.cloned.1.call-update) | async-done | bytes 294928 | tf_op jit(solution)/shard_map/psum | solution.py:46
  142.8 1.3 fusion.45
  144.1 2.8 fusion.4
  146.8 1.9 fusion.13
  149.0 2.9 cholesky.96
  152.0 0.6 compare_reduce_fusion.1
  152.6 0.7 fusion.24
  153.4 2.9 cholesky.74
  156.3 0.6 compare_reduce_fusion.3
  157.0 0.7 fusion.22
  157.7 2.4 custom-call.15
  160.1 2.5 custom-call.12
  162.6 65.3 %all-reduce.17.cloned.1.call-done = (f32[32,288]{1,0:T(8,128)}, f32[32,288]{1,0:T(8,128)}) async-done(((f32[32,288]{1,0:T(8,128)}, f32[32,288]{1,0:T(8,128)}), (f32[32,288]{1,0:T(8,128)}, f32[32,288]{1,0:T(8,128)})) %all-reduce.17.cloned.1.call-update) | async-done | bytes 73744 | tf_op jit(solution)/shard_map/psum | solution.py:53
  227.9 1.0 fusion.30
  228.9 1.6 fusion.2
  230.8 1.6 fusion.11
  232.6 127.2 %all-reduce.11.cloned.1.call-done = (f32[1152,32]{0,1:T(8,128)}, f32[1152,32]{0,1:T(8,128)}) async-done(((f32[1152,32]{0,1:T(8,128)}, f32[1152,32]{0,1:T(8,128)}), (f32[1152,32]{0,1:T(8,128)}, f32[1152,32]{0,1:T(8,128)})) %all-reduce.11.cloned.1.call-update) | async-done | bytes 294928 | tf_op jit(solution)/shard_map/psum | solution.py:46
  359.9 1.3 fusion.43
  361.1 2.8 fusion.9
  363.9 1.9 fusion
  366.1 2.9 cholesky.85
  369.1 0.6 compare_reduce_fusion.2
  369.7 0.7 fusion.23
  370.4 2.4 custom-call.13
  372.8 0.4 fusion.20
  373.3 2.9 cholesky.107
  376.2 0.6 compare_reduce_fusion
  376.9 0.7 fusion.25
  377.5 2.5 custom-call.16
  380.4 70.4 %all-reduce.15.cloned.1.call-done = (f32[32,288]{1,0:T(8,128)}, f32[32,288]{1,0:T(8,128)}) async-done(((f32[32,288]{1,0:T(8,128)}, f32[32,288]{1,0:T(8,128)}), (f32[32,288]{1,0:T(8,128)}, f32[32,288]{1,0:T(8,128)})) %all-reduce.15.cloned.1.call-update) | async-done | bytes 73744 | tf_op jit(solution)/shard_map/psum | solution.py:53
  450.8 1.0 fusion.33
  451.8 1.0 fusion.26
  452.9 1.2 fusion.44
  454.1 1.2 fusion.47
  455.4 1.1 copy-done.2
  456.8 1.9 multiply_subtract_fusion.1
  458.9 1.8 multiply_subtract_fusion
  460.8 40.2 %all-reduce.1 = f32[2304]{0:T(1024)S(1)} all-reduce(f32[2304]{0:T(1024)S(1)} %reduce.4), channel_id=2, replica_groups=mesh['rep'=8,'shard'=4] {'rep','shard'}, use_global_device_ids=true, to_apply=%region_10.14.clone | all-reduce | flops 2304 | bytes 18432
  501.0 0.6 subtract_dynamic-update-slice_fusion
  501.6 40.6 %all-reduce = f32[2304]{0:T(1024)} all-reduce(f32[2304]{0:T(1024)S(1)} %get-tuple-element.43), channel_id=1, replica_groups=mesh['rep'=8,'shard'=4] {'rep','shard'}, use_global_device_ids=true, to_apply=%add | all-reduce | flops 2304 | bytes 18432
  542.3 3.5 fusion.8
  545.7 3.1 copy.51
  548.8 2.6 all-gather.5.cloned.1.call-done
  551.4 3.0 copy.52
  (59 shorter events, 2.8 us)
Async XLA Ops:
  7.2 2.0 copy-start
  7.2 135.6 %all-reduce.13.cloned.1.call-start = ((), (), s32[]{:S(2)}) async-start(), calls=%async_computation.3 | async-start | bytes 589824 | tf_op jit(solution)/shard_map/psum | solution.py:46
  7.2 3.6 copy-start.7
  9.2 1.6 copy-start.6
  10.8 0.8 copy-start.8
  13.2 214.6 %all-reduce.17.cloned.1.call-start = ((), (), s32[]{:S(2)}) async-start(), calls=%async_computation.5 | async-start | bytes 196608 | tf_op jit(solution)/shard_map/psum | solution.py:53
  142.8 4.1 copy-start.5
  157.0 202.9 %all-reduce.11.cloned.1.call-start = ((), (), s32[]{:S(2)}) async-start(), calls=%async_computation.2 | async-start | bytes 589824 | tf_op jit(solution)/shard_map/psum | solution.py:46
  227.9 2.7 copy-start.9
  232.4 218.4 %all-reduce.15.cloned.1.call-start = ((), (), s32[]{:S(2)}) async-start(), calls=%async_computation.4 | async-start | bytes 196608 | tf_op jit(solution)/shard_map/psum | solution.py:53
  359.8 4.1 copy-start.3
  363.9 8.9 %copy-start.4 = (f32[1152,32]{0,1:T(8,128)S(1)}, f32[1152,32]{0,1:T(8,128)}, u32[]{:S(2)}) copy-start(f32[1152,32]{0,1:T(8,128)} %get-tuple-element.35) | copy-start | bytes 442372
  380.0 165.7 %all-gather.3.cloned.1.call-start = ((), (), s32[]{:S(2)}) async-start(), calls=%async_computation | async-start | bytes 1990656 | tf_op jit(solution)/shard_map/all_gather | solution.py:72
  454.1 2.6 copy-start.1
  455.4 1.1 copy-start.2
  456.8 4.0 copy-start.10
  458.7 42.3 %copy-start.11 = (f32[72]{0:T(128)S(1)}, f32[72]{0:T(128)}, u32[]{:S(2)}) copy-start(f32[72]{0:T(128)} %param.30) | copy-start | bytes 868
  458.7 42.3 %copy-start.12 = (f32[72]{0:T(128)S(1)}, f32[72]{0:T(128)}, u32[]{:S(2)}) copy-start(f32[72]{0:T(128)} %param.29) | copy-start | bytes 868
  458.7 92.7 %all-gather.5.cloned.1.call-start = ((), (), s32[]{:S(2)}) async-start(), calls=%async_computation.1 | async-start | bytes 1990656 | tf_op jit(solution)/shard_map/all_gather | solution.py:73
Sparse Core Ops, SparseCore 0:
  14.0 128.6 all-reduce.12
  157.1 70.6 all-reduce.16
  234.8 125.0 all-reduce.10
  380.1 70.5 all-reduce.14
  458.8 44.8 all-gather.2
  505.8 45.6 all-gather.4
where the time goes:
time: 562 us; the launch traced here: 561 us
  waiting for transfers between devices  395 us (70%)
  blocking collectives  80.8 us (14%)
  other arithmetic  36.7 us (7%)
  matrix products  25.3 us (5%)
  between operations  14.4 us (3%)
  local copies, waits for them, and re-layouts  8.65 us (2%)
    psum x2, waiting for transfers between devices, per_device(): left_q, left_o = lax.psum((part_q, part_o), ('rep', 'shard'))  257 us
    psum x2, waiting for transfers between devices, per_device(): summed_q, summed_o = lax.psum((reduce_q, reduce_o), 'rep')  136 us
    unnamed x2, blocking collectives  80.8 us
    dot_general x14, matrix products, product(): return jnp.dot(left, right, precision=highest)  21.2 us
    another operation x8, other arithmetic, unwhiten(): return jax.scipy.linalg.solve_triangular(lower, factor.T, lower=True).T  12.4 us
  transfers between devices with their start and end apart: 6, of which 5 were waited for; matrix products, arithmetic and copies ran while one was open for 3% of the time, Pallas kernels for 0%

commit v1 on v0

v1 whole, which is shorter than its diff:
```python
import jax
import jax.numpy as jnp
from jax import lax
from jax.sharding import PartitionSpec as P

ROUNDS = 2
AXES = ("rep", "shard")

highest = lax.Precision.HIGHEST
decay_rate = 0.9
step_size = 0.1


def product(left, right):
    return jnp.dot(left, right, precision=highest)


def halves(count):
    masks = []
    mask = 1
    while mask < count:
        masks.append(mask)
        mask *= 2
    return masks


def swap(block, axis, mask, count):
    pairs = [(i, i ^ mask) for i in range(count)]
    return lax.ppermute(block, axis, pairs)


def sum_over(block, axis, count):
    for mask in halves(count):
        block = block + swap(block, axis, mask, count)
    return block


def sum_over_all(part, n_rep, n_shard):
    place = lax.axis_index("shard")
    bits = [(mask, (place & mask) != 0) for mask in halves(n_shard)]
    for mask, high in bits:
        half = part.shape[0] // 2
        low_rows, high_rows = part[:half], part[half:]
        keep = jnp.where(high, high_rows, low_rows)
        give = jnp.where(high, low_rows, high_rows)
        part = keep + swap(give, "shard", mask, n_shard)
    part = sum_over(part, "rep", n_rep)
    for mask, high in reversed(bits):
        other = swap(part, "shard", mask, n_shard)
        part = jnp.concatenate([jnp.where(high, other, part), jnp.where(high, part, other)], axis=0)
    return part


def per_device(n_rep, n_shard, q_grad, o_grad, q_error, o_error, q_basis, o_basis, q_moment, o_moment, q_weight, o_weight, norm_grads, norm_moment, norm_weight):
    rank = q_basis.shape[1]
    size = q_grad.shape[1]
    row_count = q_moment.shape[0]
    flat = norm_grads.shape[-1]
    share = norm_moment.shape[0]
    device = lax.axis_index("rep") * n_shard + lax.axis_index("shard")

    base = jnp.stack([q_weight - (step_size * decay_rate) * q_moment, o_weight - (step_size * decay_rate) * o_moment])
    bases = lax.all_gather(base, "rep", axis=0, tiled=False)

    corr_q = q_grad[0] + q_error[0]
    corr_o = o_grad[0] + o_error[0]

    grads = norm_grads.reshape(flat)
    placed = lax.dynamic_update_slice(-step_size * grads, lax.dynamic_slice(-step_size * grads, (device * share,), (share,)) + (norm_weight - (step_size * decay_rate) * norm_moment), (device * share,))
    lanes = 128
    extra = jnp.concatenate([grads.reshape(-1, lanes), placed.reshape(-1, lanes)], axis=0)
    extra_rows = extra.shape[0]
    extra = jnp.pad(extra, ((0, 2 * rank - extra_rows), (0, 0)))

    basis_q, basis_o = q_basis.T, o_basis.T
    for sweep in range(ROUNDS):
        part_q = lax.dot_general(basis_q, corr_q, (((1,), (1,)), ((), ())), precision=highest)
        part_o = lax.dot_general(basis_o, corr_o, (((1,), (1,)), ((), ())), precision=highest)
        part = jnp.concatenate([part_q, part_o], axis=0)
        if sweep == ROUNDS - 1:
            part = jnp.concatenate([part, extra], axis=1)
        left = sum_over_all(part, n_rep, n_shard)
        if sweep == ROUNDS - 1:
            extra_sum = left[:extra_rows, size:]
            left = left[:, :size]
        left_q, left_o = left[:rank], left[rank:]
        right = jnp.concatenate([product(left_q, corr_q), product(left_o, corr_o)], axis=0)
        right = sum_over(right, "rep", n_rep)
        both = left.reshape(2, rank, size)
        gram = jnp.einsum("pij,pkj->pik", both, both, precision=highest)
        lower = jnp.linalg.cholesky(gram)
        identity = jnp.broadcast_to(jnp.eye(rank, dtype=jnp.float32), (2, rank, rank))
        inverse = jax.scipy.linalg.solve_triangular(lower, identity, lower=True)
        basis_q = product(inverse[0], right[:rank])
        basis_o = product(inverse[1], right[rank:])
        if sweep == ROUNDS - 1:
            normal_q = product(inverse[0], left_q)
            normal_o = product(inverse[1], left_o)
    decoded_q = lax.dot_general(normal_q, basis_q, (((0,), (0,)), ((), ())), precision=highest)
    decoded_o = lax.dot_general(normal_o, basis_o, (((0,), (0,)), ((), ())), precision=highest)
    q_error_new = (corr_q - decoded_q)[None]
    o_error_new = (corr_o - decoded_o)[None]
    start = lax.axis_index("rep") * row_count
    slice_q = lax.dynamic_slice_in_dim(decoded_q, start, row_count, 0)
    slice_o = lax.dynamic_slice_in_dim(decoded_o, start, row_count, 0)
    q_moment_new = decay_rate * q_moment + slice_q
    o_moment_new = decay_rate * o_moment + slice_o
    q_weight_new = bases[:, 0].reshape(size, -1) - step_size * decoded_q
    o_weight_new = bases[:, 1].reshape(size, -1) - step_size * decoded_o
    half = extra_rows // 2
    norm_sum = extra_sum[:half].reshape(flat)
    norm_weight_new = extra_sum[half:].reshape(flat)
    norm_moment_new = decay_rate * norm_moment + lax.dynamic_slice(norm_sum, (device * share,), (share,))
    return (
        q_weight_new,
        o_weight_new,
        q_moment_new,
        o_moment_new,
        q_error_new,
        o_error_new,
        norm_weight_new,
        norm_moment_new,
    )


def solution(mesh):
    n_rep, n_shard = mesh.shape["rep"], mesh.shape["shard"]

    def whole(*arrays):
        return per_device(n_rep, n_shard, *arrays)

    return jax.shard_map(
        whole,
        mesh=mesh,
        in_specs=(
            P("rep", None, "shard"),
            P("rep", None, "shard"),
            P("rep", None, "shard"),
            P("rep", None, "shard"),
            P("shard", None),
            P("shard", None),
            P("rep", "shard"),
            P("rep", "shard"),
            P("rep", "shard"),
            P("rep", "shard"),
            P("rep", "shard", None),
            P(("rep", "shard")),
            P(("rep", "shard")),
        ),
        out_specs=(
            P(None, "shard"),
            P(None, "shard"),
            P("rep", "shard"),
            P("rep", "shard"),
            P("rep", None, "shard"),
            P("rep", None, "shard"),
            P(),
            P(("rep", "shard")),
        ),
        check_vma=False,
    )
```

time: 562 us -> 189 us (0.34)
  waiting for transfers between devices: 395 us -> 79.6 us
  blocking collectives: 80.8 us -> 0 us
  starting transfers between devices: 0.43 us -> 27.6 us
  matrix products: 25.3 us -> 13.6 us
  local copies, waits for them, and re-layouts: 8.65 us -> 16.2 us
    psum x4 -> x0, waiting for transfers between devices: 392 us -> none  [the longest x2 257 us: per_device(): left_q, left_o = lax.psum((part_q, part_o), ('rep', 'shard'))]
    unnamed x2 -> x0, blocking collectives: 80.8 us -> none
    ppermute x0 -> x20, waiting for transfers between devices: none -> 54.7 us  [swap(): return lax.ppermute(block, axis, pairs)]
    ppermute x0 -> x20, starting transfers between devices: none -> 27.5 us  [swap(): return lax.ppermute(block, axis, pairs)]
    all_gather x2 -> x1, waiting for transfers between devices: 2.64 us -> 24.9 us  [per_device(): bases = lax.all_gather(base, 'rep', axis=0, tiled=False)]
    dot_general x14 -> x10, matrix products: 21.2 us -> 6.18 us  [product(): return jnp.dot(left, right, precision=highest)]
    dot_general x0 -> x8, matrix products: none -> 6.93 us  [the longest x2 1.82 us: per_device(): lax.dot_general(basis_q, corr_q, (((1,), (1,)), ((), ())), precision=high...]
    another operation x0 -> x2, local copies, waits for them, and re-layouts: none -> 6.11 us  [the longest x1 3.06 us: per_device(): o_weight_new = bases[:, 1].reshape(size, -1) - step_size * decoded_o]
  transfers between devices with their start and end apart: 6 -> 21, of which waited for: 5 -> 18; matrix products, arithmetic and copies ran while one was open for 3% -> 17% of each run, Pallas kernels for 0% -> 0%
where the time goes in v1:
time: 189 us; the launch traced here: 188 us
  waiting for transfers between devices  79.6 us (42%)
  other arithmetic  36.7 us (19%)
  starting transfers between devices  27.6 us (15%)
  local copies, waits for them, and re-layouts  16.2 us (9%)
  between operations  14.6 us (8%)
  matrix products  13.6 us (7%)
    ppermute x20, waiting for transfers between devices, swap(): return lax.ppermute(block, axis, pairs)  54.7 us
    ppermute x20, starting transfers between devices, swap(): return lax.ppermute(block, axis, pairs)  27.5 us
    all_gather x1, waiting for transfers between devices, per_device(): bases = lax.all_gather(base, 'rep', axis=0, tiled=False)  24.9 us
    another operation x7, other arithmetic, per_device(): lower = jnp.linalg.cholesky(gram)  12.2 us
    another operation x5, other arithmetic, per_device(): inverse = jax.scipy.linalg.solve_triangular(lower, identity, lower=True)  9.98 us
    dot_general x10, matrix products, product(): return jnp.dot(left, right, precision=highest)  6.18 us
    unnamed x46, local copies, waits for them, and re-layouts  5.92 us
    slice x1, local copies, waits for them, and re-layouts, per_device(): o_weight_new = bases[:, 1].reshape(size, -1) - step_size * decoded_o  4.05 us
  transfers between devices with their start and end apart: 21, of which 18 were waited for; matrix products, arithmetic and copies ran while one was open for 17% of the time, Pallas kernels for 0%

profile of v1, /device:TPU:0, one launch (start us, length us, event | category | flops | bytes accessed | tf_op | source)
XLA Modules:
  0.0 188.3 jit_solution(9700708179838353414)
XLA Ops:
  7.2 2.0 %add.97 = f32[1,1152,288]{1,2,0:T(8,128)S(1)} add(f32[1,1152,288]{1,2,0:T(8,128)} %param.16, f32[1,1152,288]{1,2,0:T(8,128)} %param.18) | non-fusion elementwise | flops 331776 | bytes 3981312 | tf_op jit(solution)/shard_map/add | solution.py:65
  13.9 2.9 %collective-permute-start.1 = (f32[16,1152]{1,0:T(8,128)S(1)}, f32[16,1152]{1,0:T(8,128)S(1)}, u32[]{:S(2)}, u32[]{:S(2)}) collective-permute-start(f32[16,1152]{1,0:T(8,128)S(1)} %slice_select_fusion.2), channel_id=1, source_target_pairs={{0,2},{1,3},{2,0},{3,1},{4,6},{5,7},{6,4},{7,5},{8,10},{9,11},{10,... | collective-permute-start | bytes 221192 | tf_op jit(solution)/shard_map/ppermute | solution.py:29
  16.8 2.6 %collective-permute-done.1 = f32[16,1152]{1,0:T(8,128)S(1)} collective-permute-done((f32[16,1152]{1,0:T(8,128)S(1)}, f32[16,1152]{1,0:T(8,128)S(1)}, u32[]{:S(2)}, u32[]{:S(2)}) %collective-permute-start.1) | collective-permute-done | bytes 73760 | tf_op jit(solution)/shard_map/ppermute | solution.py:29
  19.4 1.9 collective-permute-start.2
  21.4 2.5 %collective-permute-done.2 = f32[16,1152]{1,0:T(8,128)S(1)} collective-permute-done((f32[16,1152]{1,0:T(8,128)S(1)}, f32[16,1152]{1,0:T(8,128)S(1)}, u32[]{:S(2)}, u32[]{:S(2)}) %collective-permute-start.2) | collective-permute-done | bytes 73760 | tf_op jit(solution)/shard_map/ppermute | solution.py:29
  23.9 1.9 %collective-permute-start.3 = (f32[16,1152]{1,0:T(8,128)S(1)}, f32[16,1152]{1,0:T(8,128)S(1)}, u32[]{:S(2)}, u32[]{:S(2)}) collective-permute-start(f32[16,1152]{1,0:T(8,128)S(1)} %add.101), channel_id=1, source_target_pairs={{0,8},{4,12},{8,0},{12,4},{16,24},{20,28},{24,16},{28,20},{1,9},{5... | collective-permute-start | bytes 221192 | tf_op jit(solution)/shard_map/ppermute | solution.py:29
  26.0 2.3 %collective-permute-done.3 = f32[16,1152]{1,0:T(8,128)S(1)} collective-permute-done((f32[16,1152]{1,0:T(8,128)S(1)}, f32[16,1152]{1,0:T(8,128)S(1)}, u32[]{:S(2)}, u32[]{:S(2)}) %collective-permute-start.3) | collective-permute-done | bytes 73760 | tf_op jit(solution)/shard_map/ppermute | solution.py:29
  28.3 3.7 %collective-permute-start.4 = (f32[16,1152]{1,0:T(8,128)S(1)}, f32[16,1152]{1,0:T(8,128)S(1)}, u32[]{:S(2)}, u32[]{:S(2)}) collective-permute-start(f32[16,1152]{1,0:T(8,128)S(1)} %add.102), channel_id=1, source_target_pairs={{0,16},{4,20},{8,24},{12,28},{16,0},{20,4},{24,8},{28,12},{1,17},{... | collective-permute-start | bytes 221192 | tf_op jit(solution)/shard_map/ppermute | solution.py:29
  32.0 3.1 %collective-permute-done.4 = f32[16,1152]{1,0:T(8,128)S(1)} collective-permute-done((f32[16,1152]{1,0:T(8,128)S(1)}, f32[16,1152]{1,0:T(8,128)S(1)}, u32[]{:S(2)}, u32[]{:S(2)}) %collective-permute-start.4) | collective-permute-done | bytes 73760 | tf_op jit(solution)/shard_map/ppermute | solution.py:29
  35.1 1.6 collective-permute-start.5
  36.7 2.9 %collective-permute-done.5 = f32[16,1152]{1,0:T(8,128)S(1)} collective-permute-done((f32[16,1152]{1,0:T(8,128)S(1)}, f32[16,1152]{1,0:T(8,128)S(1)}, u32[]{:S(2)}, u32[]{:S(2)}) %collective-permute-start.5) | collective-permute-done | bytes 73760 | tf_op jit(solution)/shard_map/ppermute | solution.py:29
  39.7 1.3 collective-permute-done.6
  41.0 1.2 fusion.4
  42.3 1.2 fusion.13
  44.0 6.0 %custom-call.8 = f32[2,32,32]{2,1,0:T(8,128)S(1)} custom-call(f32[2,32,32]{2,1,0:T(8,128)S(1)} %fusion.38), custom_call_target="Cholesky" | custom-call | tf_op jit(solution)/shard_map/jit(cholesky)/cholesky | solution.py:91
  50.1 1.6 collective-permute-start.7
  51.9 3.2 %collective-permute-done.7 = f32[64,288]{1,0:T(8,128)S(1)} collective-permute-done((f32[64,288]{1,0:T(8,128)S(1)}, f32[64,288]{1,0:T(8,128)S(1)}, u32[]{:S(2)}, u32[]{:S(2)}) %collective-permute-start.7) | collective-permute-done | bytes 73760 | tf_op jit(solution)/shard_map/ppermute | solution.py:29
  55.7 4.9 %custom-call.9 = f32[2,1,32,32]{2,3,1,0:T(8,128)S(1)} custom-call(f32[2,1,32,32]{3,2,1,0:T(8,128)S(1)} %select_bitcast_fusion.2), custom_call_target="InvertDiagBlocksLowerTriangular" | custom-call | tf_op jit(solution)/shard_map/jit(_solve_triangular)/vmap()/triangular_solve | solution.py:93
  60.6 3.3 %collective-permute-start.9 = (f32[64,288]{1,0:T(8,128)S(1)}, f32[64,288]{1,0:T(8,128)S(1)}, u32[]{:S(2)}, u32[]{:S(2)}) collective-permute-start(f32[64,288]{1,0:T(8,128)S(1)} %add.105), channel_id=1, source_target_pairs={{0,16},{4,20},{8,24},{12,28},{16,0},{20,4},{24,8},{28,12},{1,17},{... | collective-permute-start | bytes 221192 | tf_op jit(solution)/shard_map/ppermute | solution.py:29
  64.2 3.9 %collective-permute-done.9 = f32[64,288]{1,0:T(8,128)S(1)} collective-permute-done((f32[64,288]{1,0:T(8,128)S(1)}, f32[64,288]{1,0:T(8,128)S(1)}, u32[]{:S(2)}, u32[]{:S(2)}) %collective-permute-start.9) | collective-permute-done | bytes 73760 | tf_op jit(solution)/shard_map/ppermute | solution.py:29
  70.4 1.4 collective-permute-done.10
  71.9 1.5 collective-permute-start.11
  73.4 3.0 %collective-permute-done.11 = f32[16,1280]{1,0:T(8,128)S(1)} collective-permute-done((f32[16,1280]{1,0:T(8,128)S(1)}, f32[16,1280]{1,0:T(8,128)S(1)}, u32[]{:S(2)}, u32[]{:S(2)}) %collective-permute-start.11) | collective-permute-done | bytes 81952 | tf_op jit(solution)/shard_map/ppermute | solution.py:29
  76.4 1.6 collective-permute-start.12
  78.0 2.9 %collective-permute-done.12 = f32[16,1280]{1,0:T(8,128)S(1)} collective-permute-done((f32[16,1280]{1,0:T(8,128)S(1)}, f32[16,1280]{1,0:T(8,128)S(1)}, u32[]{:S(2)}, u32[]{:S(2)}) %collective-permute-start.12) | collective-permute-done | bytes 81952 | tf_op jit(solution)/shard_map/ppermute | solution.py:29
  81.0 4.4 %collective-permute-done.13 = f32[16,1280]{1,0:T(8,128)S(1)} collective-permute-done((f32[16,1280]{1,0:T(8,128)S(1)}, f32[16,1280]{1,0:T(8,128)S(1)}, u32[]{:S(2)}, u32[]{:S(2)}) %collective-permute-start.13) | collective-permute-done | bytes 81952 | tf_op jit(solution)/shard_map/ppermute | solution.py:29
  85.5 2.1 %collective-permute-start.14 = (f32[16,1280]{1,0:T(8,128)S(1)}, f32[16,1280]{1,0:T(8,128)S(1)}, u32[]{:S(2)}, u32[]{:S(2)}) collective-permute-start(f32[16,1280]{1,0:T(8,128)S(1)} %add.113), channel_id=1, source_target_pairs={{0,16},{4,20},{8,24},{12,28},{16,0},{20,4},{24,8},{28,12},{1,17},{... | collective-permute-start | bytes 245768 | tf_op jit(solution)/shard_map/ppermute | solution.py:29
  87.6 3.9 %collective-permute-done.14 = f32[16,1280]{1,0:T(8,128)S(1)} collective-permute-done((f32[16,1280]{1,0:T(8,128)S(1)}, f32[16,1280]{1,0:T(8,128)S(1)}, u32[]{:S(2)}, u32[]{:S(2)}) %collective-permute-start.14) | collective-permute-done | bytes 81952 | tf_op jit(solution)/shard_map/ppermute | solution.py:29
  91.4 1.6 collective-permute-start.15
  93.0 3.0 %collective-permute-done.15 = f32[16,1280]{1,0:T(8,128)S(1)} collective-permute-done((f32[16,1280]{1,0:T(8,128)S(1)}, f32[16,1280]{1,0:T(8,128)S(1)}, u32[]{:S(2)}, u32[]{:S(2)}) %collective-permute-start.15) | collective-permute-done | bytes 81952 | tf_op jit(solution)/shard_map/ppermute | solution.py:29
  98.6 1.0 broadcast_select_fusion
  99.7 1.2 fusion.9
  100.9 1.2 fusion
  102.8 1.5 collective-permute-start.17
  104.9 5.9 %custom-call.10 = f32[2,32,32]{2,1,0:T(8,128)S(1)} custom-call(f32[2,32,32]{2,1,0:T(8,128)S(1)} %fusion.35), custom_call_target="Cholesky" | custom-call | tf_op jit(solution)/shard_map/jit(cholesky)/cholesky | solution.py:91
  111.0 4.9 %custom-call.11 = f32[2,1,32,32]{2,3,1,0:T(8,128)S(1)} custom-call(f32[2,1,32,32]{3,2,1,0:T(8,128)S(1)} %select_bitcast_fusion.1), custom_call_target="InvertDiagBlocksLowerTriangular" | custom-call | tf_op jit(solution)/shard_map/jit(_solve_triangular)/vmap()/triangular_solve | solution.py:93
  118.4 7.6 %collective-permute-done.18 = f32[64,288]{1,0:T(8,128)S(1)} collective-permute-done((f32[64,288]{1,0:T(8,128)S(1)}, f32[64,288]{1,0:T(8,128)S(1)}, u32[]{:S(2)}, u32[]{:S(2)}) %collective-permute-start.18) | collective-permute-done | bytes 73760 | tf_op jit(solution)/shard_map/ppermute | solution.py:29
  127.5 5.9 %collective-permute-done.19 = f32[64,288]{1,0:T(8,128)S(1)} collective-permute-done((f32[64,288]{1,0:T(8,128)S(1)}, f32[64,288]{1,0:T(8,128)S(1)}, u32[]{:S(2)}, u32[]{:S(2)}) %collective-permute-start.19) | collective-permute-done | bytes 73760 | tf_op jit(solution)/shard_map/ppermute | solution.py:29
  133.7 1.2 fusion.53
  135.0 1.2 fusion.54
  136.2 1.2 copy-done.1
  138.3 1.8 copy.66
  140.9 24.9 %all-gather.3.cloned.1.call-done = f32[16,144,288]{2,1,0:T(8,128)} async-done(((f32[2,144,288]{2,1,0:T(8,128)}), f32[16,144,288]{2,1,0:T(8,128)}) %all-gather.3.cloned.1.call-update) | async-done | bytes 2654224 | tf_op jit(solution)/shard_map/all_gather | solution.py:63
  165.8 4.1 %fusion.50 = (f32[8,1,144,288]{3,2,1,0:T(8,128)}, f32[8,1,144,288]{3,2,1,0:T(8,128)}) fusion(f32[8,2,144,288]{3,2,1,0:T(8,128)} %bitcast.105), kind=kLoop, calls=%fused_computation.104 | loop fusion | bytes 5308416 | tf_op jit(solution)/shard_map/slice | solution.py:109
  169.9 3.1 %copy.62 = f32[1152,288]{0,1:T(8,128)} copy(f32[1152,288]{1,0:T(8,128)} %bitcast.104) | data formatting | bytes 2654208 | tf_op jit(solution)/shard_map/reshape;squeeze | solution.py:109
  172.9 3.0 %copy.60 = f32[1152,288]{0,1:T(8,128)} copy(f32[1152,288]{1,0:T(8,128)} %bitcast.103) | data formatting | bytes 2654208 | tf_op jit(solution)/shard_map/reshape;squeeze | solution.py:108
  176.0 3.6 %fusion.8 = (f32[1,1152,288]{1,2,0:T(8,128)}, f32[1152,288]{0,1:T(8,128)}) fusion(f32[1152,288]{0,1:T(8,128)} %copy-done.3, f32[1,1152,288]{1,2,0:T(8,128)S(1)} %add.97, f32[1152,288]{0,1:T(8,128)} %copy.60), kind=kLoop, calls=%fused_computation.9 | loop fusion | flops 995328 | bytes 6635520 | tf_op jit(solution)/shard_map/broadcast_in_dim | solution.py:101
  179.6 1.8 fusion.17
  (124 shorter events, 19.3 us)
Async XLA Ops:
  7.2 2.0 %copy-start = (f32[288,32]{0,1:T(8,128)S(1)}, f32[288,32]{0,1:T(8,128)}, u32[]{:S(2)}) copy-start(f32[288,32]{0,1:T(8,128)} %param.20) | copy-start | bytes 110596
  7.2 158.6 %all-gather.3.cloned.1.call-start = ((), (), s32[]{:S(2)}) async-start(), calls=%async_computation | async-start | bytes 3981312 | tf_op jit(solution)/shard_map/all_gather | solution.py:63
  7.2 2.9 %copy-start.6 = (f32[1,1152,288]{1,2,0:T(8,128)S(1)}, f32[1,1152,288]{1,2,0:T(8,128)}, u32[]{:S(2)}) copy-start(f32[1,1152,288]{1,2,0:T(8,128)} %param.19) | copy-start | bytes 3981316
  9.2 1.4 copy-start.5
  10.6 0.8 copy-start.16
  11.4 9.9 %copy-start.17 = (f32[1,1,2304]{2,1,0:T(1,128)S(1)}, f32[1,1,2304]{2,1,0:T(1,128)}, u32[]{:S(2)}) copy-start(f32[1,1,2304]{2,1,0:T(1,128)} %param.26) | copy-start | bytes 27652
  11.4 14.4 %copy-start.18 = (f32[72]{0:T(128)S(1)}, f32[72]{0:T(128)}, u32[]{:S(2)}) copy-start(f32[72]{0:T(128)} %param.27) | copy-start | bytes 868
  11.4 14.4 %copy-start.20 = (f32[72]{0:T(128)S(1)}, f32[72]{0:T(128)}, u32[]{:S(2)}) copy-start(f32[72]{0:T(128)} %param.28) | copy-start | bytes 868
  12.3 1.5 collective-permute-start
  13.9 5.5 %collective-permute-start.1 = (f32[16,1152]{1,0:T(8,128)S(1)}, f32[16,1152]{1,0:T(8,128)S(1)}, u32[]{:S(2)}, u32[]{:S(2)}) collective-permute-start(f32[16,1152]{1,0:T(8,128)S(1)} %slice_select_fusion.2), channel_id=1, source_target_pairs={{0,2},{1,3},{2,0},{3,1},{4,6},{5,7},{6,4},{7,5},{8,10},{9,11},{10,... | collective-permute-start | bytes 221192 | tf_op jit(solution)/shard_map/ppermute | solution.py:29
  19.4 4.4 %collective-permute-start.2 = (f32[16,1152]{1,0:T(8,128)S(1)}, f32[16,1152]{1,0:T(8,128)S(1)}, u32[]{:S(2)}, u32[]{:S(2)}) collective-permute-start(f32[16,1152]{1,0:T(8,128)S(1)} %select_add_fusion.2), channel_id=1, source_target_pairs={{0,4},{4,0},{8,12},{12,8},{16,20},{20,16},{24,28},{28,24},{1,5},{5... | collective-permute-start | bytes 221192 | tf_op jit(solution)/shard_map/ppermute | solution.py:29
  23.9 4.4 %collective-permute-start.3 = (f32[16,1152]{1,0:T(8,128)S(1)}, f32[16,1152]{1,0:T(8,128)S(1)}, u32[]{:S(2)}, u32[]{:S(2)}) collective-permute-start(f32[16,1152]{1,0:T(8,128)S(1)} %add.101), channel_id=1, source_target_pairs={{0,8},{4,12},{8,0},{12,4},{16,24},{20,28},{24,16},{28,20},{1,9},{5... | collective-permute-start | bytes 221192 | tf_op jit(solution)/shard_map/ppermute | solution.py:29
  28.3 6.8 %collective-permute-start.4 = (f32[16,1152]{1,0:T(8,128)S(1)}, f32[16,1152]{1,0:T(8,128)S(1)}, u32[]{:S(2)}, u32[]{:S(2)}) collective-permute-start(f32[16,1152]{1,0:T(8,128)S(1)} %add.102), channel_id=1, source_target_pairs={{0,16},{4,20},{8,24},{12,28},{16,0},{20,4},{24,8},{28,12},{1,17},{... | collective-permute-start | bytes 221192 | tf_op jit(solution)/shard_map/ppermute | solution.py:29
  32.0 32.0 %copy-start.14 = (f32[32,32]{1,0:T(8,128)}, f32[32,32]{1,0:T(8,128)S(1)}, u32[]{:S(2)}) copy-start(f32[32,32]{1,0:T(8,128)S(1)} %fusion.42) | copy-start | bytes 12292
  35.1 4.4 %collective-permute-start.5 = (f32[16,1152]{1,0:T(8,128)S(1)}, f32[16,1152]{1,0:T(8,128)S(1)}, u32[]{:S(2)}, u32[]{:S(2)}) collective-permute-start(f32[16,1152]{1,0:T(8,128)S(1)} %add.103), channel_id=1, source_target_pairs={{0,2},{1,3},{2,0},{3,1},{4,6},{5,7},{6,4},{7,5},{8,10},{9,11},{10,... | collective-permute-start | bytes 221192 | tf_op jit(solution)/shard_map/ppermute | solution.py:29
  39.6 1.4 collective-permute-start.6
  50.1 4.9 %collective-permute-start.7 = (f32[64,288]{1,0:T(8,128)S(1)}, f32[64,288]{1,0:T(8,128)S(1)}, u32[]{:S(2)}, u32[]{:S(2)}) collective-permute-start(f32[64,288]{1,0:T(8,128)S(1)} %pad_maximum_fusion.5), channel_id=1, source_target_pairs={{0,4},{4,0},{8,12},{12,8},{16,20},{20,16},{24,28},{28,24},{1,5},{5... | collective-permute-start | bytes 221192 | tf_op jit(solution)/shard_map/ppermute | solution.py:29
  55.0 5.5 %collective-permute-start.8 = (f32[64,288]{1,0:T(8,128)S(1)}, f32[64,288]{1,0:T(8,128)S(1)}, u32[]{:S(2)}, u32[]{:S(2)}) collective-permute-start(f32[64,288]{1,0:T(8,128)S(1)} %fusion.48), channel_id=1, source_target_pairs={{0,8},{4,12},{8,0},{12,4},{16,24},{20,28},{24,16},{28,20},{1,9},{5... | collective-permute-start | bytes 221192 | tf_op jit(solution)/shard_map/ppermute | solution.py:29
  60.6 7.5 %collective-permute-start.9 = (f32[64,288]{1,0:T(8,128)S(1)}, f32[64,288]{1,0:T(8,128)S(1)}, u32[]{:S(2)}, u32[]{:S(2)}) collective-permute-start(f32[64,288]{1,0:T(8,128)S(1)} %add.105), channel_id=1, source_target_pairs={{0,16},{4,20},{8,24},{12,28},{16,0},{20,4},{24,8},{28,12},{1,17},{... | collective-permute-start | bytes 221192 | tf_op jit(solution)/shard_map/ppermute | solution.py:29
  70.3 26.4 %copy-start.8 = (f32[144,288]{1,0:T(8,128)S(1)}, f32[144,288]{1,0:T(8,128)}, u32[]{:S(2)}) copy-start(f32[144,288]{1,0:T(8,128)} %param.22) | copy-start | bytes 497668
  70.3 26.4 %copy-start.9 = (f32[144,288]{1,0:T(8,128)S(1)}, f32[144,288]{1,0:T(8,128)}, u32[]{:S(2)}) copy-start(f32[144,288]{1,0:T(8,128)} %param.23) | copy-start | bytes 497668
  70.3 26.4 %copy-start.12 = (f32[144,288]{1,0:T(8,128)S(1)}, f32[144,288]{1,0:T(8,128)}, u32[]{:S(2)}) copy-start(f32[144,288]{1,0:T(8,128)} %param.25) | copy-start | bytes 497668
  70.3 26.4 %copy-start.13 = (f32[144,288]{1,0:T(8,128)S(1)}, f32[144,288]{1,0:T(8,128)}, u32[]{:S(2)}) copy-start(f32[144,288]{1,0:T(8,128)} %param.24) | copy-start | bytes 497668
  70.4 1.5 collective-permute-start.10
  71.9 4.6 %collective-permute-start.11 = (f32[16,1280]{1,0:T(8,128)S(1)}, f32[16,1280]{1,0:T(8,128)S(1)}, u32[]{:S(2)}, u32[]{:S(2)}) collective-permute-start(f32[16,1280]{1,0:T(8,128)S(1)} %slice_select_fusion.1), channel_id=1, source_target_pairs={{0,2},{1,3},{2,0},{3,1},{4,6},{5,7},{6,4},{7,5},{8,10},{9,11},{10,... | collective-permute-start | bytes 245768 | tf_op jit(solution)/shard_map/ppermute | solution.py:29
  76.4 4.5 %collective-permute-start.12 = (f32[16,1280]{1,0:T(8,128)S(1)}, f32[16,1280]{1,0:T(8,128)S(1)}, u32[]{:S(2)}, u32[]{:S(2)}) collective-permute-start(f32[16,1280]{1,0:T(8,128)S(1)} %select_add_fusion.1), channel_id=1, source_target_pairs={{0,4},{4,0},{8,12},{12,8},{16,20},{20,16},{24,28},{28,24},{1,5},{5... | collective-permute-start | bytes 245768 | tf_op jit(solution)/shard_map/ppermute | solution.py:29
  81.0 4.5 %collective-permute-start.13 = (f32[16,1280]{1,0:T(8,128)S(1)}, f32[16,1280]{1,0:T(8,128)S(1)}, u32[]{:S(2)}, u32[]{:S(2)}) collective-permute-start(f32[16,1280]{1,0:T(8,128)S(1)} %add.112), channel_id=1, source_target_pairs={{0,8},{4,12},{8,0},{12,4},{16,24},{20,28},{24,16},{28,20},{1,9},{5... | collective-permute-start | bytes 245768 | tf_op jit(solution)/shard_map/ppermute | solution.py:29
  85.5 5.9 %collective-permute-start.14 = (f32[16,1280]{1,0:T(8,128)S(1)}, f32[16,1280]{1,0:T(8,128)S(1)}, u32[]{:S(2)}, u32[]{:S(2)}) collective-permute-start(f32[16,1280]{1,0:T(8,128)S(1)} %add.113), channel_id=1, source_target_pairs={{0,16},{4,20},{8,24},{12,28},{16,0},{20,4},{24,8},{28,12},{1,17},{... | collective-permute-start | bytes 245768 | tf_op jit(solution)/shard_map/ppermute | solution.py:29
  91.4 4.5 %collective-permute-start.15 = (f32[16,1280]{1,0:T(8,128)S(1)}, f32[16,1280]{1,0:T(8,128)S(1)}, u32[]{:S(2)}, u32[]{:S(2)}) collective-permute-start(f32[16,1280]{1,0:T(8,128)S(1)} %add.114), channel_id=1, source_target_pairs={{0,2},{1,3},{2,0},{3,1},{4,6},{5,7},{6,4},{7,5},{8,10},{9,11},{10,... | collective-permute-start | bytes 245768 | tf_op jit(solution)/shard_map/ppermute | solution.py:29
  96.0 1.6 copy-start.11
  96.0 1.6 copy-start.10
  96.7 1.9 %collective-permute-start.16 = (f32[32,1280]{1,0:T(8,128)}, f32[32,1280]{1,0:T(8,128)}, u32[]{:S(2)}, u32[]{:S(2)}) collective-permute-start(f32[32,1280]{1,0:T(8,128)} %pad_maximum_fusion.3), channel_id=1, source_target_pairs={{0,1},{1,0},{2,3},{3,2},{4,5},{5,4},{6,7},{7,6},{8,9},{9,8},{10,11... | collective-permute-start | bytes 491528 | tf_op jit(solution)/shard_map/ppermute | solution.py:29
  100.9 15.0 %copy-start.15 = (f32[32,32]{1,0:T(8,128)S(1)}, f32[32,32]{1,0:T(8,128)}, u32[]{:S(2)}) copy-start(f32[32,32]{1,0:T(8,128)} %copy-done.14) | copy-start | bytes 12292
  102.8 13.9 %collective-permute-start.17 = (f32[64,288]{1,0:T(8,128)}, f32[64,288]{1,0:T(8,128)}, u32[]{:S(2)}, u32[]{:S(2)}) collective-permute-start(f32[64,288]{1,0:T(8,128)} %pad_maximum_fusion.6), channel_id=1, source_target_pairs={{0,4},{4,0},{8,12},{12,8},{16,20},{20,16},{24,28},{28,24},{1,5},{5... | collective-permute-start | bytes 221192 | tf_op jit(solution)/shard_map/ppermute | solution.py:29
  104.4 22.5 %copy-start.19 = (f32[72]{0:T(128)S(1)}, f32[72]{0:T(128)}, u32[]{:S(2)}) copy-start(f32[72]{0:T(128)} %param.27) | copy-start | bytes 868
  117.6 8.4 %collective-permute-start.18 = (f32[64,288]{1,0:T(8,128)S(1)}, f32[64,288]{1,0:T(8,128)S(1)}, u32[]{:S(2)}, u32[]{:S(2)}) collective-permute-start(f32[64,288]{1,0:T(8,128)S(1)} %fusion.47), channel_id=1, source_target_pairs={{0,8},{4,12},{8,0},{12,4},{16,24},{20,28},{24,16},{28,20},{1,9},{5... | collective-permute-start | bytes 221192 | tf_op jit(solution)/shard_map/ppermute | solution.py:29
  126.0 7.3 %collective-permute-start.19 = (f32[64,288]{1,0:T(8,128)S(1)}, f32[64,288]{1,0:T(8,128)S(1)}, u32[]{:S(2)}, u32[]{:S(2)}) collective-permute-start(f32[64,288]{1,0:T(8,128)S(1)} %add.116), channel_id=1, source_target_pairs={{0,16},{4,20},{8,24},{12,28},{16,0},{20,4},{24,8},{28,12},{1,17},{... | collective-permute-start | bytes 221192 | tf_op jit(solution)/shard_map/ppermute | solution.py:29
  133.7 3.7 %copy-start.7 = (f32[144,288]{0,1:T(8,128)S(1)}, f32[144,288]{0,1:T(8,128)}, u32[]{:S(2)}) copy-start(f32[144,288]{0,1:T(8,128)} %copy.64) | copy-start | bytes 497668
  135.0 3.3 %copy-start.3 = (f32[1152,288]{0,1:T(8,128)}, f32[1152,288]{0,1:T(8,128)S(1)}, u32[]{:S(2)}) copy-start(f32[1152,288]{0,1:T(8,128)S(1)} %fusion.53) | copy-start | bytes 3981316
  136.2 1.2 copy-start.1
  176.0 3.6 %copy-start.2 = (f32[1152,288]{0,1:T(8,128)S(1)}, f32[1152,288]{0,1:T(8,128)}, u32[]{:S(2)}) copy-start(f32[1152,288]{0,1:T(8,128)} %copy-done.1) | copy-start | bytes 3981316
  176.0 3.6 %copy-start.4 = (f32[1152,288]{0,1:T(8,128)S(1)}, f32[1152,288]{0,1:T(8,128)}, u32[]{:S(2)}) copy-start(f32[1152,288]{0,1:T(8,128)} %copy.62) | copy-start | bytes 3981316
Sparse Core Ops, SparseCore 0:
  97.7 68.0 all-gather.2

commit v2 on v1

v2 whole, which is shorter than its diff:
```python
import functools

import jax
import jax.numpy as jnp
from jax import lax
from jax.experimental import pallas as pl
from jax.experimental.pallas import tpu as pltpu
from jax.sharding import PartitionSpec as P

ROUNDS = 2
GROUP = 8

highest = lax.Precision.HIGHEST
decay_rate = 0.9
step_size = 0.1
NT = (((1,), (1,)), ((), ()))
TN = (((0,), (0,)), ((), ()))


def product(left, right):
    return jnp.dot(left, right, precision=highest)


def halves(count):
    masks = []
    mask = 1
    while mask < count:
        masks.append(mask)
        mask *= 2
    return masks


def swap(block, axis, mask, count):
    pairs = [(i, i ^ mask) for i in range(count)]
    return lax.ppermute(block, axis, pairs)


def sum_over(block, count, gather, stage):
    for mask in halves(count):
        block = gather.before(block, stage, mask)
        block = block + swap(block, "rep", mask, count)
        block = gather.after(block, stage, mask)
    return block


def sum_over_all(part, n_rep, n_shard, gather, stage):
    place = lax.axis_index("shard")
    bits = [(mask, (place & mask) != 0) for mask in halves(n_shard)]
    for mask, high in bits:
        half = part.shape[0] // 2
        low_rows, high_rows = part[:half], part[half:]
        keep = jnp.where(high, high_rows, low_rows)
        give = jnp.where(high, low_rows, high_rows)
        part = keep + swap(give, "shard", mask, n_shard)
    part = sum_over(part, n_rep, gather, stage)
    for mask, high in reversed(bits):
        other = swap(part, "shard", mask, n_shard)
        part = jnp.concatenate([jnp.where(high, other, part), jnp.where(high, part, other)], axis=0)
    return part


class Gather:
    def __init__(self, own, count):
        self.count = count
        self.blocks = [own]
        self.turned = []
        self.paired = count == 8
        self.waiting = {}
        if self.paired:
            self.near = swap(own, "rep", 2, count)

    def before(self, value, stage, mask):
        if not self.paired:
            return value
        if (stage, mask) == (0, 2):
            value, self.near = lax.optimization_barrier((value, self.near))
        if (stage, mask) == (1, 1):
            value, first = lax.optimization_barrier((value, self.turned[0]))
            self.turned[0] = first
        if (stage, mask) == (1, 2):
            value, self.far = lax.optimization_barrier((value, self.far))
        if (stage, mask) == (2, 2):
            value, self.last = lax.optimization_barrier((value, self.last))
        if (stage, mask) == (3, 1):
            value, second = lax.optimization_barrier((value, self.turned[1]))
            self.turned[1] = second
        return value

    def after(self, value, stage, mask):
        if not self.paired:
            return value
        if (stage, mask) == (0, 1):
            value, pair = lax.optimization_barrier((value, jnp.concatenate([self.blocks[0], self.near])))
            self.pairs = [pair]
            self.turned.append(swap(pair, "rep", 1, self.count))
        if (stage, mask) == (0, 4):
            value, own = lax.optimization_barrier((value, self.blocks[0]))
            self.far = swap(own, "rep", 4, self.count)
        if (stage, mask) == (1, 4):
            value, near = lax.optimization_barrier((value, self.near))
            self.last = swap(near, "rep", 4, self.count)
        if (stage, mask) == (2, 1):
            value, pair = lax.optimization_barrier((value, jnp.concatenate([self.far, self.last])))
            self.pairs.append(pair)
            self.turned.append(swap(pair, "rep", 1, self.count))
        return value


def eliminate(gram_q, gram_o, rank):
    width = 4 * rank
    lane = lax.broadcasted_iota(jnp.int32, (rank, width), 1)
    row = lax.broadcasted_iota(jnp.int32, (rank, width), 0)
    square = (rank, rank)
    eye = (lax.broadcasted_iota(jnp.int32, square, 0) == lax.broadcasted_iota(jnp.int32, square, 1)).astype(jnp.float32)
    work = jnp.concatenate([gram_q, eye, gram_o, eye], axis=1)
    first = lane < 2 * rank
    scale = jnp.ones((rank, width), jnp.float32)
    for base in range(0, rank, GROUP):
        columns = []
        for k in range(base, base + GROUP):
            of_q = jnp.broadcast_to(work[:, k : k + 1], (rank, width))
            of_o = jnp.broadcast_to(work[:, 2 * rank + k : 2 * rank + k + 1], (rank, width))
            columns.append(jnp.where(first, of_q, of_o))
        for j in range(GROUP):
            k = base + j
            pivot = columns[j][k : k + 1]
            factor = jnp.where(row > k, columns[j] * (1.0 / pivot), 0.0)
            scale = jnp.where(row == k, pivot, scale)
            for i in range(j + 1, GROUP):
                columns[i] = columns[i] - factor * columns[i][k : k + 1]
            work = work - factor * work[k : k + 1]
    work = work * lax.rsqrt(scale)
    return work[:, rank : 2 * rank], work[:, 3 * rank :]


def inverse_kernel(rank, left_ref, inverse_ref, *normal_ref):
    left_q, left_o = left_ref[:rank, :], left_ref[rank:, :]
    gram_q = lax.dot_general(left_q, left_q, NT, precision=highest, preferred_element_type=jnp.float32)
    gram_o = lax.dot_general(left_o, left_o, NT, precision=highest, preferred_element_type=jnp.float32)
    inverse_q, inverse_o = eliminate(gram_q, gram_o, rank)
    inverse_ref[0] = inverse_q
    inverse_ref[1] = inverse_o
    if normal_ref:
        normal_q = jnp.dot(inverse_q, left_q, precision=highest, preferred_element_type=jnp.float32)
        normal_o = jnp.dot(inverse_o, left_o, precision=highest, preferred_element_type=jnp.float32)
        normal_ref[0][...] = jnp.concatenate([normal_q, normal_o], axis=0).T


def inverse_of(left, with_normal):
    rank, size = left.shape[0] // 2, left.shape[1]
    shapes = [jax.ShapeDtypeStruct((2, rank, rank), jnp.float32)]
    if with_normal:
        shapes.append(jax.ShapeDtypeStruct((size, 2 * rank), jnp.float32))
    cost = pl.CostEstimate(flops=20_000_000, bytes_accessed=left.size * 4, transcendentals=0)
    return pl.pallas_call(functools.partial(inverse_kernel, rank), out_shape=shapes, cost_estimate=cost, name="inverse")(left)


def finish_kernel(count, rank, place_ref, corr_q, corr_o, normal, inverse, right, moment_q, moment_o, *refs):
    pairs, outs, z_ref = refs[: count // 2], refs[count // 2 : -1], refs[-1]
    weight_q, weight_o, new_moment_q, new_moment_o, error_q, error_o = outs
    step = pl.program_id(0)

    @pl.when(step == 0)
    def _():
        z_ref[0] = jnp.dot(inverse[0], right[:rank, :], precision=highest, preferred_element_type=jnp.float32)
        z_ref[1] = jnp.dot(inverse[1], right[rank:, :], precision=highest, preferred_element_type=jnp.float32)

    normal_q, normal_o = normal[:, :rank], normal[:, rank:]
    decoded_q = jnp.dot(normal_q, z_ref[0], precision=highest, preferred_element_type=jnp.float32)
    decoded_o = jnp.dot(normal_o, z_ref[1], precision=highest, preferred_element_type=jnp.float32)
    error_q[0] = corr_q[...] - decoded_q
    error_o[0] = corr_o[...] - decoded_o
    for j, pair in enumerate(pairs):

        @pl.when(step // 2 == j)
        def _(pair=pair):
            weight_q[...] = pair[0] - step_size * decoded_q
            weight_o[...] = pair[1] - step_size * decoded_o

    @pl.when(step == 0)
    def _():
        new_moment_q[...] = decay_rate * moment_q[...] + decoded_q
        new_moment_o[...] = decay_rate * moment_o[...] + decoded_o


def finish(count, corr_q, corr_o, normal, inverse, right, moment_q, moment_o, pairs):
    size, width = corr_q.shape
    rows = moment_q.shape[0]
    rank = inverse.shape[1]
    place = lax.axis_index("rep").astype(jnp.int32).reshape(1)

    def block(k, place):
        return place[0] ^ ((2 * k) % count + (2 * k) // count)

    def by_rows(columns):
        return pl.BlockSpec((rows, columns), lambda k, place: (block(k, place), 0))

    def whole(shape):
        return pl.BlockSpec(shape, lambda k, place: (0,) * len(shape))

    def pair_spec(j):
        return pl.BlockSpec((2, rows, width), lambda k, place: (jnp.clip(k - 2 * j, 0, 1), 0, 0))

    error = pl.BlockSpec((1, rows, width), lambda k, place: (0, block(k, place), 0))
    f32 = functools.partial(jax.ShapeDtypeStruct, dtype=jnp.float32)
    return pl.pallas_call(
        functools.partial(finish_kernel, count, rank),
        grid_spec=pltpu.PrefetchScalarGridSpec(
            num_scalar_prefetch=1,
            grid=(count,),
            in_specs=[by_rows(width), by_rows(width), by_rows(2 * rank), whole(inverse.shape), whole(right.shape), whole(moment_q.shape), whole(moment_o.shape)]
            + [pair_spec(j) for j in range(count // 2)],
            out_specs=[by_rows(width), by_rows(width), whole(moment_q.shape), whole(moment_o.shape), error, error],
            scratch_shapes=[pltpu.VMEM((2, rank, width), jnp.float32)],
        ),
        out_shape=[f32((size, width)), f32((size, width)), f32((rows, width)), f32((rows, width)), f32((1, size, width)), f32((1, size, width))],
        compiler_params=pltpu.CompilerParams(vmem_limit_bytes=32 * 1024 * 1024),
        name="finish",
    )(place, corr_q, corr_o, normal, inverse, right, moment_q, moment_o, *pairs)


def finish_plain(corr_q, corr_o, normal, inverse, right, moment_q, moment_o, base):
    size = corr_q.shape[0]
    rows = moment_q.shape[0]
    rank = inverse.shape[1]
    decoded_q = product(normal[:, :rank], product(inverse[0], right[:rank]))
    decoded_o = product(normal[:, rank:], product(inverse[1], right[rank:]))
    start = lax.axis_index("rep") * rows
    moment_q = decay_rate * moment_q + lax.dynamic_slice_in_dim(decoded_q, start, rows, 0)
    moment_o = decay_rate * moment_o + lax.dynamic_slice_in_dim(decoded_o, start, rows, 0)
    bases = lax.all_gather(base, "rep", axis=1, tiled=True)
    weight_q, weight_o = bases[0] - step_size * decoded_q, bases[1] - step_size * decoded_o
    return weight_q, weight_o, moment_q, moment_o, (corr_q - decoded_q)[None], (corr_o - decoded_o)[None]


def per_device(n_rep, n_shard, q_grad, o_grad, q_error, o_error, q_basis, o_basis, q_moment, o_moment, q_weight, o_weight, norm_grads, norm_moment, norm_weight):
    rank = q_basis.shape[1]
    size = q_grad.shape[1]
    flat = norm_grads.shape[-1]
    share = norm_moment.shape[0]
    device = lax.axis_index("rep") * n_shard + lax.axis_index("shard")

    base = jnp.stack([q_weight - (step_size * decay_rate) * q_moment, o_weight - (step_size * decay_rate) * o_moment])
    gather = Gather(base, n_rep)

    corr_q = q_grad[0] + q_error[0]
    corr_o = o_grad[0] + o_error[0]

    grads = norm_grads.reshape(flat)
    placed = lax.dynamic_update_slice(-step_size * grads, lax.dynamic_slice(-step_size * grads, (device * share,), (share,)) + (norm_weight - (step_size * decay_rate) * norm_moment), (device * share,))
    lanes = 128
    extra = jnp.concatenate([grads.reshape(-1, lanes), placed.reshape(-1, lanes)], axis=0)
    extra_rows = extra.shape[0]
    extra = jnp.pad(extra, ((0, 2 * rank - extra_rows), (0, 0)))

    basis_q, basis_o = q_basis.T, o_basis.T
    for sweep in range(ROUNDS):
        part_q = lax.dot_general(basis_q, corr_q, NT, precision=highest)
        part_o = lax.dot_general(basis_o, corr_o, NT, precision=highest)
        part = jnp.concatenate([part_q, part_o], axis=0)
        if sweep == ROUNDS - 1:
            part = jnp.concatenate([part, extra], axis=1)
        left = sum_over_all(part, n_rep, n_shard, gather, 2 * sweep)
        if sweep == ROUNDS - 1:
            extra_sum = left[:extra_rows, size:]
            left = left[:, :size]
        right = jnp.concatenate([product(left[:rank], corr_q), product(left[rank:], corr_o)], axis=0)
        right = sum_over(right, n_rep, gather, 2 * sweep + 1)
        if sweep < ROUNDS - 1:
            (inverse,) = inverse_of(left, False)
            basis_q = product(inverse[0], right[:rank])
            basis_o = product(inverse[1], right[rank:])
    inverse, normal = inverse_of(left, True)
    if gather.paired:
        pairs = [pair.reshape((4,) + pair.shape[1:]) for pair in (gather.pairs + gather.turned)]
        outs = finish(n_rep, corr_q, corr_o, normal, inverse, right, q_moment, o_moment, pairs)
    else:
        outs = finish_plain(corr_q, corr_o, normal, inverse, right, q_moment, o_moment, base)
    q_weight_new, o_weight_new, q_moment_new, o_moment_new, q_error_new, o_error_new = outs
    half = extra_rows // 2
    norm_sum = extra_sum[:half].reshape(flat)
    norm_weight_new = extra_sum[half:].reshape(flat)
    norm_moment_new = decay_rate * norm_moment + lax.dynamic_slice(norm_sum, (device * share,), (share,))
    return (
        q_weight_new,
        o_weight_new,
        q_moment_new,
        o_moment_new,
        q_error_new,
        o_error_new,
        norm_weight_new,
        norm_moment_new,
    )


def solution(mesh):
    n_rep, n_shard = mesh.shape["rep"], mesh.shape["shard"]

    def whole(*arrays):
        return per_device(n_rep, n_shard, *arrays)

    return jax.shard_map(
        whole,
        mesh=mesh,
        in_specs=(
            P("rep", None, "shard"),
            P("rep", None, "shard"),
            P("rep", None, "shard"),
            P("rep", None, "shard"),
            P("shard", None),
            P("shard", None),
            P("rep", "shard"),
            P("rep", "shard"),
            P("rep", "shard"),
            P("rep", "shard"),
            P("rep", "shard", None),
            P(("rep", "shard")),
            P(("rep", "shard")),
        ),
        out_specs=(
            P(None, "shard"),
            P(None, "shard"),
            P("rep", "shard"),
            P("rep", "shard"),
            P("rep", None, "shard"),
            P("rep", None, "shard"),
            P(),
            P(("rep", "shard")),
        ),
        check_vma=False,
    )
```

time: 189 us -> 193 us (1.021)
  other arithmetic: 36.7 us -> 8.53 us
  waiting for transfers between devices: 79.6 us -> 95.3 us
  local copies, waits for them, and re-layouts: 16.2 us -> 30.1 us
  between operations: 14.6 us -> 1.13 us
  Pallas kernels: 0 us -> 12.2 us
  starting transfers between devices: 27.6 us -> 33.6 us
    ppermute x20 -> x25, waiting for transfers between devices: 54.7 us -> 95.3 us  [swap(): return lax.ppermute(block, axis, pairs)]
    all_gather x1 -> x0, waiting for transfers between devices: 24.9 us -> none  [per_device(): bases = lax.all_gather(base, 'rep', axis=0, tiled=False)]
    another operation x12 -> x0, other arithmetic: 22.2 us -> none  [the longest x7 12.2 us: per_device(): lower = jnp.linalg.cholesky(gram)]
    unnamed x46 -> x66, local copies, waits for them, and re-layouts: 5.92 us -> 25.1 us
    pallas_call x0 -> x3, Pallas kernels: none -> 12.2 us  [the longest x2 6.53 us: inverse_of(): pl.pallas_call(functools.partial(inverse_kernel, rank), out_shape=shapes,...]
    another operation x2 -> x0, local copies, waits for them, and re-layouts: 6.11 us -> none  [the longest x1 3.06 us: per_device(): o_weight_new = bases[:, 1].reshape(size, -1) - step_size * decoded_o]
    ppermute x20 -> x25, starting transfers between devices: 27.5 us -> 33.6 us  [swap(): return lax.ppermute(block, axis, pairs)]
    broadcast_in_dim x2 -> x0, other arithmetic: 5.42 us -> none  [the longest x1 3.58 us: per_device(): q_error_new = (corr_q - decoded_q)[None]]
  transfers between devices with their start and end apart: 21 -> 25, of which waited for: 18 -> 21; matrix products, arithmetic and copies ran while one was open for 17% -> 8% of each run, Pallas kernels for 0% -> 3%
where the time goes in v2:
time: 193 us
  waiting for transfers between devices  95.3 us (49%)
  starting transfers between devices  33.6 us (17%)
  local copies, waits for them, and re-layouts  30.1 us (16%)
  Pallas kernels  12.2 us (6%)
  matrix products  11.8 us (6%)
  other arithmetic  8.53 us (4%)
    ppermute x25, waiting for transfers between devices, swap(): return lax.ppermute(block, axis, pairs)  95.3 us
    ppermute x25, starting transfers between devices, swap(): return lax.ppermute(block, axis, pairs)  33.6 us
    unnamed x66, local copies, waits for them, and re-layouts  25.1 us
    dot_general x6, matrix products, product(): return jnp.dot(left, right, precision=highest)  8.17 us
    pallas_call x2, Pallas kernels, inverse_of(): pl.pallas_call(functools.partial(inverse_kernel, rank), out_shape=shapes,...  6.53 us
    pallas_call x1, Pallas kernels, finish(): pl.pallas_call(functools.partial(finish_kernel, count, rank), grid_spec=p...  5.71 us
  transfers between devices with their start and end apart: 25, of which 21 were waited for; matrix products, arithmetic and copies ran while one was open for 8% of the time, Pallas kernels for 3%

profile of v2, /device:TPU:0, one launch (start us, length us, event | category | flops | bytes accessed | tf_op | source)
XLA Modules:
  0.0 192.7 jit_solution(8482098134961907936)
XLA Ops:
  0.7 2.0 %add.74 = f32[1,1152,288]{1,2,0:T(8,128)S(1)} add(f32[1,1152,288]{1,2,0:T(8,128)} %param.13, f32[1,1152,288]{1,2,0:T(8,128)} %param.15) | non-fusion elementwise | flops 331776 | bytes 3981312 | tf_op jit(solution)/shard_map/add | solution.py:246
  8.3 2.9 %collective-permute-start.1 = (f32[16,1152]{1,0:T(8,128)S(1)}, f32[16,1152]{1,0:T(8,128)S(1)}, u32[]{:S(2)}, u32[]{:S(2)}) collective-permute-start(f32[16,1152]{1,0:T(8,128)S(1)} %slice_select_fusion.2), channel_id=1, source_target_pairs={{0,2},{1,3},{2,0},{3,1},{4,6},{5,7},{6,4},{7,5},{8,10},{9,11},{10,... | collective-permute-start | bytes 221192 | tf_op jit(solution)/shard_map/ppermute | solution.py:35
  11.2 1.6 collective-permute-start.3
  13.8 1.9 collective-permute-start.2
  15.6 2.6 %collective-permute-done.2 = f32[16,1152]{1,0:T(8,128)S(1)} collective-permute-done((f32[16,1152]{1,0:T(8,128)S(1)}, f32[16,1152]{1,0:T(8,128)S(1)}, u32[]{:S(2)}, u32[]{:S(2)}) %collective-permute-start.2) | collective-permute-done | bytes 73760 | tf_op jit(solution)/shard_map/ppermute | solution.py:35
  18.2 5.0 %collective-permute-done.3 = f32[2,144,288]{2,1,0:T(8,128)S(1)} collective-permute-done((f32[2,144,288]{2,1,0:T(8,128)S(1)}, f32[2,144,288]{2,1,0:T(8,128)S(1)}, u32[]{:S(2)}, u32[]{:S(2)}) %collective-permute-start.3) | collective-permute-done | bytes 331808 | tf_op jit(solution)/shard_map/ppermute | solution.py:35
  23.3 1.6 collective-permute-start.4
  24.9 2.8 %collective-permute-done.4 = f32[16,1152]{1,0:T(8,128)S(1)} collective-permute-done((f32[16,1152]{1,0:T(8,128)S(1)}, f32[16,1152]{1,0:T(8,128)S(1)}, u32[]{:S(2)}, u32[]{:S(2)}) %collective-permute-start.4) | collective-permute-done | bytes 73760 | tf_op jit(solution)/shard_map/ppermute | solution.py:35
  27.7 2.7 %collective-permute-start.5 = (f32[16,1152]{1,0:T(8,128)S(1)}, f32[16,1152]{1,0:T(8,128)S(1)}, u32[]{:S(2)}, u32[]{:S(2)}) collective-permute-start(f32[16,1152]{1,0:T(8,128)S(1)} %add.81), channel_id=1, source_target_pairs={{0,16},{4,20},{8,24},{12,28},{16,0},{20,4},{24,8},{28,12},{1,17},{... | collective-permute-start | bytes 221192 | tf_op jit(solution)/shard_map/ppermute | solution.py:35
  30.4 2.7 %collective-permute-done.5 = f32[16,1152]{1,0:T(8,128)S(1)} collective-permute-done((f32[16,1152]{1,0:T(8,128)S(1)}, f32[16,1152]{1,0:T(8,128)S(1)}, u32[]{:S(2)}, u32[]{:S(2)}) %collective-permute-start.5) | collective-permute-done | bytes 73760 | tf_op jit(solution)/shard_map/ppermute | solution.py:35
  33.5 4.0 %collective-permute-done.6 = f32[16,1152]{1,0:T(8,128)S(1)} collective-permute-done((f32[16,1152]{1,0:T(8,128)S(1)}, f32[16,1152]{1,0:T(8,128)S(1)}, u32[]{:S(2)}, u32[]{:S(2)}) %collective-permute-start.6) | collective-permute-done | bytes 73760 | tf_op jit(solution)/shard_map/ppermute | solution.py:35
  37.7 1.6 collective-permute-start.8
  39.2 2.7 %collective-permute-start.10 = (f32[2,144,288]{2,1,0:T(8,128)}, f32[2,144,288]{2,1,0:T(8,128)}, u32[]{:S(2)}, u32[]{:S(2)}) collective-permute-start(f32[2,144,288]{2,1,0:T(8,128)} %copy-done.24), channel_id=1, source_target_pairs={{0,16},{4,20},{8,24},{12,28},{16,0},{20,4},{24,8},{28,12},{1,17},{... | collective-permute-start | bytes 995336 | tf_op jit(solution)/shard_map/ppermute | solution.py:35
  44.5 15.3 %collective-permute-done.8.refs_2_ = f32[4,144,288]{2,1,0:T(8,128)S(1)} collective-permute-done((f32[4,144,288]{2,1,0:T(8,128)S(1)}, f32[4,144,288]{2,1,0:T(8,128)S(1)}, u32[]{:S(2)}, u32[]{:S(2)}) %collective-permute-start.8) | collective-permute-done | bytes 663584 | tf_op jit(solution)/shard_map/ppermute | solution.py:35
  60.7 1.5 collective-permute-start.9
  62.4 2.9 %collective-permute-done.9 = f32[64,288]{1,0:T(8,128)S(1)} collective-permute-done((f32[64,288]{1,0:T(8,128)S(1)}, f32[64,288]{1,0:T(8,128)S(1)}, u32[]{:S(2)}, u32[]{:S(2)}) %collective-permute-start.9) | collective-permute-done | bytes 73760 | tf_op jit(solution)/shard_map/ppermute | solution.py:35
  65.3 1.6 collective-permute-start.11
  67.0 3.0 %collective-permute-done.11 = f32[64,288]{1,0:T(8,128)S(1)} collective-permute-done((f32[64,288]{1,0:T(8,128)S(1)}, f32[64,288]{1,0:T(8,128)S(1)}, u32[]{:S(2)}, u32[]{:S(2)}) %collective-permute-start.11) | collective-permute-done | bytes 73760 | tf_op jit(solution)/shard_map/ppermute | solution.py:35
  70.0 2.9 %collective-permute-start.12 = (f32[64,288]{1,0:T(8,128)S(1)}, f32[64,288]{1,0:T(8,128)S(1)}, u32[]{:S(2)}, u32[]{:S(2)}) collective-permute-start(f32[64,288]{1,0:T(8,128)S(1)} %add.84), channel_id=1, source_target_pairs={{0,16},{4,20},{8,24},{12,28},{16,0},{20,4},{24,8},{28,12},{1,17},{... | collective-permute-start | bytes 221192 | tf_op jit(solution)/shard_map/ppermute | solution.py:35
  73.6 2.9 %inverse.2 = f32[2,32,32]{2,1,0:T(8,128)} custom-call(f32[64,1152]{1,0:T(8,128)} %pad_maximum_fusion.4.left_ref), custom_call_target="tpu_custom_call" | custom-call | flops 20000000 | bytes 294912 | tf_op jit(solution)/shard_map/inverse/pallas_call | solution.py:155
  80.4 1.4 collective-permute-done.13
  82.4 1.8 collective-permute-start.16
  84.3 2.1 %collective-permute-done.14 = f32[16,1280]{1,0:T(8,128)S(1)} collective-permute-done((f32[16,1280]{1,0:T(8,128)S(1)}, f32[16,1280]{1,0:T(8,128)S(1)}, u32[]{:S(2)}, u32[]{:S(2)}) %collective-permute-start.14) | collective-permute-done | bytes 81952 | tf_op jit(solution)/shard_map/ppermute | solution.py:35
  86.4 1.6 collective-permute-start.15
  88.0 2.9 %collective-permute-done.15 = f32[16,1280]{1,0:T(8,128)S(1)} collective-permute-done((f32[16,1280]{1,0:T(8,128)S(1)}, f32[16,1280]{1,0:T(8,128)S(1)}, u32[]{:S(2)}, u32[]{:S(2)}) %collective-permute-start.15) | collective-permute-done | bytes 81952 | tf_op jit(solution)/shard_map/ppermute | solution.py:35
  90.9 13.8 %collective-permute-done.16 = f32[2,144,288]{2,1,0:T(8,128)S(1)} collective-permute-done((f32[2,144,288]{2,1,0:T(8,128)S(1)}, f32[2,144,288]{2,1,0:T(8,128)S(1)}, u32[]{:S(2)}, u32[]{:S(2)}) %collective-permute-start.16) | collective-permute-done | bytes 331808 | tf_op jit(solution)/shard_map/ppermute | solution.py:35
  104.8 2.0 %pad_maximum_fusion.1.refs_1_ = f32[4,144,288]{2,1,0:T(8,128)} fusion(f32[2,144,288]{2,1,0:T(8,128)S(1)} %collective-permute-done.16, f32[2,144,288]{2,1,0:T(8,128)} %collective-permute-done.10), kind=kLoop, calls=%fused_computation.17 | loop fusion | flops 165888 | bytes 1327104 | tf_op jit(solution)/shard_map/concatenate | solution.py:103
  106.7 4.4 %collective-permute-done.17 = f32[16,1280]{1,0:T(8,128)S(1)} collective-permute-done((f32[16,1280]{1,0:T(8,128)S(1)}, f32[16,1280]{1,0:T(8,128)S(1)}, u32[]{:S(2)}, u32[]{:S(2)}) %collective-permute-start.17) | collective-permute-done | bytes 81952 | tf_op jit(solution)/shard_map/ppermute | solution.py:35
  111.2 1.6 collective-permute-start.18
  112.7 4.6 %collective-permute-done.18 = f32[16,1280]{1,0:T(8,128)S(1)} collective-permute-done((f32[16,1280]{1,0:T(8,128)S(1)}, f32[16,1280]{1,0:T(8,128)S(1)}, u32[]{:S(2)}, u32[]{:S(2)}) %collective-permute-start.18) | collective-permute-done | bytes 81952 | tf_op jit(solution)/shard_map/ppermute | solution.py:35
  117.3 1.6 collective-permute-start.19
  118.9 3.0 %collective-permute-done.19 = f32[16,1280]{1,0:T(8,128)S(1)} collective-permute-done((f32[16,1280]{1,0:T(8,128)S(1)}, f32[16,1280]{1,0:T(8,128)S(1)}, u32[]{:S(2)}, u32[]{:S(2)}) %collective-permute-start.19) | collective-permute-done | bytes 81952 | tf_op jit(solution)/shard_map/ppermute | solution.py:35
  121.9 1.9 copy.29
  123.8 3.1 %copy.30 = f32[1,1152,288]{2,1,0:T(8,128)} copy(f32[1,1152,288]{1,2,0:T(8,128)} %copy-done.19) | data formatting | bytes 2654208 | tf_op jit(solution)/shard_map/add | solution.py:247
  126.9 1.5 collective-permute-start.21
  129.4 2.6 %fusion.8 = f32[32,288]{1,0:T(8,128)S(1)} fusion(f32[1,1152,288]{1,2,0:T(8,128)} %copy-done.19, f32[32,1280]{1,0:T(8,128)S(1)} %get-tuple-element.76), kind=kOutput, calls=%fused_computation.8 | convolution fusion | flops 127401984 | bytes 1511424 | tf_op jit(solution)/shard_map/dot_general | solution.py:21
  133.2 16.0 %collective-permute-done.21.refs_3_ = f32[4,144,288]{2,1,0:T(8,128)S(1)} collective-permute-done((f32[4,144,288]{2,1,0:T(8,128)}, f32[4,144,288]{2,1,0:T(8,128)S(1)}, u32[]{:S(2)}, u32[]{:S(2)}) %collective-permute-start.21) | collective-permute-done | bytes 663584 | tf_op jit(solution)/shard_map/ppermute | solution.py:35
  150.1 1.5 collective-permute-start.22
  152.4 2.4 %collective-permute-done.22 = f32[64,288]{1,0:T(8,128)S(1)} collective-permute-done((f32[64,288]{1,0:T(8,128)S(1)}, f32[64,288]{1,0:T(8,128)S(1)}, u32[]{:S(2)}, u32[]{:S(2)}) %collective-permute-start.22) | collective-permute-done | bytes 73760 | tf_op jit(solution)/shard_map/ppermute | solution.py:35
  155.4 4.0 %collective-permute-done.23 = f32[64,288]{1,0:T(8,128)S(1)} collective-permute-done((f32[64,288]{1,0:T(8,128)S(1)}, f32[64,288]{1,0:T(8,128)S(1)}, u32[]{:S(2)}, u32[]{:S(2)}) %collective-permute-start.23) | collective-permute-done | bytes 73760 | tf_op jit(solution)/shard_map/ppermute | solution.py:35
  161.2 3.6 %inverse.3 = (f32[2,32,32]{2,1,0:T(8,128)}, f32[1152,64]{1,0:T(8,128)}) custom-call(f32[64,1152]{1,0:T(8,128)} %fusion.16.left_ref), custom_call_target="tpu_custom_call" | custom-call | flops 20000000 | bytes 294912 | tf_op jit(solution)/shard_map/inverse/pallas_call | solution.py:155
  165.7 1.5 copy-done.1
  172.5 5.7 %finish.1 = (f32[1152,288]{1,0:T(8,128)S(1)}, f32[1152,288]{1,0:T(8,128)S(1)}, f32[144,288]{1,0:T(8,128)}, f32[144,288]{1,0:T(8,128)}, f32[1,1152,288]{2,1,0:T(8,128)S(1)}, /*index=5*/f32[1,1152,288]{2,1,0:T(8,128)S(1)}) custom-call(s32[1]{0:T(128)} %bitcast.place_ref, f32[1152,288]{1,0:T(8,128)S(1)} %bitcast.57, f32[1152,288]{1,0:T(8,128)S(1)} %bitcast.58, ...), custom_call_target="tpu_custom_call" | custom-call | tf_op jit(solution)/shard_map/finish/pallas_call | solution.py:206
  178.2 1.3 copy-done.3
  183.2 3.2 %copy.31 = f32[1152,288]{0,1:T(8,128)} copy(f32[1152,288]{1,0:T(8,128)} %copy-done.8) | data formatting | bytes 2654208
  186.4 1.6 copy.32
  187.9 3.2 %copy.33 = f32[1,1152,288]{1,2,0:T(8,128)} copy(f32[1,1152,288]{2,1,0:T(8,128)} %copy-done.5) | data formatting | bytes 2654208
  191.1 1.6 copy.34
  (125 shorter events, 32.4 us)
Async XLA Ops:
  0.6 2.0 %copy-start = (f32[288,32]{0,1:T(8,128)S(1)}, f32[288,32]{0,1:T(8,128)}, u32[]{:S(2)}) copy-start(f32[288,32]{0,1:T(8,128)} %param.17) | copy-start | bytes 110596
  0.7 3.0 %copy-start.23 = (f32[1,1152,288]{1,2,0:T(8,128)S(1)}, f32[1,1152,288]{1,2,0:T(8,128)}, u32[]{:S(2)}) copy-start(f32[1,1152,288]{1,2,0:T(8,128)} %param.16) | copy-start | bytes 3981316
  2.6 75.8 %copy-start.17 = (f32[1,1152,288]{1,2,0:T(8,128)}, f32[1,1152,288]{1,2,0:T(8,128)S(1)}, u32[]{:S(2)}) copy-start(f32[1,1152,288]{1,2,0:T(8,128)S(1)} %add.74) | copy-start | bytes 3981316
  2.7 1.8 copy-start.22
  4.5 1.2 copy-start.27
  5.7 1.5 copy-start.13
  5.7 1.5 copy-start.14
  5.7 1.5 copy-start.25
  5.7 1.5 copy-start.26
  6.7 1.5 collective-permute-start
  8.3 5.5 %collective-permute-start.1 = (f32[16,1152]{1,0:T(8,128)S(1)}, f32[16,1152]{1,0:T(8,128)S(1)}, u32[]{:S(2)}, u32[]{:S(2)}) collective-permute-start(f32[16,1152]{1,0:T(8,128)S(1)} %slice_select_fusion.2), channel_id=1, source_target_pairs={{0,2},{1,3},{2,0},{3,1},{4,6},{5,7},{6,4},{7,5},{8,10},{9,11},{10,... | collective-permute-start | bytes 221192 | tf_op jit(solution)/shard_map/ppermute | solution.py:35
  11.2 7.0 %copy-start.24 = (f32[2,144,288]{2,1,0:T(8,128)}, f32[2,144,288]{2,1,0:T(8,128)S(1)}, u32[]{:S(2)}) copy-start(f32[2,144,288]{2,1,0:T(8,128)S(1)} %pad_maximum_fusion.2) | copy-start | bytes 995332
  11.2 12.0 %collective-permute-start.3 = (f32[2,144,288]{2,1,0:T(8,128)S(1)}, f32[2,144,288]{2,1,0:T(8,128)S(1)}, u32[]{:S(2)}, u32[]{:S(2)}) collective-permute-start(f32[2,144,288]{2,1,0:T(8,128)S(1)} %pad_maximum_fusion.2), channel_id=1, source_target_pairs={{0,8},{4,12},{8,0},{12,4},{16,24},{20,28},{24,16},{28,20},{1,9},{5... | collective-permute-start | bytes 995336 | tf_op jit(solution)/shard_map/ppermute | solution.py:35
  13.8 4.4 %collective-permute-start.2 = (f32[16,1152]{1,0:T(8,128)S(1)}, f32[16,1152]{1,0:T(8,128)S(1)}, u32[]{:S(2)}, u32[]{:S(2)}) collective-permute-start(f32[16,1152]{1,0:T(8,128)S(1)} %select_add_fusion.2), channel_id=1, source_target_pairs={{0,4},{4,0},{8,12},{12,8},{16,20},{20,16},{24,28},{28,24},{1,5},{5... | collective-permute-start | bytes 221192 | tf_op jit(solution)/shard_map/ppermute | solution.py:35
  18.2 19.4 %copy-start.28 = (f32[1,1,2304]{2,1,0:T(1,128)S(1)}, f32[1,1,2304]{2,1,0:T(1,128)}, u32[]{:S(2)}) copy-start(f32[1,1,2304]{2,1,0:T(1,128)} %param.23) | copy-start | bytes 27652
  23.3 4.4 %collective-permute-start.4 = (f32[16,1152]{1,0:T(8,128)S(1)}, f32[16,1152]{1,0:T(8,128)S(1)}, u32[]{:S(2)}, u32[]{:S(2)}) collective-permute-start(f32[16,1152]{1,0:T(8,128)S(1)} %add.80), channel_id=1, source_target_pairs={{0,8},{4,12},{8,0},{12,4},{16,24},{20,28},{24,16},{28,20},{1,9},{5... | collective-permute-start | bytes 221192 | tf_op jit(solution)/shard_map/ppermute | solution.py:35
  27.7 5.3 %collective-permute-start.5 = (f32[16,1152]{1,0:T(8,128)S(1)}, f32[16,1152]{1,0:T(8,128)S(1)}, u32[]{:S(2)}, u32[]{:S(2)}) collective-permute-start(f32[16,1152]{1,0:T(8,128)S(1)} %add.81), channel_id=1, source_target_pairs={{0,16},{4,20},{8,24},{12,28},{16,0},{20,4},{24,8},{28,12},{1,17},{... | collective-permute-start | bytes 221192 | tf_op jit(solution)/shard_map/ppermute | solution.py:35
  33.1 4.4 %collective-permute-start.6 = (f32[16,1152]{1,0:T(8,128)S(1)}, f32[16,1152]{1,0:T(8,128)S(1)}, u32[]{:S(2)}, u32[]{:S(2)}) collective-permute-start(f32[16,1152]{1,0:T(8,128)S(1)} %add.82), channel_id=1, source_target_pairs={{0,2},{1,3},{2,0},{3,1},{4,6},{5,7},{6,4},{7,5},{8,10},{9,11},{10,... | collective-permute-start | bytes 221192 | tf_op jit(solution)/shard_map/ppermute | solution.py:35
  33.5 9.7 %copy-start.20 = (f32[1,1152,288]{1,2,0:T(8,128)S(1)}, f32[1,1152,288]{1,2,0:T(8,128)}, u32[]{:S(2)}) copy-start(f32[1,1152,288]{1,2,0:T(8,128)} %copy-done.19) | copy-start | bytes 3981316
  37.5 4.4 %collective-permute-start.7 = (f32[32,1152]{1,0:T(8,128)S(1)}, f32[32,1152]{1,0:T(8,128)S(1)}, u32[]{:S(2)}, u32[]{:S(2)}) collective-permute-start(f32[32,1152]{1,0:T(8,128)S(1)} %pad_maximum_fusion.6), channel_id=1, source_target_pairs={{0,1},{1,0},{2,3},{3,2},{4,5},{5,4},{6,7},{7,6},{8,9},{9,8},{10,11... | collective-permute-start | bytes 442376 | tf_op jit(solution)/shard_map/ppermute | solution.py:35
  37.7 22.1 %collective-permute-start.8 = (f32[4,144,288]{2,1,0:T(8,128)S(1)}, f32[4,144,288]{2,1,0:T(8,128)S(1)}, u32[]{:S(2)}, u32[]{:S(2)}) collective-permute-start(f32[4,144,288]{2,1,0:T(8,128)S(1)} %pad_maximum_fusion.refs_0_), channel_id=1, source_target_pairs={{0,4},{4,0},{8,12},{12,8},{16,20},{20,16},{24,28},{28,24},{1,5},{5... | collective-permute-start | bytes 1990664 | tf_op jit(solution)/shard_map/ppermute | solution.py:35
  39.2 26.1 %collective-permute-start.10 = (f32[2,144,288]{2,1,0:T(8,128)}, f32[2,144,288]{2,1,0:T(8,128)}, u32[]{:S(2)}, u32[]{:S(2)}) collective-permute-start(f32[2,144,288]{2,1,0:T(8,128)} %copy-done.24), channel_id=1, source_target_pairs={{0,16},{4,20},{8,24},{12,28},{16,0},{20,4},{24,8},{28,12},{1,17},{... | collective-permute-start | bytes 995336 | tf_op jit(solution)/shard_map/ppermute | solution.py:35
  41.9 20.3 %copy-start.29 = (f32[72]{0:T(128)S(1)}, f32[72]{0:T(128)}, u32[]{:S(2)}) copy-start(f32[72]{0:T(128)} %param.24) | copy-start | bytes 868
  41.9 20.3 %copy-start.30 = (f32[72]{0:T(128)S(1)}, f32[72]{0:T(128)}, u32[]{:S(2)}) copy-start(f32[72]{0:T(128)} %param.25) | copy-start | bytes 868
  60.7 4.6 %collective-permute-start.9 = (f32[64,288]{1,0:T(8,128)S(1)}, f32[64,288]{1,0:T(8,128)S(1)}, u32[]{:S(2)}, u32[]{:S(2)}) collective-permute-start(f32[64,288]{1,0:T(8,128)S(1)} %pad_maximum_fusion.7), channel_id=1, source_target_pairs={{0,4},{4,0},{8,12},{12,8},{16,20},{20,16},{24,28},{28,24},{1,5},{5... | collective-permute-start | bytes 221192 | tf_op jit(solution)/shard_map/ppermute | solution.py:35
  65.3 4.7 %collective-permute-start.11 = (f32[64,288]{1,0:T(8,128)S(1)}, f32[64,288]{1,0:T(8,128)S(1)}, u32[]{:S(2)}, u32[]{:S(2)}) collective-permute-start(f32[64,288]{1,0:T(8,128)S(1)} %add.83), channel_id=1, source_target_pairs={{0,8},{4,12},{8,0},{12,4},{16,24},{20,28},{24,16},{28,20},{1,9},{5... | collective-permute-start | bytes 221192 | tf_op jit(solution)/shard_map/ppermute | solution.py:35
  70.0 6.5 %collective-permute-start.12 = (f32[64,288]{1,0:T(8,128)S(1)}, f32[64,288]{1,0:T(8,128)S(1)}, u32[]{:S(2)}, u32[]{:S(2)}) collective-permute-start(f32[64,288]{1,0:T(8,128)S(1)} %add.84), channel_id=1, source_target_pairs={{0,16},{4,20},{8,24},{12,28},{16,0},{20,4},{24,8},{28,12},{1,17},{... | collective-permute-start | bytes 221192 | tf_op jit(solution)/shard_map/ppermute | solution.py:35
  76.5 2.8 %copy-start.21 = (f32[1,1152,288]{1,2,0:T(8,128)S(1)}, f32[1,1152,288]{1,2,0:T(8,128)}, u32[]{:S(2)}) copy-start(f32[1,1152,288]{1,2,0:T(8,128)} %copy-done.19) | copy-start | bytes 3981316
  80.3 1.5 collective-permute-start.13
  81.8 4.6 %collective-permute-start.14 = (f32[16,1280]{1,0:T(8,128)S(1)}, f32[16,1280]{1,0:T(8,128)S(1)}, u32[]{:S(2)}, u32[]{:S(2)}) collective-permute-start(f32[16,1280]{1,0:T(8,128)S(1)} %slice_select_fusion.1), channel_id=1, source_target_pairs={{0,2},{1,3},{2,0},{3,1},{4,6},{5,7},{6,4},{7,5},{8,10},{9,11},{10,... | collective-permute-start | bytes 245768 | tf_op jit(solution)/shard_map/ppermute | solution.py:35
  82.4 22.3 %collective-permute-start.16 = (f32[2,144,288]{2,1,0:T(8,128)S(1)}, f32[2,144,288]{2,1,0:T(8,128)S(1)}, u32[]{:S(2)}, u32[]{:S(2)}) collective-permute-start(f32[2,144,288]{2,1,0:T(8,128)S(1)} %collective-permute-done.3), channel_id=1, source_target_pairs={{0,16},{4,20},{8,24},{12,28},{16,0},{20,4},{24,8},{28,12},{1,17},{... | collective-permute-start | bytes 995336 | tf_op jit(solution)/shard_map/ppermute | solution.py:35
  86.4 4.5 %collective-permute-start.15 = (f32[16,1280]{1,0:T(8,128)S(1)}, f32[16,1280]{1,0:T(8,128)S(1)}, u32[]{:S(2)}, u32[]{:S(2)}) collective-permute-start(f32[16,1280]{1,0:T(8,128)S(1)} %select_add_fusion.1), channel_id=1, source_target_pairs={{0,4},{4,0},{8,12},{12,8},{16,20},{20,16},{24,28},{28,24},{1,5},{5... | collective-permute-start | bytes 245768 | tf_op jit(solution)/shard_map/ppermute | solution.py:35
  106.7 4.4 %collective-permute-start.17 = (f32[16,1280]{1,0:T(8,128)S(1)}, f32[16,1280]{1,0:T(8,128)S(1)}, u32[]{:S(2)}, u32[]{:S(2)}) collective-permute-start(f32[16,1280]{1,0:T(8,128)S(1)} %add.91), channel_id=1, source_target_pairs={{0,8},{4,12},{8,0},{12,4},{16,24},{20,28},{24,16},{28,20},{1,9},{5... | collective-permute-start | bytes 245768 | tf_op jit(solution)/shard_map/ppermute | solution.py:35
  111.2 6.1 %collective-permute-start.18 = (f32[16,1280]{1,0:T(8,128)S(1)}, f32[16,1280]{1,0:T(8,128)S(1)}, u32[]{:S(2)}, u32[]{:S(2)}) collective-permute-start(f32[16,1280]{1,0:T(8,128)S(1)} %add.92), channel_id=1, source_target_pairs={{0,16},{4,20},{8,24},{12,28},{16,0},{20,4},{24,8},{28,12},{1,17},{... | collective-permute-start | bytes 245768 | tf_op jit(solution)/shard_map/ppermute | solution.py:35
  117.3 4.5 %collective-permute-start.19 = (f32[16,1280]{1,0:T(8,128)S(1)}, f32[16,1280]{1,0:T(8,128)S(1)}, u32[]{:S(2)}, u32[]{:S(2)}) collective-permute-start(f32[16,1280]{1,0:T(8,128)S(1)} %add.93), channel_id=1, source_target_pairs={{0,2},{1,3},{2,0},{3,1},{4,6},{5,7},{6,4},{7,5},{8,10},{9,11},{10,... | collective-permute-start | bytes 245768 | tf_op jit(solution)/shard_map/ppermute | solution.py:35
  121.9 6.6 %collective-permute-start.20 = (f32[32,1280]{1,0:T(8,128)S(1)}, f32[32,1280]{1,0:T(8,128)}, u32[]{:S(2)}, u32[]{:S(2)}) collective-permute-start(f32[32,1280]{1,0:T(8,128)S(1)} %pad_maximum_fusion.5), channel_id=1, source_target_pairs={{0,1},{1,0},{2,3},{3,2},{4,5},{5,4},{6,7},{7,6},{8,9},{9,8},{10,11... | collective-permute-start | bytes 491528 | tf_op jit(solution)/shard_map/ppermute | solution.py:35
  126.9 5.0 %copy-start.18 = (f32[1,1152,288]{1,2,0:T(8,128)S(1)}, f32[1,1152,288]{1,2,0:T(8,128)}, u32[]{:S(2)}) copy-start(f32[1,1152,288]{1,2,0:T(8,128)} %copy-done.17) | copy-start | bytes 3981316
  126.9 22.3 %collective-permute-start.21 = (f32[4,144,288]{2,1,0:T(8,128)}, f32[4,144,288]{2,1,0:T(8,128)S(1)}, u32[]{:S(2)}, u32[]{:S(2)}) collective-permute-start(f32[4,144,288]{2,1,0:T(8,128)} %pad_maximum_fusion.1.refs_1_), channel_id=1, source_target_pairs={{0,4},{4,0},{8,12},{12,8},{16,20},{20,16},{24,28},{28,24},{1,5},{5... | collective-permute-start | bytes 1990664 | tf_op jit(solution)/shard_map/ppermute | solution.py:35
  150.1 4.6 %collective-permute-start.22 = (f32[64,288]{1,0:T(8,128)S(1)}, f32[64,288]{1,0:T(8,128)S(1)}, u32[]{:S(2)}, u32[]{:S(2)}) collective-permute-start(f32[64,288]{1,0:T(8,128)S(1)} %pad_maximum_fusion.8), channel_id=1, source_target_pairs={{0,4},{4,0},{8,12},{12,8},{16,20},{20,16},{24,28},{28,24},{1,5},{5... | collective-permute-start | bytes 221192 | tf_op jit(solution)/shard_map/ppermute | solution.py:35
  154.7 4.7 %collective-permute-start.23 = (f32[64,288]{1,0:T(8,128)S(1)}, f32[64,288]{1,0:T(8,128)S(1)}, u32[]{:S(2)}, u32[]{:S(2)}) collective-permute-start(f32[64,288]{1,0:T(8,128)S(1)} %add.94), channel_id=1, source_target_pairs={{0,8},{4,12},{8,0},{12,4},{16,24},{20,28},{24,16},{28,20},{1,9},{5... | collective-permute-start | bytes 221192 | tf_op jit(solution)/shard_map/ppermute | solution.py:35
  159.4 6.3 %collective-permute-start.24 = (f32[64,288]{1,0:T(8,128)S(1)}, f32[64,288]{1,0:T(8,128)S(1)}, u32[]{:S(2)}, u32[]{:S(2)}) collective-permute-start(f32[64,288]{1,0:T(8,128)S(1)} %add.95), channel_id=1, source_target_pairs={{0,16},{4,20},{8,24},{12,28},{16,0},{20,4},{24,8},{28,12},{1,17},{... | collective-permute-start | bytes 221192 | tf_op jit(solution)/shard_map/ppermute | solution.py:35
  165.7 1.5 copy-start.1
  178.2 1.3 copy-start.3
  179.5 1.2 copy-start.5
  180.7 1.2 copy-start.6
  182.0 1.2 copy-start.8
  183.2 3.2 %copy-start.7 = (f32[1152,288]{1,0:T(8,128)S(1)}, f32[1152,288]{1,0:T(8,128)}, u32[]{:S(2)}) copy-start(f32[1152,288]{1,0:T(8,128)} %copy-done.6) | copy-start | bytes 3981316
  187.9 3.2 %copy-start.4 = (f32[1,1152,288]{2,1,0:T(8,128)S(1)}, f32[1,1152,288]{2,1,0:T(8,128)}, u32[]{:S(2)}) copy-start(f32[1,1152,288]{2,1,0:T(8,128)} %copy-done.3) | copy-start | bytes 3981316
  (8 other events, 8.2 us)

commit v3 on v1

v3 whole, which is shorter than its diff:
```python
import functools

import jax
import jax.numpy as jnp
from jax import lax
from jax.experimental import pallas as pl
from jax.experimental.pallas import tpu as pltpu
from jax.sharding import PartitionSpec as P

ROUNDS = 2
GROUP = 8
LANES = 128

highest = lax.Precision.HIGHEST
decay_rate = 0.9
step_size = 0.1
f32 = jnp.float32
bf16 = jnp.bfloat16
NN = (((1,), (0,)), ((), ()))
NT = (((1,), (1,)), ((), ()))
TN = (((0,), (0,)), ((), ()))
TT = (((0,), (1,)), ((), ()))

IN_HBM = pl.BlockSpec(memory_space=pltpu.HBM)
IN_VMEM = pl.BlockSpec(memory_space=pltpu.VMEM)
GRANT = pltpu.CompilerParams(vmem_limit_bytes=40 * 2**20)


def hold(space, *arrays):
    return [pltpu.with_memory_space_constraint(array, space) for array in arrays]


def exact(left, right, dims):
    return lax.dot_general(left, right, dims, precision=highest, preferred_element_type=f32)


def three(x):
    high = x.astype(bf16)
    rest = x - high.astype(f32)
    middle = rest.astype(bf16)
    low = (rest - middle.astype(f32)).astype(bf16)
    return high, middle, low


def stacked(left, right, dims):
    rows = left.shape[0]
    left_high, left_middle, left_low = three(left)
    right_high, right_middle, right_low = three(right)
    lefts = jnp.concatenate([left_high, left_middle, left_low], axis=0)
    of_high = lax.dot_general(lefts, right_high, dims, preferred_element_type=f32)
    of_middle = lax.dot_general(lefts[: 2 * rows], right_middle, dims, preferred_element_type=f32)
    of_low = lax.dot_general(left_high, right_low, dims, preferred_element_type=f32)
    small = (of_high[2 * rows :] + of_middle[rows:]) + of_low
    return of_high[:rows] + ((of_high[rows : 2 * rows] + of_middle[:rows]) + small)


def halves(count):
    masks = []
    mask = 1
    while mask < count:
        masks.append(mask)
        mask *= 2
    return masks


def swap(block, axis, mask, count):
    pairs = [(i, i ^ mask) for i in range(count)]
    return lax.ppermute(block, axis, pairs)


def sum_over(block, count, gather, stage):
    for mask in halves(count):
        block = gather.before(block, stage, mask)
        block = block + swap(block, "rep", mask, count)
        block = gather.after(block, stage, mask)
    return block


def sum_over_all(part, n_rep, n_shard, gather, stage):
    place = lax.axis_index("shard")
    bits = [(mask, (place & mask) != 0) for mask in halves(n_shard)]
    for mask, high in bits:
        half = part.shape[0] // 2
        low_rows, high_rows = part[:half], part[half:]
        keep = jnp.where(high, high_rows, low_rows)
        give = jnp.where(high, low_rows, high_rows)
        part = keep + swap(give, "shard", mask, n_shard)
    part = sum_over(part, n_rep, gather, stage)
    for mask, high in reversed(bits):
        other = swap(part, "shard", mask, n_shard)
        part = jnp.concatenate([jnp.where(high, other, part), jnp.where(high, part, other)], axis=0)
    return part


class Gather:
    PLAN = (
        ("turned", "own", 1, None, (0, 1)),
        ("near", "own", 2, None, (0, 2)),
        ("turned_near", "near", 1, (0, 2), (1, 1)),
        ("far", "own", 4, (0, 4), (1, 2)),
        ("turned_far", "far", 1, (1, 2), (2, 1)),
        ("last", "near", 4, (1, 4), (2, 2)),
        ("turned_last", "last", 1, (2, 2), (3, 1)),
    )
    PLACES = {"own": 0, "turned": 1, "near": 2, "far": 4, "last": 6, "turned_near": 3, "turned_far": 5, "turned_last": 7}

    def __init__(self, own, count):
        self.count = count
        self.blocks = {"own": own}
        self.paired = count == 8 and own.shape[0] % 8 == 0
        self.send(None)

    def send(self, point):
        if self.paired:
            for name, source, mask, after, _ in self.PLAN:
                if after == point:
                    self.blocks[name] = swap(self.blocks[source], "rep", mask, self.count)

    def before(self, value, stage, mask):
        if self.paired:
            for name, _, _, _, by in self.PLAN:
                if by == (stage, mask):
                    value, self.blocks[name] = lax.optimization_barrier((value, self.blocks[name]))
        return value

    def after(self, value, stage, mask):
        if self.paired:
            for name, source, _, after, _ in self.PLAN:
                if after == (stage, mask):
                    value, self.blocks[source] = lax.optimization_barrier((value, self.blocks[source]))
            self.send((stage, mask))
        return value

    def turned_rows(self):
        rows = None
        for names in (("own", "near"), ("turned", "turned_near"), ("far", "last"), ("turned_far",), ("turned_last",)):
            rows = insert(rows, [self.blocks[name] for name in names], [self.PLACES[name] for name in names], self.count)
        return rows


def insert_kernel(masks, place_ref, *refs):
    blocks, rows, out = refs[: len(masks)], refs[len(masks) : -1], refs[-1]
    if not rows:
        out[...] = jnp.zeros_like(out)
    height = out.shape[0]
    window = 2 * LANES
    lane = lax.broadcasted_iota(jnp.int32, (height, window), 1)
    for block, mask in zip(blocks, masks):
        count = block.shape[0]
        index = place_ref[0] ^ mask
        shift = index * (count - LANES)
        turned = jnp.concatenate([block[...].T, jnp.zeros((height, window - count), f32)], axis=1)
        turned = pltpu.roll(turned, shift, 1)
        at = pl.ds(pl.multiple_of(index * LANES, LANES), window)
        out[:, at] = jnp.where((lane >= shift) & (lane < shift + count), turned, out[:, at])


def insert(rows, blocks, masks, count):
    height, width = blocks[0].shape[1], blocks[0].shape[0] * count
    place = lax.axis_index("rep").astype(jnp.int32).reshape(1)
    old = [] if rows is None else hold(pltpu.VMEM, rows)
    return pl.pallas_call(
        functools.partial(insert_kernel, masks),
        in_specs=[pl.BlockSpec(memory_space=pltpu.SMEM)] + [IN_VMEM] * (len(blocks) + len(old)),
        out_specs=IN_VMEM,
        out_shape=pltpu.VMEM((height, width), f32),
        input_output_aliases={1 + len(blocks): 0} if old else {},
        cost_estimate=pl.CostEstimate(flops=1_000_000 * len(blocks), bytes_accessed=2_000_000 * len(blocks), transcendentals=0),
        name="insert",
    )(place, *blocks, *old)


def first_kernel(chunks, grad_q, grad_o, error_q, error_o, basis_q, basis_o, corr_q, corr_o, part, buffer, bases, sems, base_sems):
    rank, size = basis_q.shape[0], corr_q.shape[1]
    lanes = size // chunks
    base_copies = [pltpu.make_async_copy(source, bases.at[k], base_sems.at[k]) for k, source in enumerate((basis_q, basis_o))]
    copies = {}
    for copy in base_copies:
        copy.start()
    for c in range(chunks):
        at = pl.ds(c * lanes, lanes)
        for j, source in enumerate((grad_q, error_q, grad_o, error_o)):
            copies[c, j] = pltpu.make_async_copy(source.at[:, at], buffer.at[j, :, at], sems.at[c, j])
            copies[c, j].start()
    for copy in base_copies:
        copy.wait()
    for c in range(chunks):
        at = pl.ds(c * lanes, lanes)
        for k, corr in enumerate((corr_q, corr_o)):
            copies[c, 2 * k].wait()
            copies[c, 2 * k + 1].wait()
            total = buffer[2 * k, :, at] + buffer[2 * k + 1, :, at]
            corr[:, at] = total
            part[k * rank : (k + 1) * rank, at] = stacked(bases[k], total, NN)


def first(grads, errors, basis_q, basis_o):
    width, size = grads[0].shape
    rank = basis_q.shape[0]
    chunks = 3 if size % (3 * LANES) == 0 else 1
    return pl.pallas_call(
        functools.partial(first_kernel, chunks),
        in_specs=[IN_HBM] * 6,
        out_specs=[IN_VMEM] * 3,
        out_shape=[pltpu.VMEM((width, size), f32)] * 2 + [jax.ShapeDtypeStruct((2 * rank, size), f32)],
        scratch_shapes=[
            pltpu.VMEM((4, width, size), f32),
            pltpu.VMEM((2, rank, width), f32),
            pltpu.SemaphoreType.DMA((chunks, 4)),
            pltpu.SemaphoreType.DMA((2,)),
        ],
        compiler_params=GRANT,
        name="first",
    )(*hold(pltpu.HBM, *grads, *errors, basis_q, basis_o))


def right_kernel(left, corr_q, corr_o, out):
    rank = left.shape[0] // 2
    out[...] = jnp.concatenate([stacked(left[:rank, :], corr_q[...], NT), stacked(left[rank:, :], corr_o[...], NT)], axis=1)


def right_of(left, corr_q, corr_o):
    rank, width = left.shape[0] // 2, corr_q.shape[0]
    return pl.pallas_call(
        right_kernel,
        in_specs=[IN_VMEM] * 3,
        out_specs=IN_VMEM,
        out_shape=jax.ShapeDtypeStruct((rank, 2 * width), f32),
        compiler_params=GRANT,
        name="right",
    )(left, *hold(pltpu.VMEM, corr_q, corr_o))


def left_kernel(right, inverse, corr_q, corr_o, *refs):
    extra, out = refs[:-1], refs[-1]
    rank, width = right.shape[0], right.shape[1] // 2
    size = corr_q.shape[1]
    basis_q = exact(inverse[0], right[:, :width], NN)
    basis_o = exact(inverse[1], right[:, width:], NN)
    out[:rank, :size] = stacked(basis_q, corr_q[...], NN)
    out[rank:, :size] = stacked(basis_o, corr_o[...], NN)
    if extra:
        out[:, size:] = extra[0][...]


def left_of(right, inverse, corr_q, corr_o, extra):
    rank, size = right.shape[0], corr_q.shape[1]
    lanes = size + sum(array.shape[1] for array in extra)
    return pl.pallas_call(
        left_kernel,
        in_specs=[IN_VMEM] * (4 + len(extra)),
        out_specs=IN_VMEM,
        out_shape=jax.ShapeDtypeStruct((2 * rank, lanes), f32),
        compiler_params=GRANT,
        name="left",
    )(right, inverse, *hold(pltpu.VMEM, corr_q, corr_o), *extra)


def eliminate(gram_q, gram_o, rank):
    width = 4 * rank
    lane = lax.broadcasted_iota(jnp.int32, (rank, width), 1)
    row = lax.broadcasted_iota(jnp.int32, (rank, width), 0)
    square = (rank, rank)
    eye = (lax.broadcasted_iota(jnp.int32, square, 0) == lax.broadcasted_iota(jnp.int32, square, 1)).astype(f32)
    work = jnp.concatenate([gram_q, eye, gram_o, eye], axis=1)
    first_half = lane < 2 * rank
    scale = jnp.ones((rank, width), f32)
    for base in range(0, rank, GROUP):
        columns = []
        for k in range(base, base + GROUP):
            of_q = jnp.broadcast_to(work[:, k : k + 1], (rank, width))
            of_o = jnp.broadcast_to(work[:, 2 * rank + k : 2 * rank + k + 1], (rank, width))
            columns.append(jnp.where(first_half, of_q, of_o))
        for j in range(GROUP):
            k = base + j
            pivot = columns[j][k : k + 1]
            factor = jnp.where(row > k, columns[j] * (1.0 / pivot), 0.0)
            scale = jnp.where(row == k, pivot, scale)
            for i in range(j + 1, GROUP):
                columns[i] = columns[i] - factor * columns[i][k : k + 1]
            work = work - factor * work[k : k + 1]
    work = work * lax.rsqrt(scale)
    return work[:, rank : 2 * rank], work[:, 3 * rank :]


def inverse_kernel(left, out):
    rank, size = out.shape[1], left.shape[1]
    left_q, left_o = left[:rank, :], left[rank:, :]
    out[0], out[1] = eliminate(exact(left_q, left_q, NT), exact(left_o, left_o, NT), rank)


def inverse_of(left):
    rank = left.shape[0] // 2
    return pl.pallas_call(
        inverse_kernel,
        out_shape=jax.ShapeDtypeStruct((2, rank, rank), f32),
        cost_estimate=pl.CostEstimate(flops=20_000_000, bytes_accessed=left.size * 4, transcendentals=0),
        name="inverse",
    )(left)


def normal_kernel(left, inverse, normal, stack):
    rank = inverse.shape[1]
    for p in range(2):
        factor = exact(inverse[p], left[p * rank : (p + 1) * rank, :], NN)
        normal[p * rank : (p + 1) * rank, :] = factor
        high, middle, low = three(factor)
        stack[p] = jnp.concatenate([high, middle, low, high, middle, high], axis=0)


def normal_of(left, inverse):
    rank, size = inverse.shape[1], left.shape[1]
    return pl.pallas_call(
        normal_kernel,
        out_shape=[jax.ShapeDtypeStruct((2 * rank, size), f32), jax.ShapeDtypeStruct((2, 6 * rank, size), bf16)],
        cost_estimate=pl.CostEstimate(flops=20_000_000, bytes_accessed=left.size * 4, transcendentals=0),
        name="normal",
    )(left, inverse)


def finish_kernel(chunks, corr_q, corr_o, rows, stack, inverse, right, own, moment_q, moment_o, *refs):
    outs, buffer, new_moments, sems, moment_sems = refs[:6], refs[6], refs[7], refs[8], refs[9]
    rank, width = inverse.shape[1], moment_q.shape[1]
    height = width // chunks
    copies = []
    for p, corr in enumerate((corr_q, corr_o)):
        factor = right[:, p * width : (p + 1) * width]
        high, middle, low = three(exact(factor, inverse[p], TT))
        lefts = jnp.concatenate([high, high, high, middle, middle, low], axis=1)
        for c in range(chunks):
            at = pl.ds(c * height, height)
            decoded = lax.dot_general(lefts[c * height : (c + 1) * height], stack[p], NN, preferred_element_type=f32)
            buffer[p, at, :] = rows[pl.ds(p * width + c * height, height), :] - step_size * decoded
            buffer[2 + p, at, :] = corr[at, :] - decoded
            for k in (p, 2 + p):
                copies.append(pltpu.make_async_copy(buffer.at[k, at, :], outs[k].at[at, :], sems.at[k, c]))
                copies[-1].start()
    for p, moment in enumerate((moment_q, moment_o)):
        factor = right[:, p * width : (p + 1) * width]
        basis = exact(inverse[p], factor, NN)
        new_moments[p] = decay_rate * moment[...] + exact(own[p * rank : (p + 1) * rank, :], basis, TN)
        copies.append(pltpu.make_async_copy(new_moments.at[p], outs[4 + p], moment_sems.at[p]))
        copies[-1].start()
    for copy in copies:
        copy.wait()


def finish(corr_q, corr_o, rows, stack, inverse, right, own, moment_q, moment_o):
    width, size = corr_q.shape
    chunks = 3
    return pl.pallas_call(
        functools.partial(finish_kernel, chunks),
        in_specs=[IN_VMEM] * 9,
        out_specs=[IN_HBM] * 6,
        out_shape=[pltpu.HBM((width, size), f32)] * 4 + [pltpu.HBM(moment_q.shape, f32)] * 2,
        scratch_shapes=[
            pltpu.VMEM((4, width, size), f32),
            pltpu.VMEM((2,) + moment_q.shape, f32),
            pltpu.SemaphoreType.DMA((4, chunks)),
            pltpu.SemaphoreType.DMA((2,)),
        ],
        compiler_params=GRANT,
        name="finish",
    )(*hold(pltpu.VMEM, corr_q, corr_o, rows), stack, inverse, right, own, moment_q, moment_o)


def finish_plain(corr_q, corr_o, base, normal, inverse, right, moment_q, moment_o):
    rank, width = inverse.shape[1], moment_q.shape[1]
    rows = moment_q.shape[0]
    start = lax.axis_index("rep") * rows
    bases = lax.all_gather(base, "rep", axis=0, tiled=True)
    weights, moments, errors = [], [], []
    for p, (corr, moment) in enumerate(((corr_q, moment_q), (corr_o, moment_o))):
        at = slice(p * width, (p + 1) * width)
        basis = exact(inverse[p], right[:, at], NN)
        decoded = exact(basis, normal[p * rank : (p + 1) * rank], TN)
        weights.append(bases[:, at].T - step_size * decoded)
        moments.append(decay_rate * moment + lax.dynamic_slice_in_dim(decoded, start, rows, 1).T)
        errors.append(corr - decoded)
    return weights + errors + moments


def per_device(n_rep, n_shard, q_grad, o_grad, q_error, o_error, q_basis, o_basis, q_moment, o_moment, q_weight, o_weight, norm_grads, norm_moment, norm_weight):
    rank = q_basis.shape[1]
    size = q_grad.shape[1]
    flat = norm_grads.shape[-1]
    share = norm_moment.shape[0]
    row_count = q_moment.shape[0]
    device = lax.axis_index("rep") * n_shard + lax.axis_index("shard")
    keep = step_size * decay_rate

    base = jnp.concatenate([q_weight - keep * q_moment, o_weight - keep * o_moment], axis=1)
    gather = Gather(base, n_rep)

    grads = norm_grads.reshape(flat)
    own_grads = lax.dynamic_slice(grads, (device * share,), (share,))
    placed = lax.dynamic_update_slice(-step_size * grads, (norm_weight - keep * norm_moment) - step_size * own_grads, (device * share,))
    extra = jnp.concatenate([grads.reshape(-1, LANES), placed.reshape(-1, LANES)], axis=0)
    extra_rows = extra.shape[0]
    extra = jnp.pad(extra, ((0, 2 * rank - extra_rows), (0, 0)))

    corr_q, corr_o, part = first((q_grad[0].T, o_grad[0].T), (q_error[0].T, o_error[0].T), q_basis.T, o_basis.T)
    for sweep in range(ROUNDS):
        last = sweep == ROUNDS - 1
        left = sum_over_all(part, n_rep, n_shard, gather, 2 * sweep)
        if last:
            extra_sum = left[:extra_rows, size:]
            left = left[:, :size]
        right = right_of(left, corr_q, corr_o)
        inverse = inverse_of(left)
        right = sum_over(right, n_rep, gather, 2 * sweep + 1)
        if not last:
            part = left_of(right, inverse, corr_q, corr_o, [extra] if sweep == ROUNDS - 2 else [])
    normal, stack = normal_of(left, inverse)
    if gather.paired:
        own = lax.dynamic_slice_in_dim(normal, lax.axis_index("rep") * row_count, row_count, 1)
        outs = finish(corr_q, corr_o, gather.turned_rows(), stack, inverse, right, own, q_moment, o_moment)
    else:
        outs = finish_plain(corr_q, corr_o, base, normal, inverse, right, q_moment, o_moment)
    weight_q, weight_o, error_q, error_o, q_moment_new, o_moment_new = outs
    half = extra_rows // 2
    norm_sum = extra_sum[:half].reshape(flat)
    norm_weight_new = extra_sum[half:].reshape(flat)
    norm_moment_new = decay_rate * norm_moment + lax.dynamic_slice(norm_sum, (device * share,), (share,))
    return (
        weight_q.T,
        weight_o.T,
        q_moment_new,
        o_moment_new,
        error_q.T[None],
        error_o.T[None],
        norm_weight_new,
        norm_moment_new,
    )


def solution(mesh):
    n_rep, n_shard = mesh.shape["rep"], mesh.shape["shard"]

    def whole(*arrays):
        return per_device(n_rep, n_shard, *arrays)

    return jax.shard_map(
        whole,
        mesh=mesh,
        in_specs=(
            P("rep", None, "shard"),
            P("rep", None, "shard"),
            P("rep", None, "shard"),
            P("rep", None, "shard"),
            P("shard", None),
            P("shard", None),
            P("rep", "shard"),
            P("rep", "shard"),
            P("rep", "shard"),
            P("rep", "shard"),
            P("rep", "shard", None),
            P(("rep", "shard")),
            P(("rep", "shard")),
        ),
        out_specs=(
            P(None, "shard"),
            P(None, "shard"),
            P("rep", "shard"),
            P("rep", "shard"),
            P("rep", None, "shard"),
            P("rep", None, "shard"),
            P(),
            P(("rep", "shard")),
        ),
        check_vma=False,
    )
```

time: 189 us -> 156 us (0.83)
  Pallas kernels: 0 us -> 28.7 us
  other arithmetic: 36.7 us -> 9.54 us
  matrix products: 13.6 us -> 0 us
  between operations: 14.6 us -> 1.26 us
  local copies, waits for them, and re-layouts: 16.2 us -> 11.2 us
  waiting for transfers between devices: 79.6 us -> 76.9 us
    pallas_call x0 -> x13, Pallas kernels: none -> 28.7 us  [the longest x5 8.43 us: insert(): pl.pallas_call(functools.partial(insert_kernel, masks), in_specs=[pl.Bloc...]
    all_gather x1 -> x0, waiting for transfers between devices: 24.9 us -> none  [per_device(): bases = lax.all_gather(base, 'rep', axis=0, tiled=False)]
    another operation x14 -> x0, other arithmetic: 23.1 us -> none  [the longest x7 12.2 us: per_device(): lower = jnp.linalg.cholesky(gram)]
    ppermute x20 -> x27, waiting for transfers between devices: 54.7 us -> 76.9 us  [swap(): return lax.ppermute(block, axis, pairs)]
    dot_general x18 -> x0, matrix products: 13.1 us -> none  [the longest x10 6.18 us: product(): return jnp.dot(left, right, precision=highest)]
    another operation x2 -> x0, local copies, waits for them, and re-layouts: 6.11 us -> none  [the longest x1 3.06 us: per_device(): o_weight_new = bases[:, 1].reshape(size, -1) - step_size * decoded_o]
    broadcast_in_dim x2 -> x0, other arithmetic: 5.42 us -> none  [the longest x1 3.58 us: per_device(): q_error_new = (corr_q - decoded_q)[None]]
    slice x1 -> x0, local copies, waits for them, and re-layouts: 4.05 us -> none  [per_device(): o_weight_new = bases[:, 1].reshape(size, -1) - step_size * decoded_o]
  transfers between devices with their start and end apart: 21 -> 27, of which waited for: 18 -> 22; matrix products, arithmetic and copies ran while one was open for 17% -> 4% of each run, Pallas kernels for 0% -> 13%
where the time goes in v3:
time: 156 us; the launch traced here: 155 us
  waiting for transfers between devices  76.9 us (49%)
  Pallas kernels  28.7 us (18%)
  starting transfers between devices  27.7 us (18%)
  local copies, waits for them, and re-layouts  11.2 us (7%)
  other arithmetic  9.54 us (6%)
    ppermute x27, waiting for transfers between devices, swap(): return lax.ppermute(block, axis, pairs)  76.9 us
    ppermute x27, starting transfers between devices, swap(): return lax.ppermute(block, axis, pairs)  27.7 us
    unnamed x60, local copies, waits for them, and re-layouts  9.6 us
    pallas_call x5, Pallas kernels, insert(): pl.pallas_call(functools.partial(insert_kernel, masks), in_specs=[pl.Bloc...  8.43 us
    pallas_call x2, Pallas kernels, inverse_of(): pl.pallas_call(inverse_kernel, out_shape=jax.ShapeDtypeStruct((2, rank, r...  5.76 us
    pallas_call x1, Pallas kernels, first(): pl.pallas_call(functools.partial(first_kernel, chunks), in_specs=[IN_HBM]...  4.51 us
    pallas_call x1, Pallas kernels, finish(): pl.pallas_call(functools.partial(finish_kernel, chunks), in_specs=[IN_VME...  3.47 us
  transfers between devices with their start and end apart: 27, of which 22 were waited for; matrix products, arithmetic and copies ran while one was open for 4% of the time, Pallas kernels for 13%

profile of v3, /device:TPU:0, one launch (start us, length us, event | category | flops | bytes accessed | tf_op | source)
XLA Modules:
  0.0 155.3 jit_solution(1563767938184814491)
XLA Ops:
  0.7 4.5 %first.1 = (f32[288,1152]{1,0:T(8,128)S(1)}, f32[288,1152]{1,0:T(8,128)S(1)}, f32[64,1152]{1,0:T(8,128)S(1)}) custom-call(f32[288,1152]{1,0:T(8,128)} %bitcast.33, f32[288,1152]{1,0:T(8,128)} %bitcast.34, f32[288,1152]{1,0:T(8,128)} %bitcast.35, f32[288,1152]{1,0:T(8,128)} %bitcast.36, f32[32,288]{1,0:T(8,128)} %bitcast.37, f32[32,288]{1,0:T(8,128)} %bitcast.38), custom_call_target="tpu_custom_call" | custom-call | tf_op jit(solution)/shard_map/first/pallas_call | solution.py:201
  8.7 2.9 %collective-permute-start.1 = (f32[16,1152]{1,0:T(8,128)S(1)}, f32[16,1152]{1,0:T(8,128)S(1)}, u32[]{:S(2)}, u32[]{:S(2)}) collective-permute-start(f32[16,1152]{1,0:T(8,128)S(1)} %slice_select_fusion.3), channel_id=1, source_target_pairs={{0,2},{1,3},{2,0},{3,1},{4,6},{5,7},{6,4},{7,5},{8,10},{9,11},{10,... | collective-permute-start | bytes 221192 | tf_op jit(solution)/shard_map/ppermute | solution.py:68
  11.8 1.6 %collective-permute-start.4 = (f32[144,576]{1,0:T(8,128)S(1)}, f32[144,576]{1,0:T(8,128)S(1)}, u32[]{:S(2)}, u32[]{:S(2)}) collective-permute-start(f32[144,576]{1,0:T(8,128)S(1)} %pad_maximum_fusion.refs_0_), channel_id=1, source_target_pairs={{0,8},{4,12},{8,0},{12,4},{16,24},{20,28},{24,16},{28,20},{1,9},{5... | collective-permute-start | bytes 995336 | tf_op jit(solution)/shard_map/ppermute | solution.py:68
  13.4 1.5 collective-permute-start.2
  15.0 8.5 %collective-permute-done.2.refs_0_ = f32[144,576]{1,0:T(8,128)S(1)} collective-permute-done((f32[144,576]{1,0:T(8,128)S(1)}, f32[144,576]{1,0:T(8,128)S(1)}, u32[]{:S(2)}, u32[]{:S(2)}) %collective-permute-start.2) | collective-permute-done | bytes 331808 | tf_op jit(solution)/shard_map/ppermute | solution.py:68
  23.5 1.5 collective-permute-start.3
  25.0 2.8 %collective-permute-done.3 = f32[16,1152]{1,0:T(8,128)S(1)} collective-permute-done((f32[16,1152]{1,0:T(8,128)S(1)}, f32[16,1152]{1,0:T(8,128)S(1)}, u32[]{:S(2)}, u32[]{:S(2)}) %collective-permute-start.3) | collective-permute-done | bytes 73760 | tf_op jit(solution)/shard_map/ppermute | solution.py:68
  28.4 3.9 %collective-permute-done.5 = f32[16,1152]{1,0:T(8,128)S(1)} collective-permute-done((f32[16,1152]{1,0:T(8,128)S(1)}, f32[16,1152]{1,0:T(8,128)S(1)}, u32[]{:S(2)}, u32[]{:S(2)}) %collective-permute-start.5) | collective-permute-done | bytes 73760 | tf_op jit(solution)/shard_map/ppermute | solution.py:68
  32.3 2.7 %collective-permute-start.6 = (f32[16,1152]{1,0:T(8,128)S(1)}, f32[16,1152]{1,0:T(8,128)S(1)}, u32[]{:S(2)}, u32[]{:S(2)}) collective-permute-start(f32[16,1152]{1,0:T(8,128)S(1)} %add.67), channel_id=1, source_target_pairs={{0,16},{4,20},{8,24},{12,28},{16,0},{20,4},{24,8},{28,12},{1,17},{... | collective-permute-start | bytes 221192 | tf_op jit(solution)/shard_map/ppermute | solution.py:68
  35.0 3.3 %collective-permute-done.6 = f32[16,1152]{1,0:T(8,128)S(1)} collective-permute-done((f32[16,1152]{1,0:T(8,128)S(1)}, f32[16,1152]{1,0:T(8,128)S(1)}, u32[]{:S(2)}, u32[]{:S(2)}) %collective-permute-start.6) | collective-permute-done | bytes 73760 | tf_op jit(solution)/shard_map/ppermute | solution.py:68
  38.8 3.9 %collective-permute-done.7 = f32[16,1152]{1,0:T(8,128)S(1)} collective-permute-done((f32[16,1152]{1,0:T(8,128)S(1)}, f32[16,1152]{1,0:T(8,128)S(1)}, u32[]{:S(2)}, u32[]{:S(2)}) %collective-permute-start.7) | collective-permute-done | bytes 73760 | tf_op jit(solution)/shard_map/ppermute | solution.py:68
  43.4 1.5 collective-permute-start.9
  45.0 1.9 %collective-permute-start.11 = (f32[144,576]{1,0:T(8,128)S(1)}, f32[144,576]{1,0:T(8,128)S(1)}, u32[]{:S(2)}, u32[]{:S(2)}) collective-permute-start(f32[144,576]{1,0:T(8,128)S(1)} %pad_maximum_fusion.refs_0_), channel_id=1, source_target_pairs={{0,16},{4,20},{8,24},{12,28},{16,0},{20,4},{24,8},{28,12},{1,17},{... | collective-permute-start | bytes 995336 | tf_op jit(solution)/shard_map/ppermute | solution.py:68
  47.9 1.5 right.2
  49.4 5.0 %collective-permute-done.9.refs_1_ = f32[144,576]{1,0:T(8,128)S(1)} collective-permute-done((f32[144,576]{1,0:T(8,128)S(1)}, f32[144,576]{1,0:T(8,128)S(1)}, u32[]{:S(2)}, u32[]{:S(2)}) %collective-permute-start.9) | collective-permute-done | bytes 331808 | tf_op jit(solution)/shard_map/ppermute | solution.py:68
  54.4 1.5 collective-permute-start.10
  56.0 2.9 %collective-permute-done.10 = f32[32,576]{1,0:T(8,128)S(1)} collective-permute-done((f32[32,576]{1,0:T(8,128)S(1)}, f32[32,576]{1,0:T(8,128)S(1)}, u32[]{:S(2)}, u32[]{:S(2)}) %collective-permute-start.10) | collective-permute-done | bytes 73760 | tf_op jit(solution)/shard_map/ppermute | solution.py:68
  58.9 4.9 %collective-permute-done.11.refs_0_ = f32[144,576]{1,0:T(8,128)S(1)} collective-permute-done((f32[144,576]{1,0:T(8,128)S(1)}, f32[144,576]{1,0:T(8,128)S(1)}, u32[]{:S(2)}, u32[]{:S(2)}) %collective-permute-start.11) | collective-permute-done | bytes 331808 | tf_op jit(solution)/shard_map/ppermute | solution.py:68
  64.1 4.1 %collective-permute-done.12 = f32[32,576]{1,0:T(8,128)S(1)} collective-permute-done((f32[32,576]{1,0:T(8,128)S(1)}, f32[32,576]{1,0:T(8,128)S(1)}, u32[]{:S(2)}, u32[]{:S(2)}) %collective-permute-start.12) | collective-permute-done | bytes 73760 | tf_op jit(solution)/shard_map/ppermute | solution.py:68
  69.4 2.9 %inverse.2 = f32[2,32,32]{2,1,0:T(8,128)} custom-call(f32[64,1152]{1,0:T(8,128)} %copy-done.7), custom_call_target="tpu_custom_call" | custom-call | flops 20000000 | bytes 294912 | tf_op jit(solution)/shard_map/inverse/pallas_call | solution.py:294
  72.3 1.9 %collective-permute-done.13 = f32[32,576]{1,0:T(8,128)S(1)} collective-permute-done((f32[32,576]{1,0:T(8,128)S(1)}, f32[32,576]{1,0:T(8,128)S(1)}, u32[]{:S(2)}, u32[]{:S(2)}) %collective-permute-start.13) | collective-permute-done | bytes 73760 | tf_op jit(solution)/shard_map/ppermute | solution.py:68
  76.3 1.4 collective-permute-done.14
  79.4 2.9 %collective-permute-done.15 = f32[16,1280]{1,0:T(8,128)S(1)} collective-permute-done((f32[16,1280]{1,0:T(8,128)S(1)}, f32[16,1280]{1,0:T(8,128)S(1)}, u32[]{:S(2)}, u32[]{:S(2)}) %collective-permute-start.15) | collective-permute-done | bytes 81952 | tf_op jit(solution)/shard_map/ppermute | solution.py:68
  82.3 6.4 %collective-permute-done.16.refs_0_ = f32[144,576]{1,0:T(8,128)S(1)} collective-permute-done((f32[144,576]{1,0:T(8,128)S(1)}, f32[144,576]{1,0:T(8,128)S(1)}, u32[]{:S(2)}, u32[]{:S(2)}) %collective-permute-start.16) | collective-permute-done | bytes 331808 | tf_op jit(solution)/shard_map/ppermute | solution.py:68
  89.1 4.0 %collective-permute-done.17 = f32[16,1280]{1,0:T(8,128)S(1)} collective-permute-done((f32[16,1280]{1,0:T(8,128)S(1)}, f32[16,1280]{1,0:T(8,128)S(1)}, u32[]{:S(2)}, u32[]{:S(2)}) %collective-permute-start.17) | collective-permute-done | bytes 81952 | tf_op jit(solution)/shard_map/ppermute | solution.py:68
  93.1 4.2 %collective-permute-done.18.refs_1_ = f32[144,576]{1,0:T(8,128)S(1)} collective-permute-done((f32[144,576]{1,0:T(8,128)S(1)}, f32[144,576]{1,0:T(8,128)S(1)}, u32[]{:S(2)}, u32[]{:S(2)}) %collective-permute-start.18) | collective-permute-done | bytes 331808 | tf_op jit(solution)/shard_map/ppermute | solution.py:68
  97.4 4.4 %collective-permute-done.19 = f32[16,1280]{1,0:T(8,128)S(1)} collective-permute-done((f32[16,1280]{1,0:T(8,128)S(1)}, f32[16,1280]{1,0:T(8,128)S(1)}, u32[]{:S(2)}, u32[]{:S(2)}) %collective-permute-start.19) | collective-permute-done | bytes 81952 | tf_op jit(solution)/shard_map/ppermute | solution.py:68
  102.4 5.3 %collective-permute-done.20 = f32[16,1280]{1,0:T(8,128)S(1)} collective-permute-done((f32[16,1280]{1,0:T(8,128)S(1)}, f32[16,1280]{1,0:T(8,128)S(1)}, u32[]{:S(2)}, u32[]{:S(2)}) %collective-permute-start.20) | collective-permute-done | bytes 81952 | tf_op jit(solution)/shard_map/ppermute | solution.py:68
  107.8 1.6 %collective-permute-start.21 = (f32[16,1280]{1,0:T(8,128)S(1)}, f32[16,1280]{1,0:T(8,128)S(1)}, u32[]{:S(2)}, u32[]{:S(2)}) collective-permute-start(f32[16,1280]{1,0:T(8,128)S(1)} %add.78), channel_id=1, source_target_pairs={{0,2},{1,3},{2,0},{3,1},{4,6},{5,7},{6,4},{7,5},{8,10},{9,11},{10,... | collective-permute-start | bytes 245768 | tf_op jit(solution)/shard_map/ppermute | solution.py:68
  109.3 2.9 %collective-permute-done.21 = f32[16,1280]{1,0:T(8,128)S(1)} collective-permute-done((f32[16,1280]{1,0:T(8,128)S(1)}, f32[16,1280]{1,0:T(8,128)S(1)}, u32[]{:S(2)}, u32[]{:S(2)}) %collective-permute-start.21) | collective-permute-done | bytes 81952 | tf_op jit(solution)/shard_map/ppermute | solution.py:68
  113.0 1.9 %insert.5.refs_2_ = f32[576,1152]{1,0:T(8,128)S(1)} custom-call(s32[1]{0:T(128)} %bitcast.10.place_ref, f32[144,576]{1,0:T(8,128)} %copy-done.16, f32[144,576]{1,0:T(8,128)} %copy-done.17), custom_call_target="tpu_custom_call" | custom-call | flops 2000000 | bytes 4000000 | tf_op jit(solution)/shard_map/insert/pallas_call | solution.py:162
  114.9 1.9 %insert.6.refs_2_ = f32[576,1152]{1,0:T(8,128)S(1)} custom-call(s32[1]{0:T(128)} %bitcast.10.place_ref, f32[144,576]{1,0:T(8,128)} %copy-done.18, f32[144,576]{1,0:T(8,128)} %copy-done.21, f32[576,1152]{1,0:T(8,128)S(1)} %insert.5.refs_2_), custom_call_target="tpu_custom_call", output_to_operand_aliasing={{}: (3, {})} | custom-call | flops 2000000 | bytes 4000000 | tf_op jit(solution)/shard_map/insert/pallas_call | solution.py:162
  116.8 1.6 %collective-permute-start.23 = (f32[144,576]{1,0:T(8,128)S(1)}, f32[144,576]{1,0:T(8,128)S(1)}, u32[]{:S(2)}, u32[]{:S(2)}) collective-permute-start(f32[144,576]{1,0:T(8,128)S(1)} %copy-done.23), channel_id=1, source_target_pairs={{0,4},{4,0},{8,12},{12,8},{16,20},{20,16},{24,28},{28,24},{1,5},{5... | collective-permute-start | bytes 995336 | tf_op jit(solution)/shard_map/ppermute | solution.py:68
  118.4 1.8 %insert.7.refs_1_ = f32[576,1152]{1,0:T(8,128)S(1)} custom-call(s32[1]{0:T(128)} %bitcast.10.place_ref, f32[144,576]{1,0:T(8,128)} %copy-done.19, f32[144,576]{1,0:T(8,128)} %copy-done.22, f32[576,1152]{1,0:T(8,128)S(1)} %insert.6.refs_2_), custom_call_target="tpu_custom_call", output_to_operand_aliasing={{}: (3, {})} | custom-call | flops 2000000 | bytes 4000000 | tf_op jit(solution)/shard_map/insert/pallas_call | solution.py:162
  120.2 1.4 insert.8.refs_1_
  122.6 1.3 copy-done.1
  123.9 1.3 copy-done.4
  125.2 1.5 right.3
  127.9 1.5 collective-permute-start.24
  130.0 2.3 %collective-permute-done.24 = f32[32,576]{1,0:T(8,128)S(1)} collective-permute-done((f32[32,576]{1,0:T(8,128)S(1)}, f32[32,576]{1,0:T(8,128)S(1)}, u32[]{:S(2)}, u32[]{:S(2)}) %collective-permute-start.24) | collective-permute-done | bytes 73760 | tf_op jit(solution)/shard_map/ppermute | solution.py:68
  133.0 2.9 %inverse.3 = f32[2,32,32]{2,1,0:T(8,128)} custom-call(f32[64,1152]{1,0:T(8,128)} %copy-done.6), custom_call_target="tpu_custom_call" | custom-call | flops 20000000 | bytes 294912 | tf_op jit(solution)/shard_map/inverse/pallas_call | solution.py:294
  135.9 2.4 %normal.1 = (f32[64,1152]{1,0:T(8,128)}, bf16[2,192,1152]{2,1,0:T(8,128)(2,1)}) custom-call(f32[64,1152]{1,0:T(8,128)} %copy-done.6, f32[2,32,32]{2,1,0:T(8,128)} %inverse.3), custom_call_target="tpu_custom_call" | custom-call | flops 20000000 | bytes 294912 | tf_op jit(solution)/shard_map/normal/pallas_call | solution.py:313
  138.9 2.3 %collective-permute-start.26 = (f32[32,576]{1,0:T(8,128)}, f32[32,576]{1,0:T(8,128)}, u32[]{:S(2)}, u32[]{:S(2)}) collective-permute-start(f32[32,576]{1,0:T(8,128)} %add.80), channel_id=1, source_target_pairs={{0,16},{4,20},{8,24},{12,28},{16,0},{20,4},{24,8},{28,12},{1,17},{... | collective-permute-start | bytes 221192 | tf_op jit(solution)/shard_map/ppermute | solution.py:68
  141.2 1.6 %constant_dynamic-slice_fusion.own = f32[64,144]{1,0:T(8,128)} fusion(f32[64,1152]{1,0:T(8,128)} %get-tuple-element.71, s32[]{:T(128)S(6)} %select_n.109), kind=kLoop, calls=%fused_computation.34 | loop fusion | bytes 73732 | tf_op jit(solution)/shard_map/dynamic_slice | solution.py:416
  142.9 1.5 insert.9.rows
  145.5 1.3 copy-done.2
  146.8 1.3 copy-done.5
  151.6 3.5 %finish.1 = (f32[288,1152]{1,0:T(8,128)}, f32[288,1152]{1,0:T(8,128)}, f32[288,1152]{1,0:T(8,128)}, f32[288,1152]{1,0:T(8,128)}, f32[144,288]{1,0:T(8,128)}, /*index=5*/f32[144,288]{1,0:T(8,128)}) custom-call(f32[288,1152]{1,0:T(8,128)S(1)} %copy-done.2, f32[288,1152]{1,0:T(8,128)S(1)} %copy-done.5, f32[576,1152]{1,0:T(8,128)S(1)} %insert.9.rows, ...), custom_call_target="tpu_custom_call" | custom-call | tf_op jit(solution)/shard_map/finish/pallas_call | solution.py:351
  (115 shorter events, 22.2 us)
Async XLA Ops:
  0.6 5.8 %copy-start.9 = (f32[144,288]{1,0:T(8,128)S(1)}, f32[144,288]{1,0:T(8,128)}, u32[]{:S(2)}) copy-start(f32[144,288]{1,0:T(8,128)} %moment_o.1) | copy-start | bytes 497668
  0.7 5.8 %copy-start.11 = (f32[144,288]{1,0:T(8,128)S(1)}, f32[144,288]{1,0:T(8,128)}, u32[]{:S(2)}) copy-start(f32[144,288]{1,0:T(8,128)} %moment_q.1) | copy-start | bytes 497668
  5.2 69.0 %copy-start = (f32[288,1152]{1,0:T(8,128)}, f32[288,1152]{1,0:T(8,128)S(1)}, u32[]{:S(2)}) copy-start(f32[288,1152]{1,0:T(8,128)S(1)} %get-tuple-element.43.corr_q) | copy-start | bytes 3981316
  5.2 69.0 %copy-start.3 = (f32[288,1152]{1,0:T(8,128)}, f32[288,1152]{1,0:T(8,128)S(1)}, u32[]{:S(2)}) copy-start(f32[288,1152]{1,0:T(8,128)S(1)} %get-tuple-element.44.corr_o) | copy-start | bytes 3981316
  6.0 1.8 %collective-permute-start = (f32[32,1152]{1,0:T(8,128)}, f32[32,1152]{1,0:T(8,128)}, u32[]{:S(2)}, u32[]{:S(2)}) collective-permute-start(f32[32,1152]{1,0:T(8,128)} %slice_select_fusion.1), channel_id=1, source_target_pairs={{0,1},{1,0},{2,3},{3,2},{4,5},{5,4},{6,7},{7,6},{8,9},{9,8},{10,11... | collective-permute-start | bytes 442376 | tf_op jit(solution)/shard_map/ppermute | solution.py:68
  8.7 6.2 %collective-permute-start.1 = (f32[16,1152]{1,0:T(8,128)S(1)}, f32[16,1152]{1,0:T(8,128)S(1)}, u32[]{:S(2)}, u32[]{:S(2)}) collective-permute-start(f32[16,1152]{1,0:T(8,128)S(1)} %slice_select_fusion.3), channel_id=1, source_target_pairs={{0,2},{1,3},{2,0},{3,1},{4,6},{5,7},{6,4},{7,5},{8,10},{9,11},{10,... | collective-permute-start | bytes 221192 | tf_op jit(solution)/shard_map/ppermute | solution.py:68
  11.8 36.1 %copy-start.16 = (f32[144,576]{1,0:T(8,128)}, f32[144,576]{1,0:T(8,128)S(1)}, u32[]{:S(2)}) copy-start(f32[144,576]{1,0:T(8,128)S(1)} %pad_maximum_fusion.refs_0_) | copy-start | bytes 995332
  11.8 16.1 %collective-permute-start.4 = (f32[144,576]{1,0:T(8,128)S(1)}, f32[144,576]{1,0:T(8,128)S(1)}, u32[]{:S(2)}, u32[]{:S(2)}) collective-permute-start(f32[144,576]{1,0:T(8,128)S(1)} %pad_maximum_fusion.refs_0_), channel_id=1, source_target_pairs={{0,8},{4,12},{8,0},{12,4},{16,24},{20,28},{24,16},{28,20},{1,9},{5... | collective-permute-start | bytes 995336 | tf_op jit(solution)/shard_map/ppermute | solution.py:68
  13.4 10.1 %collective-permute-start.2 = (f32[144,576]{1,0:T(8,128)S(1)}, f32[144,576]{1,0:T(8,128)S(1)}, u32[]{:S(2)}, u32[]{:S(2)}) collective-permute-start(f32[144,576]{1,0:T(8,128)S(1)} %pad_maximum_fusion.refs_0_), channel_id=1, source_target_pairs={{0,4},{4,0},{8,12},{12,8},{16,20},{20,16},{24,28},{28,24},{1,5},{5... | collective-permute-start | bytes 995336 | tf_op jit(solution)/shard_map/ppermute | solution.py:68
  23.5 15.3 %copy-start.18 = (f32[144,576]{1,0:T(8,128)}, f32[144,576]{1,0:T(8,128)S(1)}, u32[]{:S(2)}) copy-start(f32[144,576]{1,0:T(8,128)S(1)} %collective-permute-done.2.refs_0_) | copy-start | bytes 995332
  23.5 4.4 %collective-permute-start.3 = (f32[16,1152]{1,0:T(8,128)S(1)}, f32[16,1152]{1,0:T(8,128)S(1)}, u32[]{:S(2)}, u32[]{:S(2)}) collective-permute-start(f32[16,1152]{1,0:T(8,128)S(1)} %select_add_fusion.3), channel_id=1, source_target_pairs={{0,4},{4,0},{8,12},{12,8},{16,20},{20,16},{24,28},{28,24},{1,5},{5... | collective-permute-start | bytes 221192 | tf_op jit(solution)/shard_map/ppermute | solution.py:68
  27.9 50.9 %copy-start.17 = (f32[144,576]{1,0:T(8,128)}, f32[144,576]{1,0:T(8,128)S(1)}, u32[]{:S(2)}) copy-start(f32[144,576]{1,0:T(8,128)S(1)} %collective-permute-done.4.refs_1_) | copy-start | bytes 995332
  27.9 4.4 %collective-permute-start.5 = (f32[16,1152]{1,0:T(8,128)S(1)}, f32[16,1152]{1,0:T(8,128)S(1)}, u32[]{:S(2)}, u32[]{:S(2)}) collective-permute-start(f32[16,1152]{1,0:T(8,128)S(1)} %add.66), channel_id=1, source_target_pairs={{0,8},{4,12},{8,0},{12,4},{16,24},{20,28},{24,16},{28,20},{1,9},{5... | collective-permute-start | bytes 221192 | tf_op jit(solution)/shard_map/ppermute | solution.py:68
  32.3 6.0 %collective-permute-start.6 = (f32[16,1152]{1,0:T(8,128)S(1)}, f32[16,1152]{1,0:T(8,128)S(1)}, u32[]{:S(2)}, u32[]{:S(2)}) collective-permute-start(f32[16,1152]{1,0:T(8,128)S(1)} %add.67), channel_id=1, source_target_pairs={{0,16},{4,20},{8,24},{12,28},{16,0},{20,4},{24,8},{28,12},{1,17},{... | collective-permute-start | bytes 221192 | tf_op jit(solution)/shard_map/ppermute | solution.py:68
  38.3 4.4 %collective-permute-start.7 = (f32[16,1152]{1,0:T(8,128)S(1)}, f32[16,1152]{1,0:T(8,128)S(1)}, u32[]{:S(2)}, u32[]{:S(2)}) collective-permute-start(f32[16,1152]{1,0:T(8,128)S(1)} %add.68), channel_id=1, source_target_pairs={{0,2},{1,3},{2,0},{3,1},{4,6},{5,7},{6,4},{7,5},{8,10},{9,11},{10,... | collective-permute-start | bytes 221192 | tf_op jit(solution)/shard_map/ppermute | solution.py:68
  43.4 3.4 %collective-permute-start.8 = (f32[32,1152]{1,0:T(8,128)}, f32[32,1152]{1,0:T(8,128)}, u32[]{:S(2)}, u32[]{:S(2)}) collective-permute-start(f32[32,1152]{1,0:T(8,128)} %pad_maximum_fusion.3), channel_id=1, source_target_pairs={{0,1},{1,0},{2,3},{3,2},{4,5},{5,4},{6,7},{7,6},{8,9},{9,8},{10,11... | collective-permute-start | bytes 442376 | tf_op jit(solution)/shard_map/ppermute | solution.py:68
  43.4 11.0 %collective-permute-start.9 = (f32[144,576]{1,0:T(8,128)S(1)}, f32[144,576]{1,0:T(8,128)S(1)}, u32[]{:S(2)}, u32[]{:S(2)}) collective-permute-start(f32[144,576]{1,0:T(8,128)S(1)} %collective-permute-done.4.refs_1_), channel_id=1, source_target_pairs={{0,4},{4,0},{8,12},{12,8},{16,20},{20,16},{24,28},{28,24},{1,5},{5... | collective-permute-start | bytes 995336 | tf_op jit(solution)/shard_map/ppermute | solution.py:68
  45.0 18.8 %collective-permute-start.11 = (f32[144,576]{1,0:T(8,128)S(1)}, f32[144,576]{1,0:T(8,128)S(1)}, u32[]{:S(2)}, u32[]{:S(2)}) collective-permute-start(f32[144,576]{1,0:T(8,128)S(1)} %pad_maximum_fusion.refs_0_), channel_id=1, source_target_pairs={{0,16},{4,20},{8,24},{12,28},{16,0},{20,4},{24,8},{28,12},{1,17},{... | collective-permute-start | bytes 995336 | tf_op jit(solution)/shard_map/ppermute | solution.py:68
  47.9 1.6 %copy-start.7 = (f32[64,1152]{1,0:T(8,128)}, f32[64,1152]{1,0:T(8,128)S(1)}, u32[]{:S(2)}) copy-start(f32[64,1152]{1,0:T(8,128)S(1)} %pad_maximum_fusion.1.left) | copy-start | bytes 884740
  47.9 8.1 %copy-start.26 = (f32[1,1,2304]{2,1,0:T(1,128)S(1)}, f32[1,1,2304]{2,1,0:T(1,128)}, u32[]{:S(2)}) copy-start(f32[1,1,2304]{2,1,0:T(1,128)} %param.23) | copy-start | bytes 27652
  47.9 15.9 %copy-start.27 = (f32[72]{0:T(128)S(1)}, f32[72]{0:T(128)}, u32[]{:S(2)}) copy-start(f32[72]{0:T(128)} %param.24) | copy-start | bytes 868
  47.9 15.9 %copy-start.29 = (f32[72]{0:T(128)S(1)}, f32[72]{0:T(128)}, u32[]{:S(2)}) copy-start(f32[72]{0:T(128)} %param.25) | copy-start | bytes 868
  54.4 14.9 %copy-start.21 = (f32[144,576]{1,0:T(8,128)}, f32[144,576]{1,0:T(8,128)S(1)}, u32[]{:S(2)}) copy-start(f32[144,576]{1,0:T(8,128)S(1)} %collective-permute-done.9.refs_1_) | copy-start | bytes 995332
  54.4 4.4 %collective-permute-start.10 = (f32[32,576]{1,0:T(8,128)S(1)}, f32[32,576]{1,0:T(8,128)S(1)}, u32[]{:S(2)}, u32[]{:S(2)}) collective-permute-start(f32[32,576]{1,0:T(8,128)S(1)} %right.2), channel_id=1, source_target_pairs={{0,4},{4,0},{8,12},{12,8},{16,20},{20,16},{24,28},{28,24},{1,5},{5... | collective-permute-start | bytes 221192 | tf_op jit(solution)/shard_map/ppermute | solution.py:68
  63.8 5.6 %copy-start.19 = (f32[144,576]{1,0:T(8,128)}, f32[144,576]{1,0:T(8,128)S(1)}, u32[]{:S(2)}) copy-start(f32[144,576]{1,0:T(8,128)S(1)} %collective-permute-done.11.refs_0_) | copy-start | bytes 995332
  63.8 4.4 %collective-permute-start.12 = (f32[32,576]{1,0:T(8,128)S(1)}, f32[32,576]{1,0:T(8,128)S(1)}, u32[]{:S(2)}, u32[]{:S(2)}) collective-permute-start(f32[32,576]{1,0:T(8,128)S(1)} %add.69), channel_id=1, source_target_pairs={{0,8},{4,12},{8,0},{12,4},{16,24},{20,28},{24,16},{28,20},{1,9},{5... | collective-permute-start | bytes 221192 | tf_op jit(solution)/shard_map/ppermute | solution.py:68
  68.2 6.0 %collective-permute-start.13 = (f32[32,576]{1,0:T(8,128)S(1)}, f32[32,576]{1,0:T(8,128)S(1)}, u32[]{:S(2)}, u32[]{:S(2)}) collective-permute-start(f32[32,576]{1,0:T(8,128)S(1)} %add.70), channel_id=1, source_target_pairs={{0,16},{4,20},{8,24},{12,28},{16,0},{20,4},{24,8},{28,12},{1,17},{... | collective-permute-start | bytes 221192 | tf_op jit(solution)/shard_map/ppermute | solution.py:68
  76.2 2.2 %copy-start.20 = (f32[144,576]{1,0:T(8,128)S(1)}, f32[144,576]{1,0:T(8,128)}, u32[]{:S(2)}) copy-start(f32[144,576]{1,0:T(8,128)} %copy-done.19) | copy-start | bytes 995332
  76.2 1.5 collective-permute-start.14
  77.7 4.6 %collective-permute-start.15 = (f32[16,1280]{1,0:T(8,128)S(1)}, f32[16,1280]{1,0:T(8,128)S(1)}, u32[]{:S(2)}, u32[]{:S(2)}) collective-permute-start(f32[16,1280]{1,0:T(8,128)S(1)} %slice_select_fusion.2), channel_id=1, source_target_pairs={{0,2},{1,3},{2,0},{3,1},{4,6},{5,7},{6,4},{7,5},{8,10},{9,11},{10,... | collective-permute-start | bytes 245768 | tf_op jit(solution)/shard_map/ppermute | solution.py:68
  78.3 10.4 %collective-permute-start.16 = (f32[144,576]{1,0:T(8,128)S(1)}, f32[144,576]{1,0:T(8,128)S(1)}, u32[]{:S(2)}, u32[]{:S(2)}) collective-permute-start(f32[144,576]{1,0:T(8,128)S(1)} %copy-done.20), channel_id=1, source_target_pairs={{0,4},{4,0},{8,12},{12,8},{16,20},{20,16},{24,28},{28,24},{1,5},{5... | collective-permute-start | bytes 995336 | tf_op jit(solution)/shard_map/ppermute | solution.py:68
  78.8 18.6 %collective-permute-start.18 = (f32[144,576]{1,0:T(8,128)S(1)}, f32[144,576]{1,0:T(8,128)S(1)}, u32[]{:S(2)}, u32[]{:S(2)}) collective-permute-start(f32[144,576]{1,0:T(8,128)S(1)} %collective-permute-done.4.refs_1_), channel_id=1, source_target_pairs={{0,16},{4,20},{8,24},{12,28},{16,0},{20,4},{24,8},{28,12},{1,17},{... | collective-permute-start | bytes 995336 | tf_op jit(solution)/shard_map/ppermute | solution.py:68
  88.7 23.6 %copy-start.24 = (f32[144,576]{1,0:T(8,128)}, f32[144,576]{1,0:T(8,128)S(1)}, u32[]{:S(2)}) copy-start(f32[144,576]{1,0:T(8,128)S(1)} %collective-permute-done.16.refs_0_) | copy-start | bytes 995332
  88.7 4.4 %collective-permute-start.17 = (f32[16,1280]{1,0:T(8,128)S(1)}, f32[16,1280]{1,0:T(8,128)S(1)}, u32[]{:S(2)}, u32[]{:S(2)}) collective-permute-start(f32[16,1280]{1,0:T(8,128)S(1)} %select_add_fusion.2), channel_id=1, source_target_pairs={{0,4},{4,0},{8,12},{12,8},{16,20},{20,16},{24,28},{28,24},{1,5},{5... | collective-permute-start | bytes 245768 | tf_op jit(solution)/shard_map/ppermute | solution.py:68
  97.4 12.0 %copy-start.22 = (f32[144,576]{1,0:T(8,128)}, f32[144,576]{1,0:T(8,128)S(1)}, u32[]{:S(2)}) copy-start(f32[144,576]{1,0:T(8,128)S(1)} %collective-permute-done.18.refs_1_) | copy-start | bytes 995332
  97.4 4.4 %collective-permute-start.19 = (f32[16,1280]{1,0:T(8,128)S(1)}, f32[16,1280]{1,0:T(8,128)S(1)}, u32[]{:S(2)}, u32[]{:S(2)}) collective-permute-start(f32[16,1280]{1,0:T(8,128)S(1)} %add.76), channel_id=1, source_target_pairs={{0,8},{4,12},{8,0},{12,4},{16,24},{20,28},{24,16},{28,20},{1,9},{5... | collective-permute-start | bytes 245768 | tf_op jit(solution)/shard_map/ppermute | solution.py:68
  101.8 5.9 %collective-permute-start.20 = (f32[16,1280]{1,0:T(8,128)S(1)}, f32[16,1280]{1,0:T(8,128)S(1)}, u32[]{:S(2)}, u32[]{:S(2)}) collective-permute-start(f32[16,1280]{1,0:T(8,128)S(1)} %add.77), channel_id=1, source_target_pairs={{0,16},{4,20},{8,24},{12,28},{16,0},{20,4},{24,8},{28,12},{1,17},{... | collective-permute-start | bytes 245768 | tf_op jit(solution)/shard_map/ppermute | solution.py:68
  107.8 4.5 %collective-permute-start.21 = (f32[16,1280]{1,0:T(8,128)S(1)}, f32[16,1280]{1,0:T(8,128)S(1)}, u32[]{:S(2)}, u32[]{:S(2)}) collective-permute-start(f32[16,1280]{1,0:T(8,128)S(1)} %add.78), channel_id=1, source_target_pairs={{0,2},{1,3},{2,0},{3,1},{4,6},{5,7},{6,4},{7,5},{8,10},{9,11},{10,... | collective-permute-start | bytes 245768 | tf_op jit(solution)/shard_map/ppermute | solution.py:68
  113.0 8.6 %collective-permute-start.22 = (f32[32,1280]{1,0:T(8,128)}, f32[32,1280]{1,0:T(8,128)}, u32[]{:S(2)}, u32[]{:S(2)}) collective-permute-start(f32[32,1280]{1,0:T(8,128)} %pad_maximum_fusion.2), channel_id=1, source_target_pairs={{0,1},{1,0},{2,3},{3,2},{4,5},{5,4},{6,7},{7,6},{8,9},{9,8},{10,11... | collective-permute-start | bytes 491528 | tf_op jit(solution)/shard_map/ppermute | solution.py:68
  114.9 1.9 %copy-start.23 = (f32[144,576]{1,0:T(8,128)S(1)}, f32[144,576]{1,0:T(8,128)}, u32[]{:S(2)}) copy-start(f32[144,576]{1,0:T(8,128)} %copy-done.22) | copy-start | bytes 995332
  116.8 11.1 %collective-permute-start.23 = (f32[144,576]{1,0:T(8,128)S(1)}, f32[144,576]{1,0:T(8,128)S(1)}, u32[]{:S(2)}, u32[]{:S(2)}) collective-permute-start(f32[144,576]{1,0:T(8,128)S(1)} %copy-done.23), channel_id=1, source_target_pairs={{0,4},{4,0},{8,12},{12,8},{16,20},{20,16},{24,28},{28,24},{1,5},{5... | collective-permute-start | bytes 995336 | tf_op jit(solution)/shard_map/ppermute | solution.py:68
  125.2 1.5 copy-start.6
  125.2 7.2 %copy-start.28 = (f32[72]{0:T(128)S(1)}, f32[72]{0:T(128)}, u32[]{:S(2)}) copy-start(f32[72]{0:T(128)} %param.24) | copy-start | bytes 868
  127.9 13.4 %copy-start.25 = (f32[144,576]{1,0:T(8,128)}, f32[144,576]{1,0:T(8,128)S(1)}, u32[]{:S(2)}) copy-start(f32[144,576]{1,0:T(8,128)S(1)} %collective-permute-done.23.refs_0_) | copy-start | bytes 995332
  127.9 4.4 %collective-permute-start.24 = (f32[32,576]{1,0:T(8,128)S(1)}, f32[32,576]{1,0:T(8,128)S(1)}, u32[]{:S(2)}, u32[]{:S(2)}) collective-permute-start(f32[32,576]{1,0:T(8,128)S(1)} %right.3), channel_id=1, source_target_pairs={{0,4},{4,0},{8,12},{12,8},{16,20},{20,16},{24,28},{28,24},{1,5},{5... | collective-permute-start | bytes 221192 | tf_op jit(solution)/shard_map/ppermute | solution.py:68
  132.3 5.9 %collective-permute-start.25 = (f32[32,576]{1,0:T(8,128)S(1)}, f32[32,576]{1,0:T(8,128)S(1)}, u32[]{:S(2)}, u32[]{:S(2)}) collective-permute-start(f32[32,576]{1,0:T(8,128)S(1)} %add.79), channel_id=1, source_target_pairs={{0,8},{4,12},{8,0},{12,4},{16,24},{20,28},{24,16},{28,20},{1,9},{5... | collective-permute-start | bytes 221192 | tf_op jit(solution)/shard_map/ppermute | solution.py:68
  138.9 5.7 %collective-permute-start.26 = (f32[32,576]{1,0:T(8,128)}, f32[32,576]{1,0:T(8,128)}, u32[]{:S(2)}, u32[]{:S(2)}) collective-permute-start(f32[32,576]{1,0:T(8,128)} %add.80), channel_id=1, source_target_pairs={{0,16},{4,20},{8,24},{12,28},{16,0},{20,4},{24,8},{28,12},{1,17},{... | collective-permute-start | bytes 221192 | tf_op jit(solution)/shard_map/ppermute | solution.py:68
  142.9 2.6 %copy-start.8 = (bf16[2,192,1152]{2,1,0:T(8,128)(2,1)S(1)}, bf16[2,192,1152]{2,1,0:T(8,128)(2,1)}, u32[]{:S(2)}) copy-start(bf16[2,192,1152]{2,1,0:T(8,128)(2,1)} %get-tuple-element.69.stack) | copy-start | bytes 2654212
  (9 other events, 9.5 us)

commit v4 on v3

--- a/solution.py
+++ b/solution.py
@@ -19,11 +19,13 @@
 NN = (((1,), (0,)), ((), ()))
 NT = (((1,), (1,)), ((), ()))
 TN = (((0,), (0,)), ((), ()))
-TT = (((0,), (1,)), ((), ()))
 
 IN_HBM = pl.BlockSpec(memory_space=pltpu.HBM)
 IN_VMEM = pl.BlockSpec(memory_space=pltpu.VMEM)
-GRANT = pltpu.CompilerParams(vmem_limit_bytes=40 * 2**20)
+SMALL = pltpu.CompilerParams(vmem_limit_bytes=8 * 2**20)
+LARGE = pltpu.CompilerParams(vmem_limit_bytes=16 * 2**20)
+QUICK = pl.CostEstimate(flops=1000, bytes_accessed=1000, transcendentals=0)
+SLOW = pl.CostEstimate(flops=1000, bytes_accessed=6_000_000, transcendentals=0)
 
 
 def hold(space, *arrays):
@@ -71,9 +73,10 @@
 def sum_over(block, count, gather, stage):
     for mask in halves(count):
         block = gather.before(block, stage, mask)
-        block = block + swap(block, "rep", mask, count)
+        block = gather.start_tasks(block, stage, mask)
+        block = block + gather.end_tasks(swap(block, "rep", mask, count), stage, mask)
         block = gather.after(block, stage, mask)
-    return block
+    return gather.before(block, stage, 0)
 
 
 def sum_over_all(part, n_rep, n_shard, gather, stage):
@@ -94,20 +97,30 @@
 
 class Gather:
     PLAN = (
-        ("turned", "own", 1, None, (0, 1)),
         ("near", "own", 2, None, (0, 2)),
-        ("turned_near", "near", 1, (0, 2), (1, 1)),
+        ("turned", "own", 1, (0, 1), (0, 0)),
         ("far", "own", 4, (0, 4), (1, 2)),
-        ("turned_far", "far", 1, (1, 2), (2, 1)),
-        ("last", "near", 4, (1, 4), (2, 2)),
-        ("turned_last", "last", 1, (2, 2), (3, 1)),
+        ("turned_near", "near", 1, (1, 1), (1, 0)),
+        ("last", "far", 2, (1, 4), (2, 2)),
+        ("turned_far", "far", 1, (2, 1), (2, 0)),
+        ("turned_last", "last", 1, (3, 1), (3, 0)),
     )
+    INSERTS = {
+        (1, 4): ("own", "near"),
+        (2, 1): ("turned", "turned_near"),
+        (2, 2): ("far",),
+        (2, 4): ("last",),
+        (3, 4): ("turned_far",),
+    }
     PLACES = {"own": 0, "turned": 1, "near": 2, "far": 4, "last": 6, "turned_near": 3, "turned_far": 5, "turned_last": 7}
 
     def __init__(self, own, count):
         self.count = count
         self.blocks = {"own": own}
         self.paired = count == 8 and own.shape[0] % 8 == 0
+        self.rows = None
+        self.tasks = {}
+        self.results = {}
         self.send(None)
 
     def send(self, point):
@@ -115,6 +128,28 @@
             for name, source, mask, after, _ in self.PLAN:
                 if after == point:
                     self.blocks[name] = swap(self.blocks[source], "rep", mask, self.count)
+
+    def start_tasks(self, value, stage, mask):
+        point = (stage, mask)
+        if point in self.tasks:
+            task, *inputs = self.tasks[point]
+            value, *inputs = lax.optimization_barrier((value, *inputs))
+            self.results[point] = task(*inputs)
+        if self.paired and point in self.INSERTS:
+            value, *blocks = lax.optimization_barrier((value, *(self.blocks[name] for name in self.INSERTS[point])))
+            self.insert(blocks, self.INSERTS[point])
+        return value
+
+    def end_tasks(self, value, stage, mask):
+        point = (stage, mask)
+        if point in self.tasks:
+            value, self.results[point] = lax.optimization_barrier((value, self.results[point]))
+        if self.paired and point in self.INSERTS:
+            value, self.rows = lax.optimization_barrier((value, self.rows))
+        return value
+
+    def insert(self, blocks, names):
+        self.rows = insert(self.rows, blocks, [self.PLACES[name] for name in names], self.count)
 
     def before(self, value, stage, mask):
         if self.paired:
@@ -130,12 +165,6 @@
                     value, self.blocks[source] = lax.optimization_barrier((value, self.blocks[source]))
             self.send((stage, mask))
         return value
-
-    def turned_rows(self):
-        rows = None
-        for names in (("own", "near"), ("turned", "turned_near"), ("far", "last"), ("turned_far",), ("turned_last",)):
-            rows = insert(rows, [self.blocks[name] for name in names], [self.PLACES[name] for name in names], self.count)
-        return rows
 
 
 def insert_kernel(masks, place_ref, *refs):
@@ -165,7 +194,8 @@
         out_specs=IN_VMEM,
         out_shape=pltpu.VMEM((height, width), f32),
         input_output_aliases={1 + len(blocks): 0} if old else {},
-        cost_estimate=pl.CostEstimate(flops=1_000_000 * len(blocks), bytes_accessed=2_000_000 * len(blocks), transcendentals=0),
+        compiler_params=SMALL,
+        cost_estimate=SLOW,
         name="insert",
     )(place, *blocks, *old)
 
@@ -202,14 +232,14 @@
         functools.partial(first_kernel, chunks),
         in_specs=[IN_HBM] * 6,
         out_specs=[IN_VMEM] * 3,
-        out_shape=[pltpu.VMEM((width, size), f32)] * 2 + [jax.ShapeDtypeStruct((2 * rank, size), f32)],
+        out_shape=[pltpu.VMEM((width, size), f32)] * 2 + [pltpu.VMEM((2 * rank, size), f32)],
         scratch_shapes=[
             pltpu.VMEM((4, width, size), f32),
             pltpu.VMEM((2, rank, width), f32),
             pltpu.SemaphoreType.DMA((chunks, 4)),
             pltpu.SemaphoreType.DMA((2,)),
         ],
-        compiler_params=GRANT,
+        compiler_params=LARGE,
         name="first",
     )(*hold(pltpu.HBM, *grads, *errors, basis_q, basis_o))
 
@@ -225,8 +255,9 @@
         right_kernel,
         in_specs=[IN_VMEM] * 3,
         out_specs=IN_VMEM,
-        out_shape=jax.ShapeDtypeStruct((rank, 2 * width), f32),
-        compiler_params=GRANT,
+        out_shape=pltpu.VMEM((rank, 2 * width), f32),
+        compiler_params=SMALL,
+        cost_estimate=QUICK,
         name="right",
     )(left, *hold(pltpu.VMEM, corr_q, corr_o))
 
@@ -250,8 +281,9 @@
         left_kernel,
         in_specs=[IN_VMEM] * (4 + len(extra)),
         out_specs=IN_VMEM,
-        out_shape=jax.ShapeDtypeStruct((2 * rank, lanes), f32),
-        compiler_params=GRANT,
+        out_shape=pltpu.VMEM((2 * rank, lanes), f32),
+        compiler_params=SMALL,
+        cost_estimate=QUICK,
         name="left",
     )(right, inverse, *hold(pltpu.VMEM, corr_q, corr_o), *extra)
 
@@ -293,29 +325,36 @@
     rank = left.shape[0] // 2
     return pl.pallas_call(
         inverse_kernel,
-        out_shape=jax.ShapeDtypeStruct((2, rank, rank), f32),
-        cost_estimate=pl.CostEstimate(flops=20_000_000, bytes_accessed=left.size * 4, transcendentals=0),
+        out_shape=pltpu.VMEM((2, rank, rank), f32),
+        compiler_params=SMALL,
+        cost_estimate=SLOW,
         name="inverse",
     )(left)
 
 
-def normal_kernel(left, inverse, normal, stack):
-    rank = inverse.shape[1]
+def stack_kernel(place_ref, left, stack, own):
+    rank = left.shape[0] // 2
     for p in range(2):
-        factor = exact(inverse[p], left[p * rank : (p + 1) * rank, :], NN)
-        normal[p * rank : (p + 1) * rank, :] = factor
-        high, middle, low = three(factor)
+        high, middle, low = three(left[p * rank : (p + 1) * rank, :])
         stack[p] = jnp.concatenate([high, middle, low, high, middle, high], axis=0)
-
-
-def normal_of(left, inverse):
-    rank, size = inverse.shape[1], left.shape[1]
-    return pl.pallas_call(
-        normal_kernel,
-        out_shape=[jax.ShapeDtypeStruct((2 * rank, size), f32), jax.ShapeDtypeStruct((2, 6 * rank, size), bf16)],
-        cost_estimate=pl.CostEstimate(flops=20_000_000, bytes_accessed=left.size * 4, transcendentals=0),
-        name="normal",
-    )(left, inverse)
+    count = own.shape[1]
+    index = place_ref[0]
+    window = left[:, pl.ds(pl.multiple_of(index * LANES, LANES), 2 * LANES)]
+    own[...] = pltpu.roll(window, 2 * LANES - index * (count - LANES), 1)[:, :count]
+
+
+def stack_of(left, count):
+    rank, size = left.shape[0] // 2, left.shape[1]
+    place = lax.axis_index("rep").astype(jnp.int32).reshape(1)
+    return pl.pallas_call(
+        stack_kernel,
+        in_specs=[pl.BlockSpec(memory_space=pltpu.SMEM), IN_VMEM],
+        out_specs=[IN_VMEM] * 2,
+        out_shape=[pltpu.VMEM((2, 6 * rank, size), bf16), pltpu.VMEM((2 * rank, count), f32)],
+        compiler_params=SMALL,
+        cost_estimate=SLOW,
+        name="stack",
+    )(place, left)
 
 
 def finish_kernel(chunks, corr_q, corr_o, rows, stack, inverse, right, own, moment_q, moment_o, *refs):
@@ -325,7 +364,8 @@
     copies = []
     for p, corr in enumerate((corr_q, corr_o)):
         factor = right[:, p * width : (p + 1) * width]
-        high, middle, low = three(exact(factor, inverse[p], TT))
+        scaled = exact(inverse[p], exact(inverse[p], factor, NN), TN)
+        high, middle, low = three(scaled.T)
         lefts = jnp.concatenate([high, high, high, middle, middle, low], axis=1)
         for c in range(chunks):
             at = pl.ds(c * height, height)
@@ -337,8 +377,8 @@
                 copies[-1].start()
     for p, moment in enumerate((moment_q, moment_o)):
         factor = right[:, p * width : (p + 1) * width]
-        basis = exact(inverse[p], factor, NN)
-        new_moments[p] = decay_rate * moment[...] + exact(own[p * rank : (p + 1) * rank, :], basis, TN)
+        scaled = exact(inverse[p], exact(inverse[p], factor, NN), TN)
+        new_moments[p] = decay_rate * moment[...] + exact(own[p * rank : (p + 1) * rank, :], scaled, TN)
         copies.append(pltpu.make_async_copy(new_moments.at[p], outs[4 + p], moment_sems.at[p]))
         copies[-1].start()
     for copy in copies:
@@ -359,12 +399,12 @@
             pltpu.SemaphoreType.DMA((4, chunks)),
             pltpu.SemaphoreType.DMA((2,)),
         ],
-        compiler_params=GRANT,
+        compiler_params=LARGE,
         name="finish",
     )(*hold(pltpu.VMEM, corr_q, corr_o, rows), stack, inverse, right, own, moment_q, moment_o)
 
 
-def finish_plain(corr_q, corr_o, base, normal, inverse, right, moment_q, moment_o):
+def finish_plain(corr_q, corr_o, base, left, inverse, right, moment_q, moment_o):
     rank, width = inverse.shape[1], moment_q.shape[1]
     rows = moment_q.shape[0]
     start = lax.axis_index("rep") * rows
@@ -372,8 +412,8 @@
     weights, moments, errors = [], [], []
     for p, (corr, moment) in enumerate(((corr_q, moment_q), (corr_o, moment_o))):
         at = slice(p * width, (p + 1) * width)
-        basis = exact(inverse[p], right[:, at], NN)
-        decoded = exact(basis, normal[p * rank : (p + 1) * rank], TN)
+        scaled = exact(inverse[p], exact(inverse[p], right[:, at], NN), TN)
+        decoded = exact(scaled, left[p * rank : (p + 1) * rank], TN)
         weights.append(bases[:, at].T - step_size * decoded)
         moments.append(decay_rate * moment + lax.dynamic_slice_in_dim(decoded, start, rows, 1).T)
         errors.append(corr - decoded)
@@ -407,16 +447,19 @@
             extra_sum = left[:extra_rows, size:]
             left = left[:, :size]
         right = right_of(left, corr_q, corr_o)
-        inverse = inverse_of(left)
+        if last and gather.paired:
+            gather.tasks[3, 1] = (functools.partial(stack_of, count=row_count), left)
+        gather.tasks[2 * sweep + 1, 2] = (inverse_of, left)
         right = sum_over(right, n_rep, gather, 2 * sweep + 1)
+        inverse = gather.results[2 * sweep + 1, 2]
         if not last:
             part = left_of(right, inverse, corr_q, corr_o, [extra] if sweep == ROUNDS - 2 else [])
-    normal, stack = normal_of(left, inverse)
     if gather.paired:
-        own = lax.dynamic_slice_in_dim(normal, lax.axis_index("rep") * row_count, row_count, 1)
-        outs = finish(corr_q, corr_o, gather.turned_rows(), stack, inverse, right, own, q_moment, o_moment)
+        stack, own = gather.results[3, 1]
+        gather.insert([gather.blocks["turned_last"]], ["turned_last"])
+        outs = finish(corr_q, corr_o, gather.rows, stack, inverse, right, own, q_moment, o_moment)
     else:
-        outs = finish_plain(corr_q, corr_o, base, normal, inverse, right, q_moment, o_moment)
+        outs = finish_plain(corr_q, corr_o, base, left, inverse, right, q_moment, o_moment)
     weight_q, weight_o, error_q, error_o, q_moment_new, o_moment_new = outs
     half = extra_rows // 2
     norm_sum = extra_sum[:half].reshape(flat)

time: 156 us -> 120 us (0.77)
  waiting for transfers between devices: 76.9 us -> 54.9 us
  starting transfers between devices: 27.7 us -> 39 us
  Pallas kernels: 28.7 us -> 18.2 us
  local copies, waits for them, and re-layouts: 11.2 us -> 1.4 us
  other arithmetic: 9.54 us -> 5.39 us
    ppermute x27, waiting for transfers between devices: 76.9 us -> 54.9 us  [swap(): return lax.ppermute(block, axis, pairs)]
    ppermute x27, starting transfers between devices: 27.7 us -> 39 us  [swap(): return lax.ppermute(block, axis, pairs)]
    unnamed x60 -> x20, local copies, waits for them, and re-layouts: 9.6 us -> 1.4 us
    pallas_call x3, Pallas kernels: 8.14 us -> 2.74 us  [the longest x2 2.6 us: inverse_of(): pl.pallas_call(inverse_kernel, out_shape=pltpu.VMEM((2, rank, rank), f32)...]
    pallas_call x5 -> x6, Pallas kernels: 8.43 us -> 3.17 us  [insert(): pl.pallas_call(functools.partial(insert_kernel, masks), in_specs=[pl.Bloc...]
    dynamic_slice x1 -> x0, local copies, waits for them, and re-layouts: 1.61 us -> none  [per_device(): lax.dynamic_slice_in_dim(normal, lax.axis_index('rep') * row_count, row_c...]
    add x12, other arithmetic: 1.69 us -> 0.13 us  [sum_over(): block + gather.end_tasks(swap(block, 'rep', mask, count), stage, mask)]
  transfers between devices with their start and end apart: 27 -> 27, of which waited for: 22 -> 22; matrix products, arithmetic and copies ran while one was open for 4% -> 3% of each run, Pallas kernels for 13% -> 6%
where the time goes in v4:
time: 120 us
  waiting for transfers between devices  54.9 us (46%)
  starting transfers between devices  39 us (32%)
  Pallas kernels  18.2 us (15%)
  other arithmetic  5.39 us (4%)
  local copies, waits for them, and re-layouts  1.4 us (1%)
    ppermute x27, waiting for transfers between devices, swap(): return lax.ppermute(block, axis, pairs)  54.9 us
    ppermute x27, starting transfers between devices, swap(): return lax.ppermute(block, axis, pairs)  39 us
    pallas_call x1, Pallas kernels, first(): pl.pallas_call(functools.partial(first_kernel, chunks), in_specs=[IN_HBM]...  4.47 us
    pallas_call x1, Pallas kernels, finish(): pl.pallas_call(functools.partial(finish_kernel, chunks), in_specs=[IN_VME...  3.68 us
    pallas_call x6, Pallas kernels, insert(): pl.pallas_call(functools.partial(insert_kernel, masks), in_specs=[pl.Bloc...  3.17 us
    pallas_call x2, Pallas kernels, right_of(): pl.pallas_call(right_kernel, in_specs=[IN_VMEM] * 3, out_specs=IN_VMEM, o...  2.94 us
    pallas_call x2, Pallas kernels, inverse_of(): pl.pallas_call(inverse_kernel, out_shape=pltpu.VMEM((2, rank, rank), f32)...  2.6 us
  transfers between devices with their start and end apart: 27, of which 22 were waited for; matrix products, arithmetic and copies ran while one was open for 3% of the time, Pallas kernels for 6%

profile of v4, /device:TPU:0, one launch (start us, length us, event | category | flops | bytes accessed | tf_op | source)
XLA Modules:
  0.0 120.1 jit_solution(6341804614773541720)
XLA Ops:
  0.7 4.5 %first.1 = (f32[288,1152]{1,0:T(8,128)S(1)}, f32[288,1152]{1,0:T(8,128)S(1)}, f32[64,1152]{1,0:T(8,128)S(1)}) custom-call(f32[288,1152]{1,0:T(8,128)} %bitcast.33, f32[288,1152]{1,0:T(8,128)} %bitcast.34, f32[288,1152]{1,0:T(8,128)} %bitcast.35, f32[288,1152]{1,0:T(8,128)} %bitcast.36, f32[32,288]{1,0:T(8,128)} %bitcast.37, f32[32,288]{1,0:T(8,128)} %bitcast.38), custom_call_target="tpu_custom_call" | custom-call | tf_op jit(solution)/shard_map/first/pallas_call | solution.py:231
  6.3 1.1 multiply_subtract_fusion
  7.5 2.9 %collective-permute-start.1 = (f32[16,1152]{1,0:T(8,128)S(1)}, f32[16,1152]{1,0:T(8,128)S(1)}, u32[]{:S(2)}, u32[]{:S(2)}) collective-permute-start(f32[16,1152]{1,0:T(8,128)S(1)} %slice_select_fusion.3), channel_id=1, source_target_pairs={{0,2},{1,3},{2,0},{3,1},{4,6},{5,7},{6,4},{7,5},{8,10},{9,11},{10,... | collective-permute-start | bytes 221192 | tf_op jit(solution)/shard_map/ppermute | solution.py:70
  10.6 1.6 %collective-permute-start.3 = (f32[144,576]{1,0:T(8,128)S(1)}, f32[144,576]{1,0:T(8,128)S(1)}, u32[]{:S(2)}, u32[]{:S(2)}) collective-permute-start(f32[144,576]{1,0:T(8,128)S(1)} %pad_maximum_fusion.refs_0_), channel_id=1, source_target_pairs={{0,8},{4,12},{8,0},{12,4},{16,24},{20,28},{24,16},{28,20},{1,9},{5... | collective-permute-start | bytes 995336 | tf_op jit(solution)/shard_map/ppermute | solution.py:70
  12.2 0.8 collective-permute-done.1
  13.1 1.9 %collective-permute-start.2 = (f32[16,1152]{1,0:T(8,128)S(1)}, f32[16,1152]{1,0:T(8,128)S(1)}, u32[]{:S(2)}, u32[]{:S(2)}) collective-permute-start(f32[16,1152]{1,0:T(8,128)S(1)} %select_add_fusion.3), channel_id=1, source_target_pairs={{0,4},{4,0},{8,12},{12,8},{16,20},{20,16},{24,28},{28,24},{1,5},{5... | collective-permute-start | bytes 221192 | tf_op jit(solution)/shard_map/ppermute | solution.py:70
  14.9 2.6 %collective-permute-done.2 = f32[16,1152]{1,0:T(8,128)S(1)} collective-permute-done((f32[16,1152]{1,0:T(8,128)S(1)}, f32[16,1152]{1,0:T(8,128)S(1)}, u32[]{:S(2)}, u32[]{:S(2)}) %collective-permute-start.2) | collective-permute-done | bytes 73760 | tf_op jit(solution)/shard_map/ppermute | solution.py:70
  17.5 1.9 %collective-permute-start.6 = (f32[144,576]{1,0:T(8,128)S(1)}, f32[144,576]{1,0:T(8,128)S(1)}, u32[]{:S(2)}, u32[]{:S(2)}) collective-permute-start(f32[144,576]{1,0:T(8,128)S(1)} %pad_maximum_fusion.refs_0_), channel_id=1, source_target_pairs={{0,4},{4,0},{8,12},{12,8},{16,20},{20,16},{24,28},{28,24},{1,5},{5... | collective-permute-start | bytes 995336 | tf_op jit(solution)/shard_map/ppermute | solution.py:70
  19.4 1.7 %collective-permute-done.3.refs_1_ = f32[144,576]{1,0:T(8,128)S(1)} collective-permute-done((f32[144,576]{1,0:T(8,128)S(1)}, f32[144,576]{1,0:T(8,128)S(1)}, u32[]{:S(2)}, u32[]{:S(2)}) %collective-permute-start.3) | collective-permute-done | bytes 331808 | tf_op jit(solution)/shard_map/ppermute | solution.py:70
  21.0 1.6 %collective-permute-start.4 = (f32[16,1152]{1,0:T(8,128)S(1)}, f32[16,1152]{1,0:T(8,128)S(1)}, u32[]{:S(2)}, u32[]{:S(2)}) collective-permute-start(f32[16,1152]{1,0:T(8,128)S(1)} %add.63), channel_id=1, source_target_pairs={{0,8},{4,12},{8,0},{12,4},{16,24},{20,28},{24,16},{28,20},{1,9},{5... | collective-permute-start | bytes 221192 | tf_op jit(solution)/shard_map/ppermute | solution.py:70
  22.6 2.8 %collective-permute-done.4 = f32[16,1152]{1,0:T(8,128)S(1)} collective-permute-done((f32[16,1152]{1,0:T(8,128)S(1)}, f32[16,1152]{1,0:T(8,128)S(1)}, u32[]{:S(2)}, u32[]{:S(2)}) %collective-permute-start.4) | collective-permute-done | bytes 73760 | tf_op jit(solution)/shard_map/ppermute | solution.py:70
  25.4 2.7 %collective-permute-start.5 = (f32[16,1152]{1,0:T(8,128)S(1)}, f32[16,1152]{1,0:T(8,128)S(1)}, u32[]{:S(2)}, u32[]{:S(2)}) collective-permute-start(f32[16,1152]{1,0:T(8,128)S(1)} %add.64), channel_id=1, source_target_pairs={{0,16},{4,20},{8,24},{12,28},{16,0},{20,4},{24,8},{28,12},{1,17},{... | collective-permute-start | bytes 221192 | tf_op jit(solution)/shard_map/ppermute | solution.py:70
  28.0 2.7 %collective-permute-done.5 = f32[16,1152]{1,0:T(8,128)S(1)} collective-permute-done((f32[16,1152]{1,0:T(8,128)S(1)}, f32[16,1152]{1,0:T(8,128)S(1)}, u32[]{:S(2)}, u32[]{:S(2)}) %collective-permute-start.5) | collective-permute-done | bytes 73760 | tf_op jit(solution)/shard_map/ppermute | solution.py:70
  31.8 4.0 %collective-permute-done.7 = f32[16,1152]{1,0:T(8,128)S(1)} collective-permute-done((f32[16,1152]{1,0:T(8,128)S(1)}, f32[16,1152]{1,0:T(8,128)S(1)}, u32[]{:S(2)}, u32[]{:S(2)}) %collective-permute-start.7) | collective-permute-done | bytes 73760 | tf_op jit(solution)/shard_map/ppermute | solution.py:70
  37.2 2.7 %collective-permute-start.10 = (f32[144,576]{1,0:T(8,128)S(1)}, f32[144,576]{1,0:T(8,128)S(1)}, u32[]{:S(2)}, u32[]{:S(2)}) collective-permute-start(f32[144,576]{1,0:T(8,128)S(1)} %pad_maximum_fusion.refs_0_), channel_id=1, source_target_pairs={{0,16},{4,20},{8,24},{12,28},{16,0},{20,4},{24,8},{28,12},{1,17},{... | collective-permute-start | bytes 995336 | tf_op jit(solution)/shard_map/ppermute | solution.py:70
  39.8 1.0 broadcast_select_fusion.3
  40.9 1.5 %right.2 = f32[32,576]{1,0:T(8,128)S(1)} custom-call(f32[64,1152]{1,0:T(8,128)S(1)} %pad_maximum_fusion.1.left, f32[288,1152]{1,0:T(8,128)S(1)} %get-tuple-element.80.corr_q, f32[288,1152]{1,0:T(8,128)S(1)} %get-tuple-element.81.corr_o), custom_call_target="tpu_custom_call" | custom-call | flops 1000 | bytes 1000 | tf_op jit(solution)/shard_map/right/pallas_call | solution.py:254
  42.4 1.6 %collective-permute-start.9 = (f32[32,576]{1,0:T(8,128)S(1)}, f32[32,576]{1,0:T(8,128)S(1)}, u32[]{:S(2)}, u32[]{:S(2)}) collective-permute-start(f32[32,576]{1,0:T(8,128)S(1)} %right.2), channel_id=1, source_target_pairs={{0,4},{4,0},{8,12},{12,8},{16,20},{20,16},{24,28},{28,24},{1,5},{5... | collective-permute-start | bytes 221192 | tf_op jit(solution)/shard_map/ppermute | solution.py:70
  44.0 3.0 %collective-permute-done.9 = f32[32,576]{1,0:T(8,128)S(1)} collective-permute-done((f32[32,576]{1,0:T(8,128)S(1)}, f32[32,576]{1,0:T(8,128)S(1)}, u32[]{:S(2)}, u32[]{:S(2)}) %collective-permute-start.9) | collective-permute-done | bytes 73760 | tf_op jit(solution)/shard_map/ppermute | solution.py:70
  47.0 10.0 %collective-permute-done.10.refs_0_ = f32[144,576]{1,0:T(8,128)S(1)} collective-permute-done((f32[144,576]{1,0:T(8,128)S(1)}, f32[144,576]{1,0:T(8,128)S(1)}, u32[]{:S(2)}, u32[]{:S(2)}) %collective-permute-start.10) | collective-permute-done | bytes 331808 | tf_op jit(solution)/shard_map/ppermute | solution.py:70
  57.7 1.5 %collective-permute-start.13 = (f32[144,576]{1,0:T(8,128)S(1)}, f32[144,576]{1,0:T(8,128)S(1)}, u32[]{:S(2)}, u32[]{:S(2)}) collective-permute-start(f32[144,576]{1,0:T(8,128)S(1)} %copy-done.5), channel_id=1, source_target_pairs={{0,4},{4,0},{8,12},{12,8},{16,20},{20,16},{24,28},{28,24},{1,5},{5... | collective-permute-start | bytes 995336 | tf_op jit(solution)/shard_map/ppermute | solution.py:70
  59.5 1.3 %inverse.2 = f32[2,32,32]{2,1,0:T(8,128)S(1)} custom-call(f32[64,1152]{1,0:T(8,128)S(1)} %pad_maximum_fusion.1.left), custom_call_target="tpu_custom_call" | custom-call | flops 1000 | bytes 6000000 | tf_op jit(solution)/shard_map/inverse/pallas_call | solution.py:326
  61.4 2.8 %collective-permute-start.12 = (f32[32,576]{1,0:T(8,128)S(1)}, f32[32,576]{1,0:T(8,128)S(1)}, u32[]{:S(2)}, u32[]{:S(2)}) collective-permute-start(f32[32,576]{1,0:T(8,128)S(1)} %add.67), channel_id=1, source_target_pairs={{0,16},{4,20},{8,24},{12,28},{16,0},{20,4},{24,8},{28,12},{1,17},{... | collective-permute-start | bytes 221192 | tf_op jit(solution)/shard_map/ppermute | solution.py:70
  64.2 0.9 insert.6.refs_2_
  65.1 3.0 %collective-permute-done.12 = f32[32,576]{1,0:T(8,128)S(1)} collective-permute-done((f32[32,576]{1,0:T(8,128)S(1)}, f32[32,576]{1,0:T(8,128)S(1)}, u32[]{:S(2)}, u32[]{:S(2)}) %collective-permute-start.12) | collective-permute-done | bytes 73760 | tf_op jit(solution)/shard_map/ppermute | solution.py:70
  68.1 1.2 left.1
  69.4 1.4 %collective-permute-done.14 = f32[32,1280]{1,0:T(8,128)S(1)} collective-permute-done((f32[32,1280]{1,0:T(8,128)S(1)}, f32[32,1280]{1,0:T(8,128)S(1)}, u32[]{:S(2)}, u32[]{:S(2)}) %collective-permute-start.14) | collective-permute-done | bytes 163872 | tf_op jit(solution)/shard_map/ppermute | solution.py:70
  71.5 0.9 collective-permute-start.17
  72.4 3.0 %collective-permute-done.15 = f32[16,1280]{1,0:T(8,128)S(1)} collective-permute-done((f32[16,1280]{1,0:T(8,128)S(1)}, f32[16,1280]{1,0:T(8,128)S(1)}, u32[]{:S(2)}, u32[]{:S(2)}) %collective-permute-start.15) | collective-permute-done | bytes 81952 | tf_op jit(solution)/shard_map/ppermute | solution.py:70
  75.4 1.4 %collective-permute-start.16 = (f32[16,1280]{1,0:T(8,128)S(1)}, f32[16,1280]{1,0:T(8,128)S(1)}, u32[]{:S(2)}, u32[]{:S(2)}) collective-permute-start(f32[16,1280]{1,0:T(8,128)S(1)} %select_add_fusion.2), channel_id=1, source_target_pairs={{0,4},{4,0},{8,12},{12,8},{16,20},{20,16},{24,28},{28,24},{1,5},{5... | collective-permute-start | bytes 245768 | tf_op jit(solution)/shard_map/ppermute | solution.py:70
  77.6 2.3 %collective-permute-done.16 = f32[16,1280]{1,0:T(8,128)S(1)} collective-permute-done((f32[16,1280]{1,0:T(8,128)S(1)}, f32[16,1280]{1,0:T(8,128)S(1)}, u32[]{:S(2)}, u32[]{:S(2)}) %collective-permute-start.16) | collective-permute-done | bytes 81952 | tf_op jit(solution)/shard_map/ppermute | solution.py:70
  79.9 1.4 %collective-permute-start.20 = (f32[144,576]{1,0:T(8,128)S(1)}, f32[144,576]{1,0:T(8,128)S(1)}, u32[]{:S(2)}, u32[]{:S(2)}) collective-permute-start(f32[144,576]{1,0:T(8,128)S(1)} %collective-permute-done.10.refs_0_), channel_id=1, source_target_pairs={{0,4},{4,0},{8,12},{12,8},{16,20},{20,16},{24,28},{28,24},{1,5},{5... | collective-permute-start | bytes 995336 | tf_op jit(solution)/shard_map/ppermute | solution.py:70
  81.8 0.9 collective-permute-start.18
  83.1 3.1 %collective-permute-done.18 = f32[16,1280]{1,0:T(8,128)S(1)} collective-permute-done((f32[16,1280]{1,0:T(8,128)S(1)}, f32[16,1280]{1,0:T(8,128)S(1)}, u32[]{:S(2)}, u32[]{:S(2)}) %collective-permute-start.18) | collective-permute-done | bytes 81952 | tf_op jit(solution)/shard_map/ppermute | solution.py:70
  86.3 3.8 %collective-permute-start.19 = (f32[16,1280]{1,0:T(8,128)S(1)}, f32[16,1280]{1,0:T(8,128)S(1)}, u32[]{:S(2)}, u32[]{:S(2)}) collective-permute-start(f32[16,1280]{1,0:T(8,128)S(1)} %add.74), channel_id=1, source_target_pairs={{0,16},{4,20},{8,24},{12,28},{16,0},{20,4},{24,8},{28,12},{1,17},{... | collective-permute-start | bytes 245768 | tf_op jit(solution)/shard_map/ppermute | solution.py:70
  90.5 2.4 %collective-permute-done.19 = f32[16,1280]{1,0:T(8,128)S(1)} collective-permute-done((f32[16,1280]{1,0:T(8,128)S(1)}, f32[16,1280]{1,0:T(8,128)S(1)}, u32[]{:S(2)}, u32[]{:S(2)}) %collective-permute-start.19) | collective-permute-done | bytes 81952 | tf_op jit(solution)/shard_map/ppermute | solution.py:70
  92.9 1.5 %collective-permute-start.21 = (f32[16,1280]{1,0:T(8,128)S(1)}, f32[16,1280]{1,0:T(8,128)S(1)}, u32[]{:S(2)}, u32[]{:S(2)}) collective-permute-start(f32[16,1280]{1,0:T(8,128)S(1)} %add.75), channel_id=1, source_target_pairs={{0,2},{1,3},{2,0},{3,1},{4,6},{5,7},{6,4},{7,5},{8,10},{9,11},{10,... | collective-permute-start | bytes 245768 | tf_op jit(solution)/shard_map/ppermute | solution.py:70
  94.4 3.0 %collective-permute-done.21 = f32[16,1280]{1,0:T(8,128)S(1)} collective-permute-done((f32[16,1280]{1,0:T(8,128)S(1)}, f32[16,1280]{1,0:T(8,128)S(1)}, u32[]{:S(2)}, u32[]{:S(2)}) %collective-permute-start.21) | collective-permute-done | bytes 81952 | tf_op jit(solution)/shard_map/ppermute | solution.py:70
  97.5 1.4 %collective-permute-done.22 = f32[32,1280]{1,0:T(8,128)S(1)} collective-permute-done((f32[32,1280]{1,0:T(8,128)S(1)}, f32[32,1280]{1,0:T(8,128)S(1)}, u32[]{:S(2)}, u32[]{:S(2)}) %collective-permute-start.22) | collective-permute-done | bytes 163872 | tf_op jit(solution)/shard_map/ppermute | solution.py:70
  99.0 1.5 %right.3 = f32[32,576]{1,0:T(8,128)S(1)} custom-call(f32[64,1152]{1,0:T(8,128)S(1)} %fusion.left, f32[288,1152]{1,0:T(8,128)S(1)} %get-tuple-element.80.corr_q, f32[288,1152]{1,0:T(8,128)S(1)} %get-tuple-element.81.corr_o), custom_call_target="tpu_custom_call" | custom-call | flops 1000 | bytes 1000 | tf_op jit(solution)/shard_map/right/pallas_call | solution.py:254
  100.5 1.5 %collective-permute-start.23 = (f32[32,576]{1,0:T(8,128)S(1)}, f32[32,576]{1,0:T(8,128)S(1)}, u32[]{:S(2)}, u32[]{:S(2)}) collective-permute-start(f32[32,576]{1,0:T(8,128)S(1)} %right.3), channel_id=1, source_target_pairs={{0,4},{4,0},{8,12},{12,8},{16,20},{20,16},{24,28},{28,24},{1,5},{5... | collective-permute-start | bytes 221192 | tf_op jit(solution)/shard_map/ppermute | solution.py:70
  102.1 2.9 %collective-permute-done.23 = f32[32,576]{1,0:T(8,128)S(1)} collective-permute-done((f32[32,576]{1,0:T(8,128)S(1)}, f32[32,576]{1,0:T(8,128)S(1)}, u32[]{:S(2)}, u32[]{:S(2)}) %collective-permute-start.23) | collective-permute-done | bytes 73760 | tf_op jit(solution)/shard_map/ppermute | solution.py:70
  105.1 1.5 %collective-permute-start.26 = (f32[144,576]{1,0:T(8,128)S(1)}, f32[144,576]{1,0:T(8,128)S(1)}, u32[]{:S(2)}, u32[]{:S(2)}) collective-permute-start(f32[144,576]{1,0:T(8,128)S(1)} %collective-permute-done.17.refs_0_), channel_id=1, source_target_pairs={{0,4},{4,0},{8,12},{12,8},{16,20},{20,16},{24,28},{28,24},{1,5},{5... | collective-permute-start | bytes 995336 | tf_op jit(solution)/shard_map/ppermute | solution.py:70
  107.2 1.3 %inverse.3 = f32[2,32,32]{2,1,0:T(8,128)S(1)} custom-call(f32[64,1152]{1,0:T(8,128)S(1)} %fusion.left), custom_call_target="tpu_custom_call" | custom-call | flops 1000 | bytes 6000000 | tf_op jit(solution)/shard_map/inverse/pallas_call | solution.py:326
  108.5 1.0 collective-permute-done.24
  109.6 2.6 %collective-permute-start.25 = (f32[32,576]{1,0:T(8,128)S(1)}, f32[32,576]{1,0:T(8,128)S(1)}, u32[]{:S(2)}, u32[]{:S(2)}) collective-permute-start(f32[32,576]{1,0:T(8,128)S(1)} %add.77), channel_id=1, source_target_pairs={{0,16},{4,20},{8,24},{12,28},{16,0},{20,4},{24,8},{28,12},{1,17},{... | collective-permute-start | bytes 221192 | tf_op jit(solution)/shard_map/ppermute | solution.py:70
  113.1 2.7 %collective-permute-done.25 = f32[32,576]{1,0:T(8,128)S(1)} collective-permute-done((f32[32,576]{1,0:T(8,128)S(1)}, f32[32,576]{1,0:T(8,128)S(1)}, u32[]{:S(2)}, u32[]{:S(2)}) %collective-permute-start.25) | collective-permute-done | bytes 73760 | tf_op jit(solution)/shard_map/ppermute | solution.py:70
  116.3 3.7 %finish.1 = (f32[288,1152]{1,0:T(8,128)}, f32[288,1152]{1,0:T(8,128)}, f32[288,1152]{1,0:T(8,128)}, f32[288,1152]{1,0:T(8,128)}, f32[144,288]{1,0:T(8,128)}, /*index=5*/f32[144,288]{1,0:T(8,128)}) custom-call(f32[288,1152]{1,0:T(8,128)S(1)} %get-tuple-element.80.corr_q, f32[288,1152]{1,0:T(8,128)S(1)} %get-tuple-element.81.corr_o, ...), custom_call_target="tpu_custom_call" | custom-call | tf_op jit(solution)/shard_map/finish/pallas_call | solution.py:391
  (75 shorter events, 10.7 us)
Async XLA Ops:
  0.6 5.6 %copy-start = (f32[144,288]{1,0:T(8,128)S(1)}, f32[144,288]{1,0:T(8,128)}, u32[]{:S(2)}) copy-start(f32[144,288]{1,0:T(8,128)} %moment_o.1) | copy-start | bytes 497668
  0.7 5.6 %copy-start.1 = (f32[144,288]{1,0:T(8,128)S(1)}, f32[144,288]{1,0:T(8,128)}, u32[]{:S(2)}) copy-start(f32[144,288]{1,0:T(8,128)} %moment_q.1) | copy-start | bytes 497668
  5.8 1.7 %collective-permute-start = (f32[32,1152]{1,0:T(8,128)}, f32[32,1152]{1,0:T(8,128)S(1)}, u32[]{:S(2)}, u32[]{:S(2)}) collective-permute-start(f32[32,1152]{1,0:T(8,128)} %slice_select_fusion.1), channel_id=1, source_target_pairs={{0,1},{1,0},{2,3},{3,2},{4,5},{5,4},{6,7},{7,6},{8,9},{9,8},{10,11... | collective-permute-start | bytes 442376 | tf_op jit(solution)/shard_map/ppermute | solution.py:70
  7.5 5.5 %collective-permute-start.1 = (f32[16,1152]{1,0:T(8,128)S(1)}, f32[16,1152]{1,0:T(8,128)S(1)}, u32[]{:S(2)}, u32[]{:S(2)}) collective-permute-start(f32[16,1152]{1,0:T(8,128)S(1)} %slice_select_fusion.3), channel_id=1, source_target_pairs={{0,2},{1,3},{2,0},{3,1},{4,6},{5,7},{6,4},{7,5},{8,10},{9,11},{10,... | collective-permute-start | bytes 221192 | tf_op jit(solution)/shard_map/ppermute | solution.py:70
  10.6 10.4 %collective-permute-start.3 = (f32[144,576]{1,0:T(8,128)S(1)}, f32[144,576]{1,0:T(8,128)S(1)}, u32[]{:S(2)}, u32[]{:S(2)}) collective-permute-start(f32[144,576]{1,0:T(8,128)S(1)} %pad_maximum_fusion.refs_0_), channel_id=1, source_target_pairs={{0,8},{4,12},{8,0},{12,4},{16,24},{20,28},{24,16},{28,20},{1,9},{5... | collective-permute-start | bytes 995336 | tf_op jit(solution)/shard_map/ppermute | solution.py:70
  13.1 4.4 %collective-permute-start.2 = (f32[16,1152]{1,0:T(8,128)S(1)}, f32[16,1152]{1,0:T(8,128)S(1)}, u32[]{:S(2)}, u32[]{:S(2)}) collective-permute-start(f32[16,1152]{1,0:T(8,128)S(1)} %select_add_fusion.3), channel_id=1, source_target_pairs={{0,4},{4,0},{8,12},{12,8},{16,20},{20,16},{24,28},{28,24},{1,5},{5... | collective-permute-start | bytes 221192 | tf_op jit(solution)/shard_map/ppermute | solution.py:70
  17.5 13.2 %collective-permute-start.6 = (f32[144,576]{1,0:T(8,128)S(1)}, f32[144,576]{1,0:T(8,128)S(1)}, u32[]{:S(2)}, u32[]{:S(2)}) collective-permute-start(f32[144,576]{1,0:T(8,128)S(1)} %pad_maximum_fusion.refs_0_), channel_id=1, source_target_pairs={{0,4},{4,0},{8,12},{12,8},{16,20},{20,16},{24,28},{28,24},{1,5},{5... | collective-permute-start | bytes 995336 | tf_op jit(solution)/shard_map/ppermute | solution.py:70
  21.0 9.7 %copy-start.4 = (f32[144,576]{1,0:T(8,128)}, f32[144,576]{1,0:T(8,128)S(1)}, u32[]{:S(2)}) copy-start(f32[144,576]{1,0:T(8,128)S(1)} %collective-permute-done.3.refs_1_) | copy-start | bytes 995332
  21.0 4.4 %collective-permute-start.4 = (f32[16,1152]{1,0:T(8,128)S(1)}, f32[16,1152]{1,0:T(8,128)S(1)}, u32[]{:S(2)}, u32[]{:S(2)}) collective-permute-start(f32[16,1152]{1,0:T(8,128)S(1)} %add.63), channel_id=1, source_target_pairs={{0,8},{4,12},{8,0},{12,4},{16,24},{20,28},{24,16},{28,20},{1,9},{5... | collective-permute-start | bytes 221192 | tf_op jit(solution)/shard_map/ppermute | solution.py:70
  25.4 5.3 %collective-permute-start.5 = (f32[16,1152]{1,0:T(8,128)S(1)}, f32[16,1152]{1,0:T(8,128)S(1)}, u32[]{:S(2)}, u32[]{:S(2)}) collective-permute-start(f32[16,1152]{1,0:T(8,128)S(1)} %add.64), channel_id=1, source_target_pairs={{0,16},{4,20},{8,24},{12,28},{16,0},{20,4},{24,8},{28,12},{1,17},{... | collective-permute-start | bytes 221192 | tf_op jit(solution)/shard_map/ppermute | solution.py:70
  30.7 0.7 copy-start.2
  31.5 4.4 %collective-permute-start.7 = (f32[16,1152]{1,0:T(8,128)S(1)}, f32[16,1152]{1,0:T(8,128)S(1)}, u32[]{:S(2)}, u32[]{:S(2)}) collective-permute-start(f32[16,1152]{1,0:T(8,128)S(1)} %add.65), channel_id=1, source_target_pairs={{0,2},{1,3},{2,0},{3,1},{4,6},{5,7},{6,4},{7,5},{8,10},{9,11},{10,... | collective-permute-start | bytes 221192 | tf_op jit(solution)/shard_map/ppermute | solution.py:70
  35.8 0.6 copy-start.6
  37.1 2.7 %collective-permute-start.8 = (f32[32,1152]{1,0:T(8,128)}, f32[32,1152]{1,0:T(8,128)}, u32[]{:S(2)}, u32[]{:S(2)}) collective-permute-start(f32[32,1152]{1,0:T(8,128)} %pad_maximum_fusion.3), channel_id=1, source_target_pairs={{0,1},{1,0},{2,3},{3,2},{4,5},{5,4},{6,7},{7,6},{8,9},{9,8},{10,11... | collective-permute-start | bytes 442376 | tf_op jit(solution)/shard_map/ppermute | solution.py:70
  37.2 19.8 %collective-permute-start.10 = (f32[144,576]{1,0:T(8,128)S(1)}, f32[144,576]{1,0:T(8,128)S(1)}, u32[]{:S(2)}, u32[]{:S(2)}) collective-permute-start(f32[144,576]{1,0:T(8,128)S(1)} %pad_maximum_fusion.refs_0_), channel_id=1, source_target_pairs={{0,16},{4,20},{8,24},{12,28},{16,0},{20,4},{24,8},{28,12},{1,17},{... | collective-permute-start | bytes 995336 | tf_op jit(solution)/shard_map/ppermute | solution.py:70
  40.8 3.1 %copy-start.7 = (f32[1,1,2304]{2,1,0:T(1,128)S(1)}, f32[1,1,2304]{2,1,0:T(1,128)}, u32[]{:S(2)}) copy-start(f32[1,1,2304]{2,1,0:T(1,128)} %param.23) | copy-start | bytes 27652
  40.8 16.9 %copy-start.5 = (f32[144,576]{1,0:T(8,128)S(1)}, f32[144,576]{1,0:T(8,128)}, u32[]{:S(2)}) copy-start(f32[144,576]{1,0:T(8,128)} %copy-done.4) | copy-start | bytes 995332
  40.9 18.4 %copy-start.8 = (f32[72]{0:T(128)S(1)}, f32[72]{0:T(128)}, u32[]{:S(2)}) copy-start(f32[72]{0:T(128)} %param.24) | copy-start | bytes 868
  40.9 18.4 %copy-start.9 = (f32[72]{0:T(128)S(1)}, f32[72]{0:T(128)}, u32[]{:S(2)}) copy-start(f32[72]{0:T(128)} %param.25) | copy-start | bytes 868
  42.4 4.6 %collective-permute-start.9 = (f32[32,576]{1,0:T(8,128)S(1)}, f32[32,576]{1,0:T(8,128)S(1)}, u32[]{:S(2)}, u32[]{:S(2)}) collective-permute-start(f32[32,576]{1,0:T(8,128)S(1)} %right.2), channel_id=1, source_target_pairs={{0,4},{4,0},{8,12},{12,8},{16,20},{20,16},{24,28},{28,24},{1,5},{5... | collective-permute-start | bytes 221192 | tf_op jit(solution)/shard_map/ppermute | solution.py:70
  57.0 4.4 %collective-permute-start.11 = (f32[32,576]{1,0:T(8,128)S(1)}, f32[32,576]{1,0:T(8,128)S(1)}, u32[]{:S(2)}, u32[]{:S(2)}) collective-permute-start(f32[32,576]{1,0:T(8,128)S(1)} %add.66), channel_id=1, source_target_pairs={{0,8},{4,12},{8,0},{12,4},{16,24},{20,28},{24,16},{28,20},{1,9},{5... | collective-permute-start | bytes 221192 | tf_op jit(solution)/shard_map/ppermute | solution.py:70
  57.7 10.4 %collective-permute-start.13 = (f32[144,576]{1,0:T(8,128)S(1)}, f32[144,576]{1,0:T(8,128)S(1)}, u32[]{:S(2)}, u32[]{:S(2)}) collective-permute-start(f32[144,576]{1,0:T(8,128)S(1)} %copy-done.5), channel_id=1, source_target_pairs={{0,4},{4,0},{8,12},{12,8},{16,20},{20,16},{24,28},{28,24},{1,5},{5... | collective-permute-start | bytes 995336 | tf_op jit(solution)/shard_map/ppermute | solution.py:70
  61.4 6.7 %collective-permute-start.12 = (f32[32,576]{1,0:T(8,128)S(1)}, f32[32,576]{1,0:T(8,128)S(1)}, u32[]{:S(2)}, u32[]{:S(2)}) collective-permute-start(f32[32,576]{1,0:T(8,128)S(1)} %add.67), channel_id=1, source_target_pairs={{0,16},{4,20},{8,24},{12,28},{16,0},{20,4},{24,8},{28,12},{1,17},{... | collective-permute-start | bytes 221192 | tf_op jit(solution)/shard_map/ppermute | solution.py:70
  69.3 7.6 %copy-start.3 = (f32[144,576]{1,0:T(8,128)S(1)}, f32[144,576]{1,0:T(8,128)}, u32[]{:S(2)}) copy-start(f32[144,576]{1,0:T(8,128)} %copy-done.2) | copy-start | bytes 995332
  69.3 1.5 %collective-permute-start.14 = (f32[32,1280]{1,0:T(8,128)S(1)}, f32[32,1280]{1,0:T(8,128)S(1)}, u32[]{:S(2)}, u32[]{:S(2)}) collective-permute-start(f32[32,1280]{1,0:T(8,128)S(1)} %slice_select_fusion), channel_id=1, source_target_pairs={{0,1},{1,0},{2,3},{3,2},{4,5},{5,4},{6,7},{7,6},{8,9},{9,8},{10,11... | collective-permute-start | bytes 491528 | tf_op jit(solution)/shard_map/ppermute | solution.py:70
  70.8 4.6 %collective-permute-start.15 = (f32[16,1280]{1,0:T(8,128)S(1)}, f32[16,1280]{1,0:T(8,128)S(1)}, u32[]{:S(2)}, u32[]{:S(2)}) collective-permute-start(f32[16,1280]{1,0:T(8,128)S(1)} %slice_select_fusion.2), channel_id=1, source_target_pairs={{0,2},{1,3},{2,0},{3,1},{4,6},{5,7},{6,4},{7,5},{8,10},{9,11},{10,... | collective-permute-start | bytes 245768 | tf_op jit(solution)/shard_map/ppermute | solution.py:70
  71.5 10.4 %collective-permute-start.17 = (f32[144,576]{1,0:T(8,128)S(1)}, f32[144,576]{1,0:T(8,128)S(1)}, u32[]{:S(2)}, u32[]{:S(2)}) collective-permute-start(f32[144,576]{1,0:T(8,128)S(1)} %collective-permute-done.10.refs_0_), channel_id=1, source_target_pairs={{0,8},{4,12},{8,0},{12,4},{16,24},{20,28},{24,16},{28,20},{1,9},{5... | collective-permute-start | bytes 995336 | tf_op jit(solution)/shard_map/ppermute | solution.py:70
  75.4 4.5 %collective-permute-start.16 = (f32[16,1280]{1,0:T(8,128)S(1)}, f32[16,1280]{1,0:T(8,128)S(1)}, u32[]{:S(2)}, u32[]{:S(2)}) collective-permute-start(f32[16,1280]{1,0:T(8,128)S(1)} %select_add_fusion.2), channel_id=1, source_target_pairs={{0,4},{4,0},{8,12},{12,8},{16,20},{20,16},{24,28},{28,24},{1,5},{5... | collective-permute-start | bytes 245768 | tf_op jit(solution)/shard_map/ppermute | solution.py:70
  79.9 13.0 %collective-permute-start.20 = (f32[144,576]{1,0:T(8,128)S(1)}, f32[144,576]{1,0:T(8,128)S(1)}, u32[]{:S(2)}, u32[]{:S(2)}) collective-permute-start(f32[144,576]{1,0:T(8,128)S(1)} %collective-permute-done.10.refs_0_), channel_id=1, source_target_pairs={{0,4},{4,0},{8,12},{12,8},{16,20},{20,16},{24,28},{28,24},{1,5},{5... | collective-permute-start | bytes 995336 | tf_op jit(solution)/shard_map/ppermute | solution.py:70
  81.8 4.4 %collective-permute-start.18 = (f32[16,1280]{1,0:T(8,128)S(1)}, f32[16,1280]{1,0:T(8,128)S(1)}, u32[]{:S(2)}, u32[]{:S(2)}) collective-permute-start(f32[16,1280]{1,0:T(8,128)S(1)} %add.73), channel_id=1, source_target_pairs={{0,8},{4,12},{8,0},{12,4},{16,24},{20,28},{24,16},{28,20},{1,9},{5... | collective-permute-start | bytes 245768 | tf_op jit(solution)/shard_map/ppermute | solution.py:70
  86.3 6.6 %collective-permute-start.19 = (f32[16,1280]{1,0:T(8,128)S(1)}, f32[16,1280]{1,0:T(8,128)S(1)}, u32[]{:S(2)}, u32[]{:S(2)}) collective-permute-start(f32[16,1280]{1,0:T(8,128)S(1)} %add.74), channel_id=1, source_target_pairs={{0,16},{4,20},{8,24},{12,28},{16,0},{20,4},{24,8},{28,12},{1,17},{... | collective-permute-start | bytes 245768 | tf_op jit(solution)/shard_map/ppermute | solution.py:70
  92.9 4.5 %collective-permute-start.21 = (f32[16,1280]{1,0:T(8,128)S(1)}, f32[16,1280]{1,0:T(8,128)S(1)}, u32[]{:S(2)}, u32[]{:S(2)}) collective-permute-start(f32[16,1280]{1,0:T(8,128)S(1)} %add.75), channel_id=1, source_target_pairs={{0,2},{1,3},{2,0},{3,1},{4,6},{5,7},{6,4},{7,5},{8,10},{9,11},{10,... | collective-permute-start | bytes 245768 | tf_op jit(solution)/shard_map/ppermute | solution.py:70
  97.5 1.5 %collective-permute-start.22 = (f32[32,1280]{1,0:T(8,128)S(1)}, f32[32,1280]{1,0:T(8,128)S(1)}, u32[]{:S(2)}, u32[]{:S(2)}) collective-permute-start(f32[32,1280]{1,0:T(8,128)S(1)} %pad_maximum_fusion.2), channel_id=1, source_target_pairs={{0,1},{1,0},{2,3},{3,2},{4,5},{5,4},{6,7},{7,6},{8,9},{9,8},{10,11... | collective-permute-start | bytes 491528 | tf_op jit(solution)/shard_map/ppermute | solution.py:70
  100.5 4.6 %collective-permute-start.23 = (f32[32,576]{1,0:T(8,128)S(1)}, f32[32,576]{1,0:T(8,128)S(1)}, u32[]{:S(2)}, u32[]{:S(2)}) collective-permute-start(f32[32,576]{1,0:T(8,128)S(1)} %right.3), channel_id=1, source_target_pairs={{0,4},{4,0},{8,12},{12,8},{16,20},{20,16},{24,28},{28,24},{1,5},{5... | collective-permute-start | bytes 221192 | tf_op jit(solution)/shard_map/ppermute | solution.py:70
  105.0 4.5 %collective-permute-start.24 = (f32[32,576]{1,0:T(8,128)S(1)}, f32[32,576]{1,0:T(8,128)S(1)}, u32[]{:S(2)}, u32[]{:S(2)}) collective-permute-start(f32[32,576]{1,0:T(8,128)S(1)} %add.76), channel_id=1, source_target_pairs={{0,8},{4,12},{8,0},{12,4},{16,24},{20,28},{24,16},{28,20},{1,9},{5... | collective-permute-start | bytes 221192 | tf_op jit(solution)/shard_map/ppermute | solution.py:70
  105.1 10.7 %collective-permute-start.26 = (f32[144,576]{1,0:T(8,128)S(1)}, f32[144,576]{1,0:T(8,128)S(1)}, u32[]{:S(2)}, u32[]{:S(2)}) collective-permute-start(f32[144,576]{1,0:T(8,128)S(1)} %collective-permute-done.17.refs_0_), channel_id=1, source_target_pairs={{0,4},{4,0},{8,12},{12,8},{16,20},{20,16},{24,28},{28,24},{1,5},{5... | collective-permute-start | bytes 995336 | tf_op jit(solution)/shard_map/ppermute | solution.py:70
  109.6 6.3 %collective-permute-start.25 = (f32[32,576]{1,0:T(8,128)S(1)}, f32[32,576]{1,0:T(8,128)S(1)}, u32[]{:S(2)}, u32[]{:S(2)}) collective-permute-start(f32[32,576]{1,0:T(8,128)S(1)} %add.77), channel_id=1, source_target_pairs={{0,16},{4,20},{8,24},{12,28},{16,0},{20,4},{24,8},{28,12},{1,17},{... | collective-permute-start | bytes 221192 | tf_op jit(solution)/shard_map/ppermute | solution.py:70

commit v5 on v4

--- a/solution.py
+++ b/solution.py
@@ -22,6 +22,7 @@
 
 IN_HBM = pl.BlockSpec(memory_space=pltpu.HBM)
 IN_VMEM = pl.BlockSpec(memory_space=pltpu.VMEM)
+IN_SMEM = pl.BlockSpec(memory_space=pltpu.SMEM)
 SMALL = pltpu.CompilerParams(vmem_limit_bytes=8 * 2**20)
 LARGE = pltpu.CompilerParams(vmem_limit_bytes=16 * 2**20)
 QUICK = pl.CostEstimate(flops=1000, bytes_accessed=1000, transcendentals=0)
@@ -79,45 +80,86 @@
     return gather.before(block, stage, 0)
 
 
-def sum_over_all(part, n_rep, n_shard, gather, stage):
-    place = lax.axis_index("shard")
-    bits = [(mask, (place & mask) != 0) for mask in halves(n_shard)]
-    for mask, high in bits:
-        half = part.shape[0] // 2
-        low_rows, high_rows = part[:half], part[half:]
-        keep = jnp.where(high, high_rows, low_rows)
-        give = jnp.where(high, low_rows, high_rows)
-        part = keep + swap(give, "shard", mask, n_shard)
-    part = sum_over(part, n_rep, gather, stage)
-    for mask, high in reversed(bits):
-        other = swap(part, "shard", mask, n_shard)
-        part = jnp.concatenate([jnp.where(high, other, part), jnp.where(high, part, other)], axis=0)
-    return part
+def sum_over_all(keep, give, bits, n_rep, n_shard, gather, stage):
+    masks = halves(n_shard)
+    for k, mask in enumerate(masks):
+        got = swap(give, "shard", mask, n_shard)
+        if k < len(masks) - 1:
+            keep, give = split(keep, got, bits[k + 1])
+            keep = gather.before(keep, stage, "core")
+    part = sum_over(keep + got, n_rep, gather, stage)
+    for mask, bit in reversed(list(zip(masks, bits))[1:]):
+        part = join(part, swap(part, "shard", mask, n_shard), bit)
+        part = gather.before(part, stage, "x")
+    return part, swap(part, "shard", masks[0], n_shard)
+
+
+def split_kernel(bit_ref, ours, got, keep, give):
+    total = ours[...] + got[...]
+    half = total.shape[0] // 2
+    high = bit_ref[0] != 0
+    keep[...] = jnp.where(high, total[half:], total[:half])
+    give[...] = jnp.where(high, total[:half], total[half:])
+
+
+def split(ours, got, bit):
+    half = pltpu.VMEM((ours.shape[0] // 2, ours.shape[1]), f32)
+    return pl.pallas_call(
+        split_kernel,
+        in_specs=[IN_SMEM, IN_VMEM, IN_VMEM],
+        out_specs=[IN_VMEM] * 2,
+        out_shape=[half, half],
+        compiler_params=SMALL,
+        cost_estimate=QUICK,
+        name="split",
+    )(bit, ours, got)
+
+
+def joined(bit_ref, ours, got):
+    high = bit_ref[0] != 0
+    return jnp.concatenate([jnp.where(high, got, ours), jnp.where(high, ours, got)], axis=0)
+
+
+def join_kernel(bit_ref, ours, got, whole):
+    whole[...] = joined(bit_ref, ours[...], got[...])
+
+
+def join(ours, got, bit):
+    return pl.pallas_call(
+        join_kernel,
+        in_specs=[IN_SMEM, IN_VMEM, IN_VMEM],
+        out_specs=IN_VMEM,
+        out_shape=pltpu.VMEM((2 * ours.shape[0], ours.shape[1]), f32),
+        compiler_params=SMALL,
+        cost_estimate=QUICK,
+        name="join",
+    )(bit, ours, got)
 
 
 class Gather:
     PLAN = (
         ("near", "own", 2, None, (0, 2)),
-        ("turned", "own", 1, (0, 1), (0, 0)),
-        ("far", "own", 4, (0, 4), (1, 2)),
-        ("turned_near", "near", 1, (1, 1), (1, 0)),
-        ("last", "far", 2, (1, 4), (2, 2)),
-        ("turned_far", "far", 1, (2, 1), (2, 0)),
-        ("turned_last", "last", 1, (3, 1), (3, 0)),
+        ("turned", "own", 1, (0, 1), (0, "x")),
+        ("far_a", "own_a", 4, (0, 4), (1, 2)),
+        ("turned_near", "near", 1, (1, 1), (2, "core")),
+        ("far_b", "own_b", 4, (1, 4), (2, 2)),
+        ("turned_far", "far", 1, (2, 1), (2, "x")),
+        ("last", "far", 2, (2, 4), (3, 2)),
+        ("turned_last", "last", 1, ("ahead", 3, 2), (3, 0)),
     )
     INSERTS = {
         (1, 4): ("own", "near"),
         (2, 1): ("turned", "turned_near"),
-        (2, 2): ("far",),
-        (2, 4): ("last",),
-        (3, 4): ("turned_far",),
+        (2, 4): ("far",),
+        (3, 4): ("turned_far", "last"),
     }
     PLACES = {"own": 0, "turned": 1, "near": 2, "far": 4, "last": 6, "turned_near": 3, "turned_far": 5, "turned_last": 7}
 
     def __init__(self, own, count):
         self.count = count
-        self.blocks = {"own": own}
-        self.paired = count == 8 and own.shape[0] % 8 == 0
+        half = own.shape[0] // 2
+        self.blocks = {"own": own, "own_a": own[:half], "own_b": own[half:]}
+        self.paired = count == 8 and own.shape[0] % 16 == 0
         self.rows = None
         self.tasks = {}
         self.results = {}
@@ -127,6 +169,8 @@
         if self.paired:
             for name, source, mask, after, _ in self.PLAN:
                 if after == point:
+                    if source == "far" and source not in self.blocks:
+                        self.blocks["far"] = jnp.concatenate([self.blocks["far_a"], self.blocks["far_b"]], axis=0)
                     self.blocks[name] = swap(self.blocks[source], "rep", mask, self.count)
 
     def start_tasks(self, value, stage, mask):
@@ -156,12 +200,13 @@
             for name, _, _, _, by in self.PLAN:
                 if by == (stage, mask):
                     value, self.blocks[name] = lax.optimization_barrier((value, self.blocks[name]))
+            self.send(("ahead", stage, mask))
         return value
 
     def after(self, value, stage, mask):
         if self.paired:
             for name, source, _, after, _ in self.PLAN:
-                if after == (stage, mask):
+                if after == (stage, mask) and source in self.blocks:
                     value, self.blocks[source] = lax.optimization_barrier((value, self.blocks[source]))
             self.send((stage, mask))
         return value
@@ -190,7 +235,7 @@
     old = [] if rows is None else hold(pltpu.VMEM, rows)
     return pl.pallas_call(
         functools.partial(insert_kernel, masks),
-        in_specs=[pl.BlockSpec(memory_space=pltpu.SMEM)] + [IN_VMEM] * (len(blocks) + len(old)),
+        in_specs=[IN_SMEM] + [IN_VMEM] * (len(blocks) + len(old)),
         out_specs=IN_VMEM,
         out_shape=pltpu.VMEM((height, width), f32),
         input_output_aliases={1 + len(blocks): 0} if old else {},
@@ -200,8 +245,9 @@
     )(place, *blocks, *old)
 
 
-def first_kernel(chunks, grad_q, grad_o, error_q, error_o, basis_q, basis_o, corr_q, corr_o, part, buffer, bases, sems, base_sems):
-    rank, size = basis_q.shape[0], corr_q.shape[1]
+def first_kernel(chunks, bit_ref, grad_q, grad_o, error_q, error_o, basis_q, basis_o, corr_q, corr_o, keep, give, buffer, bases, sems, base_sems):
+    size = corr_q.shape[1]
+    high = bit_ref[0] != 0
     lanes = size // chunks
     base_copies = [pltpu.make_async_copy(source, bases.at[k], base_sems.at[k]) for k, source in enumerate((basis_q, basis_o))]
     copies = {}
@@ -216,23 +262,26 @@
         copy.wait()
     for c in range(chunks):
         at = pl.ds(c * lanes, lanes)
+        parts = []
         for k, corr in enumerate((corr_q, corr_o)):
             copies[c, 2 * k].wait()
             copies[c, 2 * k + 1].wait()
             total = buffer[2 * k, :, at] + buffer[2 * k + 1, :, at]
             corr[:, at] = total
-            part[k * rank : (k + 1) * rank, at] = stacked(bases[k], total, NN)
-
-
-def first(grads, errors, basis_q, basis_o):
+            parts.append(stacked(bases[k], total, NN))
+        keep[:, at] = jnp.where(high, parts[1], parts[0])
+        give[:, at] = jnp.where(high, parts[0], parts[1])
+
+
+def first(grads, errors, basis_q, basis_o, bit):
     width, size = grads[0].shape
     rank = basis_q.shape[0]
     chunks = 3 if size % (3 * LANES) == 0 else 1
     return pl.pallas_call(
         functools.partial(first_kernel, chunks),
-        in_specs=[IN_HBM] * 6,
-        out_specs=[IN_VMEM] * 3,
-        out_shape=[pltpu.VMEM((width, size), f32)] * 2 + [pltpu.VMEM((2 * rank, size), f32)],
+        in_specs=[IN_SMEM] + [IN_HBM] * 6,
+        out_specs=[IN_VMEM] * 4,
+        out_shape=[pltpu.VMEM((width, size), f32)] * 2 + [pltpu.VMEM((rank, size), f32)] * 2,
         scratch_shapes=[
             pltpu.VMEM((4, width, size), f32),
             pltpu.VMEM((2, rank, width), f32),
@@ -241,51 +290,63 @@
         ],
         compiler_params=LARGE,
         name="first",
-    )(*hold(pltpu.HBM, *grads, *errors, basis_q, basis_o))
-
-
-def right_kernel(left, corr_q, corr_o, out):
-    rank = left.shape[0] // 2
-    out[...] = jnp.concatenate([stacked(left[:rank, :], corr_q[...], NT), stacked(left[rank:, :], corr_o[...], NT)], axis=1)
-
-
-def right_of(left, corr_q, corr_o):
-    rank, width = left.shape[0] // 2, corr_q.shape[0]
+    )(bit, *hold(pltpu.HBM, *grads, *errors, basis_q, basis_o))
+
+
+def right_kernel(bit_ref, ours, got, corr_q, corr_o, right, left, *extra):
+    rank, size = ours.shape[0], corr_q.shape[1]
+    whole = joined(bit_ref, ours[...], got[...])
+    left[...] = whole[:, :size]
+    if extra:
+        extra[0][...] = whole[:, size:]
+    right[...] = jnp.concatenate([stacked(whole[:rank, :size], corr_q[...], NT), stacked(whole[rank:, :size], corr_o[...], NT)], axis=1)
+
+
+def right_of(ours, got, bit, corr_q, corr_o):
+    rank = ours.shape[0]
+    width, size = corr_q.shape
+    beside = ours.shape[1] - size
+    shapes = [(rank, 2 * width), (2 * rank, size)] + ([(2 * rank, beside)] if beside else [])
     return pl.pallas_call(
         right_kernel,
-        in_specs=[IN_VMEM] * 3,
-        out_specs=IN_VMEM,
-        out_shape=pltpu.VMEM((rank, 2 * width), f32),
+        in_specs=[IN_SMEM] + [IN_VMEM] * 4,
+        out_specs=[IN_VMEM] * len(shapes),
+        out_shape=[pltpu.VMEM(shape, f32) for shape in shapes],
         compiler_params=SMALL,
         cost_estimate=QUICK,
         name="right",
-    )(left, *hold(pltpu.VMEM, corr_q, corr_o))
-
-
-def left_kernel(right, inverse, corr_q, corr_o, *refs):
-    extra, out = refs[:-1], refs[-1]
+    )(bit, ours, got, *hold(pltpu.VMEM, corr_q, corr_o))
+
+
+def left_kernel(bit_ref, right, inverse, corr_q, corr_o, *refs):
+    extra, keep, give = refs[:-2], refs[-2], refs[-1]
     rank, width = right.shape[0], right.shape[1] // 2
     size = corr_q.shape[1]
+    high = bit_ref[0] != 0
     basis_q = exact(inverse[0], right[:, :width], NN)
     basis_o = exact(inverse[1], right[:, width:], NN)
-    out[:rank, :size] = stacked(basis_q, corr_q[...], NN)
-    out[rank:, :size] = stacked(basis_o, corr_o[...], NN)
+    part_q = stacked(basis_q, corr_q[...], NN)
+    part_o = stacked(basis_o, corr_o[...], NN)
+    keep[:, :size] = jnp.where(high, part_o, part_q)
+    give[:, :size] = jnp.where(high, part_q, part_o)
     if extra:
-        out[:, size:] = extra[0][...]
-
-
-def left_of(right, inverse, corr_q, corr_o, extra):
+        low_rows, high_rows = extra[0][:rank, :], extra[0][rank:, :]
+        keep[:, size:] = jnp.where(high, high_rows, low_rows)
+        give[:, size:] = jnp.where(high, low_rows, high_rows)
+
+
+def left_of(right, inverse, bit, corr_q, corr_o, extra):
     rank, size = right.shape[0], corr_q.shape[1]
-    lanes = size + sum(array.shape[1] for array in extra)
+    half = pltpu.VMEM((rank, size + sum(array.shape[1] for array in extra)), f32)
     return pl.pallas_call(
         left_kernel,
-        in_specs=[IN_VMEM] * (4 + len(extra)),
-        out_specs=IN_VMEM,
-        out_shape=pltpu.VMEM((2 * rank, lanes), f32),
+        in_specs=[IN_SMEM] + [IN_VMEM] * (4 + len(extra)),
+        out_specs=[IN_VMEM] * 2,
+        out_shape=[half, half],
         compiler_params=SMALL,
         cost_estimate=QUICK,
         name="left",
-    )(right, inverse, *hold(pltpu.VMEM, corr_q, corr_o), *extra)
+    )(bit, right, inverse, *hold(pltpu.VMEM, corr_q, corr_o), *extra)
 
 
 def eliminate(gram_q, gram_o, rank):
@@ -348,7 +409,7 @@
     place = lax.axis_index("rep").astype(jnp.int32).reshape(1)
     return pl.pallas_call(
         stack_kernel,
-        in_specs=[pl.BlockSpec(memory_space=pltpu.SMEM), IN_VMEM],
+        in_specs=[IN_SMEM, IN_VMEM],
         out_specs=[IN_VMEM] * 2,
         out_shape=[pltpu.VMEM((2, 6 * rank, size), bf16), pltpu.VMEM((2 * rank, count), f32)],
         compiler_params=SMALL,
@@ -427,35 +488,35 @@
     share = norm_moment.shape[0]
     row_count = q_moment.shape[0]
     device = lax.axis_index("rep") * n_shard + lax.axis_index("shard")
-    keep = step_size * decay_rate
-
-    base = jnp.concatenate([q_weight - keep * q_moment, o_weight - keep * o_moment], axis=1)
+    drop = step_size * decay_rate
+
+    base = jnp.concatenate([q_weight - drop * q_moment, o_weight - drop * o_moment], axis=1)
     gather = Gather(base, n_rep)
 
     grads = norm_grads.reshape(flat)
     own_grads = lax.dynamic_slice(grads, (device * share,), (share,))
-    placed = lax.dynamic_update_slice(-step_size * grads, (norm_weight - keep * norm_moment) - step_size * own_grads, (device * share,))
+    placed = lax.dynamic_update_slice(-step_size * grads, (norm_weight - drop * norm_moment) - step_size * own_grads, (device * share,))
     extra = jnp.concatenate([grads.reshape(-1, LANES), placed.reshape(-1, LANES)], axis=0)
     extra_rows = extra.shape[0]
     extra = jnp.pad(extra, ((0, 2 * rank - extra_rows), (0, 0)))
 
-    corr_q, corr_o, part = first((q_grad[0].T, o_grad[0].T), (q_error[0].T, o_error[0].T), q_basis.T, o_basis.T)
+    place = lax.axis_index("shard")
+    bits = [((place // mask) % 2).astype(jnp.int32).reshape(1) for mask in halves(n_shard)]
+    corr_q, corr_o, keep, give = first((q_grad[0].T, o_grad[0].T), (q_error[0].T, o_error[0].T), q_basis.T, o_basis.T, bits[0])
     for sweep in range(ROUNDS):
         last = sweep == ROUNDS - 1
-        left = sum_over_all(part, n_rep, n_shard, gather, 2 * sweep)
-        if last:
-            extra_sum = left[:extra_rows, size:]
-            left = left[:, :size]
-        right = right_of(left, corr_q, corr_o)
+        ours, got = sum_over_all(keep, give, bits, n_rep, n_shard, gather, 2 * sweep)
+        right, left, *extra_sum = right_of(ours, got, bits[0], corr_q, corr_o)
         if last and gather.paired:
-            gather.tasks[3, 1] = (functools.partial(stack_of, count=row_count), left)
-        gather.tasks[2 * sweep + 1, 2] = (inverse_of, left)
+            gather.tasks[3, 4] = (functools.partial(stack_of, count=row_count), left)
+        gather.tasks[2 * sweep + 1, 1] = (inverse_of, left)
         right = sum_over(right, n_rep, gather, 2 * sweep + 1)
-        inverse = gather.results[2 * sweep + 1, 2]
+        inverse = gather.results[2 * sweep + 1, 1]
         if not last:
-            part = left_of(right, inverse, corr_q, corr_o, [extra] if sweep == ROUNDS - 2 else [])
+            keep, give = left_of(right, inverse, bits[0], corr_q, corr_o, [extra] if sweep == ROUNDS - 2 else [])
+    extra_sum = extra_sum[0][:extra_rows]
     if gather.paired:
-        stack, own = gather.results[3, 1]
+        stack, own = gather.results[3, 4]
         gather.insert([gather.blocks["turned_last"]], ["turned_last"])
         outs = finish(corr_q, corr_o, gather.rows, stack, inverse, right, own, q_moment, o_moment)
     else:

time: 120 us -> 113 us (0.942)
  starting transfers between devices: 39 us -> 30.8 us
  Pallas kernels: 18.2 us -> 22.4 us
  waiting for transfers between devices: 54.9 us -> 51.5 us
  local copies, waits for them, and re-layouts: 1.4 us -> 3.92 us
  other arithmetic: 5.39 us -> 3.15 us
    ppermute x27 -> x28, starting transfers between devices: 39 us -> 30.8 us  [swap(): return lax.ppermute(block, axis, pairs)]
    pallas_call x11 -> x14, Pallas kernels: 11.9 us -> 16.1 us  [the longest x1 5.16 us: first(): pl.pallas_call(functools.partial(first_kernel, chunks), in_specs=[IN_SMEM...]
    ppermute x27 -> x28, waiting for transfers between devices: 54.9 us -> 51.5 us  [swap(): return lax.ppermute(block, axis, pairs)]
    unnamed x20 -> x29, local copies, waits for them, and re-layouts: 1.4 us -> 3.3 us
    select_n x8 -> x0, other arithmetic: 1.76 us -> none  [the longest x3 1.01 us: sum_over_all(): jnp.where(high, other, part)]
  transfers between devices with their start and end apart: 27 -> 28, of which waited for: 22 -> 20; matrix products, arithmetic and copies ran while one was open for 3% -> 4% of each run, Pallas kernels for 6% -> 12%
where the time goes in v5:
time: 113 us
  waiting for transfers between devices  51.5 us (46%)
  starting transfers between devices  30.8 us (27%)
  Pallas kernels  22.4 us (20%)
  local copies, waits for them, and re-layouts  3.92 us (3%)
  other arithmetic  3.15 us (3%)
  between operations  1.16 us (1%)
    ppermute x28, waiting for transfers between devices, swap(): return lax.ppermute(block, axis, pairs)  51.5 us
    ppermute x28, starting transfers between devices, swap(): return lax.ppermute(block, axis, pairs)  30.8 us
    pallas_call x1, Pallas kernels, first(): pl.pallas_call(functools.partial(first_kernel, chunks), in_specs=[IN_SMEM...  5.16 us
    pallas_call x5, Pallas kernels, insert(): pl.pallas_call(functools.partial(insert_kernel, masks), in_specs=[IN_SMEM...  4.03 us
    pallas_call x2, Pallas kernels, right_of(): pl.pallas_call(right_kernel, in_specs=[IN_SMEM] + [IN_VMEM] * 4, out_spec...  3.95 us
    pallas_call x1, Pallas kernels, finish(): pl.pallas_call(functools.partial(finish_kernel, chunks), in_specs=[IN_VME...  3.68 us
    unnamed x29, local copies, waits for them, and re-layouts  3.3 us
    pallas_call x2, Pallas kernels, inverse_of(): pl.pallas_call(inverse_kernel, out_shape=pltpu.VMEM((2, rank, rank), f32)...  2.6 us
  transfers between devices with their start and end apart: 28, of which 20 were waited for; matrix products, arithmetic and copies ran while one was open for 4% of the time, Pallas kernels for 12%

profile of v5, /device:TPU:0, one launch (start us, length us, event | category | flops | bytes accessed | tf_op | source)
XLA Modules:
  0.0 113.0 jit_solution(8412578865172085656)
XLA Ops:
  0.7 5.2 %first.1 = (f32[288,1152]{1,0:T(8,128)S(1)}, f32[288,1152]{1,0:T(8,128)S(1)}, f32[32,1152]{1,0:T(8,128)S(1)}, f32[32,1152]{1,0:T(8,128)}) custom-call(s32[1]{0:T(128)} %bitcast.bit_ref, f32[288,1152]{1,0:T(8,128)} %bitcast.35, f32[288,1152]{1,0:T(8,128)} %bitcast.36, f32[288,1152]{1,0:T(8,128)} %bitcast.37, f32[288,1152]{1,0:T(8,128)} %bitcast.38, ...), custom_call_target="tpu_custom_call" | custom-call | tf_op jit(solution)/shard_map/first/pallas_call | solution.py:280
  7.3 2.7 %collective-permute-start.3 = (f32[144,576]{1,0:T(8,128)S(1)}, f32[144,576]{1,0:T(8,128)}, u32[]{:S(2)}, u32[]{:S(2)}) collective-permute-start(f32[144,576]{1,0:T(8,128)S(1)} %pad_maximum_fusion.refs_0_), channel_id=1, source_target_pairs={{0,8},{4,12},{8,0},{12,4},{16,24},{20,28},{24,16},{28,20},{1,9},{5... | collective-permute-start | bytes 995336 | tf_op jit(solution)/shard_map/ppermute | solution.py:71
  10.0 0.9 copy-done.5
  10.9 0.9 split.2
  11.8 1.6 %collective-permute-start.1 = (f32[16,1152]{1,0:T(8,128)S(1)}, f32[16,1152]{1,0:T(8,128)S(1)}, u32[]{:S(2)}, u32[]{:S(2)}) collective-permute-start(f32[16,1152]{1,0:T(8,128)S(1)} %get-tuple-element.91), channel_id=1, source_target_pairs={{0,2},{1,3},{2,0},{3,1},{4,6},{5,7},{6,4},{7,5},{8,10},{9,11},{10,... | collective-permute-start | bytes 221192 | tf_op jit(solution)/shard_map/ppermute | solution.py:71
  13.4 2.9 %collective-permute-done.1 = f32[16,1152]{1,0:T(8,128)S(1)} collective-permute-done((f32[16,1152]{1,0:T(8,128)S(1)}, f32[16,1152]{1,0:T(8,128)S(1)}, u32[]{:S(2)}, u32[]{:S(2)}) %collective-permute-start.1) | collective-permute-done | bytes 73760 | tf_op jit(solution)/shard_map/ppermute | solution.py:71
  16.3 1.6 %collective-permute-start.2 = (f32[16,1152]{1,0:T(8,128)S(1)}, f32[16,1152]{1,0:T(8,128)S(1)}, u32[]{:S(2)}, u32[]{:S(2)}) collective-permute-start(f32[16,1152]{1,0:T(8,128)S(1)} %add.66), channel_id=1, source_target_pairs={{0,4},{4,0},{8,12},{12,8},{16,20},{20,16},{24,28},{28,24},{1,5},{5... | collective-permute-start | bytes 221192 | tf_op jit(solution)/shard_map/ppermute | solution.py:71
  17.8 2.8 %collective-permute-done.2 = f32[16,1152]{1,0:T(8,128)S(1)} collective-permute-done((f32[16,1152]{1,0:T(8,128)S(1)}, f32[16,1152]{1,0:T(8,128)S(1)}, u32[]{:S(2)}, u32[]{:S(2)}) %collective-permute-start.2) | collective-permute-done | bytes 73760 | tf_op jit(solution)/shard_map/ppermute | solution.py:71
  20.7 1.6 %collective-permute-start.7 = (f32[144,576]{1,0:T(8,128)S(1)}, f32[144,576]{1,0:T(8,128)S(1)}, u32[]{:S(2)}, u32[]{:S(2)}) collective-permute-start(f32[144,576]{1,0:T(8,128)S(1)} %pad_maximum_fusion.refs_0_), channel_id=1, source_target_pairs={{0,4},{4,0},{8,12},{12,8},{16,20},{20,16},{24,28},{28,24},{1,5},{5... | collective-permute-start | bytes 995336 | tf_op jit(solution)/shard_map/ppermute | solution.py:71
  23.0 3.7 %collective-permute-done.4 = f32[16,1152]{1,0:T(8,128)S(1)} collective-permute-done((f32[16,1152]{1,0:T(8,128)S(1)}, f32[16,1152]{1,0:T(8,128)S(1)}, u32[]{:S(2)}, u32[]{:S(2)}) %collective-permute-start.4) | collective-permute-done | bytes 73760 | tf_op jit(solution)/shard_map/ppermute | solution.py:71
  26.6 3.1 %collective-permute-start.5 = (f32[16,1152]{1,0:T(8,128)S(1)}, f32[16,1152]{1,0:T(8,128)S(1)}, u32[]{:S(2)}, u32[]{:S(2)}) collective-permute-start(f32[16,1152]{1,0:T(8,128)S(1)} %add.68), channel_id=1, source_target_pairs={{0,16},{4,20},{8,24},{12,28},{16,0},{20,4},{24,8},{28,12},{1,17},{... | collective-permute-start | bytes 221192 | tf_op jit(solution)/shard_map/ppermute | solution.py:71
  29.8 1.9 %fusion.1 = (f32[72,576]{1,0:T(8,128)}, f32[72,576]{1,0:T(8,128)}) fusion(f32[144,288]{1,0:T(8,128)} %copy-done.7, f32[144,288]{1,0:T(8,128)} %copy-done.6), kind=kLoop, calls=%fused_computation.8 | loop fusion | flops 82944 | bytes 663552 | tf_op jit(solution)/shard_map/concatenate | solution.py:493
  31.7 1.2 %collective-permute-done.5 = f32[16,1152]{1,0:T(8,128)S(1)} collective-permute-done((f32[16,1152]{1,0:T(8,128)S(1)}, f32[16,1152]{1,0:T(8,128)S(1)}, u32[]{:S(2)}, u32[]{:S(2)}) %collective-permute-start.5) | collective-permute-done | bytes 73760 | tf_op jit(solution)/shard_map/ppermute | solution.py:71
  32.9 1.6 %collective-permute-start.6 = (f32[16,1152]{1,0:T(8,128)S(1)}, f32[16,1152]{1,0:T(8,128)S(1)}, u32[]{:S(2)}, u32[]{:S(2)}) collective-permute-start(f32[16,1152]{1,0:T(8,128)S(1)} %add.69.ours), channel_id=1, source_target_pairs={{0,2},{1,3},{2,0},{3,1},{4,6},{5,7},{6,4},{7,5},{8,10},{9,11},{10,... | collective-permute-start | bytes 221192 | tf_op jit(solution)/shard_map/ppermute | solution.py:71
  34.5 2.9 %collective-permute-done.6.got = f32[16,1152]{1,0:T(8,128)S(1)} collective-permute-done((f32[16,1152]{1,0:T(8,128)S(1)}, f32[16,1152]{1,0:T(8,128)S(1)}, u32[]{:S(2)}, u32[]{:S(2)}) %collective-permute-start.6) | collective-permute-done | bytes 73760 | tf_op jit(solution)/shard_map/ppermute | solution.py:71
  38.0 0.7 copy-done.2
  38.7 2.1 %collective-permute-start.10 = (f32[72,576]{1,0:T(8,128)}, f32[72,576]{1,0:T(8,128)}, u32[]{:S(2)}, u32[]{:S(2)}) collective-permute-start(f32[72,576]{1,0:T(8,128)} %get-tuple-element.102), channel_id=1, source_target_pairs={{0,16},{4,20},{8,24},{12,28},{16,0},{20,4},{24,8},{28,12},{1,17},{... | collective-permute-start | bytes 497672 | tf_op jit(solution)/shard_map/ppermute | solution.py:71
  40.9 2.5 %right.2 = (f32[32,576]{1,0:T(8,128)S(1)}, f32[64,1152]{1,0:T(8,128)S(1)}) custom-call(s32[1]{0:T(128)} %bitcast.bit_ref, f32[32,1152]{1,0:T(8,128)} %join.2.ours, f32[32,1152]{1,0:T(8,128)} %collective-permute-done.8.got, f32[288,1152]{1,0:T(8,128)S(1)} %get-tuple-element.86.corr_q, f32[288,1152]{1,0:T(8,128)S(1)} %get-tuple-element.87.corr_o), custom_call_target="tpu_custom_call" | custom-call | flops 1000 | bytes 1000 | tf_op jit(solution)/shard_map/right/pallas_call | solution.py:310
  43.4 0.8 collective-permute-start.9
  44.2 1.3 %inverse.2 = f32[2,32,32]{2,1,0:T(8,128)S(1)} custom-call(f32[64,1152]{1,0:T(8,128)S(1)} %get-tuple-element.98.left), custom_call_target="tpu_custom_call" | custom-call | flops 1000 | bytes 6000000 | tf_op jit(solution)/shard_map/inverse/pallas_call | solution.py:387
  45.5 2.5 %collective-permute-done.9 = f32[32,576]{1,0:T(8,128)S(1)} collective-permute-done((f32[32,576]{1,0:T(8,128)S(1)}, f32[32,576]{1,0:T(8,128)S(1)}, u32[]{:S(2)}, u32[]{:S(2)}) %collective-permute-start.9) | collective-permute-done | bytes 73760 | tf_op jit(solution)/shard_map/ppermute | solution.py:71
  48.0 2.2 %collective-permute-done.10 = f32[72,576]{1,0:T(8,128)} collective-permute-done((f32[72,576]{1,0:T(8,128)}, f32[72,576]{1,0:T(8,128)}, u32[]{:S(2)}, u32[]{:S(2)}) %collective-permute-start.10) | collective-permute-done | bytes 165920 | tf_op jit(solution)/shard_map/ppermute | solution.py:71
  51.1 3.6 %collective-permute-done.11 = f32[32,576]{1,0:T(8,128)S(1)} collective-permute-done((f32[32,576]{1,0:T(8,128)S(1)}, f32[32,576]{1,0:T(8,128)S(1)}, u32[]{:S(2)}, u32[]{:S(2)}) %collective-permute-start.11) | collective-permute-done | bytes 73760 | tf_op jit(solution)/shard_map/ppermute | solution.py:71
  54.7 1.1 collective-permute-start.12
  55.8 1.8 %insert.5.refs_2_ = f32[576,1152]{1,0:T(8,128)S(1)} custom-call(s32[1]{0:T(128)} %bitcast.11.place_ref, f32[144,576]{1,0:T(8,128)S(1)} %pad_maximum_fusion.refs_0_, f32[144,576]{1,0:T(8,128)} %collective-permute-done.3.refs_1_), custom_call_target="tpu_custom_call" | custom-call | flops 1000 | bytes 6000000 | tf_op jit(solution)/shard_map/insert/pallas_call | solution.py:236
  57.6 3.1 %collective-permute-done.12 = f32[32,576]{1,0:T(8,128)S(1)} collective-permute-done((f32[32,576]{1,0:T(8,128)S(1)}, f32[32,576]{1,0:T(8,128)S(1)}, u32[]{:S(2)}, u32[]{:S(2)}) %collective-permute-start.12) | collective-permute-done | bytes 73760 | tf_op jit(solution)/shard_map/ppermute | solution.py:71
  60.7 1.2 %left.1 = (f32[32,1280]{1,0:T(8,128)S(1)}, f32[32,1280]{1,0:T(8,128)S(1)}) custom-call(s32[1]{0:T(128)} %bitcast.bit_ref, f32[32,576]{1,0:T(8,128)S(1)} %add.72.right, f32[2,32,32]{2,1,0:T(8,128)S(1)} %inverse.2, f32[288,1152]{1,0:T(8,128)S(1)} %get-tuple-element.86.corr_q, f32[288,1152]{1,0:T(8,128)S(1)} %get-tuple-element.87.corr_o, ...), custom_call_target="tpu_custom_call" | custom-call | flops 1000 | bytes 1000 | tf_op jit(solution)/shard_map/left/pallas_call | solution.py:341
  62.6 0.8 collective-permute-done.13.got
  63.4 1.6 %collective-permute-start.15 = (f32[16,1280]{1,0:T(8,128)S(1)}, f32[16,1280]{1,0:T(8,128)S(1)}, u32[]{:S(2)}, u32[]{:S(2)}) collective-permute-start(f32[16,1280]{1,0:T(8,128)S(1)} %get-tuple-element.115), channel_id=1, source_target_pairs={{0,2},{1,3},{2,0},{3,1},{4,6},{5,7},{6,4},{7,5},{8,10},{9,11},{10,... | collective-permute-start | bytes 245768 | tf_op jit(solution)/shard_map/ppermute | solution.py:71
  64.9 0.9 constant_dynamic-update-slice_fusion.1
  65.9 2.1 %collective-permute-done.15 = f32[16,1280]{1,0:T(8,128)S(1)} collective-permute-done((f32[16,1280]{1,0:T(8,128)S(1)}, f32[16,1280]{1,0:T(8,128)S(1)}, u32[]{:S(2)}, u32[]{:S(2)}) %collective-permute-start.15) | collective-permute-done | bytes 81952 | tf_op jit(solution)/shard_map/ppermute | solution.py:71
  68.5 5.0 %collective-permute-done.17 = f32[72,576]{1,0:T(8,128)S(1)} collective-permute-done((f32[72,576]{1,0:T(8,128)S(1)}, f32[72,576]{1,0:T(8,128)S(1)}, u32[]{:S(2)}, u32[]{:S(2)}) %collective-permute-start.17) | collective-permute-done | bytes 165920 | tf_op jit(solution)/shard_map/ppermute | solution.py:71
  74.9 4.4 %collective-permute-done.18 = f32[16,1280]{1,0:T(8,128)S(1)} collective-permute-done((f32[16,1280]{1,0:T(8,128)S(1)}, f32[16,1280]{1,0:T(8,128)S(1)}, u32[]{:S(2)}, u32[]{:S(2)}) %collective-permute-start.18) | collective-permute-done | bytes 81952 | tf_op jit(solution)/shard_map/ppermute | solution.py:71
  80.2 4.9 %collective-permute-done.19 = f32[16,1280]{1,0:T(8,128)S(1)} collective-permute-done((f32[16,1280]{1,0:T(8,128)S(1)}, f32[16,1280]{1,0:T(8,128)S(1)}, u32[]{:S(2)}, u32[]{:S(2)}) %collective-permute-start.19) | collective-permute-done | bytes 81952 | tf_op jit(solution)/shard_map/ppermute | solution.py:71
  85.2 1.5 %collective-permute-start.20 = (f32[16,1280]{1,0:T(8,128)S(1)}, f32[16,1280]{1,0:T(8,128)S(1)}, u32[]{:S(2)}, u32[]{:S(2)}) collective-permute-start(f32[16,1280]{1,0:T(8,128)S(1)} %add.78.ours), channel_id=1, source_target_pairs={{0,2},{1,3},{2,0},{3,1},{4,6},{5,7},{6,4},{7,5},{8,10},{9,11},{10,... | collective-permute-start | bytes 245768 | tf_op jit(solution)/shard_map/ppermute | solution.py:71
  86.7 3.0 %collective-permute-done.20.got = f32[16,1280]{1,0:T(8,128)S(1)} collective-permute-done((f32[16,1280]{1,0:T(8,128)S(1)}, f32[16,1280]{1,0:T(8,128)S(1)}, u32[]{:S(2)}, u32[]{:S(2)}) %collective-permute-start.20) | collective-permute-done | bytes 81952 | tf_op jit(solution)/shard_map/ppermute | solution.py:71
  89.8 1.4 %collective-permute-done.22.got = f32[32,1280]{1,0:T(8,128)S(1)} collective-permute-done((f32[32,1280]{1,0:T(8,128)S(1)}, f32[32,1280]{1,0:T(8,128)S(1)}, u32[]{:S(2)}, u32[]{:S(2)}) %collective-permute-start.22) | collective-permute-done | bytes 163872 | tf_op jit(solution)/shard_map/ppermute | solution.py:71
  91.2 1.5 %right.3 = (f32[32,576]{1,0:T(8,128)S(1)}, f32[64,1152]{1,0:T(8,128)S(1)}, f32[64,128]{1,0:T(8,128)S(1)}) custom-call(s32[1]{0:T(128)} %bitcast.bit_ref, f32[32,1280]{1,0:T(8,128)S(1)} %join.3.ours, f32[32,1280]{1,0:T(8,128)S(1)} %collective-permute-done.22.got, f32[288,1152]{1,0:T(8,128)S(1)} %get-tuple-element.86.corr_q, ...), custom_call_target="tpu_custom_call" | custom-call | flops 1000 | bytes 1000 | tf_op jit(solution)/shard_map/right/pallas_call | solution.py:310
  92.6 1.6 %collective-permute-start.23 = (f32[32,576]{1,0:T(8,128)S(1)}, f32[32,576]{1,0:T(8,128)S(1)}, u32[]{:S(2)}, u32[]{:S(2)}) collective-permute-start(f32[32,576]{1,0:T(8,128)S(1)} %get-tuple-element.134), channel_id=1, source_target_pairs={{0,4},{4,0},{8,12},{12,8},{16,20},{20,16},{24,28},{28,24},{1,5},{5... | collective-permute-start | bytes 221192 | tf_op jit(solution)/shard_map/ppermute | solution.py:71
  94.2 1.3 %inverse.3 = f32[2,32,32]{2,1,0:T(8,128)S(1)} custom-call(f32[64,1152]{1,0:T(8,128)S(1)} %get-tuple-element.143.left), custom_call_target="tpu_custom_call" | custom-call | flops 1000 | bytes 6000000 | tf_op jit(solution)/shard_map/inverse/pallas_call | solution.py:387
  95.5 1.7 %collective-permute-done.23 = f32[32,576]{1,0:T(8,128)S(1)} collective-permute-done((f32[32,576]{1,0:T(8,128)S(1)}, f32[32,576]{1,0:T(8,128)S(1)}, u32[]{:S(2)}, u32[]{:S(2)}) %collective-permute-start.23) | collective-permute-done | bytes 73760 | tf_op jit(solution)/shard_map/ppermute | solution.py:71
  97.2 2.0 %collective-permute-start.25 = (f32[32,576]{1,0:T(8,128)S(1)}, f32[32,576]{1,0:T(8,128)S(1)}, u32[]{:S(2)}, u32[]{:S(2)}) collective-permute-start(f32[32,576]{1,0:T(8,128)S(1)} %add.79), channel_id=1, source_target_pairs={{0,8},{4,12},{8,0},{12,4},{16,24},{20,28},{24,16},{28,20},{1,9},{5... | collective-permute-start | bytes 221192 | tf_op jit(solution)/shard_map/ppermute | solution.py:71
  99.2 1.5 %collective-permute-start.27 = (f32[144,576]{1,0:T(8,128)S(1)}, f32[144,576]{1,0:T(8,128)S(1)}, u32[]{:S(2)}, u32[]{:S(2)}) collective-permute-start(f32[144,576]{1,0:T(8,128)S(1)} %collective-permute-done.24.refs_1_), channel_id=1, source_target_pairs={{0,4},{4,0},{8,12},{12,8},{16,20},{20,16},{24,28},{28,24},{1,5},{5... | collective-permute-start | bytes 995336 | tf_op jit(solution)/shard_map/ppermute | solution.py:71
  101.7 2.4 %collective-permute-start.26 = (f32[32,576]{1,0:T(8,128)S(1)}, f32[32,576]{1,0:T(8,128)S(1)}, u32[]{:S(2)}, u32[]{:S(2)}) collective-permute-start(f32[32,576]{1,0:T(8,128)S(1)} %add.80), channel_id=1, source_target_pairs={{0,16},{4,20},{8,24},{12,28},{16,0},{20,4},{24,8},{28,12},{1,17},{... | collective-permute-start | bytes 221192 | tf_op jit(solution)/shard_map/ppermute | solution.py:71
  104.8 0.7 insert.8.refs_1_
  105.6 1.6 %collective-permute-done.26 = f32[32,576]{1,0:T(8,128)S(1)} collective-permute-done((f32[32,576]{1,0:T(8,128)S(1)}, f32[32,576]{1,0:T(8,128)S(1)}, u32[]{:S(2)}, u32[]{:S(2)}) %collective-permute-start.26) | collective-permute-done | bytes 73760 | tf_op jit(solution)/shard_map/ppermute | solution.py:71
  107.2 1.6 %collective-permute-done.27.refs_0_ = f32[144,576]{1,0:T(8,128)S(1)} collective-permute-done((f32[144,576]{1,0:T(8,128)S(1)}, f32[144,576]{1,0:T(8,128)S(1)}, u32[]{:S(2)}, u32[]{:S(2)}) %collective-permute-start.27) | collective-permute-done | bytes 331808 | tf_op jit(solution)/shard_map/ppermute | solution.py:71
  109.2 3.7 %finish.1 = (f32[288,1152]{1,0:T(8,128)}, f32[288,1152]{1,0:T(8,128)}, f32[288,1152]{1,0:T(8,128)}, f32[288,1152]{1,0:T(8,128)}, f32[144,288]{1,0:T(8,128)}, /*index=5*/f32[144,288]{1,0:T(8,128)}) custom-call(f32[288,1152]{1,0:T(8,128)S(1)} %get-tuple-element.86.corr_q, f32[288,1152]{1,0:T(8,128)S(1)} %get-tuple-element.87.corr_o, ...), custom_call_target="tpu_custom_call" | custom-call | tf_op jit(solution)/shard_map/finish/pallas_call | solution.py:452
  (77 shorter events, 9.5 us)
Async XLA Ops:
  0.7 5.7 %copy-start = (f32[144,288]{1,0:T(8,128)S(1)}, f32[144,288]{1,0:T(8,128)}, u32[]{:S(2)}) copy-start(f32[144,288]{1,0:T(8,128)} %moment_o.1) | copy-start | bytes 497668
  0.7 5.7 %copy-start.1 = (f32[144,288]{1,0:T(8,128)S(1)}, f32[144,288]{1,0:T(8,128)}, u32[]{:S(2)}) copy-start(f32[144,288]{1,0:T(8,128)} %moment_q.1) | copy-start | bytes 497668
  0.7 5.7 %copy-start.8 = (f32[144,288]{1,0:T(8,128)S(1)}, f32[144,288]{1,0:T(8,128)}, u32[]{:S(2)}) copy-start(f32[144,288]{1,0:T(8,128)} %param.22) | copy-start | bytes 497668
  0.7 5.7 %copy-start.9 = (f32[144,288]{1,0:T(8,128)S(1)}, f32[144,288]{1,0:T(8,128)}, u32[]{:S(2)}) copy-start(f32[144,288]{1,0:T(8,128)} %param.21) | copy-start | bytes 497668
  5.9 0.7 copy-start.4
  5.9 4.1 %collective-permute-start = (f32[32,1152]{1,0:T(8,128)}, f32[32,1152]{1,0:T(8,128)}, u32[]{:S(2)}, u32[]{:S(2)}) collective-permute-start(f32[32,1152]{1,0:T(8,128)} %get-tuple-element.89), channel_id=1, source_target_pairs={{0,1},{1,0},{2,3},{3,2},{4,5},{5,4},{6,7},{7,6},{8,9},{9,8},{10,11... | collective-permute-start | bytes 442376 | tf_op jit(solution)/shard_map/ppermute | solution.py:71
  6.5 0.7 copy-start.6
  6.5 0.8 copy-start.7
  7.3 15.0 %collective-permute-start.3 = (f32[144,576]{1,0:T(8,128)S(1)}, f32[144,576]{1,0:T(8,128)}, u32[]{:S(2)}, u32[]{:S(2)}) collective-permute-start(f32[144,576]{1,0:T(8,128)S(1)} %pad_maximum_fusion.refs_0_), channel_id=1, source_target_pairs={{0,8},{4,12},{8,0},{12,4},{16,24},{20,28},{24,16},{28,20},{1,9},{5... | collective-permute-start | bytes 995336 | tf_op jit(solution)/shard_map/ppermute | solution.py:71
  10.0 0.9 copy-start.5
  11.8 4.4 %collective-permute-start.1 = (f32[16,1152]{1,0:T(8,128)S(1)}, f32[16,1152]{1,0:T(8,128)S(1)}, u32[]{:S(2)}, u32[]{:S(2)}) collective-permute-start(f32[16,1152]{1,0:T(8,128)S(1)} %get-tuple-element.91), channel_id=1, source_target_pairs={{0,2},{1,3},{2,0},{3,1},{4,6},{5,7},{6,4},{7,5},{8,10},{9,11},{10,... | collective-permute-start | bytes 221192 | tf_op jit(solution)/shard_map/ppermute | solution.py:71
  16.3 4.4 %collective-permute-start.2 = (f32[16,1152]{1,0:T(8,128)S(1)}, f32[16,1152]{1,0:T(8,128)S(1)}, u32[]{:S(2)}, u32[]{:S(2)}) collective-permute-start(f32[16,1152]{1,0:T(8,128)S(1)} %add.66), channel_id=1, source_target_pairs={{0,4},{4,0},{8,12},{12,8},{16,20},{20,16},{24,28},{28,24},{1,5},{5... | collective-permute-start | bytes 221192 | tf_op jit(solution)/shard_map/ppermute | solution.py:71
  20.7 17.3 %collective-permute-start.7 = (f32[144,576]{1,0:T(8,128)S(1)}, f32[144,576]{1,0:T(8,128)S(1)}, u32[]{:S(2)}, u32[]{:S(2)}) collective-permute-start(f32[144,576]{1,0:T(8,128)S(1)} %pad_maximum_fusion.refs_0_), channel_id=1, source_target_pairs={{0,4},{4,0},{8,12},{12,8},{16,20},{20,16},{24,28},{28,24},{1,5},{5... | collective-permute-start | bytes 995336 | tf_op jit(solution)/shard_map/ppermute | solution.py:71
  22.3 4.4 %collective-permute-start.4 = (f32[16,1152]{1,0:T(8,128)S(1)}, f32[16,1152]{1,0:T(8,128)S(1)}, u32[]{:S(2)}, u32[]{:S(2)}) collective-permute-start(f32[16,1152]{1,0:T(8,128)S(1)} %add.67), channel_id=1, source_target_pairs={{0,8},{4,12},{8,0},{12,4},{16,24},{20,28},{24,16},{28,20},{1,9},{5... | collective-permute-start | bytes 221192 | tf_op jit(solution)/shard_map/ppermute | solution.py:71
  26.6 6.2 %collective-permute-start.5 = (f32[16,1152]{1,0:T(8,128)S(1)}, f32[16,1152]{1,0:T(8,128)S(1)}, u32[]{:S(2)}, u32[]{:S(2)}) collective-permute-start(f32[16,1152]{1,0:T(8,128)S(1)} %add.68), channel_id=1, source_target_pairs={{0,16},{4,20},{8,24},{12,28},{16,0},{20,4},{24,8},{28,12},{1,17},{... | collective-permute-start | bytes 221192 | tf_op jit(solution)/shard_map/ppermute | solution.py:71
  32.9 4.4 %collective-permute-start.6 = (f32[16,1152]{1,0:T(8,128)S(1)}, f32[16,1152]{1,0:T(8,128)S(1)}, u32[]{:S(2)}, u32[]{:S(2)}) collective-permute-start(f32[16,1152]{1,0:T(8,128)S(1)} %add.69.ours), channel_id=1, source_target_pairs={{0,2},{1,3},{2,0},{3,1},{4,6},{5,7},{6,4},{7,5},{8,10},{9,11},{10,... | collective-permute-start | bytes 221192 | tf_op jit(solution)/shard_map/ppermute | solution.py:71
  38.0 0.7 copy-start.2
  38.7 2.1 %collective-permute-start.8 = (f32[32,1152]{1,0:T(8,128)}, f32[32,1152]{1,0:T(8,128)}, u32[]{:S(2)}, u32[]{:S(2)}) collective-permute-start(f32[32,1152]{1,0:T(8,128)} %join.2.ours), channel_id=1, source_target_pairs={{0,1},{1,0},{2,3},{3,2},{4,5},{5,4},{6,7},{7,6},{8,9},{9,8},{10,11... | collective-permute-start | bytes 442376 | tf_op jit(solution)/shard_map/ppermute | solution.py:71
  38.7 11.5 %collective-permute-start.10 = (f32[72,576]{1,0:T(8,128)}, f32[72,576]{1,0:T(8,128)}, u32[]{:S(2)}, u32[]{:S(2)}) collective-permute-start(f32[72,576]{1,0:T(8,128)} %get-tuple-element.102), channel_id=1, source_target_pairs={{0,16},{4,20},{8,24},{12,28},{16,0},{20,4},{24,8},{28,12},{1,17},{... | collective-permute-start | bytes 497672 | tf_op jit(solution)/shard_map/ppermute | solution.py:71
  40.9 3.3 %copy-start.11 = (f32[1,1,2304]{2,1,0:T(1,128)S(1)}, f32[1,1,2304]{2,1,0:T(1,128)}, u32[]{:S(2)}) copy-start(f32[1,1,2304]{2,1,0:T(1,128)} %param.23) | copy-start | bytes 27652
  40.9 9.4 %copy-start.12 = (f32[72]{0:T(128)S(1)}, f32[72]{0:T(128)}, u32[]{:S(2)}) copy-start(f32[72]{0:T(128)} %param.24) | copy-start | bytes 868
  40.9 9.4 %copy-start.13 = (f32[72]{0:T(128)S(1)}, f32[72]{0:T(128)}, u32[]{:S(2)}) copy-start(f32[72]{0:T(128)} %param.25) | copy-start | bytes 868
  43.4 4.6 %collective-permute-start.9 = (f32[32,576]{1,0:T(8,128)S(1)}, f32[32,576]{1,0:T(8,128)S(1)}, u32[]{:S(2)}, u32[]{:S(2)}) collective-permute-start(f32[32,576]{1,0:T(8,128)S(1)} %get-tuple-element.97), channel_id=1, source_target_pairs={{0,4},{4,0},{8,12},{12,8},{16,20},{20,16},{24,28},{28,24},{1,5},{5... | collective-permute-start | bytes 221192 | tf_op jit(solution)/shard_map/ppermute | solution.py:71
  50.2 4.4 %collective-permute-start.11 = (f32[32,576]{1,0:T(8,128)S(1)}, f32[32,576]{1,0:T(8,128)S(1)}, u32[]{:S(2)}, u32[]{:S(2)}) collective-permute-start(f32[32,576]{1,0:T(8,128)S(1)} %add.70), channel_id=1, source_target_pairs={{0,8},{4,12},{8,0},{12,4},{16,24},{20,28},{24,16},{28,20},{1,9},{5... | collective-permute-start | bytes 221192 | tf_op jit(solution)/shard_map/ppermute | solution.py:71
  50.5 15.4 %collective-permute-start.14 = (f32[144,576]{1,0:T(8,128)}, f32[144,576]{1,0:T(8,128)S(1)}, u32[]{:S(2)}, u32[]{:S(2)}) collective-permute-start(f32[144,576]{1,0:T(8,128)} %collective-permute-done.3.refs_1_), channel_id=1, source_target_pairs={{0,4},{4,0},{8,12},{12,8},{16,20},{20,16},{24,28},{28,24},{1,5},{5... | collective-permute-start | bytes 995336 | tf_op jit(solution)/shard_map/ppermute | solution.py:71
  54.7 6.0 %collective-permute-start.12 = (f32[32,576]{1,0:T(8,128)S(1)}, f32[32,576]{1,0:T(8,128)S(1)}, u32[]{:S(2)}, u32[]{:S(2)}) collective-permute-start(f32[32,576]{1,0:T(8,128)S(1)} %add.71), channel_id=1, source_target_pairs={{0,16},{4,20},{8,24},{12,28},{16,0},{20,4},{24,8},{28,12},{1,17},{... | collective-permute-start | bytes 221192 | tf_op jit(solution)/shard_map/ppermute | solution.py:71
  60.7 1.3 %copy-start.10 = (f32[72,576]{1,0:T(8,128)S(1)}, f32[72,576]{1,0:T(8,128)}, u32[]{:S(2)}) copy-start(f32[72,576]{1,0:T(8,128)} %get-tuple-element.123) | copy-start | bytes 497668
  61.9 12.2 %copy-start.3 = (f32[144,576]{1,0:T(8,128)S(1)}, f32[144,576]{1,0:T(8,128)}, u32[]{:S(2)}) copy-start(f32[144,576]{1,0:T(8,128)} %copy-done.2) | copy-start | bytes 995332
  61.9 1.5 %collective-permute-start.13 = (f32[32,1280]{1,0:T(8,128)S(1)}, f32[32,1280]{1,0:T(8,128)S(1)}, u32[]{:S(2)}, u32[]{:S(2)}) collective-permute-start(f32[32,1280]{1,0:T(8,128)S(1)} %get-tuple-element.112), channel_id=1, source_target_pairs={{0,1},{1,0},{2,3},{3,2},{4,5},{5,4},{6,7},{7,6},{8,9},{9,8},{10,11... | collective-permute-start | bytes 491528 | tf_op jit(solution)/shard_map/ppermute | solution.py:71
  62.0 11.5 %collective-permute-start.17 = (f32[72,576]{1,0:T(8,128)S(1)}, f32[72,576]{1,0:T(8,128)S(1)}, u32[]{:S(2)}, u32[]{:S(2)}) collective-permute-start(f32[72,576]{1,0:T(8,128)S(1)} %copy-done.10), channel_id=1, source_target_pairs={{0,16},{4,20},{8,24},{12,28},{16,0},{20,4},{24,8},{28,12},{1,17},{... | collective-permute-start | bytes 497672 | tf_op jit(solution)/shard_map/ppermute | solution.py:71
  63.4 4.6 %collective-permute-start.15 = (f32[16,1280]{1,0:T(8,128)S(1)}, f32[16,1280]{1,0:T(8,128)S(1)}, u32[]{:S(2)}, u32[]{:S(2)}) collective-permute-start(f32[16,1280]{1,0:T(8,128)S(1)} %get-tuple-element.115), channel_id=1, source_target_pairs={{0,2},{1,3},{2,0},{3,1},{4,6},{5,7},{6,4},{7,5},{8,10},{9,11},{10,... | collective-permute-start | bytes 245768 | tf_op jit(solution)/shard_map/ppermute | solution.py:71
  68.0 6.8 %collective-permute-start.16 = (f32[16,1280]{1,0:T(8,128)S(1)}, f32[16,1280]{1,0:T(8,128)S(1)}, u32[]{:S(2)}, u32[]{:S(2)}) collective-permute-start(f32[16,1280]{1,0:T(8,128)S(1)} %add.75), channel_id=1, source_target_pairs={{0,4},{4,0},{8,12},{12,8},{16,20},{20,16},{24,28},{28,24},{1,5},{5... | collective-permute-start | bytes 245768 | tf_op jit(solution)/shard_map/ppermute | solution.py:71
  73.5 16.2 %collective-permute-start.21 = (f32[144,576]{1,0:T(8,128)S(1)}, f32[144,576]{1,0:T(8,128)S(1)}, u32[]{:S(2)}, u32[]{:S(2)}) collective-permute-start(f32[144,576]{1,0:T(8,128)S(1)} %constant_dynamic-update-slice_fusion.refs_0_), channel_id=1, source_target_pairs={{0,4},{4,0},{8,12},{12,8},{16,20},{20,16},{24,28},{28,24},{1,5},{5... | collective-permute-start | bytes 995336 | tf_op jit(solution)/shard_map/ppermute | solution.py:71
  74.8 4.5 %collective-permute-start.18 = (f32[16,1280]{1,0:T(8,128)S(1)}, f32[16,1280]{1,0:T(8,128)S(1)}, u32[]{:S(2)}, u32[]{:S(2)}) collective-permute-start(f32[16,1280]{1,0:T(8,128)S(1)} %add.76), channel_id=1, source_target_pairs={{0,8},{4,12},{8,0},{12,4},{16,24},{20,28},{24,16},{28,20},{1,9},{5... | collective-permute-start | bytes 245768 | tf_op jit(solution)/shard_map/ppermute | solution.py:71
  79.4 5.7 %collective-permute-start.19 = (f32[16,1280]{1,0:T(8,128)S(1)}, f32[16,1280]{1,0:T(8,128)S(1)}, u32[]{:S(2)}, u32[]{:S(2)}) collective-permute-start(f32[16,1280]{1,0:T(8,128)S(1)} %add.77), channel_id=1, source_target_pairs={{0,16},{4,20},{8,24},{12,28},{16,0},{20,4},{24,8},{28,12},{1,17},{... | collective-permute-start | bytes 245768 | tf_op jit(solution)/shard_map/ppermute | solution.py:71
  85.1 12.1 %collective-permute-start.24 = (f32[144,576]{1,0:T(8,128)S(1)}, f32[144,576]{1,0:T(8,128)S(1)}, u32[]{:S(2)}, u32[]{:S(2)}) collective-permute-start(f32[144,576]{1,0:T(8,128)S(1)} %constant_dynamic-update-slice_fusion.refs_0_), channel_id=1, source_target_pairs={{0,8},{4,12},{8,0},{12,4},{16,24},{20,28},{24,16},{28,20},{1,9},{5... | collective-permute-start | bytes 995336 | tf_op jit(solution)/shard_map/ppermute | solution.py:71
  85.2 4.5 %collective-permute-start.20 = (f32[16,1280]{1,0:T(8,128)S(1)}, f32[16,1280]{1,0:T(8,128)S(1)}, u32[]{:S(2)}, u32[]{:S(2)}) collective-permute-start(f32[16,1280]{1,0:T(8,128)S(1)} %add.78.ours), channel_id=1, source_target_pairs={{0,2},{1,3},{2,0},{3,1},{4,6},{5,7},{6,4},{7,5},{8,10},{9,11},{10,... | collective-permute-start | bytes 245768 | tf_op jit(solution)/shard_map/ppermute | solution.py:71
  89.7 1.5 %collective-permute-start.22 = (f32[32,1280]{1,0:T(8,128)S(1)}, f32[32,1280]{1,0:T(8,128)S(1)}, u32[]{:S(2)}, u32[]{:S(2)}) collective-permute-start(f32[32,1280]{1,0:T(8,128)S(1)} %join.3.ours), channel_id=1, source_target_pairs={{0,1},{1,0},{2,3},{3,2},{4,5},{5,4},{6,7},{7,6},{8,9},{9,8},{10,11... | collective-permute-start | bytes 491528 | tf_op jit(solution)/shard_map/ppermute | solution.py:71
  92.6 4.6 %collective-permute-start.23 = (f32[32,576]{1,0:T(8,128)S(1)}, f32[32,576]{1,0:T(8,128)S(1)}, u32[]{:S(2)}, u32[]{:S(2)}) collective-permute-start(f32[32,576]{1,0:T(8,128)S(1)} %get-tuple-element.134), channel_id=1, source_target_pairs={{0,4},{4,0},{8,12},{12,8},{16,20},{20,16},{24,28},{28,24},{1,5},{5... | collective-permute-start | bytes 221192 | tf_op jit(solution)/shard_map/ppermute | solution.py:71
  97.2 4.5 %collective-permute-start.25 = (f32[32,576]{1,0:T(8,128)S(1)}, f32[32,576]{1,0:T(8,128)S(1)}, u32[]{:S(2)}, u32[]{:S(2)}) collective-permute-start(f32[32,576]{1,0:T(8,128)S(1)} %add.79), channel_id=1, source_target_pairs={{0,8},{4,12},{8,0},{12,4},{16,24},{20,28},{24,16},{28,20},{1,9},{5... | collective-permute-start | bytes 221192 | tf_op jit(solution)/shard_map/ppermute | solution.py:71
  99.2 9.5 %collective-permute-start.27 = (f32[144,576]{1,0:T(8,128)S(1)}, f32[144,576]{1,0:T(8,128)S(1)}, u32[]{:S(2)}, u32[]{:S(2)}) collective-permute-start(f32[144,576]{1,0:T(8,128)S(1)} %collective-permute-done.24.refs_1_), channel_id=1, source_target_pairs={{0,4},{4,0},{8,12},{12,8},{16,20},{20,16},{24,28},{28,24},{1,5},{5... | collective-permute-start | bytes 995336 | tf_op jit(solution)/shard_map/ppermute | solution.py:71
  101.7 5.4 %collective-permute-start.26 = (f32[32,576]{1,0:T(8,128)S(1)}, f32[32,576]{1,0:T(8,128)S(1)}, u32[]{:S(2)}, u32[]{:S(2)}) collective-permute-start(f32[32,576]{1,0:T(8,128)S(1)} %add.80), channel_id=1, source_target_pairs={{0,16},{4,20},{8,24},{12,28},{16,0},{20,4},{24,8},{28,12},{1,17},{... | collective-permute-start | bytes 221192 | tf_op jit(solution)/shard_map/ppermute | solution.py:71

commit v6 on v5

--- a/solution.py
+++ b/solution.py
@@ -23,8 +23,8 @@
 IN_HBM = pl.BlockSpec(memory_space=pltpu.HBM)
 IN_VMEM = pl.BlockSpec(memory_space=pltpu.VMEM)
 IN_SMEM = pl.BlockSpec(memory_space=pltpu.SMEM)
-SMALL = pltpu.CompilerParams(vmem_limit_bytes=8 * 2**20)
-LARGE = pltpu.CompilerParams(vmem_limit_bytes=16 * 2**20)
+SMALL = pltpu.CompilerParams(vmem_limit_bytes=6 * 2**20)
+LARGE = pltpu.CompilerParams(vmem_limit_bytes=9 * 2**20)
 QUICK = pl.CostEstimate(flops=1000, bytes_accessed=1000, transcendentals=0)
 SLOW = pl.CostEstimate(flops=1000, bytes_accessed=6_000_000, transcendentals=0)
 
@@ -80,60 +80,64 @@
     return gather.before(block, stage, 0)
 
 
-def sum_over_all(keep, give, bits, n_rep, n_shard, gather, stage):
+def sum_over_all(keep, give, shard, n_rep, n_shard, gather, stage):
     masks = halves(n_shard)
-    for k, mask in enumerate(masks):
+    for mask, after in zip(masks, masks[1:] + [None]):
         got = swap(give, "shard", mask, n_shard)
-        if k < len(masks) - 1:
-            keep, give = split(keep, got, bits[k + 1])
+        if after is not None:
+            keep, give = split(keep, got, shard, after)
             keep = gather.before(keep, stage, "core")
     part = sum_over(keep + got, n_rep, gather, stage)
-    for mask, bit in reversed(list(zip(masks, bits))[1:]):
-        part = join(part, swap(part, "shard", mask, n_shard), bit)
+    for mask in reversed(masks[1:]):
+        part = join(part, swap(part, "shard", mask, n_shard), shard, mask)
         part = gather.before(part, stage, "x")
     return part, swap(part, "shard", masks[0], n_shard)
 
 
-def split_kernel(bit_ref, ours, got, keep, give):
+def is_high(place_ref, mask):
+    return (place_ref[0] & mask) != 0
+
+
+def split_kernel(mask, shard_ref, ours, got, keep, give):
     total = ours[...] + got[...]
     half = total.shape[0] // 2
-    high = bit_ref[0] != 0
+    high = is_high(shard_ref, mask)
     keep[...] = jnp.where(high, total[half:], total[:half])
     give[...] = jnp.where(high, total[:half], total[half:])
 
 
-def split(ours, got, bit):
+def split(ours, got, shard, mask):
     half = pltpu.VMEM((ours.shape[0] // 2, ours.shape[1]), f32)
     return pl.pallas_call(
-        split_kernel,
+        functools.partial(split_kernel, mask),
         in_specs=[IN_SMEM, IN_VMEM, IN_VMEM],
         out_specs=[IN_VMEM] * 2,
         out_shape=[half, half],
         compiler_params=SMALL,
         cost_estimate=QUICK,
         name="split",
-    )(bit, ours, got)
-
-
-def joined(bit_ref, ours, got):
-    high = bit_ref[0] != 0
+    )(shard, ours, got)
+
+
+def joined(shard_ref, mask, ours, got):
+    high = is_high(shard_ref, mask)
     return jnp.concatenate([jnp.where(high, got, ours), jnp.where(high, ours, got)], axis=0)
 
 
-def join_kernel(bit_ref, ours, got, whole):
-    whole[...] = joined(bit_ref, ours[...], got[...])
-
-
-def join(ours, got, bit):
-    return pl.pallas_call(
-        join_kernel,
+def join_kernel(mask, shard_ref, ours, got, whole):
+    whole[...] = joined(shard_ref, mask, ours[...], got[...])
+
+
+def join(ours, got, shard, mask):
+    return pl.pallas_call(
+        functools.partial(join_kernel, mask),
         in_specs=[IN_SMEM, IN_VMEM, IN_VMEM],
         out_specs=IN_VMEM,
         out_shape=pltpu.VMEM((2 * ours.shape[0], ours.shape[1]), f32),
         compiler_params=SMALL,
         cost_estimate=QUICK,
         name="join",
-    )(bit, ours, got)
+    )(shard, ours, got)
 
 
 class Gather:
@@ -155,10 +159,10 @@
     }
     PLACES = {"own": 0, "turned": 1, "near": 2, "far": 4, "last": 6, "turned_near": 3, "turned_far": 5, "turned_last": 7}
 
-    def __init__(self, own, count):
+    def __init__(self, own, own_a, own_b, place, count):
         self.count = count
-        half = own.shape[0] // 2
-        self.blocks = {"own": own, "own_a": own[:half], "own_b": own[half:]}
+        self.place = place
+        self.blocks = {"own": own, "own_a": own_a, "own_b": own_b}
         self.paired = count == 8 and own.shape[0] % 16 == 0
         self.rows = None
         self.tasks = {}
@@ -193,7 +197,7 @@
         return value
 
     def insert(self, blocks, names):
-        self.rows = insert(self.rows, blocks, [self.PLACES[name] for name in names], self.count)
+        self.rows = insert(self.place, self.rows, blocks, [self.PLACES[name] for name in names], self.count)
 
     def before(self, value, stage, mask):
         if self.paired:
@@ -229,9 +233,8 @@
         out[:, at] = jnp.where((lane >= shift) & (lane < shift + count), turned, out[:, at])
 
 
-def insert(rows, blocks, masks, count):
+def insert(place, rows, blocks, masks, count):
     height, width = blocks[0].shape[1], blocks[0].shape[0] * count
-    place = lax.axis_index("rep").astype(jnp.int32).reshape(1)
     old = [] if rows is None else hold(pltpu.VMEM, rows)
     return pl.pallas_call(
         functools.partial(insert_kernel, masks),
@@ -245,9 +248,85 @@
     )(place, *blocks, *old)
 
 
-def first_kernel(chunks, bit_ref, grad_q, grad_o, error_q, error_o, basis_q, basis_o, corr_q, corr_o, keep, give, buffer, bases, sems, base_sems):
+def base_kernel(weight_q, moment_q, weight_o, moment_o, own, *parts):
+    drop = step_size * decay_rate
+    base = jnp.concatenate([weight_q[...] - drop * moment_q[...], weight_o[...] - drop * moment_o[...]], axis=1)
+    own[...] = base
+    half = base.shape[0] // 2
+    for k, part in enumerate(parts):
+        part[...] = base[k * half : (k + 1) * half]
+
+
+def base_of(weight_q, moment_q, weight_o, moment_o):
+    rows, width = weight_q.shape[0], 2 * weight_q.shape[1]
+    shapes = [(rows, width)] + [(rows // 2, width)] * 2
+    return pl.pallas_call(
+        base_kernel,
+        in_specs=[IN_VMEM] * 4,
+        out_specs=[IN_VMEM] * 3,
+        out_shape=[pltpu.VMEM(shape, f32) for shape in shapes],
+        compiler_params=SMALL,
+        cost_estimate=QUICK,
+        name="base",
+    )(weight_q, moment_q, weight_o, moment_o)
+
+
+def window_of(n_shard, share, place_ref, shard_ref, lines):
+    start = (place_ref[0] * n_shard + shard_ref[0]) * share
+    row = lax.broadcasted_iota(jnp.int32, (lines, LANES), 0)
+    lane = lax.broadcasted_iota(jnp.int32, (lines, LANES), 1)
+    flat = row * LANES + lane
+    return lax.rem(start, LANES), (flat >= start) & (flat < start + share)
+
+
+def norm_in_kernel(n_shard, place_ref, shard_ref, grads, moment, weight, extra):
+    lines, share = grads.shape[1] // LANES, moment.shape[1]
+    shift, inside = window_of(n_shard, share, place_ref, shard_ref, lines)
+    kept = weight[...] - step_size * decay_rate * moment[...]
+    kept = jnp.concatenate([kept, jnp.zeros((1, LANES - share), f32)], axis=1)
+    kept = pltpu.roll(jnp.broadcast_to(kept, (8, LANES)), shift, 1)[:1]
+    extra[...] = jnp.zeros_like(extra)
+    for line in range(lines):
+        extra[line : line + 1, :] = grads[:, line * LANES : (line + 1) * LANES]
+    extra[extra.shape[0] // 2 : extra.shape[0] // 2 + lines, :] = jnp.where(inside, kept, 0.0) - step_size * extra[:lines, :]
+
+
+def norm_in(grads, moment, weight, rows, place, shard, n_shard):
+    return pl.pallas_call(
+        functools.partial(norm_in_kernel, n_shard),
+        in_specs=[IN_SMEM] * 2 + [IN_VMEM] * 3,
+        out_specs=IN_VMEM,
+        out_shape=pltpu.VMEM((rows, LANES), f32),
+        compiler_params=SMALL,
+        cost_estimate=QUICK,
+        name="norm_in",
+    )(place, shard, grads, moment, weight)
+
+
+def norm_out_kernel(n_shard, place_ref, shard_ref, extra, moment, new_moment, new_weight):
+    lines, share = new_weight.shape[0], moment.shape[1]
+    shift, inside = window_of(n_shard, share, place_ref, shard_ref, lines)
+    total = jnp.sum(jnp.where(inside, extra[:lines, :], 0.0), axis=0, keepdims=True)
+    total = pltpu.roll(jnp.broadcast_to(total, (8, LANES)), LANES - shift, 1)[:1, :share]
+    new_moment[...] = decay_rate * moment[...] + total
+    new_weight[...] = extra[extra.shape[0] // 2 : extra.shape[0] // 2 + lines, :]
+
+
+def norm_out(extra, moment, lines, place, shard, n_shard):
+    return pl.pallas_call(
+        functools.partial(norm_out_kernel, n_shard),
+        in_specs=[IN_SMEM] * 2 + [IN_VMEM] * 2,
+        out_specs=[IN_VMEM] * 2,
+        out_shape=[jax.ShapeDtypeStruct(moment.shape, f32), jax.ShapeDtypeStruct((lines, LANES), f32)],
+        compiler_params=SMALL,
+        cost_estimate=QUICK,
+        name="norm_out",
+    )(place, shard, extra, moment)
+
+
+def first_kernel(chunks, place_ref, shard_ref, grad_q, grad_o, error_q, error_o, basis_q, basis_o, corr_q, corr_o, keep, give, buffer, bases, sems, base_sems):
     size = corr_q.shape[1]
-    high = bit_ref[0] != 0
+    high = is_high(shard_ref, 1)
     lanes = size // chunks
     base_copies = [pltpu.make_async_copy(source, bases.at[k], base_sems.at[k]) for k, source in enumerate((basis_q, basis_o))]
     copies = {}
@@ -273,13 +352,13 @@
         give[:, at] = jnp.where(high, parts[0], parts[1])
 
 
-def first(grads, errors, basis_q, basis_o, bit):
+def first(grads, errors, basis_q, basis_o, place, shard):
     width, size = grads[0].shape
     rank = basis_q.shape[0]
     chunks = 3 if size % (3 * LANES) == 0 else 1
     return pl.pallas_call(
         functools.partial(first_kernel, chunks),
-        in_specs=[IN_SMEM] + [IN_HBM] * 6,
+        in_specs=[IN_SMEM] * 2 + [IN_HBM] * 6,
         out_specs=[IN_VMEM] * 4,
         out_shape=[pltpu.VMEM((width, size), f32)] * 2 + [pltpu.VMEM((rank, size), f32)] * 2,
         scratch_shapes=[
@@ -290,19 +369,19 @@
         ],
         compiler_params=LARGE,
         name="first",
-    )(bit, *hold(pltpu.HBM, *grads, *errors, basis_q, basis_o))
-
-
-def right_kernel(bit_ref, ours, got, corr_q, corr_o, right, left, *extra):
+    )(place, shard, *hold(pltpu.HBM, *grads, *errors, basis_q, basis_o))
+
+
+def right_kernel(shard_ref, ours, got, corr_q, corr_o, right, left, *extra):
     rank, size = ours.shape[0], corr_q.shape[1]
-    whole = joined(bit_ref, ours[...], got[...])
+    whole = joined(shard_ref, 1, ours[...], got[...])
     left[...] = whole[:, :size]
     if extra:
         extra[0][...] = whole[:, size:]
     right[...] = jnp.concatenate([stacked(whole[:rank, :size], corr_q[...], NT), stacked(whole[rank:, :size], corr_o[...], NT)], axis=1)
 
 
-def right_of(ours, got, bit, corr_q, corr_o):
+def right_of(ours, got, shard, corr_q, corr_o):
     rank = ours.shape[0]
     width, size = corr_q.shape
     beside = ours.shape[1] - size
@@ -315,14 +394,14 @@
         compiler_params=SMALL,
         cost_estimate=QUICK,
         name="right",
-    )(bit, ours, got, *hold(pltpu.VMEM, corr_q, corr_o))
-
-
-def left_kernel(bit_ref, right, inverse, corr_q, corr_o, *refs):
+    )(shard, ours, got, *hold(pltpu.VMEM, corr_q, corr_o))
+
+
+def left_kernel(shard_ref, right, inverse, corr_q, corr_o, *refs):
     extra, keep, give = refs[:-2], refs[-2], refs[-1]
     rank, width = right.shape[0], right.shape[1] // 2
     size = corr_q.shape[1]
-    high = bit_ref[0] != 0
+    high = is_high(shard_ref, 1)
     basis_q = exact(inverse[0], right[:, :width], NN)
     basis_o = exact(inverse[1], right[:, width:], NN)
     part_q = stacked(basis_q, corr_q[...], NN)
@@ -335,7 +414,7 @@
         give[:, size:] = jnp.where(high, low_rows, high_rows)
 
 
-def left_of(right, inverse, bit, corr_q, corr_o, extra):
+def left_of(right, inverse, shard, corr_q, corr_o, extra):
     rank, size = right.shape[0], corr_q.shape[1]
     half = pltpu.VMEM((rank, size + sum(array.shape[1] for array in extra)), f32)
     return pl.pallas_call(
@@ -346,7 +425,7 @@
         compiler_params=SMALL,
         cost_estimate=QUICK,
         name="left",
-    )(bit, right, inverse, *hold(pltpu.VMEM, corr_q, corr_o), *extra)
+    )(shard, right, inverse, *hold(pltpu.VMEM, corr_q, corr_o), *extra)
 
 
 def eliminate(gram_q, gram_o, rank):
@@ -404,9 +483,8 @@
     own[...] = pltpu.roll(window, 2 * LANES - index * (count - LANES), 1)[:, :count]
 
 
-def stack_of(left, count):
+def stack_of(left, place, count):
     rank, size = left.shape[0] // 2, left.shape[1]
-    place = lax.axis_index("rep").astype(jnp.int32).reshape(1)
     return pl.pallas_call(
         stack_kernel,
         in_specs=[IN_SMEM, IN_VMEM],
@@ -485,47 +563,33 @@
     rank = q_basis.shape[1]
     size = q_grad.shape[1]
     flat = norm_grads.shape[-1]
-    share = norm_moment.shape[0]
     row_count = q_moment.shape[0]
-    device = lax.axis_index("rep") * n_shard + lax.axis_index("shard")
-    drop = step_size * decay_rate
-
-    base = jnp.concatenate([q_weight - drop * q_moment, o_weight - drop * o_moment], axis=1)
-    gather = Gather(base, n_rep)
-
-    grads = norm_grads.reshape(flat)
-    own_grads = lax.dynamic_slice(grads, (device * share,), (share,))
-    placed = lax.dynamic_update_slice(-step_size * grads, (norm_weight - drop * norm_moment) - step_size * own_grads, (device * share,))
-    extra = jnp.concatenate([grads.reshape(-1, LANES), placed.reshape(-1, LANES)], axis=0)
-    extra_rows = extra.shape[0]
-    extra = jnp.pad(extra, ((0, 2 * rank - extra_rows), (0, 0)))
-
-    place = lax.axis_index("shard")
-    bits = [((place // mask) % 2).astype(jnp.int32).reshape(1) for mask in halves(n_shard)]
-    corr_q, corr_o, keep, give = first((q_grad[0].T, o_grad[0].T), (q_error[0].T, o_error[0].T), q_basis.T, o_basis.T, bits[0])
+    place = lax.axis_index("rep").astype(jnp.int32).reshape(1)
+    shard = lax.axis_index("shard").astype(jnp.int32).reshape(1)
+
+    gather = Gather(*base_of(q_weight, q_moment, o_weight, o_moment), place, n_rep)
+    norm_moment, norm_weight = norm_moment.reshape(1, -1), norm_weight.reshape(1, -1)
+    extra = norm_in(norm_grads[0], norm_moment, norm_weight, 2 * rank, place, shard, n_shard)
+    corr_q, corr_o, keep, give = first((q_grad[0].T, o_grad[0].T), (q_error[0].T, o_error[0].T), q_basis.T, o_basis.T, place, shard)
     for sweep in range(ROUNDS):
         last = sweep == ROUNDS - 1
-        ours, got = sum_over_all(keep, give, bits, n_rep, n_shard, gather, 2 * sweep)
-        right, left, *extra_sum = right_of(ours, got, bits[0], corr_q, corr_o)
+        ours, got = sum_over_all(keep, give, shard, n_rep, n_shard, gather, 2 * sweep)
+        right, left, *extra_sum = right_of(ours, got, shard, corr_q, corr_o)
         if last and gather.paired:
-            gather.tasks[3, 4] = (functools.partial(stack_of, count=row_count), left)
+            gather.tasks[3, 4] = (functools.partial(stack_of, count=row_count), left, place)
         gather.tasks[2 * sweep + 1, 1] = (inverse_of, left)
         right = sum_over(right, n_rep, gather, 2 * sweep + 1)
         inverse = gather.results[2 * sweep + 1, 1]
         if not last:
-            keep, give = left_of(right, inverse, bits[0], corr_q, corr_o, [extra] if sweep == ROUNDS - 2 else [])
-    extra_sum = extra_sum[0][:extra_rows]
+            keep, give = left_of(right, inverse, shard, corr_q, corr_o, [extra] if sweep == ROUNDS - 2 else [])
+    norm_moment_new, norm_weight_new = norm_out(extra_sum[0], norm_moment, flat // LANES, place, shard, n_shard)
     if gather.paired:
         stack, own = gather.results[3, 4]
         gather.insert([gather.blocks["turned_last"]], ["turned_last"])
         outs = finish(corr_q, corr_o, gather.rows, stack, inverse, right, own, q_moment, o_moment)
     else:
-        outs = finish_plain(corr_q, corr_o, base, left, inverse, right, q_moment, o_moment)
+        outs = finish_plain(corr_q, corr_o, gather.blocks["own"], left, inverse, right, q_moment, o_moment)
     weight_q, weight_o, error_q, error_o, q_moment_new, o_moment_new = outs
-    half = extra_rows // 2
-    norm_sum = extra_sum[:half].reshape(flat)
-    norm_weight_new = extra_sum[half:].reshape(flat)
-    norm_moment_new = decay_rate * norm_moment + lax.dynamic_slice(norm_sum, (device * share,), (share,))
     return (
         weight_q.T,
         weight_o.T,
@@ -533,8 +597,8 @@
         o_moment_new,
         error_q.T[None],
         error_o.T[None],
-        norm_weight_new,
-        norm_moment_new,
+        norm_weight_new.reshape(flat),
+        norm_moment_new.reshape(-1),
     )
 
 

time: 113 us -> 109 us (0.965)
  waiting for transfers between devices: 51.5 us -> 58 us
  local copies, waits for them, and re-layouts: 3.92 us -> 0.05 us
  Pallas kernels: 22.4 us -> 19 us
  other arithmetic: 3.15 us -> 0.15 us
    ppermute x28, waiting for transfers between devices: 51.5 us -> 58 us  [swap(): return lax.ppermute(block, axis, pairs)]
    unnamed x29 -> x15, local copies, waits for them, and re-layouts: 3.3 us -> 0.04 us
    concatenate x3 -> x0, other arithmetic: 2.04 us -> none  [the longest x2 2.04 us: per_device(): jnp.concatenate([q_weight - drop * q_moment, o_weight - drop * o_moment],...]
  transfers between devices with their start and end apart: 28 -> 28, of which waited for: 20 -> 20; matrix products, arithmetic and copies ran while one was open for 4% -> 0% of each run, Pallas kernels for 12% -> 10%
where the time goes in v6:
time: 109 us
  waiting for transfers between devices  58 us (53%)
  starting transfers between devices  30.8 us (28%)
  Pallas kernels  19 us (17%)
    ppermute x28, waiting for transfers between devices, swap(): return lax.ppermute(block, axis, pairs)  58 us
    ppermute x28, starting transfers between devices, swap(): return lax.ppermute(block, axis, pairs)  30.8 us
    pallas_call x1, Pallas kernels, first(): pl.pallas_call(functools.partial(first_kernel, chunks), in_specs=[IN_SMEM...  4.5 us
    pallas_call x1, Pallas kernels, finish(): pl.pallas_call(functools.partial(finish_kernel, chunks), in_specs=[IN_VME...  3.68 us
    pallas_call x5, Pallas kernels, insert(): pl.pallas_call(functools.partial(insert_kernel, masks), in_specs=[IN_SMEM...  3.1 us
    pallas_call x2, Pallas kernels, right_of(): pl.pallas_call(right_kernel, in_specs=[IN_SMEM] + [IN_VMEM] * 4, out_spec...  2.95 us
    pallas_call x2, Pallas kernels, inverse_of(): pl.pallas_call(inverse_kernel, out_shape=pltpu.VMEM((2, rank, rank), f32)...  2.6 us
  transfers between devices with their start and end apart: 28, of which 20 were waited for; matrix products, arithmetic and copies ran while one was open for 0% of the time, Pallas kernels for 10%

profile of v6, /device:TPU:0, one launch (start us, length us, event | category | flops | bytes accessed | tf_op | source)
XLA Modules:
  0.0 109.0 jit_solution(13807049135107008463)
XLA Ops:
  0.7 4.5 %first.1 = (f32[288,1152]{1,0:T(8,128)S(1)}, f32[288,1152]{1,0:T(8,128)S(1)}, f32[32,1152]{1,0:T(8,128)S(1)}, f32[32,1152]{1,0:T(8,128)S(1)}) custom-call(s32[1]{0:T(128)} %bitcast.place_ref, s32[1]{0:T(128)} %bitcast.1.shard_ref, f32[288,1152]{1,0:T(8,128)} %bitcast.33, f32[288,1152]{1,0:T(8,128)} %bitcast.34, f32[288,1152]{1,0:T(8,128)} %bitcast.35, ...), custom_call_target="tpu_custom_call" | custom-call | tf_op jit(solution)/shard_map/first/pallas_call | solution.py:359
  5.9 2.7 %collective-permute-start.3 = (f32[144,576]{1,0:T(8,128)S(1)}, f32[144,576]{1,0:T(8,128)S(1)}, u32[]{:S(2)}, u32[]{:S(2)}) collective-permute-start(f32[144,576]{1,0:T(8,128)S(1)} %get-tuple-element.114.refs_0_), channel_id=1, source_target_pairs={{0,8},{4,12},{8,0},{12,4},{16,24},{20,28},{24,16},{28,20},{1,9},{5... | collective-permute-start | bytes 995336 | tf_op jit(solution)/shard_map/ppermute | solution.py:71
  8.6 1.6 %collective-permute-start.1 = (f32[16,1152]{1,0:T(8,128)S(1)}, f32[16,1152]{1,0:T(8,128)S(1)}, u32[]{:S(2)}, u32[]{:S(2)}) collective-permute-start(f32[16,1152]{1,0:T(8,128)S(1)} %get-tuple-element.97), channel_id=1, source_target_pairs={{0,2},{1,3},{2,0},{3,1},{4,6},{5,7},{6,4},{7,5},{8,10},{9,11},{10,... | collective-permute-start | bytes 221192 | tf_op jit(solution)/shard_map/ppermute | solution.py:71
  10.1 2.9 %collective-permute-done.1 = f32[16,1152]{1,0:T(8,128)S(1)} collective-permute-done((f32[16,1152]{1,0:T(8,128)S(1)}, f32[16,1152]{1,0:T(8,128)S(1)}, u32[]{:S(2)}, u32[]{:S(2)}) %collective-permute-start.1) | collective-permute-done | bytes 73760 | tf_op jit(solution)/shard_map/ppermute | solution.py:71
  13.0 1.6 %collective-permute-start.2 = (f32[16,1152]{1,0:T(8,128)S(1)}, f32[16,1152]{1,0:T(8,128)S(1)}, u32[]{:S(2)}, u32[]{:S(2)}) collective-permute-start(f32[16,1152]{1,0:T(8,128)S(1)} %add.42), channel_id=1, source_target_pairs={{0,4},{4,0},{8,12},{12,8},{16,20},{20,16},{24,28},{28,24},{1,5},{5... | collective-permute-start | bytes 221192 | tf_op jit(solution)/shard_map/ppermute | solution.py:71
  14.6 2.8 %collective-permute-done.2 = f32[16,1152]{1,0:T(8,128)S(1)} collective-permute-done((f32[16,1152]{1,0:T(8,128)S(1)}, f32[16,1152]{1,0:T(8,128)S(1)}, u32[]{:S(2)}, u32[]{:S(2)}) %collective-permute-start.2) | collective-permute-done | bytes 73760 | tf_op jit(solution)/shard_map/ppermute | solution.py:71
  17.4 1.6 %collective-permute-start.7 = (f32[144,576]{1,0:T(8,128)S(1)}, f32[144,576]{1,0:T(8,128)S(1)}, u32[]{:S(2)}, u32[]{:S(2)}) collective-permute-start(f32[144,576]{1,0:T(8,128)S(1)} %get-tuple-element.114.refs_0_), channel_id=1, source_target_pairs={{0,4},{4,0},{8,12},{12,8},{16,20},{20,16},{24,28},{28,24},{1,5},{5... | collective-permute-start | bytes 995336 | tf_op jit(solution)/shard_map/ppermute | solution.py:71
  19.0 1.1 %collective-permute-start.4 = (f32[16,1152]{1,0:T(8,128)S(1)}, f32[16,1152]{1,0:T(8,128)S(1)}, u32[]{:S(2)}, u32[]{:S(2)}) collective-permute-start(f32[16,1152]{1,0:T(8,128)S(1)} %add.43), channel_id=1, source_target_pairs={{0,8},{4,12},{8,0},{12,4},{16,24},{20,28},{24,16},{28,20},{1,9},{5... | collective-permute-start | bytes 221192 | tf_op jit(solution)/shard_map/ppermute | solution.py:71
  20.1 3.3 %collective-permute-done.4 = f32[16,1152]{1,0:T(8,128)S(1)} collective-permute-done((f32[16,1152]{1,0:T(8,128)S(1)}, f32[16,1152]{1,0:T(8,128)S(1)}, u32[]{:S(2)}, u32[]{:S(2)}) %collective-permute-start.4) | collective-permute-done | bytes 73760 | tf_op jit(solution)/shard_map/ppermute | solution.py:71
  23.4 2.7 %collective-permute-start.5 = (f32[16,1152]{1,0:T(8,128)S(1)}, f32[16,1152]{1,0:T(8,128)S(1)}, u32[]{:S(2)}, u32[]{:S(2)}) collective-permute-start(f32[16,1152]{1,0:T(8,128)S(1)} %add.44), channel_id=1, source_target_pairs={{0,16},{4,20},{8,24},{12,28},{16,0},{20,4},{24,8},{28,12},{1,17},{... | collective-permute-start | bytes 221192 | tf_op jit(solution)/shard_map/ppermute | solution.py:71
  26.1 3.4 %collective-permute-done.5 = f32[16,1152]{1,0:T(8,128)S(1)} collective-permute-done((f32[16,1152]{1,0:T(8,128)S(1)}, f32[16,1152]{1,0:T(8,128)S(1)}, u32[]{:S(2)}, u32[]{:S(2)}) %collective-permute-start.5) | collective-permute-done | bytes 73760 | tf_op jit(solution)/shard_map/ppermute | solution.py:71
  29.5 1.6 %collective-permute-start.6 = (f32[16,1152]{1,0:T(8,128)S(1)}, f32[16,1152]{1,0:T(8,128)S(1)}, u32[]{:S(2)}, u32[]{:S(2)}) collective-permute-start(f32[16,1152]{1,0:T(8,128)S(1)} %add.45.ours), channel_id=1, source_target_pairs={{0,2},{1,3},{2,0},{3,1},{4,6},{5,7},{6,4},{7,5},{8,10},{9,11},{10,... | collective-permute-start | bytes 221192 | tf_op jit(solution)/shard_map/ppermute | solution.py:71
  31.1 2.9 %collective-permute-done.6.got = f32[16,1152]{1,0:T(8,128)S(1)} collective-permute-done((f32[16,1152]{1,0:T(8,128)S(1)}, f32[16,1152]{1,0:T(8,128)S(1)}, u32[]{:S(2)}, u32[]{:S(2)}) %collective-permute-start.6) | collective-permute-done | bytes 73760 | tf_op jit(solution)/shard_map/ppermute | solution.py:71
  34.0 2.0 %collective-permute-start.10 = (f32[72,576]{1,0:T(8,128)S(1)}, f32[72,576]{1,0:T(8,128)S(1)}, u32[]{:S(2)}, u32[]{:S(2)}) collective-permute-start(f32[72,576]{1,0:T(8,128)S(1)} %get-tuple-element.110), channel_id=1, source_target_pairs={{0,16},{4,20},{8,24},{12,28},{16,0},{20,4},{24,8},{28,12},{1,17},{... | collective-permute-start | bytes 497672 | tf_op jit(solution)/shard_map/ppermute | solution.py:71
  36.0 1.5 %right.2 = (f32[32,576]{1,0:T(8,128)S(1)}, f32[64,1152]{1,0:T(8,128)S(1)}) custom-call(s32[1]{0:T(128)} %bitcast.1.shard_ref, f32[32,1152]{1,0:T(8,128)S(1)} %join.2.ours, f32[32,1152]{1,0:T(8,128)S(1)} %collective-permute-done.8.got, f32[288,1152]{1,0:T(8,128)S(1)} %get-tuple-element.92.corr_q, f32[288,1152]{1,0:T(8,128)S(1)} %get-tuple-element.93.corr_o), custom_call_target="tpu_custom_call" | custom-call | flops 1000 | bytes 1000 | tf_op jit(solution)/shard_map/right/pallas_call | solution.py:389
  37.5 0.5 collective-permute-start.9
  38.1 1.3 %inverse.2 = f32[2,32,32]{2,1,0:T(8,128)S(1)} custom-call(f32[64,1152]{1,0:T(8,128)S(1)} %get-tuple-element.106.left), custom_call_target="tpu_custom_call" | custom-call | flops 1000 | bytes 6000000 | tf_op jit(solution)/shard_map/inverse/pallas_call | solution.py:466
  39.4 2.7 %collective-permute-done.9 = f32[32,576]{1,0:T(8,128)S(1)} collective-permute-done((f32[32,576]{1,0:T(8,128)S(1)}, f32[32,576]{1,0:T(8,128)S(1)}, u32[]{:S(2)}, u32[]{:S(2)}) %collective-permute-start.9) | collective-permute-done | bytes 73760 | tf_op jit(solution)/shard_map/ppermute | solution.py:71
  42.1 3.8 %collective-permute-done.10 = f32[72,576]{1,0:T(8,128)S(1)} collective-permute-done((f32[72,576]{1,0:T(8,128)S(1)}, f32[72,576]{1,0:T(8,128)S(1)}, u32[]{:S(2)}, u32[]{:S(2)}) %collective-permute-start.10) | collective-permute-done | bytes 165920 | tf_op jit(solution)/shard_map/ppermute | solution.py:71
  46.0 4.4 %collective-permute-done.11 = f32[32,576]{1,0:T(8,128)S(1)} collective-permute-done((f32[32,576]{1,0:T(8,128)S(1)}, f32[32,576]{1,0:T(8,128)S(1)}, u32[]{:S(2)}, u32[]{:S(2)}) %collective-permute-start.11) | collective-permute-done | bytes 73760 | tf_op jit(solution)/shard_map/ppermute | solution.py:71
  50.4 1.7 %collective-permute-start.12 = (f32[32,576]{1,0:T(8,128)S(1)}, f32[32,576]{1,0:T(8,128)S(1)}, u32[]{:S(2)}, u32[]{:S(2)}) collective-permute-start(f32[32,576]{1,0:T(8,128)S(1)} %add.47), channel_id=1, source_target_pairs={{0,16},{4,20},{8,24},{12,28},{16,0},{20,4},{24,8},{28,12},{1,17},{... | collective-permute-start | bytes 221192 | tf_op jit(solution)/shard_map/ppermute | solution.py:71
  52.6 0.9 insert.5.refs_2_
  53.5 3.1 %collective-permute-done.12 = f32[32,576]{1,0:T(8,128)S(1)} collective-permute-done((f32[32,576]{1,0:T(8,128)S(1)}, f32[32,576]{1,0:T(8,128)S(1)}, u32[]{:S(2)}, u32[]{:S(2)}) %collective-permute-start.12) | collective-permute-done | bytes 73760 | tf_op jit(solution)/shard_map/ppermute | solution.py:71
  56.6 1.2 %left.1 = (f32[32,1280]{1,0:T(8,128)S(1)}, f32[32,1280]{1,0:T(8,128)S(1)}) custom-call(s32[1]{0:T(128)} %bitcast.1.shard_ref, f32[32,576]{1,0:T(8,128)S(1)} %add.48.right, f32[2,32,32]{2,1,0:T(8,128)S(1)} %inverse.2, f32[288,1152]{1,0:T(8,128)S(1)} %get-tuple-element.92.corr_q, f32[288,1152]{1,0:T(8,128)S(1)} %get-tuple-element.93.corr_o, ...), custom_call_target="tpu_custom_call" | custom-call | flops 1000 | bytes 1000 | tf_op jit(solution)/shard_map/left/pallas_call | solution.py:420
  57.8 1.0 collective-permute-start.17
  59.2 1.6 %collective-permute-start.15 = (f32[16,1280]{1,0:T(8,128)S(1)}, f32[16,1280]{1,0:T(8,128)S(1)}, u32[]{:S(2)}, u32[]{:S(2)}) collective-permute-start(f32[16,1280]{1,0:T(8,128)S(1)} %get-tuple-element.124), channel_id=1, source_target_pairs={{0,2},{1,3},{2,0},{3,1},{4,6},{5,7},{6,4},{7,5},{8,10},{9,11},{10,... | collective-permute-start | bytes 245768 | tf_op jit(solution)/shard_map/ppermute | solution.py:71
  60.8 1.0 collective-permute-done.14.refs_1_
  61.8 2.0 %collective-permute-done.15 = f32[16,1280]{1,0:T(8,128)S(1)} collective-permute-done((f32[16,1280]{1,0:T(8,128)S(1)}, f32[16,1280]{1,0:T(8,128)S(1)}, u32[]{:S(2)}, u32[]{:S(2)}) %collective-permute-start.15) | collective-permute-done | bytes 81952 | tf_op jit(solution)/shard_map/ppermute | solution.py:71
  64.0 5.7 %collective-permute-done.17 = f32[72,576]{1,0:T(8,128)S(1)} collective-permute-done((f32[72,576]{1,0:T(8,128)S(1)}, f32[72,576]{1,0:T(8,128)S(1)}, u32[]{:S(2)}, u32[]{:S(2)}) %collective-permute-start.17) | collective-permute-done | bytes 165920 | tf_op jit(solution)/shard_map/ppermute | solution.py:71
  69.8 0.7 insert.6.refs_1_
  70.7 4.4 %collective-permute-done.18 = f32[16,1280]{1,0:T(8,128)S(1)} collective-permute-done((f32[16,1280]{1,0:T(8,128)S(1)}, f32[16,1280]{1,0:T(8,128)S(1)}, u32[]{:S(2)}, u32[]{:S(2)}) %collective-permute-start.18) | collective-permute-done | bytes 81952 | tf_op jit(solution)/shard_map/ppermute | solution.py:71
  75.1 0.9 collective-permute-start.19
  76.4 5.0 %collective-permute-done.19 = f32[16,1280]{1,0:T(8,128)S(1)} collective-permute-done((f32[16,1280]{1,0:T(8,128)S(1)}, f32[16,1280]{1,0:T(8,128)S(1)}, u32[]{:S(2)}, u32[]{:S(2)}) %collective-permute-start.19) | collective-permute-done | bytes 81952 | tf_op jit(solution)/shard_map/ppermute | solution.py:71
  81.5 1.5 %collective-permute-start.20 = (f32[16,1280]{1,0:T(8,128)S(1)}, f32[16,1280]{1,0:T(8,128)S(1)}, u32[]{:S(2)}, u32[]{:S(2)}) collective-permute-start(f32[16,1280]{1,0:T(8,128)S(1)} %add.52.ours), channel_id=1, source_target_pairs={{0,2},{1,3},{2,0},{3,1},{4,6},{5,7},{6,4},{7,5},{8,10},{9,11},{10,... | collective-permute-start | bytes 245768 | tf_op jit(solution)/shard_map/ppermute | solution.py:71
  83.0 3.0 %collective-permute-done.20.got = f32[16,1280]{1,0:T(8,128)S(1)} collective-permute-done((f32[16,1280]{1,0:T(8,128)S(1)}, f32[16,1280]{1,0:T(8,128)S(1)}, u32[]{:S(2)}, u32[]{:S(2)}) %collective-permute-start.20) | collective-permute-done | bytes 81952 | tf_op jit(solution)/shard_map/ppermute | solution.py:71
  86.1 1.4 %collective-permute-done.22.got = f32[32,1280]{1,0:T(8,128)S(1)} collective-permute-done((f32[32,1280]{1,0:T(8,128)S(1)}, f32[32,1280]{1,0:T(8,128)S(1)}, u32[]{:S(2)}, u32[]{:S(2)}) %collective-permute-start.22) | collective-permute-done | bytes 163872 | tf_op jit(solution)/shard_map/ppermute | solution.py:71
  87.5 1.5 %right.3 = (f32[32,576]{1,0:T(8,128)S(1)}, f32[64,1152]{1,0:T(8,128)S(1)}, f32[64,128]{1,0:T(8,128)S(1)}) custom-call(s32[1]{0:T(128)} %bitcast.1.shard_ref, f32[32,1280]{1,0:T(8,128)S(1)} %join.3.ours, f32[32,1280]{1,0:T(8,128)S(1)} %collective-permute-done.22.got, f32[288,1152]{1,0:T(8,128)S(1)} %get-tuple-element.92.corr_q, ...), custom_call_target="tpu_custom_call" | custom-call | flops 1000 | bytes 1000 | tf_op jit(solution)/shard_map/right/pallas_call | solution.py:389
  89.0 1.5 %collective-permute-start.23 = (f32[32,576]{1,0:T(8,128)S(1)}, f32[32,576]{1,0:T(8,128)S(1)}, u32[]{:S(2)}, u32[]{:S(2)}) collective-permute-start(f32[32,576]{1,0:T(8,128)S(1)} %get-tuple-element.143), channel_id=1, source_target_pairs={{0,4},{4,0},{8,12},{12,8},{16,20},{20,16},{24,28},{28,24},{1,5},{5... | collective-permute-start | bytes 221192 | tf_op jit(solution)/shard_map/ppermute | solution.py:71
  90.5 1.3 %inverse.3 = f32[2,32,32]{2,1,0:T(8,128)S(1)} custom-call(f32[64,1152]{1,0:T(8,128)S(1)} %get-tuple-element.153.left), custom_call_target="tpu_custom_call" | custom-call | flops 1000 | bytes 6000000 | tf_op jit(solution)/shard_map/inverse/pallas_call | solution.py:466
  91.8 1.7 %collective-permute-done.23 = f32[32,576]{1,0:T(8,128)S(1)} collective-permute-done((f32[32,576]{1,0:T(8,128)S(1)}, f32[32,576]{1,0:T(8,128)S(1)}, u32[]{:S(2)}, u32[]{:S(2)}) %collective-permute-start.23) | collective-permute-done | bytes 73760 | tf_op jit(solution)/shard_map/ppermute | solution.py:71
  93.5 1.5 %collective-permute-start.27 = (f32[144,576]{1,0:T(8,128)S(1)}, f32[144,576]{1,0:T(8,128)S(1)}, u32[]{:S(2)}, u32[]{:S(2)}) collective-permute-start(f32[144,576]{1,0:T(8,128)S(1)} %collective-permute-done.24.refs_1_), channel_id=1, source_target_pairs={{0,4},{4,0},{8,12},{12,8},{16,20},{20,16},{24,28},{28,24},{1,5},{5... | collective-permute-start | bytes 995336 | tf_op jit(solution)/shard_map/ppermute | solution.py:71
  95.0 1.9 %collective-permute-start.25 = (f32[32,576]{1,0:T(8,128)S(1)}, f32[32,576]{1,0:T(8,128)S(1)}, u32[]{:S(2)}, u32[]{:S(2)}) collective-permute-start(f32[32,576]{1,0:T(8,128)S(1)} %add.53), channel_id=1, source_target_pairs={{0,8},{4,12},{8,0},{12,4},{16,24},{20,28},{24,16},{28,20},{1,9},{5... | collective-permute-start | bytes 221192 | tf_op jit(solution)/shard_map/ppermute | solution.py:71
  97.0 2.5 %collective-permute-done.25 = f32[32,576]{1,0:T(8,128)S(1)} collective-permute-done((f32[32,576]{1,0:T(8,128)S(1)}, f32[32,576]{1,0:T(8,128)S(1)}, u32[]{:S(2)}, u32[]{:S(2)}) %collective-permute-start.25) | collective-permute-done | bytes 73760 | tf_op jit(solution)/shard_map/ppermute | solution.py:71
  99.5 2.4 %collective-permute-start.26 = (f32[32,576]{1,0:T(8,128)S(1)}, f32[32,576]{1,0:T(8,128)S(1)}, u32[]{:S(2)}, u32[]{:S(2)}) collective-permute-start(f32[32,576]{1,0:T(8,128)S(1)} %add.54), channel_id=1, source_target_pairs={{0,16},{4,20},{8,24},{12,28},{16,0},{20,4},{24,8},{28,12},{1,17},{... | collective-permute-start | bytes 221192 | tf_op jit(solution)/shard_map/ppermute | solution.py:71
  101.9 0.6 norm_out.1
  102.6 0.7 insert.8.refs_1_
  103.4 1.5 %collective-permute-done.26 = f32[32,576]{1,0:T(8,128)S(1)} collective-permute-done((f32[32,576]{1,0:T(8,128)S(1)}, f32[32,576]{1,0:T(8,128)S(1)}, u32[]{:S(2)}, u32[]{:S(2)}) %collective-permute-start.26) | collective-permute-done | bytes 73760 | tf_op jit(solution)/shard_map/ppermute | solution.py:71
  105.3 3.7 %finish.1 = (f32[288,1152]{1,0:T(8,128)}, f32[288,1152]{1,0:T(8,128)}, f32[288,1152]{1,0:T(8,128)}, f32[288,1152]{1,0:T(8,128)}, f32[144,288]{1,0:T(8,128)}, /*index=5*/f32[144,288]{1,0:T(8,128)}) custom-call(f32[288,1152]{1,0:T(8,128)S(1)} %get-tuple-element.92.corr_q, f32[288,1152]{1,0:T(8,128)S(1)} %get-tuple-element.93.corr_o, ...), custom_call_target="tpu_custom_call" | custom-call | tf_op jit(solution)/shard_map/finish/pallas_call | solution.py:530
  (58 shorter events, 3.4 us)
Async XLA Ops:
  0.6 5.1 %copy-start = (f32[144,288]{1,0:T(8,128)S(1)}, f32[144,288]{1,0:T(8,128)}, u32[]{:S(2)}) copy-start(f32[144,288]{1,0:T(8,128)} %moment_q.3) | copy-start | bytes 497668
  0.7 5.1 %copy-start.1 = (f32[144,288]{1,0:T(8,128)S(1)}, f32[144,288]{1,0:T(8,128)}, u32[]{:S(2)}) copy-start(f32[144,288]{1,0:T(8,128)} %moment_o.3) | copy-start | bytes 497668
  0.7 5.1 %copy-start.2 = (f32[144,288]{1,0:T(8,128)S(1)}, f32[144,288]{1,0:T(8,128)}, u32[]{:S(2)}) copy-start(f32[144,288]{1,0:T(8,128)} %weight_q.1) | copy-start | bytes 497668
  0.7 5.0 %copy-start.3 = (f32[144,288]{1,0:T(8,128)S(1)}, f32[144,288]{1,0:T(8,128)}, u32[]{:S(2)}) copy-start(f32[144,288]{1,0:T(8,128)} %weight_o.1) | copy-start | bytes 497668
  5.2 3.4 %collective-permute-start = (f32[32,1152]{1,0:T(8,128)S(1)}, f32[32,1152]{1,0:T(8,128)S(1)}, u32[]{:S(2)}, u32[]{:S(2)}) collective-permute-start(f32[32,1152]{1,0:T(8,128)S(1)} %get-tuple-element.95), channel_id=1, source_target_pairs={{0,1},{1,0},{2,3},{3,2},{4,5},{5,4},{6,7},{7,6},{8,9},{9,8},{10,11... | collective-permute-start | bytes 442376 | tf_op jit(solution)/shard_map/ppermute | solution.py:71
  5.9 13.2 %collective-permute-start.3 = (f32[144,576]{1,0:T(8,128)S(1)}, f32[144,576]{1,0:T(8,128)S(1)}, u32[]{:S(2)}, u32[]{:S(2)}) collective-permute-start(f32[144,576]{1,0:T(8,128)S(1)} %get-tuple-element.114.refs_0_), channel_id=1, source_target_pairs={{0,8},{4,12},{8,0},{12,4},{16,24},{20,28},{24,16},{28,20},{1,9},{5... | collective-permute-start | bytes 995336 | tf_op jit(solution)/shard_map/ppermute | solution.py:71
  8.6 4.4 %collective-permute-start.1 = (f32[16,1152]{1,0:T(8,128)S(1)}, f32[16,1152]{1,0:T(8,128)S(1)}, u32[]{:S(2)}, u32[]{:S(2)}) collective-permute-start(f32[16,1152]{1,0:T(8,128)S(1)} %get-tuple-element.97), channel_id=1, source_target_pairs={{0,2},{1,3},{2,0},{3,1},{4,6},{5,7},{6,4},{7,5},{8,10},{9,11},{10,... | collective-permute-start | bytes 221192 | tf_op jit(solution)/shard_map/ppermute | solution.py:71
  13.0 4.4 %collective-permute-start.2 = (f32[16,1152]{1,0:T(8,128)S(1)}, f32[16,1152]{1,0:T(8,128)S(1)}, u32[]{:S(2)}, u32[]{:S(2)}) collective-permute-start(f32[16,1152]{1,0:T(8,128)S(1)} %add.42), channel_id=1, source_target_pairs={{0,4},{4,0},{8,12},{12,8},{16,20},{20,16},{24,28},{28,24},{1,5},{5... | collective-permute-start | bytes 221192 | tf_op jit(solution)/shard_map/ppermute | solution.py:71
  17.4 16.5 %collective-permute-start.7 = (f32[144,576]{1,0:T(8,128)S(1)}, f32[144,576]{1,0:T(8,128)S(1)}, u32[]{:S(2)}, u32[]{:S(2)}) collective-permute-start(f32[144,576]{1,0:T(8,128)S(1)} %get-tuple-element.114.refs_0_), channel_id=1, source_target_pairs={{0,4},{4,0},{8,12},{12,8},{16,20},{20,16},{24,28},{28,24},{1,5},{5... | collective-permute-start | bytes 995336 | tf_op jit(solution)/shard_map/ppermute | solution.py:71
  19.0 4.4 %collective-permute-start.4 = (f32[16,1152]{1,0:T(8,128)S(1)}, f32[16,1152]{1,0:T(8,128)S(1)}, u32[]{:S(2)}, u32[]{:S(2)}) collective-permute-start(f32[16,1152]{1,0:T(8,128)S(1)} %add.43), channel_id=1, source_target_pairs={{0,8},{4,12},{8,0},{12,4},{16,24},{20,28},{24,16},{28,20},{1,9},{5... | collective-permute-start | bytes 221192 | tf_op jit(solution)/shard_map/ppermute | solution.py:71
  23.4 6.1 %collective-permute-start.5 = (f32[16,1152]{1,0:T(8,128)S(1)}, f32[16,1152]{1,0:T(8,128)S(1)}, u32[]{:S(2)}, u32[]{:S(2)}) collective-permute-start(f32[16,1152]{1,0:T(8,128)S(1)} %add.44), channel_id=1, source_target_pairs={{0,16},{4,20},{8,24},{12,28},{16,0},{20,4},{24,8},{28,12},{1,17},{... | collective-permute-start | bytes 221192 | tf_op jit(solution)/shard_map/ppermute | solution.py:71
  29.5 4.4 %collective-permute-start.6 = (f32[16,1152]{1,0:T(8,128)S(1)}, f32[16,1152]{1,0:T(8,128)S(1)}, u32[]{:S(2)}, u32[]{:S(2)}) collective-permute-start(f32[16,1152]{1,0:T(8,128)S(1)} %add.45.ours), channel_id=1, source_target_pairs={{0,2},{1,3},{2,0},{3,1},{4,6},{5,7},{6,4},{7,5},{8,10},{9,11},{10,... | collective-permute-start | bytes 221192 | tf_op jit(solution)/shard_map/ppermute | solution.py:71
  34.0 2.1 %collective-permute-start.8 = (f32[32,1152]{1,0:T(8,128)S(1)}, f32[32,1152]{1,0:T(8,128)S(1)}, u32[]{:S(2)}, u32[]{:S(2)}) collective-permute-start(f32[32,1152]{1,0:T(8,128)S(1)} %join.2.ours), channel_id=1, source_target_pairs={{0,1},{1,0},{2,3},{3,2},{4,5},{5,4},{6,7},{7,6},{8,9},{9,8},{10,11... | collective-permute-start | bytes 442376 | tf_op jit(solution)/shard_map/ppermute | solution.py:71
  34.0 11.9 %collective-permute-start.10 = (f32[72,576]{1,0:T(8,128)S(1)}, f32[72,576]{1,0:T(8,128)S(1)}, u32[]{:S(2)}, u32[]{:S(2)}) collective-permute-start(f32[72,576]{1,0:T(8,128)S(1)} %get-tuple-element.110), channel_id=1, source_target_pairs={{0,16},{4,20},{8,24},{12,28},{16,0},{20,4},{24,8},{28,12},{1,17},{... | collective-permute-start | bytes 497672 | tf_op jit(solution)/shard_map/ppermute | solution.py:71
  36.0 16.5 %copy-start.4 = (f32[1,1,2304]{2,1,0:T(1,128)S(1)}, f32[1,1,2304]{2,1,0:T(1,128)}, u32[]{:S(2)}) copy-start(f32[1,1,2304]{2,1,0:T(1,128)} %param.23) | copy-start | bytes 27652
  36.0 16.5 %copy-start.5 = (f32[72]{0:T(128)S(1)}, f32[72]{0:T(128)}, u32[]{:S(2)}) copy-start(f32[72]{0:T(128)} %param.24) | copy-start | bytes 868
  36.0 16.5 %copy-start.6 = (f32[72]{0:T(128)S(1)}, f32[72]{0:T(128)}, u32[]{:S(2)}) copy-start(f32[72]{0:T(128)} %param.25) | copy-start | bytes 868
  37.5 4.6 %collective-permute-start.9 = (f32[32,576]{1,0:T(8,128)S(1)}, f32[32,576]{1,0:T(8,128)S(1)}, u32[]{:S(2)}, u32[]{:S(2)}) collective-permute-start(f32[32,576]{1,0:T(8,128)S(1)} %get-tuple-element.105), channel_id=1, source_target_pairs={{0,4},{4,0},{8,12},{12,8},{16,20},{20,16},{24,28},{28,24},{1,5},{5... | collective-permute-start | bytes 221192 | tf_op jit(solution)/shard_map/ppermute | solution.py:71
  46.0 4.4 %collective-permute-start.11 = (f32[32,576]{1,0:T(8,128)S(1)}, f32[32,576]{1,0:T(8,128)S(1)}, u32[]{:S(2)}, u32[]{:S(2)}) collective-permute-start(f32[32,576]{1,0:T(8,128)S(1)} %add.46), channel_id=1, source_target_pairs={{0,8},{4,12},{8,0},{12,4},{16,24},{20,28},{24,16},{28,20},{1,9},{5... | collective-permute-start | bytes 221192 | tf_op jit(solution)/shard_map/ppermute | solution.py:71
  50.4 6.2 %collective-permute-start.12 = (f32[32,576]{1,0:T(8,128)S(1)}, f32[32,576]{1,0:T(8,128)S(1)}, u32[]{:S(2)}, u32[]{:S(2)}) collective-permute-start(f32[32,576]{1,0:T(8,128)S(1)} %add.47), channel_id=1, source_target_pairs={{0,16},{4,20},{8,24},{12,28},{16,0},{20,4},{24,8},{28,12},{1,17},{... | collective-permute-start | bytes 221192 | tf_op jit(solution)/shard_map/ppermute | solution.py:71
  52.1 9.8 %collective-permute-start.14 = (f32[144,576]{1,0:T(8,128)S(1)}, f32[144,576]{1,0:T(8,128)S(1)}, u32[]{:S(2)}, u32[]{:S(2)}) collective-permute-start(f32[144,576]{1,0:T(8,128)S(1)} %collective-permute-done.3.refs_1_), channel_id=1, source_target_pairs={{0,4},{4,0},{8,12},{12,8},{16,20},{20,16},{24,28},{28,24},{1,5},{5... | collective-permute-start | bytes 995336 | tf_op jit(solution)/shard_map/ppermute | solution.py:71
  57.8 1.5 %collective-permute-start.13 = (f32[32,1280]{1,0:T(8,128)S(1)}, f32[32,1280]{1,0:T(8,128)S(1)}, u32[]{:S(2)}, u32[]{:S(2)}) collective-permute-start(f32[32,1280]{1,0:T(8,128)S(1)} %get-tuple-element.121), channel_id=1, source_target_pairs={{0,1},{1,0},{2,3},{3,2},{4,5},{5,4},{6,7},{7,6},{8,9},{9,8},{10,11... | collective-permute-start | bytes 491528 | tf_op jit(solution)/shard_map/ppermute | solution.py:71
  57.8 11.9 %collective-permute-start.17 = (f32[72,576]{1,0:T(8,128)S(1)}, f32[72,576]{1,0:T(8,128)S(1)}, u32[]{:S(2)}, u32[]{:S(2)}) collective-permute-start(f32[72,576]{1,0:T(8,128)S(1)} %get-tuple-element.132), channel_id=1, source_target_pairs={{0,16},{4,20},{8,24},{12,28},{16,0},{20,4},{24,8},{28,12},{1,17},{... | collective-permute-start | bytes 497672 | tf_op jit(solution)/shard_map/ppermute | solution.py:71
  59.2 4.6 %collective-permute-start.15 = (f32[16,1280]{1,0:T(8,128)S(1)}, f32[16,1280]{1,0:T(8,128)S(1)}, u32[]{:S(2)}, u32[]{:S(2)}) collective-permute-start(f32[16,1280]{1,0:T(8,128)S(1)} %get-tuple-element.124), channel_id=1, source_target_pairs={{0,2},{1,3},{2,0},{3,1},{4,6},{5,7},{6,4},{7,5},{8,10},{9,11},{10,... | collective-permute-start | bytes 245768 | tf_op jit(solution)/shard_map/ppermute | solution.py:71
  63.8 6.7 %collective-permute-start.16 = (f32[16,1280]{1,0:T(8,128)S(1)}, f32[16,1280]{1,0:T(8,128)S(1)}, u32[]{:S(2)}, u32[]{:S(2)}) collective-permute-start(f32[16,1280]{1,0:T(8,128)S(1)} %add.49), channel_id=1, source_target_pairs={{0,4},{4,0},{8,12},{12,8},{16,20},{20,16},{24,28},{28,24},{1,5},{5... | collective-permute-start | bytes 245768 | tf_op jit(solution)/shard_map/ppermute | solution.py:71
  69.7 16.3 %collective-permute-start.21 = (f32[144,576]{1,0:T(8,128)S(1)}, f32[144,576]{1,0:T(8,128)S(1)}, u32[]{:S(2)}, u32[]{:S(2)}) collective-permute-start(f32[144,576]{1,0:T(8,128)S(1)} %constant_dynamic-update-slice_fusion.refs_0_), channel_id=1, source_target_pairs={{0,4},{4,0},{8,12},{12,8},{16,20},{20,16},{24,28},{28,24},{1,5},{5... | collective-permute-start | bytes 995336 | tf_op jit(solution)/shard_map/ppermute | solution.py:71
  70.6 4.5 %collective-permute-start.18 = (f32[16,1280]{1,0:T(8,128)S(1)}, f32[16,1280]{1,0:T(8,128)S(1)}, u32[]{:S(2)}, u32[]{:S(2)}) collective-permute-start(f32[16,1280]{1,0:T(8,128)S(1)} %add.50), channel_id=1, source_target_pairs={{0,8},{4,12},{8,0},{12,4},{16,24},{20,28},{24,16},{28,20},{1,9},{5... | collective-permute-start | bytes 245768 | tf_op jit(solution)/shard_map/ppermute | solution.py:71
  75.1 6.3 %collective-permute-start.19 = (f32[16,1280]{1,0:T(8,128)S(1)}, f32[16,1280]{1,0:T(8,128)S(1)}, u32[]{:S(2)}, u32[]{:S(2)}) collective-permute-start(f32[16,1280]{1,0:T(8,128)S(1)} %add.51), channel_id=1, source_target_pairs={{0,16},{4,20},{8,24},{12,28},{16,0},{20,4},{24,8},{28,12},{1,17},{... | collective-permute-start | bytes 245768 | tf_op jit(solution)/shard_map/ppermute | solution.py:71
  81.4 12.1 %collective-permute-start.24 = (f32[144,576]{1,0:T(8,128)S(1)}, f32[144,576]{1,0:T(8,128)S(1)}, u32[]{:S(2)}, u32[]{:S(2)}) collective-permute-start(f32[144,576]{1,0:T(8,128)S(1)} %constant_dynamic-update-slice_fusion.refs_0_), channel_id=1, source_target_pairs={{0,8},{4,12},{8,0},{12,4},{16,24},{20,28},{24,16},{28,20},{1,9},{5... | collective-permute-start | bytes 995336 | tf_op jit(solution)/shard_map/ppermute | solution.py:71
  81.5 4.5 %collective-permute-start.20 = (f32[16,1280]{1,0:T(8,128)S(1)}, f32[16,1280]{1,0:T(8,128)S(1)}, u32[]{:S(2)}, u32[]{:S(2)}) collective-permute-start(f32[16,1280]{1,0:T(8,128)S(1)} %add.52.ours), channel_id=1, source_target_pairs={{0,2},{1,3},{2,0},{3,1},{4,6},{5,7},{6,4},{7,5},{8,10},{9,11},{10,... | collective-permute-start | bytes 245768 | tf_op jit(solution)/shard_map/ppermute | solution.py:71
  86.0 1.5 %collective-permute-start.22 = (f32[32,1280]{1,0:T(8,128)S(1)}, f32[32,1280]{1,0:T(8,128)S(1)}, u32[]{:S(2)}, u32[]{:S(2)}) collective-permute-start(f32[32,1280]{1,0:T(8,128)S(1)} %join.3.ours), channel_id=1, source_target_pairs={{0,1},{1,0},{2,3},{3,2},{4,5},{5,4},{6,7},{7,6},{8,9},{9,8},{10,11... | collective-permute-start | bytes 491528 | tf_op jit(solution)/shard_map/ppermute | solution.py:71
  89.0 4.6 %collective-permute-start.23 = (f32[32,576]{1,0:T(8,128)S(1)}, f32[32,576]{1,0:T(8,128)S(1)}, u32[]{:S(2)}, u32[]{:S(2)}) collective-permute-start(f32[32,576]{1,0:T(8,128)S(1)} %get-tuple-element.143), channel_id=1, source_target_pairs={{0,4},{4,0},{8,12},{12,8},{16,20},{20,16},{24,28},{28,24},{1,5},{5... | collective-permute-start | bytes 221192 | tf_op jit(solution)/shard_map/ppermute | solution.py:71
  93.5 11.4 %collective-permute-start.27 = (f32[144,576]{1,0:T(8,128)S(1)}, f32[144,576]{1,0:T(8,128)S(1)}, u32[]{:S(2)}, u32[]{:S(2)}) collective-permute-start(f32[144,576]{1,0:T(8,128)S(1)} %collective-permute-done.24.refs_1_), channel_id=1, source_target_pairs={{0,4},{4,0},{8,12},{12,8},{16,20},{20,16},{24,28},{28,24},{1,5},{5... | collective-permute-start | bytes 995336 | tf_op jit(solution)/shard_map/ppermute | solution.py:71
  95.0 4.4 %collective-permute-start.25 = (f32[32,576]{1,0:T(8,128)S(1)}, f32[32,576]{1,0:T(8,128)S(1)}, u32[]{:S(2)}, u32[]{:S(2)}) collective-permute-start(f32[32,576]{1,0:T(8,128)S(1)} %add.53), channel_id=1, source_target_pairs={{0,8},{4,12},{8,0},{12,4},{16,24},{20,28},{24,16},{28,20},{1,9},{5... | collective-permute-start | bytes 221192 | tf_op jit(solution)/shard_map/ppermute | solution.py:71
  99.5 5.4 %collective-permute-start.26 = (f32[32,576]{1,0:T(8,128)S(1)}, f32[32,576]{1,0:T(8,128)S(1)}, u32[]{:S(2)}, u32[]{:S(2)}) collective-permute-start(f32[32,576]{1,0:T(8,128)S(1)} %add.54), channel_id=1, source_target_pairs={{0,16},{4,20},{8,24},{12,28},{16,0},{20,4},{24,8},{28,12},{1,17},{... | collective-permute-start | bytes 221192 | tf_op jit(solution)/shard_map/ppermute | solution.py:71

commit v7 on v6

--- a/solution.py
+++ b/solution.py
@@ -10,6 +10,7 @@
 ROUNDS = 2
 GROUP = 8
 LANES = 128
+BESIDE = 8
 
 highest = lax.Precision.HIGHEST
 decay_rate = 0.9
@@ -86,11 +87,12 @@
         got = swap(give, "shard", mask, n_shard)
         if after is not None:
             keep, give = split(keep, got, shard, after)
-            keep = gather.before(keep, stage, "core")
+            keep = gather.after(gather.before(keep, stage, "core"), stage, "core")
     part = sum_over(keep + got, n_rep, gather, stage)
     for mask in reversed(masks[1:]):
-        part = join(part, swap(part, "shard", mask, n_shard), shard, mask)
-        part = gather.before(part, stage, "x")
+        part = gather.start_tasks(part, stage, "x")
+        got = gather.end_tasks(swap(part, "shard", mask, n_shard), stage, "x")
+        part = gather.before(join(part, got, shard, mask), stage, "joined")
     return part, swap(part, "shard", masks[0], n_shard)
 
 
@@ -142,19 +144,21 @@
 
 class Gather:
     PLAN = (
-        ("near", "own", 2, None, (0, 2)),
-        ("turned", "own", 1, (0, 1), (0, "x")),
-        ("far_a", "own_a", 4, (0, 4), (1, 2)),
-        ("turned_near", "near", 1, (1, 1), (2, "core")),
-        ("far_b", "own_b", 4, (1, 4), (2, 2)),
-        ("turned_far", "far", 1, (2, 1), (2, "x")),
+        ("far_a", "own_a", 4, (0, "core"), (0, 4)),
+        ("turned", "own", 1, (0, 1), (1, 1)),
+        ("near", "own", 2, (0, 4), (1, 4)),
+        ("turned_near", "near", 1, ("beside", 1, 4), (2, 2)),
+        ("far_b", "own_b", 4, (2, "core"), (2, 4)),
+        ("turned_far", "far", 1, (2, 2), (3, 1)),
         ("last", "far", 2, (2, 4), (3, 2)),
-        ("turned_last", "last", 1, ("ahead", 3, 2), (3, 0)),
+        ("turned_last", "last", 1, ("beside", 3, 2), (3, 0)),
     )
     INSERTS = {
-        (1, 4): ("own", "near"),
-        (2, 1): ("turned", "turned_near"),
-        (2, 4): ("far",),
+        (1, 4): ("own",),
+        (2, 1): ("near",),
+        (2, 2): ("turned",),
+        (2, 4): ("turned_near",),
+        (2, "x"): ("far",),
         (3, 4): ("turned_far", "last"),
     }
     PLACES = {"own": 0, "turned": 1, "near": 2, "far": 4, "last": 6, "turned_near": 3, "turned_far": 5, "turned_last": 7}
@@ -174,7 +178,7 @@
             for name, source, mask, after, _ in self.PLAN:
                 if after == point:
                     if source == "far" and source not in self.blocks:
-                        self.blocks["far"] = jnp.concatenate([self.blocks["far_a"], self.blocks["far_b"]], axis=0)
+                        self.blocks["far"] = jnp.concatenate([self.blocks["far_a"], self.blocks["far_b"][BESIDE:]], axis=0)
                     self.blocks[name] = swap(self.blocks[source], "rep", mask, self.count)
 
     def start_tasks(self, value, stage, mask):
@@ -186,6 +190,14 @@
         if self.paired and point in self.INSERTS:
             value, *blocks = lax.optimization_barrier((value, *(self.blocks[name] for name in self.INSERTS[point])))
             self.insert(blocks, self.INSERTS[point])
+        if self.paired:
+            for name, source, _, after, _ in self.PLAN:
+                if after == ("beside",) + point:
+                    if point in self.INSERTS:
+                        self.rows, self.blocks[source] = lax.optimization_barrier((self.rows, self.blocks[source]))
+                    else:
+                        self.results[point], self.blocks[source] = lax.optimization_barrier((self.results[point], self.blocks[source]))
+            self.send(("beside",) + point)
         return value
 
     def end_tasks(self, value, stage, mask):
@@ -204,7 +216,6 @@
             for name, _, _, _, by in self.PLAN:
                 if by == (stage, mask):
                     value, self.blocks[name] = lax.optimization_barrier((value, self.blocks[name]))
-            self.send(("ahead", stage, mask))
         return value
 
     def after(self, value, stage, mask):
@@ -252,14 +263,16 @@
     drop = step_size * decay_rate
     base = jnp.concatenate([weight_q[...] - drop * moment_q[...], weight_o[...] - drop * moment_o[...]], axis=1)
     own[...] = base
-    half = base.shape[0] // 2
-    for k, part in enumerate(parts):
-        part[...] = base[k * half : (k + 1) * half]
+    rows = base.shape[0]
+    first_part, second_part = parts
+    first_part[...] = base[: first_part.shape[0]]
+    second_part[...] = base[rows - second_part.shape[0] :]
 
 
 def base_of(weight_q, moment_q, weight_o, moment_o):
     rows, width = weight_q.shape[0], 2 * weight_q.shape[1]
-    shapes = [(rows, width)] + [(rows // 2, width)] * 2
+    half = rows // 2
+    shapes = [(rows, width), (half, width), (rows - half + BESIDE * (half > BESIDE), width)]
     return pl.pallas_call(
         base_kernel,
         in_specs=[IN_VMEM] * 4,
@@ -576,7 +589,7 @@
         ours, got = sum_over_all(keep, give, shard, n_rep, n_shard, gather, 2 * sweep)
         right, left, *extra_sum = right_of(ours, got, shard, corr_q, corr_o)
         if last and gather.paired:
-            gather.tasks[3, 4] = (functools.partial(stack_of, count=row_count), left, place)
+            gather.tasks[3, 2] = (functools.partial(stack_of, count=row_count), left, place)
         gather.tasks[2 * sweep + 1, 1] = (inverse_of, left)
         right = sum_over(right, n_rep, gather, 2 * sweep + 1)
         inverse = gather.results[2 * sweep + 1, 1]
@@ -584,7 +597,7 @@
             keep, give = left_of(right, inverse, shard, corr_q, corr_o, [extra] if sweep == ROUNDS - 2 else [])
     norm_moment_new, norm_weight_new = norm_out(extra_sum[0], norm_moment, flat // LANES, place, shard, n_shard)
     if gather.paired:
-        stack, own = gather.results[3, 4]
+        stack, own = gather.results[3, 2]
         gather.insert([gather.blocks["turned_last"]], ["turned_last"])
         outs = finish(corr_q, corr_o, gather.rows, stack, inverse, right, own, q_moment, o_moment)
     else:

time: 109 us -> 103 us (0.945)
  waiting for transfers between devices: 58 us -> 50.5 us
    ppermute x28, waiting for transfers between devices: 58 us -> 50.5 us  [swap(): return lax.ppermute(block, axis, pairs)]
    pallas_call x5 -> x7, Pallas kernels: 3.1 us -> 3.25 us  [insert(): pl.pallas_call(functools.partial(insert_kernel, masks), in_specs=[IN_SMEM...]
where the time goes in v7:
time: 103 us
  waiting for transfers between devices  50.5 us (49%)
  starting transfers between devices  31.8 us (31%)
  Pallas kernels  19.3 us (19%)
    ppermute x28, waiting for transfers between devices, swap(): return lax.ppermute(block, axis, pairs)  50.5 us
    ppermute x28, starting transfers between devices, swap(): return lax.ppermute(block, axis, pairs)  31.8 us
    pallas_call x1, Pallas kernels, first(): pl.pallas_call(functools.partial(first_kernel, chunks), in_specs=[IN_SMEM...  4.51 us
    pallas_call x1, Pallas kernels, finish(): pl.pallas_call(functools.partial(finish_kernel, chunks), in_specs=[IN_VME...  3.68 us
    pallas_call x7, Pallas kernels, insert(): pl.pallas_call(functools.partial(insert_kernel, masks), in_specs=[IN_SMEM...  3.25 us
    pallas_call x2, Pallas kernels, right_of(): pl.pallas_call(right_kernel, in_specs=[IN_SMEM] + [IN_VMEM] * 4, out_spec...  2.98 us
    pallas_call x2, Pallas kernels, inverse_of(): pl.pallas_call(inverse_kernel, out_shape=pltpu.VMEM((2, rank, rank), f32)...  2.6 us
  transfers between devices with their start and end apart: 28, of which 20 were waited for; matrix products, arithmetic and copies ran while one was open for 0% of the time, Pallas kernels for 10%

profile of v7, /device:TPU:0, one launch (start us, length us, event | category | flops | bytes accessed | tf_op | source)
XLA Modules:
  0.0 102.7 jit_solution(13301120885597348333)
XLA Ops:
  0.7 4.5 %first.1 = (f32[288,1152]{1,0:T(8,128)S(1)}, f32[288,1152]{1,0:T(8,128)S(1)}, f32[32,1152]{1,0:T(8,128)S(1)}, f32[32,1152]{1,0:T(8,128)S(1)}) custom-call(s32[1]{0:T(128)} %bitcast.place_ref, s32[1]{0:T(128)} %bitcast.1.shard_ref, f32[288,1152]{1,0:T(8,128)} %bitcast.33, f32[288,1152]{1,0:T(8,128)} %bitcast.34, f32[288,1152]{1,0:T(8,128)} %bitcast.35, ...), custom_call_target="tpu_custom_call" | custom-call | tf_op jit(solution)/shard_map/first/pallas_call | solution.py:372
  5.2 0.5 collective-permute-start
  5.7 1.0 collective-permute-done.got
  6.8 2.9 %collective-permute-start.1 = (f32[16,1152]{1,0:T(8,128)S(1)}, f32[16,1152]{1,0:T(8,128)S(1)}, u32[]{:S(2)}, u32[]{:S(2)}) collective-permute-start(f32[16,1152]{1,0:T(8,128)S(1)} %get-tuple-element.111), channel_id=1, source_target_pairs={{0,2},{1,3},{2,0},{3,1},{4,6},{5,7},{6,4},{7,5},{8,10},{9,11},{10,... | collective-permute-start | bytes 221192 | tf_op jit(solution)/shard_map/ppermute | solution.py:72
  9.8 2.7 %collective-permute-start.4 = (f32[72,576]{1,0:T(8,128)S(1)}, f32[72,576]{1,0:T(8,128)S(1)}, u32[]{:S(2)}, u32[]{:S(2)}) collective-permute-start(f32[72,576]{1,0:T(8,128)S(1)} %get-tuple-element.114), channel_id=1, source_target_pairs={{0,16},{4,20},{8,24},{12,28},{16,0},{20,4},{24,8},{28,12},{1,17},{... | collective-permute-start | bytes 497672 | tf_op jit(solution)/shard_map/ppermute | solution.py:72
  12.5 1.6 %collective-permute-start.2 = (f32[16,1152]{1,0:T(8,128)S(1)}, f32[16,1152]{1,0:T(8,128)S(1)}, u32[]{:S(2)}, u32[]{:S(2)}) collective-permute-start(f32[16,1152]{1,0:T(8,128)S(1)} %add.42), channel_id=1, source_target_pairs={{0,4},{4,0},{8,12},{12,8},{16,20},{20,16},{24,28},{28,24},{1,5},{5... | collective-permute-start | bytes 221192 | tf_op jit(solution)/shard_map/ppermute | solution.py:72
  14.1 2.8 %collective-permute-done.2 = f32[16,1152]{1,0:T(8,128)S(1)} collective-permute-done((f32[16,1152]{1,0:T(8,128)S(1)}, f32[16,1152]{1,0:T(8,128)S(1)}, u32[]{:S(2)}, u32[]{:S(2)}) %collective-permute-start.2) | collective-permute-done | bytes 73760 | tf_op jit(solution)/shard_map/ppermute | solution.py:72
  16.9 1.7 %collective-permute-start.3 = (f32[16,1152]{1,0:T(8,128)S(1)}, f32[16,1152]{1,0:T(8,128)S(1)}, u32[]{:S(2)}, u32[]{:S(2)}) collective-permute-start(f32[16,1152]{1,0:T(8,128)S(1)} %add.43), channel_id=1, source_target_pairs={{0,8},{4,12},{8,0},{12,4},{16,24},{20,28},{24,16},{28,20},{1,9},{5... | collective-permute-start | bytes 221192 | tf_op jit(solution)/shard_map/ppermute | solution.py:72
  18.6 1.5 %collective-permute-start.8 = (f32[144,576]{1,0:T(8,128)S(1)}, f32[144,576]{1,0:T(8,128)S(1)}, u32[]{:S(2)}, u32[]{:S(2)}) collective-permute-start(f32[144,576]{1,0:T(8,128)S(1)} %get-tuple-element.127.refs_0_), channel_id=1, source_target_pairs={{0,4},{4,0},{8,12},{12,8},{16,20},{20,16},{24,28},{28,24},{1,5},{5... | collective-permute-start | bytes 995336 | tf_op jit(solution)/shard_map/ppermute | solution.py:72
  20.1 2.6 %collective-permute-done.3 = f32[16,1152]{1,0:T(8,128)S(1)} collective-permute-done((f32[16,1152]{1,0:T(8,128)S(1)}, f32[16,1152]{1,0:T(8,128)S(1)}, u32[]{:S(2)}, u32[]{:S(2)}) %collective-permute-start.3) | collective-permute-done | bytes 73760 | tf_op jit(solution)/shard_map/ppermute | solution.py:72
  22.7 1.6 %collective-permute-start.5 = (f32[16,1152]{1,0:T(8,128)S(1)}, f32[16,1152]{1,0:T(8,128)S(1)}, u32[]{:S(2)}, u32[]{:S(2)}) collective-permute-start(f32[16,1152]{1,0:T(8,128)S(1)} %add.44), channel_id=1, source_target_pairs={{0,16},{4,20},{8,24},{12,28},{16,0},{20,4},{24,8},{28,12},{1,17},{... | collective-permute-start | bytes 221192 | tf_op jit(solution)/shard_map/ppermute | solution.py:72
  24.4 5.2 %collective-permute-done.5 = f32[16,1152]{1,0:T(8,128)S(1)} collective-permute-done((f32[16,1152]{1,0:T(8,128)S(1)}, f32[16,1152]{1,0:T(8,128)S(1)}, u32[]{:S(2)}, u32[]{:S(2)}) %collective-permute-start.5) | collective-permute-done | bytes 73760 | tf_op jit(solution)/shard_map/ppermute | solution.py:72
  29.9 4.1 %collective-permute-done.6.got = f32[16,1152]{1,0:T(8,128)S(1)} collective-permute-done((f32[16,1152]{1,0:T(8,128)S(1)}, f32[16,1152]{1,0:T(8,128)S(1)}, u32[]{:S(2)}, u32[]{:S(2)}) %collective-permute-start.6) | collective-permute-done | bytes 73760 | tf_op jit(solution)/shard_map/ppermute | solution.py:72
  34.1 1.4 %collective-permute-done.7.got = f32[32,1152]{1,0:T(8,128)S(1)} collective-permute-done((f32[32,1152]{1,0:T(8,128)S(1)}, f32[32,1152]{1,0:T(8,128)S(1)}, u32[]{:S(2)}, u32[]{:S(2)}) %collective-permute-start.7) | collective-permute-done | bytes 147488 | tf_op jit(solution)/shard_map/ppermute | solution.py:72
  35.4 1.5 %right.2 = (f32[32,576]{1,0:T(8,128)S(1)}, f32[64,1152]{1,0:T(8,128)S(1)}) custom-call(s32[1]{0:T(128)} %bitcast.1.shard_ref, f32[32,1152]{1,0:T(8,128)S(1)} %join.2.ours, f32[32,1152]{1,0:T(8,128)S(1)} %collective-permute-done.7.got, f32[288,1152]{1,0:T(8,128)S(1)} %get-tuple-element.104.corr_q, f32[288,1152]{1,0:T(8,128)S(1)} %get-tuple-element.105.corr_o), custom_call_target="tpu_custom_call" | custom-call | flops 1000 | bytes 1000 | tf_op jit(solution)/shard_map/right/pallas_call | solution.py:402
  36.9 1.5 %collective-permute-start.9 = (f32[32,576]{1,0:T(8,128)S(1)}, f32[32,576]{1,0:T(8,128)S(1)}, u32[]{:S(2)}, u32[]{:S(2)}) collective-permute-start(f32[32,576]{1,0:T(8,128)S(1)} %get-tuple-element.121), channel_id=1, source_target_pairs={{0,4},{4,0},{8,12},{12,8},{16,20},{20,16},{24,28},{28,24},{1,5},{5... | collective-permute-start | bytes 221192 | tf_op jit(solution)/shard_map/ppermute | solution.py:72
  38.5 1.3 %inverse.2 = f32[2,32,32]{2,1,0:T(8,128)S(1)} custom-call(f32[64,1152]{1,0:T(8,128)S(1)} %get-tuple-element.122.left), custom_call_target="tpu_custom_call" | custom-call | flops 1000 | bytes 6000000 | tf_op jit(solution)/shard_map/inverse/pallas_call | solution.py:479
  39.8 1.7 %collective-permute-done.9 = f32[32,576]{1,0:T(8,128)S(1)} collective-permute-done((f32[32,576]{1,0:T(8,128)S(1)}, f32[32,576]{1,0:T(8,128)S(1)}, u32[]{:S(2)}, u32[]{:S(2)}) %collective-permute-start.9) | collective-permute-done | bytes 73760 | tf_op jit(solution)/shard_map/ppermute | solution.py:72
  41.6 4.4 %collective-permute-done.10 = f32[32,576]{1,0:T(8,128)S(1)} collective-permute-done((f32[32,576]{1,0:T(8,128)S(1)}, f32[32,576]{1,0:T(8,128)S(1)}, u32[]{:S(2)}, u32[]{:S(2)}) %collective-permute-start.10) | collective-permute-done | bytes 73760 | tf_op jit(solution)/shard_map/ppermute | solution.py:72
  46.1 1.2 %collective-permute-start.12 = (f32[32,576]{1,0:T(8,128)S(1)}, f32[32,576]{1,0:T(8,128)S(1)}, u32[]{:S(2)}, u32[]{:S(2)}) collective-permute-start(f32[32,576]{1,0:T(8,128)S(1)} %add.47), channel_id=1, source_target_pairs={{0,16},{4,20},{8,24},{12,28},{16,0},{20,4},{24,8},{28,12},{1,17},{... | collective-permute-start | bytes 221192 | tf_op jit(solution)/shard_map/ppermute | solution.py:72
  47.3 0.6 insert.7.refs_1_
  47.8 1.6 %collective-permute-start.16 = (f32[144,576]{1,0:T(8,128)S(1)}, f32[144,576]{1,0:T(8,128)S(1)}, u32[]{:S(2)}, u32[]{:S(2)}) collective-permute-start(f32[144,576]{1,0:T(8,128)S(1)} %collective-permute-done.11.refs_0_), channel_id=1, source_target_pairs={{0,4},{4,0},{8,12},{12,8},{16,20},{20,16},{24,28},{28,24},{1,5},{5... | collective-permute-start | bytes 995336 | tf_op jit(solution)/shard_map/ppermute | solution.py:72
  49.5 2.5 %collective-permute-done.12 = f32[32,576]{1,0:T(8,128)S(1)} collective-permute-done((f32[32,576]{1,0:T(8,128)S(1)}, f32[32,576]{1,0:T(8,128)S(1)}, u32[]{:S(2)}, u32[]{:S(2)}) %collective-permute-start.12) | collective-permute-done | bytes 73760 | tf_op jit(solution)/shard_map/ppermute | solution.py:72
  52.0 1.2 %left.1 = (f32[32,1280]{1,0:T(8,128)S(1)}, f32[32,1280]{1,0:T(8,128)S(1)}) custom-call(s32[1]{0:T(128)} %bitcast.1.shard_ref, f32[32,576]{1,0:T(8,128)S(1)} %add.48.right, f32[2,32,32]{2,1,0:T(8,128)S(1)} %inverse.2, f32[288,1152]{1,0:T(8,128)S(1)} %get-tuple-element.104.corr_q, f32[288,1152]{1,0:T(8,128)S(1)} %get-tuple-element.105.corr_o, ...), custom_call_target="tpu_custom_call" | custom-call | flops 1000 | bytes 1000 | tf_op jit(solution)/shard_map/left/pallas_call | solution.py:433
  53.3 1.4 %collective-permute-done.13.got = f32[32,1280]{1,0:T(8,128)S(1)} collective-permute-done((f32[32,1280]{1,0:T(8,128)S(1)}, f32[32,1280]{1,0:T(8,128)S(1)}, u32[]{:S(2)}, u32[]{:S(2)}) %collective-permute-start.13) | collective-permute-done | bytes 163872 | tf_op jit(solution)/shard_map/ppermute | solution.py:72
  55.2 0.6 collective-permute-start.18
  55.8 3.5 %collective-permute-done.14 = f32[16,1280]{1,0:T(8,128)S(1)} collective-permute-done((f32[16,1280]{1,0:T(8,128)S(1)}, f32[16,1280]{1,0:T(8,128)S(1)}, u32[]{:S(2)}, u32[]{:S(2)}) %collective-permute-start.14) | collective-permute-done | bytes 81952 | tf_op jit(solution)/shard_map/ppermute | solution.py:72
  59.3 1.6 %collective-permute-start.15 = (f32[16,1280]{1,0:T(8,128)S(1)}, f32[16,1280]{1,0:T(8,128)S(1)}, u32[]{:S(2)}, u32[]{:S(2)}) collective-permute-start(f32[16,1280]{1,0:T(8,128)S(1)} %add.49), channel_id=1, source_target_pairs={{0,4},{4,0},{8,12},{12,8},{16,20},{20,16},{24,28},{28,24},{1,5},{5... | collective-permute-start | bytes 245768 | tf_op jit(solution)/shard_map/ppermute | solution.py:72
  61.3 2.5 %collective-permute-done.15 = f32[16,1280]{1,0:T(8,128)S(1)} collective-permute-done((f32[16,1280]{1,0:T(8,128)S(1)}, f32[16,1280]{1,0:T(8,128)S(1)}, u32[]{:S(2)}, u32[]{:S(2)}) %collective-permute-start.15) | collective-permute-done | bytes 81952 | tf_op jit(solution)/shard_map/ppermute | solution.py:72
  64.3 2.8 %collective-permute-done.18 = f32[80,576]{1,0:T(8,128)S(1)} collective-permute-done((f32[80,576]{1,0:T(8,128)S(1)}, f32[80,576]{1,0:T(8,128)S(1)}, u32[]{:S(2)}, u32[]{:S(2)}) %collective-permute-start.18) | collective-permute-done | bytes 184352 | tf_op jit(solution)/shard_map/ppermute | solution.py:72
  67.1 1.6 %collective-permute-done.17 = f32[16,1280]{1,0:T(8,128)S(1)} collective-permute-done((f32[16,1280]{1,0:T(8,128)S(1)}, f32[16,1280]{1,0:T(8,128)S(1)}, u32[]{:S(2)}, u32[]{:S(2)}) %collective-permute-start.17) | collective-permute-done | bytes 81952 | tf_op jit(solution)/shard_map/ppermute | solution.py:72
  69.3 1.6 %collective-permute-start.22 = (f32[144,576]{1,0:T(8,128)S(1)}, f32[144,576]{1,0:T(8,128)S(1)}, u32[]{:S(2)}, u32[]{:S(2)}) collective-permute-start(f32[144,576]{1,0:T(8,128)S(1)} %pad_maximum_fusion.refs_0_), channel_id=1, source_target_pairs={{0,4},{4,0},{8,12},{12,8},{16,20},{20,16},{24,28},{28,24},{1,5},{5... | collective-permute-start | bytes 995336 | tf_op jit(solution)/shard_map/ppermute | solution.py:72
  71.3 3.3 %collective-permute-done.19 = f32[16,1280]{1,0:T(8,128)S(1)} collective-permute-done((f32[16,1280]{1,0:T(8,128)S(1)}, f32[16,1280]{1,0:T(8,128)S(1)}, u32[]{:S(2)}, u32[]{:S(2)}) %collective-permute-start.19) | collective-permute-done | bytes 81952 | tf_op jit(solution)/shard_map/ppermute | solution.py:72
  74.7 2.2 %collective-permute-start.20 = (f32[16,1280]{1,0:T(8,128)S(1)}, f32[16,1280]{1,0:T(8,128)S(1)}, u32[]{:S(2)}, u32[]{:S(2)}) collective-permute-start(f32[16,1280]{1,0:T(8,128)S(1)} %add.52.ours), channel_id=1, source_target_pairs={{0,2},{1,3},{2,0},{3,1},{4,6},{5,7},{6,4},{7,5},{8,10},{9,11},{10,... | collective-permute-start | bytes 245768 | tf_op jit(solution)/shard_map/ppermute | solution.py:72
  77.2 2.2 %collective-permute-done.20.got = f32[16,1280]{1,0:T(8,128)S(1)} collective-permute-done((f32[16,1280]{1,0:T(8,128)S(1)}, f32[16,1280]{1,0:T(8,128)S(1)}, u32[]{:S(2)}, u32[]{:S(2)}) %collective-permute-start.20) | collective-permute-done | bytes 81952 | tf_op jit(solution)/shard_map/ppermute | solution.py:72
  79.6 1.4 %collective-permute-done.21.got = f32[32,1280]{1,0:T(8,128)S(1)} collective-permute-done((f32[32,1280]{1,0:T(8,128)S(1)}, f32[32,1280]{1,0:T(8,128)S(1)}, u32[]{:S(2)}, u32[]{:S(2)}) %collective-permute-start.21) | collective-permute-done | bytes 163872 | tf_op jit(solution)/shard_map/ppermute | solution.py:72
  80.9 1.5 %right.3 = (f32[32,576]{1,0:T(8,128)S(1)}, f32[64,1152]{1,0:T(8,128)S(1)}, f32[64,128]{1,0:T(8,128)S(1)}) custom-call(s32[1]{0:T(128)} %bitcast.1.shard_ref, f32[32,1280]{1,0:T(8,128)S(1)} %join.3.ours, f32[32,1280]{1,0:T(8,128)S(1)} %collective-permute-done.21.got, f32[288,1152]{1,0:T(8,128)S(1)} %get-tuple-element.104.corr_q, ...), custom_call_target="tpu_custom_call" | custom-call | flops 1000 | bytes 1000 | tf_op jit(solution)/shard_map/right/pallas_call | solution.py:402
  82.5 1.6 %collective-permute-start.23 = (f32[32,576]{1,0:T(8,128)S(1)}, f32[32,576]{1,0:T(8,128)S(1)}, u32[]{:S(2)}, u32[]{:S(2)}) collective-permute-start(f32[32,576]{1,0:T(8,128)S(1)} %get-tuple-element.164), channel_id=1, source_target_pairs={{0,4},{4,0},{8,12},{12,8},{16,20},{20,16},{24,28},{28,24},{1,5},{5... | collective-permute-start | bytes 221192 | tf_op jit(solution)/shard_map/ppermute | solution.py:72
  84.0 1.3 %inverse.3 = f32[2,32,32]{2,1,0:T(8,128)S(1)} custom-call(f32[64,1152]{1,0:T(8,128)S(1)} %get-tuple-element.171.left), custom_call_target="tpu_custom_call" | custom-call | flops 1000 | bytes 6000000 | tf_op jit(solution)/shard_map/inverse/pallas_call | solution.py:479
  85.3 1.7 %collective-permute-done.23 = f32[32,576]{1,0:T(8,128)S(1)} collective-permute-done((f32[32,576]{1,0:T(8,128)S(1)}, f32[32,576]{1,0:T(8,128)S(1)}, u32[]{:S(2)}, u32[]{:S(2)}) %collective-permute-start.23) | collective-permute-done | bytes 73760 | tf_op jit(solution)/shard_map/ppermute | solution.py:72
  87.2 1.6 %collective-permute-start.27 = (f32[144,576]{1,0:T(8,128)S(1)}, f32[144,576]{1,0:T(8,128)S(1)}, u32[]{:S(2)}, u32[]{:S(2)}) collective-permute-start(f32[144,576]{1,0:T(8,128)S(1)} %collective-permute-done.24.refs_1_), channel_id=1, source_target_pairs={{0,4},{4,0},{8,12},{12,8},{16,20},{20,16},{24,28},{28,24},{1,5},{5... | collective-permute-start | bytes 995336 | tf_op jit(solution)/shard_map/ppermute | solution.py:72
  88.8 1.7 %collective-permute-start.25 = (f32[32,576]{1,0:T(8,128)S(1)}, f32[32,576]{1,0:T(8,128)S(1)}, u32[]{:S(2)}, u32[]{:S(2)}) collective-permute-start(f32[32,576]{1,0:T(8,128)S(1)} %add.53), channel_id=1, source_target_pairs={{0,8},{4,12},{8,0},{12,4},{16,24},{20,28},{24,16},{28,20},{1,9},{5... | collective-permute-start | bytes 221192 | tf_op jit(solution)/shard_map/ppermute | solution.py:72
  90.5 2.7 %collective-permute-done.25 = f32[32,576]{1,0:T(8,128)S(1)} collective-permute-done((f32[32,576]{1,0:T(8,128)S(1)}, f32[32,576]{1,0:T(8,128)S(1)}, u32[]{:S(2)}, u32[]{:S(2)}) %collective-permute-start.25) | collective-permute-done | bytes 73760 | tf_op jit(solution)/shard_map/ppermute | solution.py:72
  93.2 2.4 %collective-permute-start.26 = (f32[32,576]{1,0:T(8,128)S(1)}, f32[32,576]{1,0:T(8,128)S(1)}, u32[]{:S(2)}, u32[]{:S(2)}) collective-permute-start(f32[32,576]{1,0:T(8,128)S(1)} %add.54), channel_id=1, source_target_pairs={{0,16},{4,20},{8,24},{12,28},{16,0},{20,4},{24,8},{28,12},{1,17},{... | collective-permute-start | bytes 221192 | tf_op jit(solution)/shard_map/ppermute | solution.py:72
  95.6 0.6 norm_out.1
  96.2 0.7 insert.12.refs_1_
  96.9 1.7 %collective-permute-done.26 = f32[32,576]{1,0:T(8,128)S(1)} collective-permute-done((f32[32,576]{1,0:T(8,128)S(1)}, f32[32,576]{1,0:T(8,128)S(1)}, u32[]{:S(2)}, u32[]{:S(2)}) %collective-permute-start.26) | collective-permute-done | bytes 73760 | tf_op jit(solution)/shard_map/ppermute | solution.py:72
  99.1 3.7 %finish.1 = (f32[288,1152]{1,0:T(8,128)}, f32[288,1152]{1,0:T(8,128)}, f32[288,1152]{1,0:T(8,128)}, f32[288,1152]{1,0:T(8,128)}, f32[144,288]{1,0:T(8,128)}, /*index=5*/f32[144,288]{1,0:T(8,128)}) custom-call(f32[288,1152]{1,0:T(8,128)S(1)} %get-tuple-element.104.corr_q, f32[288,1152]{1,0:T(8,128)S(1)} %get-tuple-element.105.corr_o, ...), custom_call_target="tpu_custom_call" | custom-call | tf_op jit(solution)/shard_map/finish/pallas_call | solution.py:543
  (60 shorter events, 4.4 us)
Async XLA Ops:
  0.6 9.0 %copy-start = (f32[144,288]{1,0:T(8,128)S(1)}, f32[144,288]{1,0:T(8,128)}, u32[]{:S(2)}) copy-start(f32[144,288]{1,0:T(8,128)} %moment_q.3) | copy-start | bytes 497668
  0.7 9.0 %copy-start.1 = (f32[144,288]{1,0:T(8,128)S(1)}, f32[144,288]{1,0:T(8,128)}, u32[]{:S(2)}) copy-start(f32[144,288]{1,0:T(8,128)} %moment_o.3) | copy-start | bytes 497668
  0.7 9.0 %copy-start.2 = (f32[144,288]{1,0:T(8,128)S(1)}, f32[144,288]{1,0:T(8,128)}, u32[]{:S(2)}) copy-start(f32[144,288]{1,0:T(8,128)} %weight_q.1) | copy-start | bytes 497668
  0.7 9.0 %copy-start.3 = (f32[144,288]{1,0:T(8,128)S(1)}, f32[144,288]{1,0:T(8,128)}, u32[]{:S(2)}) copy-start(f32[144,288]{1,0:T(8,128)} %weight_o.1) | copy-start | bytes 497668
  5.2 1.5 %collective-permute-start = (f32[32,1152]{1,0:T(8,128)S(1)}, f32[32,1152]{1,0:T(8,128)S(1)}, u32[]{:S(2)}, u32[]{:S(2)}) collective-permute-start(f32[32,1152]{1,0:T(8,128)S(1)} %get-tuple-element.107), channel_id=1, source_target_pairs={{0,1},{1,0},{2,3},{3,2},{4,5},{5,4},{6,7},{7,6},{8,9},{9,8},{10,11... | collective-permute-start | bytes 442376 | tf_op jit(solution)/shard_map/ppermute | solution.py:72
  6.8 5.7 %collective-permute-start.1 = (f32[16,1152]{1,0:T(8,128)S(1)}, f32[16,1152]{1,0:T(8,128)S(1)}, u32[]{:S(2)}, u32[]{:S(2)}) collective-permute-start(f32[16,1152]{1,0:T(8,128)S(1)} %get-tuple-element.111), channel_id=1, source_target_pairs={{0,2},{1,3},{2,0},{3,1},{4,6},{5,7},{6,4},{7,5},{8,10},{9,11},{10,... | collective-permute-start | bytes 221192 | tf_op jit(solution)/shard_map/ppermute | solution.py:72
  9.8 12.9 %collective-permute-start.4 = (f32[72,576]{1,0:T(8,128)S(1)}, f32[72,576]{1,0:T(8,128)S(1)}, u32[]{:S(2)}, u32[]{:S(2)}) collective-permute-start(f32[72,576]{1,0:T(8,128)S(1)} %get-tuple-element.114), channel_id=1, source_target_pairs={{0,16},{4,20},{8,24},{12,28},{16,0},{20,4},{24,8},{28,12},{1,17},{... | collective-permute-start | bytes 497672 | tf_op jit(solution)/shard_map/ppermute | solution.py:72
  12.5 4.4 %collective-permute-start.2 = (f32[16,1152]{1,0:T(8,128)S(1)}, f32[16,1152]{1,0:T(8,128)S(1)}, u32[]{:S(2)}, u32[]{:S(2)}) collective-permute-start(f32[16,1152]{1,0:T(8,128)S(1)} %add.42), channel_id=1, source_target_pairs={{0,4},{4,0},{8,12},{12,8},{16,20},{20,16},{24,28},{28,24},{1,5},{5... | collective-permute-start | bytes 221192 | tf_op jit(solution)/shard_map/ppermute | solution.py:72
  16.9 5.8 %collective-permute-start.3 = (f32[16,1152]{1,0:T(8,128)S(1)}, f32[16,1152]{1,0:T(8,128)S(1)}, u32[]{:S(2)}, u32[]{:S(2)}) collective-permute-start(f32[16,1152]{1,0:T(8,128)S(1)} %add.43), channel_id=1, source_target_pairs={{0,8},{4,12},{8,0},{12,4},{16,24},{20,28},{24,16},{28,20},{1,9},{5... | collective-permute-start | bytes 221192 | tf_op jit(solution)/shard_map/ppermute | solution.py:72
  18.6 18.3 %collective-permute-start.8 = (f32[144,576]{1,0:T(8,128)S(1)}, f32[144,576]{1,0:T(8,128)S(1)}, u32[]{:S(2)}, u32[]{:S(2)}) collective-permute-start(f32[144,576]{1,0:T(8,128)S(1)} %get-tuple-element.127.refs_0_), channel_id=1, source_target_pairs={{0,4},{4,0},{8,12},{12,8},{16,20},{20,16},{24,28},{28,24},{1,5},{5... | collective-permute-start | bytes 995336 | tf_op jit(solution)/shard_map/ppermute | solution.py:72
  22.7 6.8 %collective-permute-start.5 = (f32[16,1152]{1,0:T(8,128)S(1)}, f32[16,1152]{1,0:T(8,128)S(1)}, u32[]{:S(2)}, u32[]{:S(2)}) collective-permute-start(f32[16,1152]{1,0:T(8,128)S(1)} %add.44), channel_id=1, source_target_pairs={{0,16},{4,20},{8,24},{12,28},{16,0},{20,4},{24,8},{28,12},{1,17},{... | collective-permute-start | bytes 221192 | tf_op jit(solution)/shard_map/ppermute | solution.py:72
  29.6 4.4 %collective-permute-start.6 = (f32[16,1152]{1,0:T(8,128)S(1)}, f32[16,1152]{1,0:T(8,128)S(1)}, u32[]{:S(2)}, u32[]{:S(2)}) collective-permute-start(f32[16,1152]{1,0:T(8,128)S(1)} %add.45.ours), channel_id=1, source_target_pairs={{0,2},{1,3},{2,0},{3,1},{4,6},{5,7},{6,4},{7,5},{8,10},{9,11},{10,... | collective-permute-start | bytes 221192 | tf_op jit(solution)/shard_map/ppermute | solution.py:72
  29.7 16.4 %collective-permute-start.11 = (f32[144,576]{1,0:T(8,128)S(1)}, f32[144,576]{1,0:T(8,128)S(1)}, u32[]{:S(2)}, u32[]{:S(2)}) collective-permute-start(f32[144,576]{1,0:T(8,128)S(1)} %get-tuple-element.127.refs_0_), channel_id=1, source_target_pairs={{0,8},{4,12},{8,0},{12,4},{16,24},{20,28},{24,16},{28,20},{1,9},{5... | collective-permute-start | bytes 995336 | tf_op jit(solution)/shard_map/ppermute | solution.py:72
  34.0 1.4 %collective-permute-start.7 = (f32[32,1152]{1,0:T(8,128)S(1)}, f32[32,1152]{1,0:T(8,128)S(1)}, u32[]{:S(2)}, u32[]{:S(2)}) collective-permute-start(f32[32,1152]{1,0:T(8,128)S(1)} %join.2.ours), channel_id=1, source_target_pairs={{0,1},{1,0},{2,3},{3,2},{4,5},{5,4},{6,7},{7,6},{8,9},{9,8},{10,11... | collective-permute-start | bytes 442376 | tf_op jit(solution)/shard_map/ppermute | solution.py:72
  36.9 4.6 %collective-permute-start.9 = (f32[32,576]{1,0:T(8,128)S(1)}, f32[32,576]{1,0:T(8,128)S(1)}, u32[]{:S(2)}, u32[]{:S(2)}) collective-permute-start(f32[32,576]{1,0:T(8,128)S(1)} %get-tuple-element.121), channel_id=1, source_target_pairs={{0,4},{4,0},{8,12},{12,8},{16,20},{20,16},{24,28},{28,24},{1,5},{5... | collective-permute-start | bytes 221192 | tf_op jit(solution)/shard_map/ppermute | solution.py:72
  41.5 4.5 %collective-permute-start.10 = (f32[32,576]{1,0:T(8,128)S(1)}, f32[32,576]{1,0:T(8,128)S(1)}, u32[]{:S(2)}, u32[]{:S(2)}) collective-permute-start(f32[32,576]{1,0:T(8,128)S(1)} %add.46), channel_id=1, source_target_pairs={{0,8},{4,12},{8,0},{12,4},{16,24},{20,28},{24,16},{28,20},{1,9},{5... | collective-permute-start | bytes 221192 | tf_op jit(solution)/shard_map/ppermute | solution.py:72
  46.0 3.4 %copy-start.4 = (f32[1,1,2304]{2,1,0:T(1,128)S(1)}, f32[1,1,2304]{2,1,0:T(1,128)}, u32[]{:S(2)}) copy-start(f32[1,1,2304]{2,1,0:T(1,128)} %param.23) | copy-start | bytes 27652
  46.0 3.4 %copy-start.5 = (f32[72]{0:T(128)S(1)}, f32[72]{0:T(128)}, u32[]{:S(2)}) copy-start(f32[72]{0:T(128)} %param.24) | copy-start | bytes 868
  46.1 3.4 %copy-start.6 = (f32[72]{0:T(128)S(1)}, f32[72]{0:T(128)}, u32[]{:S(2)}) copy-start(f32[72]{0:T(128)} %param.25) | copy-start | bytes 868
  46.1 5.9 %collective-permute-start.12 = (f32[32,576]{1,0:T(8,128)S(1)}, f32[32,576]{1,0:T(8,128)S(1)}, u32[]{:S(2)}, u32[]{:S(2)}) collective-permute-start(f32[32,576]{1,0:T(8,128)S(1)} %add.47), channel_id=1, source_target_pairs={{0,16},{4,20},{8,24},{12,28},{16,0},{20,4},{24,8},{28,12},{1,17},{... | collective-permute-start | bytes 221192 | tf_op jit(solution)/shard_map/ppermute | solution.py:72
  47.8 16.0 %collective-permute-start.16 = (f32[144,576]{1,0:T(8,128)S(1)}, f32[144,576]{1,0:T(8,128)S(1)}, u32[]{:S(2)}, u32[]{:S(2)}) collective-permute-start(f32[144,576]{1,0:T(8,128)S(1)} %collective-permute-done.11.refs_0_), channel_id=1, source_target_pairs={{0,4},{4,0},{8,12},{12,8},{16,20},{20,16},{24,28},{28,24},{1,5},{5... | collective-permute-start | bytes 995336 | tf_op jit(solution)/shard_map/ppermute | solution.py:72
  53.2 1.5 %collective-permute-start.13 = (f32[32,1280]{1,0:T(8,128)S(1)}, f32[32,1280]{1,0:T(8,128)S(1)}, u32[]{:S(2)}, u32[]{:S(2)}) collective-permute-start(f32[32,1280]{1,0:T(8,128)S(1)} %get-tuple-element.133), channel_id=1, source_target_pairs={{0,1},{1,0},{2,3},{3,2},{4,5},{5,4},{6,7},{7,6},{8,9},{9,8},{10,11... | collective-permute-start | bytes 491528 | tf_op jit(solution)/shard_map/ppermute | solution.py:72
  54.7 4.6 %collective-permute-start.14 = (f32[16,1280]{1,0:T(8,128)S(1)}, f32[16,1280]{1,0:T(8,128)S(1)}, u32[]{:S(2)}, u32[]{:S(2)}) collective-permute-start(f32[16,1280]{1,0:T(8,128)S(1)} %get-tuple-element.137), channel_id=1, source_target_pairs={{0,2},{1,3},{2,0},{3,1},{4,6},{5,7},{6,4},{7,5},{8,10},{9,11},{10,... | collective-permute-start | bytes 245768 | tf_op jit(solution)/shard_map/ppermute | solution.py:72
  55.2 11.9 %collective-permute-start.18 = (f32[80,576]{1,0:T(8,128)S(1)}, f32[80,576]{1,0:T(8,128)S(1)}, u32[]{:S(2)}, u32[]{:S(2)}) collective-permute-start(f32[80,576]{1,0:T(8,128)S(1)} %get-tuple-element.149), channel_id=1, source_target_pairs={{0,16},{4,20},{8,24},{12,28},{16,0},{20,4},{24,8},{28,12},{1,17},{... | collective-permute-start | bytes 552968 | tf_op jit(solution)/shard_map/ppermute | solution.py:72
  59.3 4.5 %collective-permute-start.15 = (f32[16,1280]{1,0:T(8,128)S(1)}, f32[16,1280]{1,0:T(8,128)S(1)}, u32[]{:S(2)}, u32[]{:S(2)}) collective-permute-start(f32[16,1280]{1,0:T(8,128)S(1)} %add.49), channel_id=1, source_target_pairs={{0,4},{4,0},{8,12},{12,8},{16,20},{20,16},{24,28},{28,24},{1,5},{5... | collective-permute-start | bytes 245768 | tf_op jit(solution)/shard_map/ppermute | solution.py:72
  63.8 4.9 %collective-permute-start.17 = (f32[16,1280]{1,0:T(8,128)S(1)}, f32[16,1280]{1,0:T(8,128)S(1)}, u32[]{:S(2)}, u32[]{:S(2)}) collective-permute-start(f32[16,1280]{1,0:T(8,128)S(1)} %add.50), channel_id=1, source_target_pairs={{0,8},{4,12},{8,0},{12,4},{16,24},{20,28},{24,16},{28,20},{1,9},{5... | collective-permute-start | bytes 245768 | tf_op jit(solution)/shard_map/ppermute | solution.py:72
  68.8 5.8 %collective-permute-start.19 = (f32[16,1280]{1,0:T(8,128)S(1)}, f32[16,1280]{1,0:T(8,128)S(1)}, u32[]{:S(2)}, u32[]{:S(2)}) collective-permute-start(f32[16,1280]{1,0:T(8,128)S(1)} %add.51), channel_id=1, source_target_pairs={{0,16},{4,20},{8,24},{12,28},{16,0},{20,4},{24,8},{28,12},{1,17},{... | collective-permute-start | bytes 245768 | tf_op jit(solution)/shard_map/ppermute | solution.py:72
  69.3 13.1 %collective-permute-start.22 = (f32[144,576]{1,0:T(8,128)S(1)}, f32[144,576]{1,0:T(8,128)S(1)}, u32[]{:S(2)}, u32[]{:S(2)}) collective-permute-start(f32[144,576]{1,0:T(8,128)S(1)} %pad_maximum_fusion.refs_0_), channel_id=1, source_target_pairs={{0,4},{4,0},{8,12},{12,8},{16,20},{20,16},{24,28},{28,24},{1,5},{5... | collective-permute-start | bytes 995336 | tf_op jit(solution)/shard_map/ppermute | solution.py:72
  74.6 12.4 %collective-permute-start.24 = (f32[144,576]{1,0:T(8,128)S(1)}, f32[144,576]{1,0:T(8,128)S(1)}, u32[]{:S(2)}, u32[]{:S(2)}) collective-permute-start(f32[144,576]{1,0:T(8,128)S(1)} %pad_maximum_fusion.refs_0_), channel_id=1, source_target_pairs={{0,8},{4,12},{8,0},{12,4},{16,24},{20,28},{24,16},{28,20},{1,9},{5... | collective-permute-start | bytes 995336 | tf_op jit(solution)/shard_map/ppermute | solution.py:72
  74.7 4.8 %collective-permute-start.20 = (f32[16,1280]{1,0:T(8,128)S(1)}, f32[16,1280]{1,0:T(8,128)S(1)}, u32[]{:S(2)}, u32[]{:S(2)}) collective-permute-start(f32[16,1280]{1,0:T(8,128)S(1)} %add.52.ours), channel_id=1, source_target_pairs={{0,2},{1,3},{2,0},{3,1},{4,6},{5,7},{6,4},{7,5},{8,10},{9,11},{10,... | collective-permute-start | bytes 245768 | tf_op jit(solution)/shard_map/ppermute | solution.py:72
  79.5 1.5 %collective-permute-start.21 = (f32[32,1280]{1,0:T(8,128)S(1)}, f32[32,1280]{1,0:T(8,128)S(1)}, u32[]{:S(2)}, u32[]{:S(2)}) collective-permute-start(f32[32,1280]{1,0:T(8,128)S(1)} %join.3.ours), channel_id=1, source_target_pairs={{0,1},{1,0},{2,3},{3,2},{4,5},{5,4},{6,7},{7,6},{8,9},{9,8},{10,11... | collective-permute-start | bytes 491528 | tf_op jit(solution)/shard_map/ppermute | solution.py:72
  82.5 4.6 %collective-permute-start.23 = (f32[32,576]{1,0:T(8,128)S(1)}, f32[32,576]{1,0:T(8,128)S(1)}, u32[]{:S(2)}, u32[]{:S(2)}) collective-permute-start(f32[32,576]{1,0:T(8,128)S(1)} %get-tuple-element.164), channel_id=1, source_target_pairs={{0,4},{4,0},{8,12},{12,8},{16,20},{20,16},{24,28},{28,24},{1,5},{5... | collective-permute-start | bytes 221192 | tf_op jit(solution)/shard_map/ppermute | solution.py:72
  87.2 11.5 %collective-permute-start.27 = (f32[144,576]{1,0:T(8,128)S(1)}, f32[144,576]{1,0:T(8,128)S(1)}, u32[]{:S(2)}, u32[]{:S(2)}) collective-permute-start(f32[144,576]{1,0:T(8,128)S(1)} %collective-permute-done.24.refs_1_), channel_id=1, source_target_pairs={{0,4},{4,0},{8,12},{12,8},{16,20},{20,16},{24,28},{28,24},{1,5},{5... | collective-permute-start | bytes 995336 | tf_op jit(solution)/shard_map/ppermute | solution.py:72
  88.8 4.4 %collective-permute-start.25 = (f32[32,576]{1,0:T(8,128)S(1)}, f32[32,576]{1,0:T(8,128)S(1)}, u32[]{:S(2)}, u32[]{:S(2)}) collective-permute-start(f32[32,576]{1,0:T(8,128)S(1)} %add.53), channel_id=1, source_target_pairs={{0,8},{4,12},{8,0},{12,4},{16,24},{20,28},{24,16},{28,20},{1,9},{5... | collective-permute-start | bytes 221192 | tf_op jit(solution)/shard_map/ppermute | solution.py:72
  93.2 5.4 %collective-permute-start.26 = (f32[32,576]{1,0:T(8,128)S(1)}, f32[32,576]{1,0:T(8,128)S(1)}, u32[]{:S(2)}, u32[]{:S(2)}) collective-permute-start(f32[32,576]{1,0:T(8,128)S(1)} %add.54), channel_id=1, source_target_pairs={{0,16},{4,20},{8,24},{12,28},{16,0},{20,4},{24,8},{28,12},{1,17},{... | collective-permute-start | bytes 221192 | tf_op jit(solution)/shard_map/ppermute | solution.py:72

commit v8 on v7

v8 whole, which is shorter than its diff:
```python
import functools

import jax
import jax.numpy as jnp
from jax import lax
from jax.experimental import pallas as pl
from jax.experimental.pallas import tpu as pltpu
from jax.sharding import PartitionSpec as P

ROUNDS = 2
GROUP = 8
LANES = 128

highest = lax.Precision.HIGHEST
decay_rate = 0.9
step_size = 0.1
f32 = jnp.float32
bf16 = jnp.bfloat16
NN = (((1,), (0,)), ((), ()))
NT = (((1,), (1,)), ((), ()))
TN = (((0,), (0,)), ((), ()))

IN_HBM = pl.BlockSpec(memory_space=pltpu.HBM)
IN_VMEM = pl.BlockSpec(memory_space=pltpu.VMEM)
IN_SMEM = pl.BlockSpec(memory_space=pltpu.SMEM)
SMALL = pltpu.CompilerParams(vmem_limit_bytes=6 * 2**20)
LARGE = pltpu.CompilerParams(vmem_limit_bytes=12 * 2**20)
QUICK = pl.CostEstimate(flops=1000, bytes_accessed=1000, transcendentals=0)
SLOW = pl.CostEstimate(flops=1000, bytes_accessed=6_000_000, transcendentals=0)


def hold(space, *arrays):
    return [pltpu.with_memory_space_constraint(array, space) for array in arrays]


def exact(left, right, dims):
    return lax.dot_general(left, right, dims, precision=highest, preferred_element_type=f32)


def three(x):
    high = x.astype(bf16)
    rest = x - high.astype(f32)
    middle = rest.astype(bf16)
    low = (rest - middle.astype(f32)).astype(bf16)
    return high, middle, low


def stacked(left, right, dims):
    rows = left.shape[0]
    left_high, left_middle, left_low = three(left)
    right_high, right_middle, right_low = three(right)
    lefts = jnp.concatenate([left_high, left_middle, left_low], axis=0)
    of_high = lax.dot_general(lefts, right_high, dims, preferred_element_type=f32)
    of_middle = lax.dot_general(lefts[: 2 * rows], right_middle, dims, preferred_element_type=f32)
    of_low = lax.dot_general(left_high, right_low, dims, preferred_element_type=f32)
    small = (of_high[2 * rows :] + of_middle[rows:]) + of_low
    return of_high[:rows] + ((of_high[rows : 2 * rows] + of_middle[:rows]) + small)


def halves(count):
    masks = []
    mask = 1
    while mask < count:
        masks.append(mask)
        mask *= 2
    return masks


def swap(block, axis, mask, count):
    pairs = [(i, i ^ mask) for i in range(count)]
    return lax.ppermute(block, axis, pairs)


def sum_over(block, count, gather, stage):
    for mask in halves(count):
        block = gather.before(block, stage, mask)
        block = gather.start_tasks(block, stage, mask)
        block = block + gather.end_tasks(swap(block, "rep", mask, count), stage, mask)
        block = gather.after(block, stage, mask)
    return gather.after(gather.before(block, stage, 0), stage, 0)


def sum_over_all(keep, give, shard, masks, n_rep, n_shard, gather, stage, along=None):
    keep = gather.after(keep, stage, "begin")
    partner = None
    for mask, after in zip(masks, masks[1:] + [None]):
        got = swap(give, "shard", mask, n_shard)
        if after is not None:
            keep, give = split(keep, got, shard, after)
            if along is not None and partner is None:
                give, along = lax.optimization_barrier((give, along))
                partner = swap(along, "shard", mask, n_shard)
            keep = gather.after(gather.before(keep, stage, "core"), stage, "core")
    part = sum_over(keep + got, n_rep, gather, stage)
    for mask in reversed(halves(n_shard)[1:]):
        part = gather.start_tasks(part, stage, "x")
        got = gather.end_tasks(swap(part, "shard", mask, n_shard), stage, "x")
        part = gather.before(join(part, got, shard, mask), stage, "joined")
    return part, partner


def is_high(place_ref, mask):
    return (place_ref[0] & mask) != 0


def split_kernel(mask, shard_ref, ours, got, keep, give):
    total = ours[...] + got[...]
    half = total.shape[0] // 2
    high = is_high(shard_ref, mask)
    keep[...] = jnp.where(high, total[half:], total[:half])
    give[...] = jnp.where(high, total[:half], total[half:])


def split(ours, got, shard, mask):
    half = pltpu.VMEM((ours.shape[0] // 2, ours.shape[1]), f32)
    return pl.pallas_call(
        functools.partial(split_kernel, mask),
        in_specs=[IN_SMEM, IN_VMEM, IN_VMEM],
        out_specs=[IN_VMEM] * 2,
        out_shape=[half, half],
        compiler_params=SMALL,
        cost_estimate=QUICK,
        name="split",
    )(shard, ours, got)


def joined(shard_ref, mask, ours, got):
    high = is_high(shard_ref, mask)
    return jnp.concatenate([jnp.where(high, got, ours), jnp.where(high, ours, got)], axis=0)


def join_kernel(mask, shard_ref, ours, got, whole):
    whole[...] = joined(shard_ref, mask, ours[...], got[...])


def join(ours, got, shard, mask):
    return pl.pallas_call(
        functools.partial(join_kernel, mask),
        in_specs=[IN_SMEM, IN_VMEM, IN_VMEM],
        out_specs=IN_VMEM,
        out_shape=pltpu.VMEM((2 * ours.shape[0], ours.shape[1]), f32),
        compiler_params=SMALL,
        cost_estimate=QUICK,
        name="join",
    )(shard, ours, got)


class Gather:
    PLAN = (
        ("near", "own", 2, None, (0, 4)),
        ("turned", "own", 1, (0, 1), (1, 4)),
        ("far_a", "own_a", 4, (0, 4), (1, 4)),
        ("turned_near", "near", 1, (1, 1), (2, 4)),
        ("last_a", "far_a", 2, (1, 2), (2, 2)),
        ("turned_far_a", "far_a", 1, (1, 2), (2, 2)),
        ("far_b", "own_b", 4, (2, "begin"), (2, 4)),
        ("turned_last_a", "last_a", 1, (2, 1), (2, "joined")),
        ("last_b", "far_b", 2, (2, 2), (3, 2)),
        ("turned_far_b", "far_b", 1, (2, 2), (3, 2)),
        ("turned_last_b", "last_b", 1, (3, 1), (3, 0)),
    )
    INSERTS = {
        (1, 1): ("own",),
        (1, 4): ("near",),
        (2, 1): ("turned",),
        (2, 2): ("far_a", "last_a"),
        (2, 4): ("turned_near",),
        (2, "x"): ("turned_far_a",),
        (3, 1): ("far_b",),
        (3, 4): ("turned_far_b", "last_b", "turned_last_a"),
    }
    PLACES = {"own": 0, "turned": 1, "near": 2, "far": 4, "last": 6, "turned_near": 3, "turned_far": 5, "turned_last": 7}

    def place_of(self, name):
        whole = name.removesuffix("_a").removesuffix("_b")
        skipped = self.blocks["own"].shape[0] - self.blocks[name].shape[0]
        return self.PLACES[whole], skipped if name.endswith("_b") else 0

    def __init__(self, own, own_a, own_b, place, count):
        self.count = count
        self.place = place
        self.blocks = {"own": own, "own_a": own_a, "own_b": own_b}
        self.paired = count == 8 and own.shape[0] % 16 == 0
        self.rows = None
        self.tasks = {}
        self.results = {}
        self.send(None)

    def send(self, point):
        if self.paired:
            for name, source, mask, after, _ in self.PLAN:
                if after == point:
                    self.blocks[name] = swap(self.blocks[source], "rep", mask, self.count)

    def start_tasks(self, value, stage, mask):
        point = (stage, mask)
        if point in self.tasks:
            task, *inputs = self.tasks[point]
            value, *inputs = lax.optimization_barrier((value, *inputs))
            self.results[point] = task(*inputs)
        if self.paired and point in self.INSERTS:
            value, *blocks = lax.optimization_barrier((value, *(self.blocks[name] for name in self.INSERTS[point])))
            self.insert(blocks, self.INSERTS[point])
        if self.paired:
            for name, source, _, after, _ in self.PLAN:
                if after == ("beside",) + point:
                    if point in self.INSERTS:
                        self.rows, self.blocks[source] = lax.optimization_barrier((self.rows, self.blocks[source]))
                    else:
                        self.results[point], self.blocks[source] = lax.optimization_barrier((self.results[point], self.blocks[source]))
            self.send(("beside",) + point)
        return value

    def end_tasks(self, value, stage, mask):
        point = (stage, mask)
        if point in self.tasks:
            value, self.results[point] = lax.optimization_barrier((value, self.results[point]))
        if self.paired and point in self.INSERTS:
            value, self.rows = lax.optimization_barrier((value, self.rows))
        return value

    def insert(self, blocks, names):
        self.rows = insert(self.place, self.rows, blocks, [self.place_of(name) for name in names], self.blocks["own"].shape[0], self.count)

    def before(self, value, stage, mask):
        if self.paired:
            for name, _, _, _, by in self.PLAN:
                if by == (stage, mask):
                    value, self.blocks[name] = lax.optimization_barrier((value, self.blocks[name]))
        return value

    def after(self, value, stage, mask):
        if self.paired:
            for name, source, _, after, _ in self.PLAN:
                if after == (stage, mask) and source in self.blocks:
                    value, self.blocks[source] = lax.optimization_barrier((value, self.blocks[source]))
            self.send((stage, mask))
        return value


def insert_kernel(masks, rows_each, place_ref, *refs):
    blocks, rows, out = refs[: len(masks)], refs[len(masks) : -1], refs[-1]
    if not rows:
        out[...] = jnp.zeros_like(out)
    height = out.shape[0]
    window = 2 * LANES
    lane = lax.broadcasted_iota(jnp.int32, (height, window), 1)
    for block, (mask, skipped) in zip(blocks, masks):
        count = block.shape[0]
        index = place_ref[0] ^ mask
        shift = index * (rows_each - LANES) + skipped
        turned = jnp.concatenate([block[...].T, jnp.zeros((height, window - count), f32)], axis=1)
        turned = pltpu.roll(turned, shift, 1)
        at = pl.ds(pl.multiple_of(index * LANES, LANES), window)
        out[:, at] = jnp.where((lane >= shift) & (lane < shift + count), turned, out[:, at])


def insert(place, rows, blocks, masks, rows_each, count):
    height, width = blocks[0].shape[1], rows_each * count
    old = [] if rows is None else hold(pltpu.VMEM, rows)
    return pl.pallas_call(
        functools.partial(insert_kernel, masks, rows_each),
        in_specs=[IN_SMEM] + [IN_VMEM] * (len(blocks) + len(old)),
        out_specs=IN_VMEM,
        out_shape=pltpu.VMEM((height, width), f32),
        input_output_aliases={1 + len(blocks): 0} if old else {},
        compiler_params=SMALL,
        cost_estimate=SLOW,
        name="insert",
    )(place, *blocks, *old)


def base_kernel(weight_q, moment_q, weight_o, moment_o, own, *parts):
    drop = step_size * decay_rate
    base = jnp.concatenate([weight_q[...] - drop * moment_q[...], weight_o[...] - drop * moment_o[...]], axis=1)
    own[...] = base
    rows = base.shape[0]
    first_part, second_part = parts
    first_part[...] = base[: first_part.shape[0]]
    second_part[...] = base[rows - second_part.shape[0] :]


def base_of(weight_q, moment_q, weight_o, moment_o):
    rows, width = weight_q.shape[0], 2 * weight_q.shape[1]
    half = rows // 2
    shapes = [(rows, width), (half, width), (rows - half, width)]
    return pl.pallas_call(
        base_kernel,
        in_specs=[IN_VMEM] * 4,
        out_specs=[IN_VMEM] * 3,
        out_shape=[pltpu.VMEM(shape, f32) for shape in shapes],
        compiler_params=SMALL,
        cost_estimate=QUICK,
        name="base",
    )(weight_q, moment_q, weight_o, moment_o)


def window_of(n_shard, share, place_ref, shard_ref, lines):
    start = (place_ref[0] * n_shard + shard_ref[0]) * share
    row = lax.broadcasted_iota(jnp.int32, (lines, LANES), 0)
    lane = lax.broadcasted_iota(jnp.int32, (lines, LANES), 1)
    flat = row * LANES + lane
    return lax.rem(start, LANES), (flat >= start) & (flat < start + share)


def norm_terms(n_shard, rows, place_ref, shard_ref, grads, moment, weight):
    lines, share = grads.shape[1] // LANES, moment.shape[1]
    shift, inside = window_of(n_shard, share, place_ref, shard_ref, lines)
    kept = weight[...] - step_size * decay_rate * moment[...]
    kept = jnp.concatenate([kept, jnp.zeros((1, LANES - share), f32)], axis=1)
    kept = pltpu.roll(jnp.broadcast_to(kept, (8, LANES)), shift, 1)[:1]
    square = jnp.concatenate([grads[:, line * LANES : (line + 1) * LANES] for line in range(lines)], axis=0)
    rest = jnp.zeros((rows - lines, LANES), f32)
    shares = jnp.where(inside, kept, 0.0) - step_size * square
    return jnp.concatenate([square, rest], axis=0), jnp.concatenate([shares, rest], axis=0)


def norm_out_kernel(n_shard, place_ref, shard_ref, ours, got, moment, new_moment, new_weight):
    lines, share = new_weight.shape[0], moment.shape[1]
    high = is_high(shard_ref, 1)
    sums = jnp.where(high, got[:lines, :], ours[:lines, :])
    shift, inside = window_of(n_shard, share, place_ref, shard_ref, lines)
    total = jnp.sum(jnp.where(inside, sums, 0.0), axis=0, keepdims=True)
    total = pltpu.roll(jnp.broadcast_to(total, (8, LANES)), LANES - shift, 1)[:1, :share]
    new_moment[...] = decay_rate * moment[...] + total
    new_weight[...] = jnp.where(high, ours[:lines, :], got[:lines, :])


def norm_out(ours, got, moment, place, shard, lines, n_shard):
    return pl.pallas_call(
        functools.partial(norm_out_kernel, n_shard),
        in_specs=[IN_SMEM] * 2 + [IN_VMEM] * 3,
        out_specs=[IN_VMEM] * 2,
        out_shape=[jax.ShapeDtypeStruct(moment.shape, f32), jax.ShapeDtypeStruct((lines, LANES), f32)],
        compiler_params=SMALL,
        cost_estimate=QUICK,
        name="norm_out",
    )(place, shard, ours, got, moment)


def first_kernel(chunks, n_shard, place_ref, shard_ref, *refs):
    sources, norms, (corr, give_corr, keep, give) = refs[:6], refs[6:9], refs[9:13]
    buffer, bases, norm_buffers, sems, small_sems = refs[13], refs[14], refs[15:18], refs[18], refs[19]
    rank, size = bases.shape[1], corr.shape[2]
    high = is_high(shard_ref, 1)
    lanes = size // chunks
    small = zip(sources[4:] + norms, [bases.at[0], bases.at[1], *norm_buffers])
    small_copies = [pltpu.make_async_copy(source, target, small_sems.at[k]) for k, (source, target) in enumerate(small)]
    copies = {}
    for copy in small_copies:
        copy.start()
    for c in range(chunks):
        at = pl.ds(c * lanes, lanes)
        for j, source in enumerate(sources[:4]):
            copies[c, j] = pltpu.make_async_copy(source.at[:, at], buffer.at[j, :, at], sems.at[c, j])
            copies[c, j].start()
    for copy in small_copies:
        copy.wait()
    sums, shares = norm_terms(n_shard, rank, place_ref, shard_ref, *norm_buffers)
    keep[:, size:] = jnp.where(high, shares, sums)
    give[:, size:] = jnp.where(high, sums, shares)
    for c in range(chunks):
        at = pl.ds(c * lanes, lanes)
        totals, parts = [], []
        for p in range(2):
            copies[c, p].wait()
            copies[c, 2 + p].wait()
            totals.append(buffer[p, :, at] + buffer[2 + p, :, at])
            corr[p, :, at] = totals[p]
            parts.append(stacked(bases[p], totals[p], NN))
        give_corr[:, at] = jnp.where(high, totals[0], totals[1])
        keep[:, at] = jnp.where(high, parts[1], parts[0])
        give[:, at] = jnp.where(high, parts[0], parts[1])


def first(grads, errors, bases, norms, place, shard, n_shard):
    width, size = grads[0].shape
    rank = bases[0].shape[0]
    chunks = 3 if size % (3 * LANES) == 0 else 1
    part = pltpu.VMEM((rank, size + LANES), f32)
    return pl.pallas_call(
        functools.partial(first_kernel, chunks, n_shard),
        in_specs=[IN_SMEM] * 2 + [IN_HBM] * 9,
        out_specs=[IN_VMEM] * 4,
        out_shape=[pltpu.VMEM((2, width, size), f32), pltpu.VMEM((width, size), f32), part, part],
        scratch_shapes=[
            pltpu.VMEM((4, width, size), f32),
            pltpu.VMEM((2, rank, width), f32),
            *(pltpu.VMEM(array.shape, f32) for array in norms),
            pltpu.SemaphoreType.DMA((chunks, 4)),
            pltpu.SemaphoreType.DMA((5,)),
        ],
        compiler_params=LARGE,
        name="first",
    )(place, shard, *hold(pltpu.HBM, *grads, *errors, *bases, *norms))


def both_shares(shard_ref, corr, other):
    return jnp.concatenate([corr[shard_ref[0] & 1], other[...]], axis=0)


def right_kernel(shard_ref, whole, corr, other, right, left, *extra):
    size = corr.shape[2]
    left[...] = whole[:, :size]
    if extra:
        extra[0][...] = whole[:, size:]
    right[...] = stacked(whole[:, :size], both_shares(shard_ref, corr, other), NT)


def right_of(whole, shard, corr, other):
    rank = whole.shape[0]
    width, size = other.shape
    beside = whole.shape[1] - size
    shapes = [(rank, 2 * width), (rank, size)] + ([(rank, beside)] if beside else [])
    return pl.pallas_call(
        right_kernel,
        in_specs=[IN_SMEM] + [IN_VMEM] * 3,
        out_specs=[IN_VMEM] * len(shapes),
        out_shape=[pltpu.VMEM(shape, f32) for shape in shapes],
        compiler_params=SMALL,
        cost_estimate=QUICK,
        name="right",
    )(shard, whole, *hold(pltpu.VMEM, corr, other))


def left_kernel(mask, shard_ref, right, inverse, corr, other, keep, give):
    basis = exact(inverse[0], right[...], NN)
    part = stacked(basis, both_shares(shard_ref, corr, other), NN)
    half = part.shape[0] // 2
    high = is_high(shard_ref, mask)
    keep[...] = jnp.where(high, part[half:], part[:half])
    give[...] = jnp.where(high, part[:half], part[half:])


def left_of(right, inverse, shard, mask, corr, other):
    half = pltpu.VMEM((right.shape[0] // 2, other.shape[1]), f32)
    return pl.pallas_call(
        functools.partial(left_kernel, mask),
        in_specs=[IN_SMEM] + [IN_VMEM] * 4,
        out_specs=[IN_VMEM] * 2,
        out_shape=[half, half],
        compiler_params=SMALL,
        cost_estimate=QUICK,
        name="left",
    )(shard, right, inverse, *hold(pltpu.VMEM, corr, other))


def eliminate(gram_q, gram_o, rank):
    width = 4 * rank
    lane = lax.broadcasted_iota(jnp.int32, (rank, width), 1)
    row = lax.broadcasted_iota(jnp.int32, (rank, width), 0)
    square = (rank, rank)
    eye = (lax.broadcasted_iota(jnp.int32, square, 0) == lax.broadcasted_iota(jnp.int32, square, 1)).astype(f32)
    work = jnp.concatenate([gram_q, eye, gram_o, eye], axis=1)
    first_half = lane < 2 * rank
    scale = jnp.ones((rank, width), f32)
    for base in range(0, rank, GROUP):
        columns = []
        for k in range(base, base + GROUP):
            of_q = jnp.broadcast_to(work[:, k : k + 1], (rank, width))
            of_o = jnp.broadcast_to(work[:, 2 * rank + k : 2 * rank + k + 1], (rank, width))
            columns.append(jnp.where(first_half, of_q, of_o))
        for j in range(GROUP):
            k = base + j
            pivot = columns[j][k : k + 1]
            factor = jnp.where(row > k, columns[j] * (1.0 / pivot), 0.0)
            scale = jnp.where(row == k, pivot, scale)
            for i in range(j + 1, GROUP):
                columns[i] = columns[i] - factor * columns[i][k : k + 1]
            work = work - factor * work[k : k + 1]
    work = work * lax.rsqrt(scale)
    return work[:, rank : 2 * rank], work[:, 3 * rank :]


def inverse_kernel(ours, theirs, out):
    rank = out.shape[1]
    out[0], out[1] = eliminate(exact(ours[...], ours[...], NT), exact(theirs[...], theirs[...], NT), rank)


def inverse_of(ours, theirs):
    rank = ours.shape[0]
    return pl.pallas_call(
        inverse_kernel,
        out_shape=pltpu.VMEM((2, rank, rank), f32),
        compiler_params=SMALL,
        cost_estimate=SLOW,
        name="inverse",
    )(ours, theirs)


def stack_kernel(place_ref, ours, theirs, stack, own):
    count = own.shape[2]
    index = place_ref[0]
    for p, left in enumerate((ours, theirs)):
        high, middle, low = three(left[...])
        stack[p] = jnp.concatenate([high, middle, low, high, middle, high], axis=0)
        window = left[:, pl.ds(pl.multiple_of(index * LANES, LANES), 2 * LANES)]
        own[p] = pltpu.roll(window, 2 * LANES - index * (count - LANES), 1)[:, :count]


def stack_of(ours, theirs, place, count):
    rank, size = ours.shape
    return pl.pallas_call(
        stack_kernel,
        in_specs=[IN_SMEM, IN_VMEM, IN_VMEM],
        out_specs=[IN_VMEM] * 2,
        out_shape=[pltpu.VMEM((2, 6 * rank, size), bf16), pltpu.VMEM((2, rank, count), f32)],
        compiler_params=SMALL,
        cost_estimate=SLOW,
        name="stack",
    )(place, ours, theirs)


def finish_kernel(chunks, shard_ref, corr, rows, stack, inverse, right, their_right, own, moment_q, moment_o, *refs):
    outs, (buffer, new_moments, sems) = refs[:6], refs[6:]
    width = moment_q.shape[1]
    height = width // chunks
    copies = []

    def send(index, source, to_q, to_o, sem):
        for p, target in enumerate((to_q, to_o)):

            @pl.when(index == p)
            def _(target=target):
                pltpu.make_async_copy(source, target, sem).start()

        copies.append(pltpu.make_async_copy(source, to_q, sem))

    for theirs, factor in enumerate((right, their_right)):
        index = (shard_ref[0] & 1) ^ theirs
        factor = factor[:, width * theirs : width * (theirs + 1)]
        scaled = exact(inverse[theirs], exact(inverse[theirs], factor, NN), TN)
        high, middle, low = three(scaled.T)
        lefts = jnp.concatenate([high, high, high, middle, middle, low], axis=1)
        for c in range(chunks):
            at = pl.ds(c * height, height)
            decoded = lax.dot_general(lefts[c * height : (c + 1) * height], stack[theirs], NN, preferred_element_type=f32)
            buffer[theirs, 0, at, :] = rows[pl.ds(pl.multiple_of(index * width + c * height, 8), height), :] - step_size * decoded
            buffer[theirs, 1, at, :] = corr[index, at, :] - decoded
            for k in range(2):
                send(index, buffer.at[theirs, k, at, :], outs[2 * k].at[at, :], outs[2 * k + 1].at[at, :], sems.at[theirs, k, c])
        moment = jnp.where(index == 0, moment_q[...], moment_o[...])
        new_moments[theirs] = decay_rate * moment + exact(own[theirs], scaled, TN)
        send(index, new_moments.at[theirs], outs[4], outs[5], sems.at[theirs, 2, 0])
    for copy in copies:
        copy.wait()


def finish(shard, corr, rows, stack, inverse, right, their_right, own, moment_q, moment_o):
    width, size = corr.shape[1:]
    chunks = 3
    return pl.pallas_call(
        functools.partial(finish_kernel, chunks),
        in_specs=[IN_SMEM] + [IN_VMEM] * 9,
        out_specs=[IN_HBM] * 6,
        out_shape=[pltpu.HBM((width, size), f32)] * 4 + [pltpu.HBM(moment_q.shape, f32)] * 2,
        scratch_shapes=[
            pltpu.VMEM((2, 2, width, size), f32),
            pltpu.VMEM((2,) + moment_q.shape, f32),
            pltpu.SemaphoreType.DMA((2, 3, chunks)),
        ],
        compiler_params=LARGE,
        name="finish",
    )(shard, *hold(pltpu.VMEM, corr, rows), stack, inverse, right, their_right, own, moment_q, moment_o)


def finish_plain(high, corr, base, lefts, inverse, rights, moments):
    rows, width = moments[0].shape
    start = lax.axis_index("rep") * rows
    bases = lax.all_gather(base, "rep", axis=0, tiled=True)
    decodeds = []
    for p in range(2):
        factor = rights[p][:, p * width : (p + 1) * width]
        scaled = exact(inverse[p], exact(inverse[p], factor, NN), TN)
        decodeds.append(exact(scaled, lefts[p], TN))
    ours, theirs = decodeds
    weights, new_moments, errors = [], [], []
    for p, decoded in enumerate((jnp.where(high, theirs, ours), jnp.where(high, ours, theirs))):
        weights.append(bases[:, p * width : (p + 1) * width].T - step_size * decoded)
        new_moments.append(decay_rate * moments[p] + lax.dynamic_slice_in_dim(decoded, start, rows, 1).T)
        errors.append(corr[p] - decoded)
    return weights + errors + new_moments


def per_device(n_rep, n_shard, q_grad, o_grad, q_error, o_error, q_basis, o_basis, q_moment, o_moment, q_weight, o_weight, norm_grads, norm_moment, norm_weight):
    rank = q_basis.shape[1]
    size = q_grad.shape[1]
    flat = norm_grads.shape[-1]
    row_count = q_moment.shape[0]
    place = lax.axis_index("rep").astype(jnp.int32).reshape(1)
    shard = lax.axis_index("shard").astype(jnp.int32).reshape(1)

    gather = Gather(*base_of(q_weight, q_moment, o_weight, o_moment), place, n_rep)
    norm_moment, norm_weight = norm_moment.reshape(1, -1), norm_weight.reshape(1, -1)
    norms = (norm_grads[0], norm_moment, norm_weight)
    corr, give_corr, keep, give = first((q_grad[0].T, o_grad[0].T), (q_error[0].T, o_error[0].T), (q_basis.T, o_basis.T), norms, place, shard, n_shard)
    masks = halves(n_shard)
    for sweep in range(ROUNDS):
        last = sweep == ROUNDS - 1
        if sweep == 0:
            whole, other_corr = sum_over_all(keep, give, shard, masks, n_rep, n_shard, gather, 0, give_corr)
        else:
            whole, _ = sum_over_all(keep, give, shard, masks[1:], n_rep, n_shard, gather, 2 * sweep)
        right, left, *beside = right_of(whole, shard, corr, other_corr)
        if sweep == 0:
            norm_got = swap(beside[0], "shard", masks[0], n_shard)
            gather.tasks[2, 1] = (functools.partial(norm_out, lines=flat // LANES, n_shard=n_shard), beside[0], norm_got, norm_moment, place, shard)
        theirs = swap(left, "shard", masks[0], n_shard) if last else left
        gather.tasks[2 * sweep + 1, 4 if last else 2] = (inverse_of, left, theirs)
        if last and gather.paired:
            gather.tasks[3, 2] = (functools.partial(stack_of, count=row_count), left, theirs, place)
        right = sum_over(right, n_rep, gather, 2 * sweep + 1)
        inverse = gather.results[2 * sweep + 1, 4 if last else 2]
        if not last:
            keep, give = left_of(right, inverse, shard, masks[1], corr, other_corr)
    their_right = swap(right, "shard", masks[0], n_shard)
    norm_moment_new, norm_weight_new = gather.results[2, 1]
    if gather.paired:
        stack, own = gather.results[3, 2]
        gather.insert([gather.blocks["turned_last_b"]], ["turned_last_b"])
        outs = finish(shard, corr, gather.rows, stack, inverse, right, their_right, own, q_moment, o_moment)
    else:
        outs = finish_plain((shard[0] & 1) != 0, corr, gather.blocks["own"], (left, theirs), inverse, (right, their_right), (q_moment, o_moment))
    weight_q, weight_o, error_q, error_o, q_moment_new, o_moment_new = outs
    return (
        weight_q.T,
        weight_o.T,
        q_moment_new,
        o_moment_new,
        error_q.T[None],
        error_o.T[None],
        norm_weight_new.reshape(flat),
        norm_moment_new.reshape(-1),
    )


def solution(mesh):
    n_rep, n_shard = mesh.shape["rep"], mesh.shape["shard"]

    def whole(*arrays):
        return per_device(n_rep, n_shard, *arrays)

    return jax.shard_map(
        whole,
        mesh=mesh,
        in_specs=(
            P("rep", None, "shard"),
            P("rep", None, "shard"),
            P("rep", None, "shard"),
            P("rep", None, "shard"),
            P("shard", None),
            P("shard", None),
            P("rep", "shard"),
            P("rep", "shard"),
            P("rep", "shard"),
            P("rep", "shard"),
            P("rep", "shard", None),
            P(("rep", "shard")),
            P(("rep", "shard")),
        ),
        out_specs=(
            P(None, "shard"),
            P(None, "shard"),
            P("rep", "shard"),
            P("rep", "shard"),
            P("rep", None, "shard"),
            P("rep", None, "shard"),
            P(),
            P(("rep", "shard")),
        ),
        check_vma=False,
    )
```

time: 103 us -> 103 us (level)
  waiting for transfers between devices: 50.5 us -> 44.7 us
  starting transfers between devices: 31.8 us -> 37.4 us
    ppermute x28 -> x32, waiting for transfers between devices: 50.5 us -> 44.7 us  [swap(): return lax.ppermute(block, axis, pairs)]
    ppermute x28 -> x32, starting transfers between devices: 31.8 us -> 37.4 us  [swap(): return lax.ppermute(block, axis, pairs)]
    pallas_call x14 -> x15, Pallas kernels: 15.8 us -> 16.2 us  [the longest x1 4.61 us: first(): pl.pallas_call(functools.partial(first_kernel, chunks, n_shard), in_specs...]
  transfers between devices with their start and end apart: 28 -> 32, of which waited for: 20 -> 18; matrix products, arithmetic and copies ran while one was open for 0% -> 0% of each run, Pallas kernels for 10% -> 11%
where the time goes in v8:
time: 103 us
  waiting for transfers between devices  44.7 us (43%)
  starting transfers between devices  37.4 us (36%)
  Pallas kernels  19.6 us (19%)
    ppermute x32, waiting for transfers between devices, swap(): return lax.ppermute(block, axis, pairs)  44.7 us
    ppermute x32, starting transfers between devices, swap(): return lax.ppermute(block, axis, pairs)  37.4 us
    pallas_call x1, Pallas kernels, first(): pl.pallas_call(functools.partial(first_kernel, chunks, n_shard), in_specs...  4.61 us
    pallas_call x9, Pallas kernels, insert(): pl.pallas_call(functools.partial(insert_kernel, masks, rows_each), in_spe...  4.18 us
    pallas_call x1, Pallas kernels, finish(): pl.pallas_call(functools.partial(finish_kernel, chunks), in_specs=[IN_SME...  3.45 us
    pallas_call x2, Pallas kernels, right_of(): pl.pallas_call(right_kernel, in_specs=[IN_SMEM] + [IN_VMEM] * 3, out_spec...  2.62 us
    pallas_call x2, Pallas kernels, inverse_of(): pl.pallas_call(inverse_kernel, out_shape=pltpu.VMEM((2, rank, rank), f32)...  2.6 us
  transfers between devices with their start and end apart: 32, of which 18 were waited for; matrix products, arithmetic and copies ran while one was open for 0% of the time, Pallas kernels for 11%

profile of v8, /device:TPU:0, one launch (start us, length us, event | category | flops | bytes accessed | tf_op | source)
XLA Modules:
  0.0 102.9 jit_solution(11572343379117436722)
XLA Ops:
  0.7 4.6 %first.1 = (f32[2,288,1152]{2,1,0:T(8,128)S(1)}, f32[288,1152]{1,0:T(8,128)S(1)}, f32[32,1280]{1,0:T(8,128)S(1)}, f32[32,1280]{1,0:T(8,128)S(1)}) custom-call(s32[1]{0:T(128)} %bitcast.1.place_ref, s32[1]{0:T(128)} %bitcast.shard_ref, f32[288,1152]{1,0:T(8,128)} %bitcast.31, f32[288,1152]{1,0:T(8,128)} %bitcast.32, f32[288,1152]{1,0:T(8,128)} %bitcast.33, ...), custom_call_target="tpu_custom_call" | custom-call | tf_op jit(solution)/shard_map/first/pallas_call | solution.py:381
  5.8 1.0 collective-permute-done.got
  7.5 2.8 %collective-permute-start.4 = (f32[144,576]{1,0:T(8,128)S(1)}, f32[144,576]{1,0:T(8,128)S(1)}, u32[]{:S(2)}, u32[]{:S(2)}) collective-permute-start(f32[144,576]{1,0:T(8,128)S(1)} %get-tuple-element.149.refs_0_), channel_id=1, source_target_pairs={{0,8},{4,12},{8,0},{12,4},{16,24},{20,28},{24,16},{28,20},{1,9},{5... | collective-permute-start | bytes 995336 | tf_op jit(solution)/shard_map/ppermute | solution.py:71
  10.3 1.5 %collective-permute-start.1 = (f32[16,1280]{1,0:T(8,128)S(1)}, f32[16,1280]{1,0:T(8,128)S(1)}, u32[]{:S(2)}, u32[]{:S(2)}) collective-permute-start(f32[16,1280]{1,0:T(8,128)S(1)} %get-tuple-element.139), channel_id=1, source_target_pairs={{0,2},{1,3},{2,0},{3,1},{4,6},{5,7},{6,4},{7,5},{8,10},{9,11},{10,... | collective-permute-start | bytes 245768 | tf_op jit(solution)/shard_map/ppermute | solution.py:71
  11.7 3.0 %collective-permute-done.1 = f32[16,1280]{1,0:T(8,128)S(1)} collective-permute-done((f32[16,1280]{1,0:T(8,128)S(1)}, f32[16,1280]{1,0:T(8,128)S(1)}, u32[]{:S(2)}, u32[]{:S(2)}) %collective-permute-start.1) | collective-permute-done | bytes 81952 | tf_op jit(solution)/shard_map/ppermute | solution.py:71
  14.7 1.6 %collective-permute-start.2 = (f32[16,1280]{1,0:T(8,128)S(1)}, f32[16,1280]{1,0:T(8,128)S(1)}, u32[]{:S(2)}, u32[]{:S(2)}) collective-permute-start(f32[16,1280]{1,0:T(8,128)S(1)} %add.42), channel_id=1, source_target_pairs={{0,4},{4,0},{8,12},{12,8},{16,20},{20,16},{24,28},{28,24},{1,5},{5... | collective-permute-start | bytes 245768 | tf_op jit(solution)/shard_map/ppermute | solution.py:71
  16.3 2.9 %collective-permute-done.2 = f32[16,1280]{1,0:T(8,128)S(1)} collective-permute-done((f32[16,1280]{1,0:T(8,128)S(1)}, f32[16,1280]{1,0:T(8,128)S(1)}, u32[]{:S(2)}, u32[]{:S(2)}) %collective-permute-start.2) | collective-permute-done | bytes 81952 | tf_op jit(solution)/shard_map/ppermute | solution.py:71
  19.6 1.6 %collective-permute-start.11 = (f32[144,576]{1,0:T(8,128)S(1)}, f32[144,576]{1,0:T(8,128)S(1)}, u32[]{:S(2)}, u32[]{:S(2)}) collective-permute-start(f32[144,576]{1,0:T(8,128)S(1)} %get-tuple-element.149.refs_0_), channel_id=1, source_target_pairs={{0,4},{4,0},{8,12},{12,8},{16,20},{20,16},{24,28},{28,24},{1,5},{5... | collective-permute-start | bytes 995336 | tf_op jit(solution)/shard_map/ppermute | solution.py:71
  21.3 2.5 %collective-permute-done.3 = f32[16,1280]{1,0:T(8,128)S(1)} collective-permute-done((f32[16,1280]{1,0:T(8,128)S(1)}, f32[16,1280]{1,0:T(8,128)S(1)}, u32[]{:S(2)}, u32[]{:S(2)}) %collective-permute-start.3) | collective-permute-done | bytes 81952 | tf_op jit(solution)/shard_map/ppermute | solution.py:71
  23.8 3.5 %collective-permute-start.5 = (f32[16,1280]{1,0:T(8,128)S(1)}, f32[16,1280]{1,0:T(8,128)S(1)}, u32[]{:S(2)}, u32[]{:S(2)}) collective-permute-start(f32[16,1280]{1,0:T(8,128)S(1)} %add.44), channel_id=1, source_target_pairs={{0,16},{4,20},{8,24},{12,28},{16,0},{20,4},{24,8},{28,12},{1,17},{... | collective-permute-start | bytes 245768 | tf_op jit(solution)/shard_map/ppermute | solution.py:71
  27.2 2.6 %collective-permute-done.5 = f32[16,1280]{1,0:T(8,128)S(1)} collective-permute-done((f32[16,1280]{1,0:T(8,128)S(1)}, f32[16,1280]{1,0:T(8,128)S(1)}, u32[]{:S(2)}, u32[]{:S(2)}) %collective-permute-start.5) | collective-permute-done | bytes 81952 | tf_op jit(solution)/shard_map/ppermute | solution.py:71
  29.8 1.9 %collective-permute-start.6 = (f32[16,1280]{1,0:T(8,128)S(1)}, f32[16,1280]{1,0:T(8,128)S(1)}, u32[]{:S(2)}, u32[]{:S(2)}) collective-permute-start(f32[16,1280]{1,0:T(8,128)S(1)} %add.45.ours), channel_id=1, source_target_pairs={{0,2},{1,3},{2,0},{3,1},{4,6},{5,7},{6,4},{7,5},{8,10},{9,11},{10,... | collective-permute-start | bytes 245768 | tf_op jit(solution)/shard_map/ppermute | solution.py:71
  31.7 3.3 %collective-permute-start.10 = (f32[72,576]{1,0:T(8,128)S(1)}, f32[72,576]{1,0:T(8,128)S(1)}, u32[]{:S(2)}, u32[]{:S(2)}) collective-permute-start(f32[72,576]{1,0:T(8,128)S(1)} %get-tuple-element.158), channel_id=1, source_target_pairs={{0,16},{4,20},{8,24},{12,28},{16,0},{20,4},{24,8},{28,12},{1,17},{... | collective-permute-start | bytes 497672 | tf_op jit(solution)/shard_map/ppermute | solution.py:71
  35.1 1.3 %right.2 = (f32[32,576]{1,0:T(8,128)S(1)}, f32[32,1152]{1,0:T(8,128)S(1)}, f32[32,128]{1,0:T(8,128)S(1)}) custom-call(s32[1]{0:T(128)} %bitcast.shard_ref, f32[32,1280]{1,0:T(8,128)S(1)} %join.2.whole, f32[2,288,1152]{2,1,0:T(8,128)S(1)} %get-tuple-element.133.corr, f32[288,1152]{1,0:T(8,128)S(1)} %collective-permute-done.7.other), custom_call_target="tpu_custom_call" | custom-call | flops 1000 | bytes 1000 | tf_op jit(solution)/shard_map/right/pallas_call | solution.py:415
  36.4 1.6 %collective-permute-start.8 = (f32[32,576]{1,0:T(8,128)S(1)}, f32[32,576]{1,0:T(8,128)S(1)}, u32[]{:S(2)}, u32[]{:S(2)}) collective-permute-start(f32[32,576]{1,0:T(8,128)S(1)} %get-tuple-element.148), channel_id=1, source_target_pairs={{0,4},{4,0},{8,12},{12,8},{16,20},{20,16},{24,28},{28,24},{1,5},{5... | collective-permute-start | bytes 221192 | tf_op jit(solution)/shard_map/ppermute | solution.py:71
  38.5 3.3 %collective-permute-done.8 = f32[32,576]{1,0:T(8,128)S(1)} collective-permute-done((f32[32,576]{1,0:T(8,128)S(1)}, f32[32,576]{1,0:T(8,128)S(1)}, u32[]{:S(2)}, u32[]{:S(2)}) %collective-permute-start.8) | collective-permute-done | bytes 73760 | tf_op jit(solution)/shard_map/ppermute | solution.py:71
  41.9 1.6 %collective-permute-start.20 = (f32[144,576]{1,0:T(8,128)S(1)}, f32[144,576]{1,0:T(8,128)S(1)}, u32[]{:S(2)}, u32[]{:S(2)}) collective-permute-start(f32[144,576]{1,0:T(8,128)S(1)} %collective-permute-done.4.refs_0_), channel_id=1, source_target_pairs={{0,4},{4,0},{8,12},{12,8},{16,20},{20,16},{24,28},{28,24},{1,5},{5... | collective-permute-start | bytes 995336 | tf_op jit(solution)/shard_map/ppermute | solution.py:71
  43.5 1.3 %inverse.2 = f32[2,32,32]{2,1,0:T(8,128)S(1)} custom-call(f32[32,1152]{1,0:T(8,128)S(1)} %get-tuple-element.156.ours.theirs, f32[32,1152]{1,0:T(8,128)S(1)} %get-tuple-element.156.ours.theirs), custom_call_target="tpu_custom_call" | custom-call | flops 1000 | bytes 6000000 | tf_op jit(solution)/shard_map/inverse/pallas_call | solution.py:482
  44.8 1.5 %collective-permute-done.9 = f32[32,576]{1,0:T(8,128)S(1)} collective-permute-done((f32[32,576]{1,0:T(8,128)S(1)}, f32[32,576]{1,0:T(8,128)S(1)}, u32[]{:S(2)}, u32[]{:S(2)}) %collective-permute-start.9) | collective-permute-done | bytes 73760 | tf_op jit(solution)/shard_map/ppermute | solution.py:71
  46.4 2.5 %collective-permute-start.12 = (f32[32,576]{1,0:T(8,128)S(1)}, f32[32,576]{1,0:T(8,128)S(1)}, u32[]{:S(2)}, u32[]{:S(2)}) collective-permute-start(f32[32,576]{1,0:T(8,128)S(1)} %add.47), channel_id=1, source_target_pairs={{0,16},{4,20},{8,24},{12,28},{16,0},{20,4},{24,8},{28,12},{1,17},{... | collective-permute-start | bytes 221192 | tf_op jit(solution)/shard_map/ppermute | solution.py:71
  49.3 1.1 %collective-permute-start.17 = (f32[72,576]{1,0:T(8,128)S(1)}, f32[72,576]{1,0:T(8,128)S(1)}, u32[]{:S(2)}, u32[]{:S(2)}) collective-permute-start(f32[72,576]{1,0:T(8,128)S(1)} %collective-permute-done.10.refs_0_), channel_id=1, source_target_pairs={{0,4},{4,0},{8,12},{12,8},{16,20},{20,16},{24,28},{28,24},{1,5},{5... | collective-permute-start | bytes 497672 | tf_op jit(solution)/shard_map/ppermute | solution.py:71
  50.8 3.5 %collective-permute-done.12 = f32[32,576]{1,0:T(8,128)S(1)} collective-permute-done((f32[32,576]{1,0:T(8,128)S(1)}, f32[32,576]{1,0:T(8,128)S(1)}, u32[]{:S(2)}, u32[]{:S(2)}) %collective-permute-start.12) | collective-permute-done | bytes 73760 | tf_op jit(solution)/shard_map/ppermute | solution.py:71
  54.4 1.2 %left.1 = (f32[16,1152]{1,0:T(8,128)S(1)}, f32[16,1152]{1,0:T(8,128)S(1)}) custom-call(s32[1]{0:T(128)} %bitcast.shard_ref, f32[32,576]{1,0:T(8,128)S(1)} %add.48.right, f32[2,32,32]{2,1,0:T(8,128)S(1)} %inverse.2, f32[2,288,1152]{2,1,0:T(8,128)S(1)} %get-tuple-element.133.corr, f32[288,1152]{1,0:T(8,128)S(1)} %collective-permute-done.7.other), custom_call_target="tpu_custom_call" | custom-call | flops 1000 | bytes 1000 | tf_op jit(solution)/shard_map/left/pallas_call | solution.py:437
  55.5 0.7 collective-permute-start.13
  56.2 1.8 %collective-permute-start.19 = (f32[72,576]{1,0:T(8,128)S(1)}, f32[72,576]{1,0:T(8,128)S(1)}, u32[]{:S(2)}, u32[]{:S(2)}) collective-permute-start(f32[72,576]{1,0:T(8,128)S(1)} %get-tuple-element.197), channel_id=1, source_target_pairs={{0,16},{4,20},{8,24},{12,28},{16,0},{20,4},{24,8},{28,12},{1,17},{... | collective-permute-start | bytes 497672 | tf_op jit(solution)/shard_map/ppermute | solution.py:71
  58.0 2.0 %collective-permute-done.13 = f32[16,1152]{1,0:T(8,128)S(1)} collective-permute-done((f32[16,1152]{1,0:T(8,128)S(1)}, f32[16,1152]{1,0:T(8,128)S(1)}, u32[]{:S(2)}, u32[]{:S(2)}) %collective-permute-start.13) | collective-permute-done | bytes 73760 | tf_op jit(solution)/shard_map/ppermute | solution.py:71
  60.0 1.2 %collective-permute-done.14.got = f32[32,128]{1,0:T(8,128)S(1)} collective-permute-done((f32[32,128]{1,0:T(8,128)S(1)}, f32[32,128]{1,0:T(8,128)S(1)}, u32[]{:S(2)}, u32[]{:S(2)}) %collective-permute-start.14) | collective-permute-done | bytes 16416 | tf_op jit(solution)/shard_map/ppermute | solution.py:71
  61.1 1.5 %collective-permute-start.15 = (f32[16,1152]{1,0:T(8,128)S(1)}, f32[16,1152]{1,0:T(8,128)S(1)}, u32[]{:S(2)}, u32[]{:S(2)}) collective-permute-start(f32[16,1152]{1,0:T(8,128)S(1)} %add.49), channel_id=1, source_target_pairs={{0,4},{4,0},{8,12},{12,8},{16,20},{20,16},{24,28},{28,24},{1,5},{5... | collective-permute-start | bytes 221192 | tf_op jit(solution)/shard_map/ppermute | solution.py:71
  63.1 0.6 norm_out.1
  63.7 1.8 %collective-permute-done.15 = f32[16,1152]{1,0:T(8,128)S(1)} collective-permute-done((f32[16,1152]{1,0:T(8,128)S(1)}, f32[16,1152]{1,0:T(8,128)S(1)}, u32[]{:S(2)}, u32[]{:S(2)}) %collective-permute-start.15) | collective-permute-done | bytes 73760 | tf_op jit(solution)/shard_map/ppermute | solution.py:71
  65.6 1.6 %collective-permute-start.23 = (f32[72,576]{1,0:T(8,128)S(1)}, f32[72,576]{1,0:T(8,128)S(1)}, u32[]{:S(2)}, u32[]{:S(2)}) collective-permute-start(f32[72,576]{1,0:T(8,128)S(1)} %collective-permute-done.16.refs_1_), channel_id=1, source_target_pairs={{0,4},{4,0},{8,12},{12,8},{16,20},{20,16},{24,28},{28,24},{1,5},{5... | collective-permute-start | bytes 497672 | tf_op jit(solution)/shard_map/ppermute | solution.py:71
  67.2 0.6 insert.12.refs_1_
  67.8 2.2 %collective-permute-done.18 = f32[16,1152]{1,0:T(8,128)S(1)} collective-permute-done((f32[16,1152]{1,0:T(8,128)S(1)}, f32[16,1152]{1,0:T(8,128)S(1)}, u32[]{:S(2)}, u32[]{:S(2)}) %collective-permute-start.18) | collective-permute-done | bytes 73760 | tf_op jit(solution)/shard_map/ppermute | solution.py:71
  71.0 4.6 %collective-permute-done.21 = f32[16,1152]{1,0:T(8,128)S(1)} collective-permute-done((f32[16,1152]{1,0:T(8,128)S(1)}, f32[16,1152]{1,0:T(8,128)S(1)}, u32[]{:S(2)}, u32[]{:S(2)}) %collective-permute-start.21) | collective-permute-done | bytes 73760 | tf_op jit(solution)/shard_map/ppermute | solution.py:71
  75.5 1.2 %collective-permute-start.22 = (f32[16,1152]{1,0:T(8,128)S(1)}, f32[16,1152]{1,0:T(8,128)S(1)}, u32[]{:S(2)}, u32[]{:S(2)}) collective-permute-start(f32[16,1152]{1,0:T(8,128)S(1)} %add.52.ours), channel_id=1, source_target_pairs={{0,2},{1,3},{2,0},{3,1},{4,6},{5,7},{6,4},{7,5},{8,10},{9,11},{10,... | collective-permute-start | bytes 221192 | tf_op jit(solution)/shard_map/ppermute | solution.py:71
  76.7 1.0 collective-permute-start.26
  78.1 1.9 %collective-permute-done.22.got = f32[16,1152]{1,0:T(8,128)S(1)} collective-permute-done((f32[16,1152]{1,0:T(8,128)S(1)}, f32[16,1152]{1,0:T(8,128)S(1)}, u32[]{:S(2)}, u32[]{:S(2)}) %collective-permute-start.22) | collective-permute-done | bytes 73760 | tf_op jit(solution)/shard_map/ppermute | solution.py:71
  80.0 1.3 %right.3 = (f32[32,576]{1,0:T(8,128)S(1)}, f32[32,1152]{1,0:T(8,128)S(1)}) custom-call(s32[1]{0:T(128)} %bitcast.shard_ref, f32[32,1152]{1,0:T(8,128)S(1)} %join.3.whole, f32[2,288,1152]{2,1,0:T(8,128)S(1)} %get-tuple-element.133.corr, f32[288,1152]{1,0:T(8,128)S(1)} %collective-permute-done.7.other), custom_call_target="tpu_custom_call" | custom-call | flops 1000 | bytes 1000 | tf_op jit(solution)/shard_map/right/pallas_call | solution.py:415
  81.4 1.6 %collective-permute-start.24 = (f32[32,576]{1,0:T(8,128)S(1)}, f32[32,576]{1,0:T(8,128)S(1)}, u32[]{:S(2)}, u32[]{:S(2)}) collective-permute-start(f32[32,576]{1,0:T(8,128)S(1)} %get-tuple-element.216), channel_id=1, source_target_pairs={{0,4},{4,0},{8,12},{12,8},{16,20},{20,16},{24,28},{28,24},{1,5},{5... | collective-permute-start | bytes 221192 | tf_op jit(solution)/shard_map/ppermute | solution.py:71
  83.3 3.0 %collective-permute-done.24 = f32[32,576]{1,0:T(8,128)S(1)} collective-permute-done((f32[32,576]{1,0:T(8,128)S(1)}, f32[32,576]{1,0:T(8,128)S(1)}, u32[]{:S(2)}, u32[]{:S(2)}) %collective-permute-start.24) | collective-permute-done | bytes 73760 | tf_op jit(solution)/shard_map/ppermute | solution.py:71
  86.3 1.6 %collective-permute-start.30 = (f32[72,576]{1,0:T(8,128)S(1)}, f32[72,576]{1,0:T(8,128)S(1)}, u32[]{:S(2)}, u32[]{:S(2)}) collective-permute-start(f32[72,576]{1,0:T(8,128)S(1)} %collective-permute-done.25.refs_1_), channel_id=1, source_target_pairs={{0,4},{4,0},{8,12},{12,8},{16,20},{20,16},{24,28},{28,24},{1,5},{5... | collective-permute-start | bytes 497672 | tf_op jit(solution)/shard_map/ppermute | solution.py:71
  88.0 4.3 %collective-permute-done.28 = f32[32,576]{1,0:T(8,128)S(1)} collective-permute-done((f32[32,576]{1,0:T(8,128)S(1)}, f32[32,576]{1,0:T(8,128)S(1)}, u32[]{:S(2)}, u32[]{:S(2)}) %collective-permute-start.28) | collective-permute-done | bytes 73760 | tf_op jit(solution)/shard_map/ppermute | solution.py:71
  92.3 1.0 collective-permute-start.29
  93.3 1.3 %inverse.3 = f32[2,32,32]{2,1,0:T(8,128)S(1)} custom-call(f32[32,1152]{1,0:T(8,128)S(1)} %get-tuple-element.235.ours, f32[32,1152]{1,0:T(8,128)S(1)} %collective-permute-done.27.theirs), custom_call_target="tpu_custom_call" | custom-call | flops 1000 | bytes 6000000 | tf_op jit(solution)/shard_map/inverse/pallas_call | solution.py:482
  94.6 0.8 insert.16.refs_1_
  95.5 2.6 %collective-permute-done.29 = f32[32,576]{1,0:T(8,128)S(1)} collective-permute-done((f32[32,576]{1,0:T(8,128)S(1)}, f32[32,576]{1,0:T(8,128)S(1)}, u32[]{:S(2)}, u32[]{:S(2)}) %collective-permute-start.29) | collective-permute-done | bytes 73760 | tf_op jit(solution)/shard_map/ppermute | solution.py:71
  98.5 0.9 collective-permute-done.31.their_right
  99.4 3.4 %finish.1 = (f32[288,1152]{1,0:T(8,128)}, f32[288,1152]{1,0:T(8,128)}, f32[288,1152]{1,0:T(8,128)}, f32[288,1152]{1,0:T(8,128)}, f32[144,288]{1,0:T(8,128)}, /*index=5*/f32[144,288]{1,0:T(8,128)}) custom-call(s32[1]{0:T(128)} %bitcast.shard_ref, f32[2,288,1152]{2,1,0:T(8,128)S(1)} %get-tuple-element.133.corr, f32[576,1152]{1,0:T(8,128)S(1)} %insert.17.rows, ...), custom_call_target="tpu_custom_call" | custom-call | tf_op jit(solution)/shard_map/finish/pallas_call | solution.py:552
  (62 shorter events, 6.0 us)
Async XLA Ops:
  0.6 6.7 %copy-start = (f32[144,288]{1,0:T(8,128)S(1)}, f32[144,288]{1,0:T(8,128)}, u32[]{:S(2)}) copy-start(f32[144,288]{1,0:T(8,128)} %moment_q.3) | copy-start | bytes 497668
  0.7 6.7 %copy-start.1 = (f32[144,288]{1,0:T(8,128)S(1)}, f32[144,288]{1,0:T(8,128)}, u32[]{:S(2)}) copy-start(f32[144,288]{1,0:T(8,128)} %moment_o.3) | copy-start | bytes 497668
  0.7 6.7 %copy-start.2 = (f32[144,288]{1,0:T(8,128)S(1)}, f32[144,288]{1,0:T(8,128)}, u32[]{:S(2)}) copy-start(f32[144,288]{1,0:T(8,128)} %weight_q.1) | copy-start | bytes 497668
  0.7 6.6 %copy-start.3 = (f32[144,288]{1,0:T(8,128)S(1)}, f32[144,288]{1,0:T(8,128)}, u32[]{:S(2)}) copy-start(f32[144,288]{1,0:T(8,128)} %weight_o.1) | copy-start | bytes 497668
  5.3 1.5 %collective-permute-start = (f32[32,1280]{1,0:T(8,128)S(1)}, f32[32,1280]{1,0:T(8,128)S(1)}, u32[]{:S(2)}, u32[]{:S(2)}) collective-permute-start(f32[32,1280]{1,0:T(8,128)S(1)} %get-tuple-element.135), channel_id=1, source_target_pairs={{0,1},{1,0},{2,3},{3,2},{4,5},{5,4},{6,7},{7,6},{8,9},{9,8},{10,11... | collective-permute-start | bytes 491528 | tf_op jit(solution)/shard_map/ppermute | solution.py:71
  6.9 28.2 %collective-permute-start.7 = (f32[288,1152]{1,0:T(8,128)S(1)}, f32[288,1152]{1,0:T(8,128)S(1)}, u32[]{:S(2)}, u32[]{:S(2)}) collective-permute-start(f32[288,1152]{1,0:T(8,128)S(1)} %get-tuple-element.145), channel_id=1, source_target_pairs={{0,1},{1,0},{2,3},{3,2},{4,5},{5,4},{6,7},{7,6},{8,9},{9,8},{10,11... | collective-permute-start | bytes 3981320 | tf_op jit(solution)/shard_map/ppermute | solution.py:71
  7.5 16.3 %collective-permute-start.4 = (f32[144,576]{1,0:T(8,128)S(1)}, f32[144,576]{1,0:T(8,128)S(1)}, u32[]{:S(2)}, u32[]{:S(2)}) collective-permute-start(f32[144,576]{1,0:T(8,128)S(1)} %get-tuple-element.149.refs_0_), channel_id=1, source_target_pairs={{0,8},{4,12},{8,0},{12,4},{16,24},{20,28},{24,16},{28,20},{1,9},{5... | collective-permute-start | bytes 995336 | tf_op jit(solution)/shard_map/ppermute | solution.py:71
  10.3 4.4 %collective-permute-start.1 = (f32[16,1280]{1,0:T(8,128)S(1)}, f32[16,1280]{1,0:T(8,128)S(1)}, u32[]{:S(2)}, u32[]{:S(2)}) collective-permute-start(f32[16,1280]{1,0:T(8,128)S(1)} %get-tuple-element.139), channel_id=1, source_target_pairs={{0,2},{1,3},{2,0},{3,1},{4,6},{5,7},{6,4},{7,5},{8,10},{9,11},{10,... | collective-permute-start | bytes 245768 | tf_op jit(solution)/shard_map/ppermute | solution.py:71
  14.7 4.5 %collective-permute-start.2 = (f32[16,1280]{1,0:T(8,128)S(1)}, f32[16,1280]{1,0:T(8,128)S(1)}, u32[]{:S(2)}, u32[]{:S(2)}) collective-permute-start(f32[16,1280]{1,0:T(8,128)S(1)} %add.42), channel_id=1, source_target_pairs={{0,4},{4,0},{8,12},{12,8},{16,20},{20,16},{24,28},{28,24},{1,5},{5... | collective-permute-start | bytes 245768 | tf_op jit(solution)/shard_map/ppermute | solution.py:71
  19.2 4.5 %collective-permute-start.3 = (f32[16,1280]{1,0:T(8,128)S(1)}, f32[16,1280]{1,0:T(8,128)S(1)}, u32[]{:S(2)}, u32[]{:S(2)}) collective-permute-start(f32[16,1280]{1,0:T(8,128)S(1)} %add.43), channel_id=1, source_target_pairs={{0,8},{4,12},{8,0},{12,4},{16,24},{20,28},{24,16},{28,20},{1,9},{5... | collective-permute-start | bytes 245768 | tf_op jit(solution)/shard_map/ppermute | solution.py:71
  19.6 26.8 %collective-permute-start.11 = (f32[144,576]{1,0:T(8,128)S(1)}, f32[144,576]{1,0:T(8,128)S(1)}, u32[]{:S(2)}, u32[]{:S(2)}) collective-permute-start(f32[144,576]{1,0:T(8,128)S(1)} %get-tuple-element.149.refs_0_), channel_id=1, source_target_pairs={{0,4},{4,0},{8,12},{12,8},{16,20},{20,16},{24,28},{28,24},{1,5},{5... | collective-permute-start | bytes 995336 | tf_op jit(solution)/shard_map/ppermute | solution.py:71
  23.8 6.1 %collective-permute-start.5 = (f32[16,1280]{1,0:T(8,128)S(1)}, f32[16,1280]{1,0:T(8,128)S(1)}, u32[]{:S(2)}, u32[]{:S(2)}) collective-permute-start(f32[16,1280]{1,0:T(8,128)S(1)} %add.44), channel_id=1, source_target_pairs={{0,16},{4,20},{8,24},{12,28},{16,0},{20,4},{24,8},{28,12},{1,17},{... | collective-permute-start | bytes 245768 | tf_op jit(solution)/shard_map/ppermute | solution.py:71
  29.8 5.2 %collective-permute-start.6 = (f32[16,1280]{1,0:T(8,128)S(1)}, f32[16,1280]{1,0:T(8,128)S(1)}, u32[]{:S(2)}, u32[]{:S(2)}) collective-permute-start(f32[16,1280]{1,0:T(8,128)S(1)} %add.45.ours), channel_id=1, source_target_pairs={{0,2},{1,3},{2,0},{3,1},{4,6},{5,7},{6,4},{7,5},{8,10},{9,11},{10,... | collective-permute-start | bytes 245768 | tf_op jit(solution)/shard_map/ppermute | solution.py:71
  31.7 14.7 %collective-permute-start.10 = (f32[72,576]{1,0:T(8,128)S(1)}, f32[72,576]{1,0:T(8,128)S(1)}, u32[]{:S(2)}, u32[]{:S(2)}) collective-permute-start(f32[72,576]{1,0:T(8,128)S(1)} %get-tuple-element.158), channel_id=1, source_target_pairs={{0,16},{4,20},{8,24},{12,28},{16,0},{20,4},{24,8},{28,12},{1,17},{... | collective-permute-start | bytes 497672 | tf_op jit(solution)/shard_map/ppermute | solution.py:71
  36.4 5.4 %collective-permute-start.8 = (f32[32,576]{1,0:T(8,128)S(1)}, f32[32,576]{1,0:T(8,128)S(1)}, u32[]{:S(2)}, u32[]{:S(2)}) collective-permute-start(f32[32,576]{1,0:T(8,128)S(1)} %get-tuple-element.148), channel_id=1, source_target_pairs={{0,4},{4,0},{8,12},{12,8},{16,20},{20,16},{24,28},{28,24},{1,5},{5... | collective-permute-start | bytes 221192 | tf_op jit(solution)/shard_map/ppermute | solution.py:71
  41.9 4.5 %collective-permute-start.9 = (f32[32,576]{1,0:T(8,128)S(1)}, f32[32,576]{1,0:T(8,128)S(1)}, u32[]{:S(2)}, u32[]{:S(2)}) collective-permute-start(f32[32,576]{1,0:T(8,128)S(1)} %add.46), channel_id=1, source_target_pairs={{0,8},{4,12},{8,0},{12,4},{16,24},{20,28},{24,16},{28,20},{1,9},{5... | collective-permute-start | bytes 221192 | tf_op jit(solution)/shard_map/ppermute | solution.py:71
  41.9 28.0 %collective-permute-start.20 = (f32[144,576]{1,0:T(8,128)S(1)}, f32[144,576]{1,0:T(8,128)S(1)}, u32[]{:S(2)}, u32[]{:S(2)}) collective-permute-start(f32[144,576]{1,0:T(8,128)S(1)} %collective-permute-done.4.refs_0_), channel_id=1, source_target_pairs={{0,4},{4,0},{8,12},{12,8},{16,20},{20,16},{24,28},{28,24},{1,5},{5... | collective-permute-start | bytes 995336 | tf_op jit(solution)/shard_map/ppermute | solution.py:71
  46.4 8.0 %collective-permute-start.12 = (f32[32,576]{1,0:T(8,128)S(1)}, f32[32,576]{1,0:T(8,128)S(1)}, u32[]{:S(2)}, u32[]{:S(2)}) collective-permute-start(f32[32,576]{1,0:T(8,128)S(1)} %add.47), channel_id=1, source_target_pairs={{0,16},{4,20},{8,24},{12,28},{16,0},{20,4},{24,8},{28,12},{1,17},{... | collective-permute-start | bytes 221192 | tf_op jit(solution)/shard_map/ppermute | solution.py:71
  48.9 16.6 %collective-permute-start.16 = (f32[72,576]{1,0:T(8,128)S(1)}, f32[72,576]{1,0:T(8,128)S(1)}, u32[]{:S(2)}, u32[]{:S(2)}) collective-permute-start(f32[72,576]{1,0:T(8,128)S(1)} %collective-permute-done.10.refs_0_), channel_id=1, source_target_pairs={{0,8},{4,12},{8,0},{12,4},{16,24},{20,28},{24,16},{28,20},{1,9},{5... | collective-permute-start | bytes 497672 | tf_op jit(solution)/shard_map/ppermute | solution.py:71
  49.3 16.2 %collective-permute-start.17 = (f32[72,576]{1,0:T(8,128)S(1)}, f32[72,576]{1,0:T(8,128)S(1)}, u32[]{:S(2)}, u32[]{:S(2)}) collective-permute-start(f32[72,576]{1,0:T(8,128)S(1)} %collective-permute-done.10.refs_0_), channel_id=1, source_target_pairs={{0,4},{4,0},{8,12},{12,8},{16,20},{20,16},{24,28},{28,24},{1,5},{5... | collective-permute-start | bytes 497672 | tf_op jit(solution)/shard_map/ppermute | solution.py:71
  55.5 4.4 %collective-permute-start.13 = (f32[16,1152]{1,0:T(8,128)S(1)}, f32[16,1152]{1,0:T(8,128)S(1)}, u32[]{:S(2)}, u32[]{:S(2)}) collective-permute-start(f32[16,1152]{1,0:T(8,128)S(1)} %get-tuple-element.172), channel_id=1, source_target_pairs={{0,2},{1,3},{2,0},{3,1},{4,6},{5,7},{6,4},{7,5},{8,10},{9,11},{10,... | collective-permute-start | bytes 221192 | tf_op jit(solution)/shard_map/ppermute | solution.py:71
  56.2 13.8 %collective-permute-start.19 = (f32[72,576]{1,0:T(8,128)S(1)}, f32[72,576]{1,0:T(8,128)S(1)}, u32[]{:S(2)}, u32[]{:S(2)}) collective-permute-start(f32[72,576]{1,0:T(8,128)S(1)} %get-tuple-element.197), channel_id=1, source_target_pairs={{0,16},{4,20},{8,24},{12,28},{16,0},{20,4},{24,8},{28,12},{1,17},{... | collective-permute-start | bytes 497672 | tf_op jit(solution)/shard_map/ppermute | solution.py:71
  60.0 1.2 %collective-permute-start.14 = (f32[32,128]{1,0:T(8,128)S(1)}, f32[32,128]{1,0:T(8,128)S(1)}, u32[]{:S(2)}, u32[]{:S(2)}) collective-permute-start(f32[32,128]{1,0:T(8,128)S(1)} %get-tuple-element.179.ours), channel_id=1, source_target_pairs={{0,1},{1,0},{2,3},{3,2},{4,5},{5,4},{6,7},{7,6},{8,9},{9,8},{10,11... | collective-permute-start | bytes 49160 | tf_op jit(solution)/shard_map/ppermute | solution.py:71
  60.0 3.1 %copy-start.4 = (f32[72]{0:T(128)S(1)}, f32[72]{0:T(128)}, u32[]{:S(2)}) copy-start(f32[72]{0:T(128)} %param.24) | copy-start | bytes 868
  61.1 4.4 %collective-permute-start.15 = (f32[16,1152]{1,0:T(8,128)S(1)}, f32[16,1152]{1,0:T(8,128)S(1)}, u32[]{:S(2)}, u32[]{:S(2)}) collective-permute-start(f32[16,1152]{1,0:T(8,128)S(1)} %add.49), channel_id=1, source_target_pairs={{0,4},{4,0},{8,12},{12,8},{16,20},{20,16},{24,28},{28,24},{1,5},{5... | collective-permute-start | bytes 221192 | tf_op jit(solution)/shard_map/ppermute | solution.py:71
  65.5 4.4 %collective-permute-start.18 = (f32[16,1152]{1,0:T(8,128)S(1)}, f32[16,1152]{1,0:T(8,128)S(1)}, u32[]{:S(2)}, u32[]{:S(2)}) collective-permute-start(f32[16,1152]{1,0:T(8,128)S(1)} %add.50), channel_id=1, source_target_pairs={{0,8},{4,12},{8,0},{12,4},{16,24},{20,28},{24,16},{28,20},{1,9},{5... | collective-permute-start | bytes 221192 | tf_op jit(solution)/shard_map/ppermute | solution.py:71
  65.6 14.4 %collective-permute-start.23 = (f32[72,576]{1,0:T(8,128)S(1)}, f32[72,576]{1,0:T(8,128)S(1)}, u32[]{:S(2)}, u32[]{:S(2)}) collective-permute-start(f32[72,576]{1,0:T(8,128)S(1)} %collective-permute-done.16.refs_1_), channel_id=1, source_target_pairs={{0,4},{4,0},{8,12},{12,8},{16,20},{20,16},{24,28},{28,24},{1,5},{5... | collective-permute-start | bytes 497672 | tf_op jit(solution)/shard_map/ppermute | solution.py:71
  70.0 5.5 %collective-permute-start.21 = (f32[16,1152]{1,0:T(8,128)S(1)}, f32[16,1152]{1,0:T(8,128)S(1)}, u32[]{:S(2)}, u32[]{:S(2)}) collective-permute-start(f32[16,1152]{1,0:T(8,128)S(1)} %add.51), channel_id=1, source_target_pairs={{0,16},{4,20},{8,24},{12,28},{16,0},{20,4},{24,8},{28,12},{1,17},{... | collective-permute-start | bytes 221192 | tf_op jit(solution)/shard_map/ppermute | solution.py:71
  75.5 4.4 %collective-permute-start.22 = (f32[16,1152]{1,0:T(8,128)S(1)}, f32[16,1152]{1,0:T(8,128)S(1)}, u32[]{:S(2)}, u32[]{:S(2)}) collective-permute-start(f32[16,1152]{1,0:T(8,128)S(1)} %add.52.ours), channel_id=1, source_target_pairs={{0,2},{1,3},{2,0},{3,1},{4,6},{5,7},{6,4},{7,5},{8,10},{9,11},{10,... | collective-permute-start | bytes 221192 | tf_op jit(solution)/shard_map/ppermute | solution.py:71
  76.7 9.6 %collective-permute-start.25 = (f32[72,576]{1,0:T(8,128)S(1)}, f32[72,576]{1,0:T(8,128)S(1)}, u32[]{:S(2)}, u32[]{:S(2)}) collective-permute-start(f32[72,576]{1,0:T(8,128)S(1)} %collective-permute-done.19.refs_0_), channel_id=1, source_target_pairs={{0,8},{4,12},{8,0},{12,4},{16,24},{20,28},{24,16},{28,20},{1,9},{5... | collective-permute-start | bytes 497672 | tf_op jit(solution)/shard_map/ppermute | solution.py:71
  76.7 11.1 %collective-permute-start.26 = (f32[72,576]{1,0:T(8,128)S(1)}, f32[72,576]{1,0:T(8,128)S(1)}, u32[]{:S(2)}, u32[]{:S(2)}) collective-permute-start(f32[72,576]{1,0:T(8,128)S(1)} %collective-permute-done.19.refs_0_), channel_id=1, source_target_pairs={{0,4},{4,0},{8,12},{12,8},{16,20},{20,16},{24,28},{28,24},{1,5},{5... | collective-permute-start | bytes 497672 | tf_op jit(solution)/shard_map/ppermute | solution.py:71
  81.3 6.5 %collective-permute-start.27 = (f32[32,1152]{1,0:T(8,128)S(1)}, f32[32,1152]{1,0:T(8,128)S(1)}, u32[]{:S(2)}, u32[]{:S(2)}) collective-permute-start(f32[32,1152]{1,0:T(8,128)S(1)} %get-tuple-element.235.ours), channel_id=1, source_target_pairs={{0,1},{1,0},{2,3},{3,2},{4,5},{5,4},{6,7},{7,6},{8,9},{9,8},{10,11... | collective-permute-start | bytes 442376 | tf_op jit(solution)/shard_map/ppermute | solution.py:71
  81.4 4.9 %collective-permute-start.24 = (f32[32,576]{1,0:T(8,128)S(1)}, f32[32,576]{1,0:T(8,128)S(1)}, u32[]{:S(2)}, u32[]{:S(2)}) collective-permute-start(f32[32,576]{1,0:T(8,128)S(1)} %get-tuple-element.216), channel_id=1, source_target_pairs={{0,4},{4,0},{8,12},{12,8},{16,20},{20,16},{24,28},{28,24},{1,5},{5... | collective-permute-start | bytes 221192 | tf_op jit(solution)/shard_map/ppermute | solution.py:71
  86.3 11.8 %collective-permute-start.30 = (f32[72,576]{1,0:T(8,128)S(1)}, f32[72,576]{1,0:T(8,128)S(1)}, u32[]{:S(2)}, u32[]{:S(2)}) collective-permute-start(f32[72,576]{1,0:T(8,128)S(1)} %collective-permute-done.25.refs_1_), channel_id=1, source_target_pairs={{0,4},{4,0},{8,12},{12,8},{16,20},{20,16},{24,28},{28,24},{1,5},{5... | collective-permute-start | bytes 497672 | tf_op jit(solution)/shard_map/ppermute | solution.py:71
  87.9 4.4 %collective-permute-start.28 = (f32[32,576]{1,0:T(8,128)S(1)}, f32[32,576]{1,0:T(8,128)S(1)}, u32[]{:S(2)}, u32[]{:S(2)}) collective-permute-start(f32[32,576]{1,0:T(8,128)S(1)} %add.53), channel_id=1, source_target_pairs={{0,8},{4,12},{8,0},{12,4},{16,24},{20,28},{24,16},{28,20},{1,9},{5... | collective-permute-start | bytes 221192 | tf_op jit(solution)/shard_map/ppermute | solution.py:71
  92.3 5.7 %collective-permute-start.29 = (f32[32,576]{1,0:T(8,128)S(1)}, f32[32,576]{1,0:T(8,128)S(1)}, u32[]{:S(2)}, u32[]{:S(2)}) collective-permute-start(f32[32,576]{1,0:T(8,128)S(1)} %add.54), channel_id=1, source_target_pairs={{0,16},{4,20},{8,24},{12,28},{16,0},{20,4},{24,8},{28,12},{1,17},{... | collective-permute-start | bytes 221192 | tf_op jit(solution)/shard_map/ppermute | solution.py:71
  98.1 1.3 %collective-permute-start.31 = (f32[32,576]{1,0:T(8,128)S(1)}, f32[32,576]{1,0:T(8,128)S(1)}, u32[]{:S(2)}, u32[]{:S(2)}) collective-permute-start(f32[32,576]{1,0:T(8,128)S(1)} %add.55.right), channel_id=1, source_target_pairs={{0,1},{1,0},{2,3},{3,2},{4,5},{5,4},{6,7},{7,6},{8,9},{9,8},{10,11... | collective-permute-start | bytes 221192 | tf_op jit(solution)/shard_map/ppermute | solution.py:71

commit v9 on v8

--- a/solution.py
+++ b/solution.py
@@ -147,7 +147,7 @@
 
 class Gather:
     PLAN = (
-        ("near", "own", 2, None, (0, 4)),
+        ("near", "own", 2, (0, "core"), (0, "joined")),
         ("turned", "own", 1, (0, 1), (1, 4)),
         ("far_a", "own_a", 4, (0, 4), (1, 4)),
         ("turned_near", "near", 1, (1, 1), (2, 4)),
@@ -157,12 +157,11 @@
         ("turned_last_a", "last_a", 1, (2, 1), (2, "joined")),
         ("last_b", "far_b", 2, (2, 2), (3, 2)),
         ("turned_far_b", "far_b", 1, (2, 2), (3, 2)),
-        ("turned_last_b", "last_b", 1, (3, 1), (3, 0)),
+        ("turned_last_b", "last_b", 1, (3, 1), None),
     )
     INSERTS = {
         (1, 1): ("own",),
-        (1, 4): ("near",),
-        (2, 1): ("turned",),
+        (2, 1): ("near", "turned"),
         (2, 2): ("far_a", "last_a"),
         (2, 4): ("turned_near",),
         (2, "x"): ("turned_far_a",),
@@ -318,12 +317,14 @@
 def norm_out_kernel(n_shard, place_ref, shard_ref, ours, got, moment, new_moment, new_weight):
     lines, share = new_weight.shape[0], moment.shape[1]
     high = is_high(shard_ref, 1)
-    sums = jnp.where(high, got[:lines, :], ours[:lines, :])
+    size = ours.shape[1] - LANES
+    ours, got = ours[:lines, size:], got[:lines, size:]
+    sums = jnp.where(high, got, ours)
     shift, inside = window_of(n_shard, share, place_ref, shard_ref, lines)
     total = jnp.sum(jnp.where(inside, sums, 0.0), axis=0, keepdims=True)
     total = pltpu.roll(jnp.broadcast_to(total, (8, LANES)), LANES - shift, 1)[:1, :share]
     new_moment[...] = decay_rate * moment[...] + total
-    new_weight[...] = jnp.where(high, ours[:lines, :], got[:lines, :])
+    new_weight[...] = jnp.where(high, ours, got)
 
 
 def norm_out(ours, got, moment, place, shard, lines, n_shard):
@@ -338,48 +339,39 @@
     )(place, shard, ours, got, moment)
 
 
-def first_kernel(chunks, n_shard, place_ref, shard_ref, *refs):
+def first_kernel(n_shard, place_ref, shard_ref, *refs):
     sources, norms, (corr, give_corr, keep, give) = refs[:6], refs[6:9], refs[9:13]
     buffer, bases, norm_buffers, sems, small_sems = refs[13], refs[14], refs[15:18], refs[18], refs[19]
     rank, size = bases.shape[1], corr.shape[2]
     high = is_high(shard_ref, 1)
-    lanes = size // chunks
     small = zip(sources[4:] + norms, [bases.at[0], bases.at[1], *norm_buffers])
     small_copies = [pltpu.make_async_copy(source, target, small_sems.at[k]) for k, (source, target) in enumerate(small)]
-    copies = {}
-    for copy in small_copies:
+    copies = [pltpu.make_async_copy(source, buffer.at[j], sems.at[j]) for j, source in enumerate(sources[:4])]
+    for copy in small_copies + copies:
         copy.start()
-    for c in range(chunks):
-        at = pl.ds(c * lanes, lanes)
-        for j, source in enumerate(sources[:4]):
-            copies[c, j] = pltpu.make_async_copy(source.at[:, at], buffer.at[j, :, at], sems.at[c, j])
-            copies[c, j].start()
     for copy in small_copies:
         copy.wait()
     sums, shares = norm_terms(n_shard, rank, place_ref, shard_ref, *norm_buffers)
     keep[:, size:] = jnp.where(high, shares, sums)
     give[:, size:] = jnp.where(high, sums, shares)
-    for c in range(chunks):
-        at = pl.ds(c * lanes, lanes)
-        totals, parts = [], []
-        for p in range(2):
-            copies[c, p].wait()
-            copies[c, 2 + p].wait()
-            totals.append(buffer[p, :, at] + buffer[2 + p, :, at])
-            corr[p, :, at] = totals[p]
-            parts.append(stacked(bases[p], totals[p], NN))
-        give_corr[:, at] = jnp.where(high, totals[0], totals[1])
-        keep[:, at] = jnp.where(high, parts[1], parts[0])
-        give[:, at] = jnp.where(high, parts[0], parts[1])
+    totals, parts = [], []
+    for p in range(2):
+        copies[p].wait()
+        copies[2 + p].wait()
+        totals.append(buffer[p] + buffer[2 + p])
+        corr[p] = totals[p]
+        parts.append(stacked(bases[p], totals[p], NN))
+    give_corr[...] = jnp.where(high, totals[0], totals[1])
+    keep[:, :size] = jnp.where(high, parts[1], parts[0])
+    give[:, :size] = jnp.where(high, parts[0], parts[1])
 
 
 def first(grads, errors, bases, norms, place, shard, n_shard):
     width, size = grads[0].shape
     rank = bases[0].shape[0]
-    chunks = 3 if size % (3 * LANES) == 0 else 1
     part = pltpu.VMEM((rank, size + LANES), f32)
     return pl.pallas_call(
-        functools.partial(first_kernel, chunks, n_shard),
+        functools.partial(first_kernel, n_shard),
         in_specs=[IN_SMEM] * 2 + [IN_HBM] * 9,
         out_specs=[IN_VMEM] * 4,
         out_shape=[pltpu.VMEM((2, width, size), f32), pltpu.VMEM((width, size), f32), part, part],
@@ -387,7 +379,7 @@
             pltpu.VMEM((4, width, size), f32),
             pltpu.VMEM((2, rank, width), f32),
             *(pltpu.VMEM(array.shape, f32) for array in norms),
-            pltpu.SemaphoreType.DMA((chunks, 4)),
+            pltpu.SemaphoreType.DMA((4,)),
             pltpu.SemaphoreType.DMA((5,)),
         ],
         compiler_params=LARGE,
@@ -399,28 +391,31 @@
     return jnp.concatenate([corr[shard_ref[0] & 1], other[...]], axis=0)
 
 
-def right_kernel(shard_ref, whole, corr, other, right, left, *extra):
+def right_kernel(count, shard_ref, whole, corr, other, *refs):
     size = corr.shape[2]
-    left[...] = whole[:, :size]
+    right, left, *extra = refs[count:]
+    left[:, :size] = whole[:, :size]
+    if count:
+        left[:, size:] = refs[0][...]
     if extra:
         extra[0][...] = whole[:, size:]
     right[...] = stacked(whole[:, :size], both_shares(shard_ref, corr, other), NT)
 
 
-def right_of(whole, shard, corr, other):
+def right_of(whole, shard, corr, other, *more):
     rank = whole.shape[0]
     width, size = other.shape
     beside = whole.shape[1] - size
-    shapes = [(rank, 2 * width), (rank, size)] + ([(rank, beside)] if beside else [])
-    return pl.pallas_call(
-        right_kernel,
-        in_specs=[IN_SMEM] + [IN_VMEM] * 3,
+    shapes = [(rank, 2 * width), (rank, size + sum(array.shape[1] for array in more))] + ([(rank, beside)] if beside else [])
+    return pl.pallas_call(
+        functools.partial(right_kernel, len(more)),
+        in_specs=[IN_SMEM] + [IN_VMEM] * (3 + len(more)),
         out_specs=[IN_VMEM] * len(shapes),
         out_shape=[pltpu.VMEM(shape, f32) for shape in shapes],
         compiler_params=SMALL,
         cost_estimate=QUICK,
         name="right",
-    )(shard, whole, *hold(pltpu.VMEM, corr, other))
+    )(shard, whole, *hold(pltpu.VMEM, corr, other), *more)
 
 
 def left_kernel(mask, shard_ref, right, inverse, corr, other, keep, give):
@@ -472,15 +467,16 @@
     return work[:, rank : 2 * rank], work[:, 3 * rank :]
 
 
-def inverse_kernel(ours, theirs, out):
+def inverse_kernel(size, ours, theirs, out):
     rank = out.shape[1]
-    out[0], out[1] = eliminate(exact(ours[...], ours[...], NT), exact(theirs[...], theirs[...], NT), rank)
-
-
-def inverse_of(ours, theirs):
+    left, other = ours[:, :size], theirs[:, :size]
+    out[0], out[1] = eliminate(exact(left, left, NT), exact(other, other, NT), rank)
+
+
+def inverse_of(ours, theirs, size):
     rank = ours.shape[0]
     return pl.pallas_call(
-        inverse_kernel,
+        functools.partial(inverse_kernel, size),
         out_shape=pltpu.VMEM((2, rank, rank), f32),
         compiler_params=SMALL,
         cost_estimate=SLOW,
@@ -492,14 +488,14 @@
     count = own.shape[2]
     index = place_ref[0]
     for p, left in enumerate((ours, theirs)):
-        high, middle, low = three(left[...])
+        high, middle, low = three(left[:, : stack.shape[2]])
         stack[p] = jnp.concatenate([high, middle, low, high, middle, high], axis=0)
         window = left[:, pl.ds(pl.multiple_of(index * LANES, LANES), 2 * LANES)]
         own[p] = pltpu.roll(window, 2 * LANES - index * (count - LANES), 1)[:, :count]
 
 
-def stack_of(ours, theirs, place, count):
-    rank, size = ours.shape
+def stack_of(ours, theirs, place, size, count):
+    rank = ours.shape[0]
     return pl.pallas_call(
         stack_kernel,
         in_specs=[IN_SMEM, IN_VMEM, IN_VMEM],
@@ -595,32 +591,37 @@
     norms = (norm_grads[0], norm_moment, norm_weight)
     corr, give_corr, keep, give = first((q_grad[0].T, o_grad[0].T), (q_error[0].T, o_error[0].T), (q_basis.T, o_basis.T), norms, place, shard, n_shard)
     masks = halves(n_shard)
+
+    def ending(left, theirs):
+        gains = norm_out(left, theirs, norm_moment, place, shard, flat // LANES, n_shard)
+        return (gains, *stack_of(left, theirs, place, size, row_count)) if gather.paired else (gains,)
+
     for sweep in range(ROUNDS):
         last = sweep == ROUNDS - 1
         if sweep == 0:
             whole, other_corr = sum_over_all(keep, give, shard, masks, n_rep, n_shard, gather, 0, give_corr)
         else:
             whole, _ = sum_over_all(keep, give, shard, masks[1:], n_rep, n_shard, gather, 2 * sweep)
-        right, left, *beside = right_of(whole, shard, corr, other_corr)
+        right, left, *beside = right_of(whole, shard, corr, other_corr, *([norms] if last else []))
         if sweep == 0:
-            norm_got = swap(beside[0], "shard", masks[0], n_shard)
-            gather.tasks[2, 1] = (functools.partial(norm_out, lines=flat // LANES, n_shard=n_shard), beside[0], norm_got, norm_moment, place, shard)
+            (norms,) = beside
         theirs = swap(left, "shard", masks[0], n_shard) if last else left
-        gather.tasks[2 * sweep + 1, 4 if last else 2] = (inverse_of, left, theirs)
-        if last and gather.paired:
-            gather.tasks[3, 2] = (functools.partial(stack_of, count=row_count), left, theirs, place)
+        gather.tasks[2 * sweep + 1, 4 if last else 1] = (functools.partial(inverse_of, size=size), left, theirs)
+        if last:
+            gather.tasks[3, 2] = (ending, left, theirs)
         right = sum_over(right, n_rep, gather, 2 * sweep + 1)
-        inverse = gather.results[2 * sweep + 1, 4 if last else 2]
+        inverse = gather.results[2 * sweep + 1, 4 if last else 1]
         if not last:
             keep, give = left_of(right, inverse, shard, masks[1], corr, other_corr)
     their_right = swap(right, "shard", masks[0], n_shard)
-    norm_moment_new, norm_weight_new = gather.results[2, 1]
+    (norm_moment_new, norm_weight_new), *terms = gather.results[3, 2]
     if gather.paired:
-        stack, own = gather.results[3, 2]
-        gather.insert([gather.blocks["turned_last_b"]], ["turned_last_b"])
+        stack, own = terms
+        their_right, turned = lax.optimization_barrier((their_right, gather.blocks["turned_last_b"]))
+        gather.insert([turned], ["turned_last_b"])
         outs = finish(shard, corr, gather.rows, stack, inverse, right, their_right, own, q_moment, o_moment)
     else:
-        outs = finish_plain((shard[0] & 1) != 0, corr, gather.blocks["own"], (left, theirs), inverse, (right, their_right), (q_moment, o_moment))
+        outs = finish_plain((shard[0] & 1) != 0, corr, gather.blocks["own"], (left[:, :size], theirs[:, :size]), inverse, (right, their_right), (q_moment, o_moment))
     weight_q, weight_o, error_q, error_o, q_moment_new, o_moment_new = outs
     return (
         weight_q.T,

time: 103 us -> 101 us (0.981)
  waiting for transfers between devices: 44.7 us -> 36.4 us
  starting transfers between devices: 37.4 us -> 44.4 us
    ppermute x32 -> x31, waiting for transfers between devices: 44.7 us -> 36.4 us  [swap(): return lax.ppermute(block, axis, pairs)]
    ppermute x32 -> x31, starting transfers between devices: 37.4 us -> 44.4 us  [swap(): return lax.ppermute(block, axis, pairs)]
    pallas_call x9 -> x8, Pallas kernels: 4.18 us -> 4.1 us  [insert(): pl.pallas_call(functools.partial(insert_kernel, masks, rows_each), in_spe...]
  transfers between devices with their start and end apart: 32 -> 31, of which waited for: 18 -> 18; matrix products, arithmetic and copies ran while one was open for 0% -> 0% of each run, Pallas kernels for 11% -> 11%
where the time goes in v9:
time: 101 us
  starting transfers between devices  44.4 us (44%)
  waiting for transfers between devices  36.4 us (36%)
  Pallas kernels  18.7 us (19%)
    ppermute x31, starting transfers between devices, swap(): return lax.ppermute(block, axis, pairs)  44.4 us
    ppermute x31, waiting for transfers between devices, swap(): return lax.ppermute(block, axis, pairs)  36.4 us
    pallas_call x8, Pallas kernels, insert(): pl.pallas_call(functools.partial(insert_kernel, masks, rows_each), in_spe...  4.1 us
    pallas_call x1, Pallas kernels, first(): pl.pallas_call(functools.partial(first_kernel, n_shard), in_specs=[IN_SME...  3.85 us
    pallas_call x1, Pallas kernels, finish(): pl.pallas_call(functools.partial(finish_kernel, chunks), in_specs=[IN_SME...  3.46 us
    pallas_call x2, Pallas kernels, right_of(): pl.pallas_call(functools.partial(right_kernel, len(more)), in_specs=[IN_S...  2.62 us
    pallas_call x2, Pallas kernels, inverse_of(): pl.pallas_call(functools.partial(inverse_kernel, size), out_shape=pltpu.V...  2.6 us
  transfers between devices with their start and end apart: 31, of which 18 were waited for; matrix products, arithmetic and copies ran while one was open for 0% of the time, Pallas kernels for 11%

profile of v9, /device:TPU:0, one launch (start us, length us, event | category | flops | bytes accessed | tf_op | source)
XLA Modules:
  0.0 100.7 jit_solution(7260182540707223781)
XLA Ops:
  0.7 3.9 %first.1 = (f32[2,288,1152]{2,1,0:T(8,128)S(1)}, f32[288,1152]{1,0:T(8,128)S(1)}, f32[32,1280]{1,0:T(8,128)S(1)}, f32[32,1280]{1,0:T(8,128)S(1)}) custom-call(s32[1]{0:T(128)} %bitcast.1.place_ref, s32[1]{0:T(128)} %bitcast.shard_ref, f32[288,1152]{1,0:T(8,128)} %bitcast.31, f32[288,1152]{1,0:T(8,128)} %bitcast.32, f32[288,1152]{1,0:T(8,128)} %bitcast.33, ...), custom_call_target="tpu_custom_call" | custom-call | tf_op jit(solution)/shard_map/first/pallas_call | solution.py:373
  5.1 1.0 %collective-permute-done.got = f32[32,1280]{1,0:T(8,128)S(1)} collective-permute-done((f32[32,1280]{1,0:T(8,128)S(1)}, f32[32,1280]{1,0:T(8,128)S(1)}, u32[]{:S(2)}, u32[]{:S(2)}) %collective-permute-start) | collective-permute-done | bytes 163872 | tf_op jit(solution)/shard_map/ppermute | solution.py:71
  6.5 2.6 %collective-permute-start.1 = (f32[16,1280]{1,0:T(8,128)S(1)}, f32[16,1280]{1,0:T(8,128)S(1)}, u32[]{:S(2)}, u32[]{:S(2)}) collective-permute-start(f32[16,1280]{1,0:T(8,128)S(1)} %get-tuple-element.132), channel_id=1, source_target_pairs={{0,2},{1,3},{2,0},{3,1},{4,6},{5,7},{6,4},{7,5},{8,10},{9,11},{10,... | collective-permute-start | bytes 245768 | tf_op jit(solution)/shard_map/ppermute | solution.py:71
  9.3 1.6 %collective-permute-start.6 = (f32[144,576]{1,0:T(8,128)S(1)}, f32[144,576]{1,0:T(8,128)S(1)}, u32[]{:S(2)}, u32[]{:S(2)}) collective-permute-start(f32[144,576]{1,0:T(8,128)S(1)} %get-tuple-element.147.refs_0_), channel_id=1, source_target_pairs={{0,8},{4,12},{8,0},{12,4},{16,24},{20,28},{24,16},{28,20},{1,9},{5... | collective-permute-start | bytes 995336 | tf_op jit(solution)/shard_map/ppermute | solution.py:71
  11.0 1.2 %collective-permute-done.1 = f32[16,1280]{1,0:T(8,128)S(1)} collective-permute-done((f32[16,1280]{1,0:T(8,128)S(1)}, f32[16,1280]{1,0:T(8,128)S(1)}, u32[]{:S(2)}, u32[]{:S(2)}) %collective-permute-start.1) | collective-permute-done | bytes 81952 | tf_op jit(solution)/shard_map/ppermute | solution.py:71
  12.2 1.8 %collective-permute-start.2 = (f32[16,1280]{1,0:T(8,128)S(1)}, f32[16,1280]{1,0:T(8,128)S(1)}, u32[]{:S(2)}, u32[]{:S(2)}) collective-permute-start(f32[16,1280]{1,0:T(8,128)S(1)} %add.42), channel_id=1, source_target_pairs={{0,4},{4,0},{8,12},{12,8},{16,20},{20,16},{24,28},{28,24},{1,5},{5... | collective-permute-start | bytes 245768 | tf_op jit(solution)/shard_map/ppermute | solution.py:71
  14.0 2.7 %collective-permute-done.2 = f32[16,1280]{1,0:T(8,128)S(1)} collective-permute-done((f32[16,1280]{1,0:T(8,128)S(1)}, f32[16,1280]{1,0:T(8,128)S(1)}, u32[]{:S(2)}, u32[]{:S(2)}) %collective-permute-start.2) | collective-permute-done | bytes 81952 | tf_op jit(solution)/shard_map/ppermute | solution.py:71
  16.7 1.9 %collective-permute-start.3 = (f32[16,1280]{1,0:T(8,128)S(1)}, f32[16,1280]{1,0:T(8,128)S(1)}, u32[]{:S(2)}, u32[]{:S(2)}) collective-permute-start(f32[16,1280]{1,0:T(8,128)S(1)} %add.43), channel_id=1, source_target_pairs={{0,8},{4,12},{8,0},{12,4},{16,24},{20,28},{24,16},{28,20},{1,9},{5... | collective-permute-start | bytes 245768 | tf_op jit(solution)/shard_map/ppermute | solution.py:71
  18.6 1.5 %collective-permute-start.11 = (f32[144,576]{1,0:T(8,128)S(1)}, f32[144,576]{1,0:T(8,128)S(1)}, u32[]{:S(2)}, u32[]{:S(2)}) collective-permute-start(f32[144,576]{1,0:T(8,128)S(1)} %get-tuple-element.147.refs_0_), channel_id=1, source_target_pairs={{0,4},{4,0},{8,12},{12,8},{16,20},{20,16},{24,28},{28,24},{1,5},{5... | collective-permute-start | bytes 995336 | tf_op jit(solution)/shard_map/ppermute | solution.py:71
  20.1 1.6 %collective-permute-done.3 = f32[16,1280]{1,0:T(8,128)S(1)} collective-permute-done((f32[16,1280]{1,0:T(8,128)S(1)}, f32[16,1280]{1,0:T(8,128)S(1)}, u32[]{:S(2)}, u32[]{:S(2)}) %collective-permute-start.3) | collective-permute-done | bytes 81952 | tf_op jit(solution)/shard_map/ppermute | solution.py:71
  21.7 2.7 %collective-permute-start.4 = (f32[16,1280]{1,0:T(8,128)S(1)}, f32[16,1280]{1,0:T(8,128)S(1)}, u32[]{:S(2)}, u32[]{:S(2)}) collective-permute-start(f32[16,1280]{1,0:T(8,128)S(1)} %add.44), channel_id=1, source_target_pairs={{0,16},{4,20},{8,24},{12,28},{16,0},{20,4},{24,8},{28,12},{1,17},{... | collective-permute-start | bytes 245768 | tf_op jit(solution)/shard_map/ppermute | solution.py:71
  24.4 2.9 %collective-permute-done.4 = f32[16,1280]{1,0:T(8,128)S(1)} collective-permute-done((f32[16,1280]{1,0:T(8,128)S(1)}, f32[16,1280]{1,0:T(8,128)S(1)}, u32[]{:S(2)}, u32[]{:S(2)}) %collective-permute-start.4) | collective-permute-done | bytes 81952 | tf_op jit(solution)/shard_map/ppermute | solution.py:71
  27.3 1.1 %collective-permute-start.5 = (f32[16,1280]{1,0:T(8,128)S(1)}, f32[16,1280]{1,0:T(8,128)S(1)}, u32[]{:S(2)}, u32[]{:S(2)}) collective-permute-start(f32[16,1280]{1,0:T(8,128)S(1)} %add.45.ours), channel_id=1, source_target_pairs={{0,2},{1,3},{2,0},{3,1},{4,6},{5,7},{6,4},{7,5},{8,10},{9,11},{10,... | collective-permute-start | bytes 245768 | tf_op jit(solution)/shard_map/ppermute | solution.py:71
  28.4 2.7 %collective-permute-start.10 = (f32[72,576]{1,0:T(8,128)S(1)}, f32[72,576]{1,0:T(8,128)S(1)}, u32[]{:S(2)}, u32[]{:S(2)}) collective-permute-start(f32[72,576]{1,0:T(8,128)S(1)} %get-tuple-element.151), channel_id=1, source_target_pairs={{0,16},{4,20},{8,24},{12,28},{16,0},{20,4},{24,8},{28,12},{1,17},{... | collective-permute-start | bytes 497672 | tf_op jit(solution)/shard_map/ppermute | solution.py:71
  31.9 1.3 %right.2 = (f32[32,576]{1,0:T(8,128)S(1)}, f32[32,1152]{1,0:T(8,128)S(1)}, f32[32,128]{1,0:T(8,128)S(1)}) custom-call(s32[1]{0:T(128)} %bitcast.shard_ref, f32[32,1280]{1,0:T(8,128)S(1)} %join.2.whole, f32[2,288,1152]{2,1,0:T(8,128)S(1)} %get-tuple-element.124.corr, f32[288,1152]{1,0:T(8,128)S(1)} %collective-permute-done.7.other), custom_call_target="tpu_custom_call" | custom-call | flops 1000 | bytes 1000 | tf_op jit(solution)/shard_map/right/pallas_call | solution.py:410
  33.2 1.6 %collective-permute-start.8 = (f32[32,576]{1,0:T(8,128)S(1)}, f32[32,576]{1,0:T(8,128)S(1)}, u32[]{:S(2)}, u32[]{:S(2)}) collective-permute-start(f32[32,576]{1,0:T(8,128)S(1)} %get-tuple-element.143), channel_id=1, source_target_pairs={{0,4},{4,0},{8,12},{12,8},{16,20},{20,16},{24,28},{28,24},{1,5},{5... | collective-permute-start | bytes 221192 | tf_op jit(solution)/shard_map/ppermute | solution.py:71
  35.3 1.3 %inverse.2 = f32[2,32,32]{2,1,0:T(8,128)S(1)} custom-call(f32[32,1152]{1,0:T(8,128)S(1)} %get-tuple-element.145.ours.theirs, f32[32,1152]{1,0:T(8,128)S(1)} %get-tuple-element.145.ours.theirs), custom_call_target="tpu_custom_call" | custom-call | flops 1000 | bytes 6000000 | tf_op jit(solution)/shard_map/inverse/pallas_call | solution.py:478
  36.6 1.0 %collective-permute-done.8 = f32[32,576]{1,0:T(8,128)S(1)} collective-permute-done((f32[32,576]{1,0:T(8,128)S(1)}, f32[32,576]{1,0:T(8,128)S(1)}, u32[]{:S(2)}, u32[]{:S(2)}) %collective-permute-start.8) | collective-permute-done | bytes 73760 | tf_op jit(solution)/shard_map/ppermute | solution.py:71
  37.7 2.5 %collective-permute-start.9 = (f32[32,576]{1,0:T(8,128)S(1)}, f32[32,576]{1,0:T(8,128)S(1)}, u32[]{:S(2)}, u32[]{:S(2)}) collective-permute-start(f32[32,576]{1,0:T(8,128)S(1)} %add.46), channel_id=1, source_target_pairs={{0,8},{4,12},{8,0},{12,4},{16,24},{20,28},{24,16},{28,20},{1,9},{5... | collective-permute-start | bytes 221192 | tf_op jit(solution)/shard_map/ppermute | solution.py:71
  40.2 1.5 %collective-permute-start.19 = (f32[144,576]{1,0:T(8,128)S(1)}, f32[144,576]{1,0:T(8,128)S(1)}, u32[]{:S(2)}, u32[]{:S(2)}) collective-permute-start(f32[144,576]{1,0:T(8,128)S(1)} %collective-permute-done.6.refs_0_), channel_id=1, source_target_pairs={{0,4},{4,0},{8,12},{12,8},{16,20},{20,16},{24,28},{28,24},{1,5},{5... | collective-permute-start | bytes 995336 | tf_op jit(solution)/shard_map/ppermute | solution.py:71
  41.7 1.7 %collective-permute-done.9 = f32[32,576]{1,0:T(8,128)S(1)} collective-permute-done((f32[32,576]{1,0:T(8,128)S(1)}, f32[32,576]{1,0:T(8,128)S(1)}, u32[]{:S(2)}, u32[]{:S(2)}) %collective-permute-start.9) | collective-permute-done | bytes 73760 | tf_op jit(solution)/shard_map/ppermute | solution.py:71
  43.4 3.4 %collective-permute-start.12 = (f32[32,576]{1,0:T(8,128)S(1)}, f32[32,576]{1,0:T(8,128)S(1)}, u32[]{:S(2)}, u32[]{:S(2)}) collective-permute-start(f32[32,576]{1,0:T(8,128)S(1)} %add.47), channel_id=1, source_target_pairs={{0,16},{4,20},{8,24},{12,28},{16,0},{20,4},{24,8},{28,12},{1,17},{... | collective-permute-start | bytes 221192 | tf_op jit(solution)/shard_map/ppermute | solution.py:71
  46.9 1.9 %collective-permute-start.15 = (f32[72,576]{1,0:T(8,128)S(1)}, f32[72,576]{1,0:T(8,128)S(1)}, u32[]{:S(2)}, u32[]{:S(2)}) collective-permute-start(f32[72,576]{1,0:T(8,128)S(1)} %collective-permute-done.10.refs_0_), channel_id=1, source_target_pairs={{0,8},{4,12},{8,0},{12,4},{16,24},{20,28},{24,16},{28,20},{1,9},{5... | collective-permute-start | bytes 497672 | tf_op jit(solution)/shard_map/ppermute | solution.py:71
  48.8 1.5 %collective-permute-start.16 = (f32[72,576]{1,0:T(8,128)S(1)}, f32[72,576]{1,0:T(8,128)S(1)}, u32[]{:S(2)}, u32[]{:S(2)}) collective-permute-start(f32[72,576]{1,0:T(8,128)S(1)} %collective-permute-done.10.refs_0_), channel_id=1, source_target_pairs={{0,4},{4,0},{8,12},{12,8},{16,20},{20,16},{24,28},{28,24},{1,5},{5... | collective-permute-start | bytes 497672 | tf_op jit(solution)/shard_map/ppermute | solution.py:71
  50.3 2.4 %collective-permute-done.12 = f32[32,576]{1,0:T(8,128)S(1)} collective-permute-done((f32[32,576]{1,0:T(8,128)S(1)}, f32[32,576]{1,0:T(8,128)S(1)}, u32[]{:S(2)}, u32[]{:S(2)}) %collective-permute-start.12) | collective-permute-done | bytes 73760 | tf_op jit(solution)/shard_map/ppermute | solution.py:71
  52.8 1.2 %left.1 = (f32[16,1152]{1,0:T(8,128)S(1)}, f32[16,1152]{1,0:T(8,128)S(1)}) custom-call(s32[1]{0:T(128)} %bitcast.shard_ref, f32[32,576]{1,0:T(8,128)S(1)} %add.48.right, f32[2,32,32]{2,1,0:T(8,128)S(1)} %inverse.2, f32[2,288,1152]{2,1,0:T(8,128)S(1)} %get-tuple-element.124.corr, f32[288,1152]{1,0:T(8,128)S(1)} %collective-permute-done.7.other), custom_call_target="tpu_custom_call" | custom-call | flops 1000 | bytes 1000 | tf_op jit(solution)/shard_map/left/pallas_call | solution.py:432
  53.9 1.7 %collective-permute-start.13 = (f32[16,1152]{1,0:T(8,128)S(1)}, f32[16,1152]{1,0:T(8,128)S(1)}, u32[]{:S(2)}, u32[]{:S(2)}) collective-permute-start(f32[16,1152]{1,0:T(8,128)S(1)} %get-tuple-element.160), channel_id=1, source_target_pairs={{0,2},{1,3},{2,0},{3,1},{4,6},{5,7},{6,4},{7,5},{8,10},{9,11},{10,... | collective-permute-start | bytes 221192 | tf_op jit(solution)/shard_map/ppermute | solution.py:71
  55.6 2.7 %collective-permute-done.13 = f32[16,1152]{1,0:T(8,128)S(1)} collective-permute-done((f32[16,1152]{1,0:T(8,128)S(1)}, f32[16,1152]{1,0:T(8,128)S(1)}, u32[]{:S(2)}, u32[]{:S(2)}) %collective-permute-start.13) | collective-permute-done | bytes 73760 | tf_op jit(solution)/shard_map/ppermute | solution.py:71
  58.4 1.9 %collective-permute-start.14 = (f32[16,1152]{1,0:T(8,128)S(1)}, f32[16,1152]{1,0:T(8,128)S(1)}, u32[]{:S(2)}, u32[]{:S(2)}) collective-permute-start(f32[16,1152]{1,0:T(8,128)S(1)} %add.49), channel_id=1, source_target_pairs={{0,4},{4,0},{8,12},{12,8},{16,20},{20,16},{24,28},{28,24},{1,5},{5... | collective-permute-start | bytes 221192 | tf_op jit(solution)/shard_map/ppermute | solution.py:71
  61.0 1.8 %collective-permute-done.14 = f32[16,1152]{1,0:T(8,128)S(1)} collective-permute-done((f32[16,1152]{1,0:T(8,128)S(1)}, f32[16,1152]{1,0:T(8,128)S(1)}, u32[]{:S(2)}, u32[]{:S(2)}) %collective-permute-start.14) | collective-permute-done | bytes 73760 | tf_op jit(solution)/shard_map/ppermute | solution.py:71
  63.4 1.5 %collective-permute-start.22 = (f32[72,576]{1,0:T(8,128)S(1)}, f32[72,576]{1,0:T(8,128)S(1)}, u32[]{:S(2)}, u32[]{:S(2)}) collective-permute-start(f32[72,576]{1,0:T(8,128)S(1)} %collective-permute-done.15.refs_1_), channel_id=1, source_target_pairs={{0,4},{4,0},{8,12},{12,8},{16,20},{20,16},{24,28},{28,24},{1,5},{5... | collective-permute-start | bytes 497672 | tf_op jit(solution)/shard_map/ppermute | solution.py:71
  65.5 2.5 %collective-permute-done.17 = f32[16,1152]{1,0:T(8,128)S(1)} collective-permute-done((f32[16,1152]{1,0:T(8,128)S(1)}, f32[16,1152]{1,0:T(8,128)S(1)}, u32[]{:S(2)}, u32[]{:S(2)}) %collective-permute-start.17) | collective-permute-done | bytes 73760 | tf_op jit(solution)/shard_map/ppermute | solution.py:71
  68.0 1.4 %collective-permute-start.20 = (f32[16,1152]{1,0:T(8,128)S(1)}, f32[16,1152]{1,0:T(8,128)S(1)}, u32[]{:S(2)}, u32[]{:S(2)}) collective-permute-start(f32[16,1152]{1,0:T(8,128)S(1)} %add.51), channel_id=1, source_target_pairs={{0,16},{4,20},{8,24},{12,28},{16,0},{20,4},{24,8},{28,12},{1,17},{... | collective-permute-start | bytes 221192 | tf_op jit(solution)/shard_map/ppermute | solution.py:71
  69.8 4.2 %collective-permute-done.20 = f32[16,1152]{1,0:T(8,128)S(1)} collective-permute-done((f32[16,1152]{1,0:T(8,128)S(1)}, f32[16,1152]{1,0:T(8,128)S(1)}, u32[]{:S(2)}, u32[]{:S(2)}) %collective-permute-start.20) | collective-permute-done | bytes 73760 | tf_op jit(solution)/shard_map/ppermute | solution.py:71
  74.0 1.5 %collective-permute-start.21 = (f32[16,1152]{1,0:T(8,128)S(1)}, f32[16,1152]{1,0:T(8,128)S(1)}, u32[]{:S(2)}, u32[]{:S(2)}) collective-permute-start(f32[16,1152]{1,0:T(8,128)S(1)} %add.52.ours), channel_id=1, source_target_pairs={{0,2},{1,3},{2,0},{3,1},{4,6},{5,7},{6,4},{7,5},{8,10},{9,11},{10,... | collective-permute-start | bytes 221192 | tf_op jit(solution)/shard_map/ppermute | solution.py:71
  75.6 1.4 %collective-permute-start.25 = (f32[72,576]{1,0:T(8,128)S(1)}, f32[72,576]{1,0:T(8,128)S(1)}, u32[]{:S(2)}, u32[]{:S(2)}) collective-permute-start(f32[72,576]{1,0:T(8,128)S(1)} %collective-permute-done.18.refs_0_), channel_id=1, source_target_pairs={{0,4},{4,0},{8,12},{12,8},{16,20},{20,16},{24,28},{28,24},{1,5},{5... | collective-permute-start | bytes 497672 | tf_op jit(solution)/shard_map/ppermute | solution.py:71
  77.4 1.1 %collective-permute-done.21.got = f32[16,1152]{1,0:T(8,128)S(1)} collective-permute-done((f32[16,1152]{1,0:T(8,128)S(1)}, f32[16,1152]{1,0:T(8,128)S(1)}, u32[]{:S(2)}, u32[]{:S(2)}) %collective-permute-start.21) | collective-permute-done | bytes 73760 | tf_op jit(solution)/shard_map/ppermute | solution.py:71
  78.5 1.3 %right.3 = (f32[32,576]{1,0:T(8,128)S(1)}, f32[32,1280]{1,0:T(8,128)S(1)}) custom-call(s32[1]{0:T(128)} %bitcast.shard_ref, f32[32,1152]{1,0:T(8,128)S(1)} %join.3.whole, f32[2,288,1152]{2,1,0:T(8,128)S(1)} %get-tuple-element.124.corr, f32[288,1152]{1,0:T(8,128)S(1)} %collective-permute-done.7.other, f32[32,128]{1,0:T(8,128)S(1)} %get-tuple-element.194.refs_0_), custom_call_target="tpu_custom_call" | custom-call | flops 1000 | bytes 1000 | tf_op jit(solution)/shard_map/right/pallas_call | solution.py:410
  79.9 1.3 %collective-permute-start.23 = (f32[32,576]{1,0:T(8,128)S(1)}, f32[32,576]{1,0:T(8,128)S(1)}, u32[]{:S(2)}, u32[]{:S(2)}) collective-permute-start(f32[32,576]{1,0:T(8,128)S(1)} %get-tuple-element.197), channel_id=1, source_target_pairs={{0,4},{4,0},{8,12},{12,8},{16,20},{20,16},{24,28},{28,24},{1,5},{5... | collective-permute-start | bytes 221192 | tf_op jit(solution)/shard_map/ppermute | solution.py:71
  81.5 3.3 %collective-permute-done.23 = f32[32,576]{1,0:T(8,128)S(1)} collective-permute-done((f32[32,576]{1,0:T(8,128)S(1)}, f32[32,576]{1,0:T(8,128)S(1)}, u32[]{:S(2)}, u32[]{:S(2)}) %collective-permute-start.23) | collective-permute-done | bytes 73760 | tf_op jit(solution)/shard_map/ppermute | solution.py:71
  85.4 1.0 collective-permute-start.30
  87.2 2.1 %collective-permute-done.27 = f32[32,576]{1,0:T(8,128)S(1)} collective-permute-done((f32[32,576]{1,0:T(8,128)S(1)}, f32[32,576]{1,0:T(8,128)S(1)}, u32[]{:S(2)}, u32[]{:S(2)}) %collective-permute-start.27) | collective-permute-done | bytes 73760 | tf_op jit(solution)/shard_map/ppermute | solution.py:71
  89.3 2.0 %collective-permute-start.28 = (f32[32,576]{1,0:T(8,128)S(1)}, f32[32,576]{1,0:T(8,128)S(1)}, u32[]{:S(2)}, u32[]{:S(2)}) collective-permute-start(f32[32,576]{1,0:T(8,128)S(1)} %add.54), channel_id=1, source_target_pairs={{0,16},{4,20},{8,24},{12,28},{16,0},{20,4},{24,8},{28,12},{1,17},{... | collective-permute-start | bytes 221192 | tf_op jit(solution)/shard_map/ppermute | solution.py:71
  91.3 1.3 %inverse.3 = f32[2,32,32]{2,1,0:T(8,128)S(1)} custom-call(f32[32,1280]{1,0:T(8,128)S(1)} %get-tuple-element.217.ours, f32[32,1280]{1,0:T(8,128)S(1)} %collective-permute-done.26.got.theirs), custom_call_target="tpu_custom_call" | custom-call | flops 1000 | bytes 6000000 | tf_op jit(solution)/shard_map/inverse/pallas_call | solution.py:478
  92.6 0.8 insert.14.refs_1_
  93.4 2.2 %collective-permute-done.28 = f32[32,576]{1,0:T(8,128)S(1)} collective-permute-done((f32[32,576]{1,0:T(8,128)S(1)}, f32[32,576]{1,0:T(8,128)S(1)}, u32[]{:S(2)}, u32[]{:S(2)}) %collective-permute-start.28) | collective-permute-done | bytes 73760 | tf_op jit(solution)/shard_map/ppermute | solution.py:71
  95.7 1.3 %collective-permute-done.29.their_right = f32[32,576]{1,0:T(8,128)S(1)} collective-permute-done((f32[32,576]{1,0:T(8,128)S(1)}, f32[32,576]{1,0:T(8,128)S(1)}, u32[]{:S(2)}, u32[]{:S(2)}) %collective-permute-start.29) | collective-permute-done | bytes 73760 | tf_op jit(solution)/shard_map/ppermute | solution.py:71
  97.3 3.5 %finish.1 = (f32[288,1152]{1,0:T(8,128)}, f32[288,1152]{1,0:T(8,128)}, f32[288,1152]{1,0:T(8,128)}, f32[288,1152]{1,0:T(8,128)}, f32[144,288]{1,0:T(8,128)}, /*index=5*/f32[144,288]{1,0:T(8,128)}) custom-call(s32[1]{0:T(128)} %bitcast.shard_ref, f32[2,288,1152]{2,1,0:T(8,128)S(1)} %get-tuple-element.124.corr, f32[576,1152]{1,0:T(8,128)S(1)} %insert.15.rows, ...), custom_call_target="tpu_custom_call" | custom-call | tf_op jit(solution)/shard_map/finish/pallas_call | solution.py:548
  (59 shorter events, 7.4 us)
Async XLA Ops:
  0.6 8.5 %copy-start = (f32[144,288]{1,0:T(8,128)S(1)}, f32[144,288]{1,0:T(8,128)}, u32[]{:S(2)}) copy-start(f32[144,288]{1,0:T(8,128)} %moment_q.3) | copy-start | bytes 497668
  0.7 8.5 %copy-start.1 = (f32[144,288]{1,0:T(8,128)S(1)}, f32[144,288]{1,0:T(8,128)}, u32[]{:S(2)}) copy-start(f32[144,288]{1,0:T(8,128)} %moment_o.3) | copy-start | bytes 497668
  0.7 8.5 %copy-start.2 = (f32[144,288]{1,0:T(8,128)S(1)}, f32[144,288]{1,0:T(8,128)}, u32[]{:S(2)}) copy-start(f32[144,288]{1,0:T(8,128)} %weight_q.1) | copy-start | bytes 497668
  0.7 8.5 %copy-start.3 = (f32[144,288]{1,0:T(8,128)S(1)}, f32[144,288]{1,0:T(8,128)}, u32[]{:S(2)}) copy-start(f32[144,288]{1,0:T(8,128)} %weight_o.1) | copy-start | bytes 497668
  4.5 1.5 %collective-permute-start = (f32[32,1280]{1,0:T(8,128)S(1)}, f32[32,1280]{1,0:T(8,128)S(1)}, u32[]{:S(2)}, u32[]{:S(2)}) collective-permute-start(f32[32,1280]{1,0:T(8,128)S(1)} %get-tuple-element.126), channel_id=1, source_target_pairs={{0,1},{1,0},{2,3},{3,2},{4,5},{5,4},{6,7},{7,6},{8,9},{9,8},{10,11... | collective-permute-start | bytes 491528 | tf_op jit(solution)/shard_map/ppermute | solution.py:71
  6.1 25.8 %collective-permute-start.7 = (f32[288,1152]{1,0:T(8,128)S(1)}, f32[288,1152]{1,0:T(8,128)S(1)}, u32[]{:S(2)}, u32[]{:S(2)}) collective-permute-start(f32[288,1152]{1,0:T(8,128)S(1)} %get-tuple-element.138), channel_id=1, source_target_pairs={{0,1},{1,0},{2,3},{3,2},{4,5},{5,4},{6,7},{7,6},{8,9},{9,8},{10,11... | collective-permute-start | bytes 3981320 | tf_op jit(solution)/shard_map/ppermute | solution.py:71
  6.5 5.6 %collective-permute-start.1 = (f32[16,1280]{1,0:T(8,128)S(1)}, f32[16,1280]{1,0:T(8,128)S(1)}, u32[]{:S(2)}, u32[]{:S(2)}) collective-permute-start(f32[16,1280]{1,0:T(8,128)S(1)} %get-tuple-element.132), channel_id=1, source_target_pairs={{0,2},{1,3},{2,0},{3,1},{4,6},{5,7},{6,4},{7,5},{8,10},{9,11},{10,... | collective-permute-start | bytes 245768 | tf_op jit(solution)/shard_map/ppermute | solution.py:71
  9.3 22.5 %collective-permute-start.6 = (f32[144,576]{1,0:T(8,128)S(1)}, f32[144,576]{1,0:T(8,128)S(1)}, u32[]{:S(2)}, u32[]{:S(2)}) collective-permute-start(f32[144,576]{1,0:T(8,128)S(1)} %get-tuple-element.147.refs_0_), channel_id=1, source_target_pairs={{0,8},{4,12},{8,0},{12,4},{16,24},{20,28},{24,16},{28,20},{1,9},{5... | collective-permute-start | bytes 995336 | tf_op jit(solution)/shard_map/ppermute | solution.py:71
  12.2 4.5 %collective-permute-start.2 = (f32[16,1280]{1,0:T(8,128)S(1)}, f32[16,1280]{1,0:T(8,128)S(1)}, u32[]{:S(2)}, u32[]{:S(2)}) collective-permute-start(f32[16,1280]{1,0:T(8,128)S(1)} %add.42), channel_id=1, source_target_pairs={{0,4},{4,0},{8,12},{12,8},{16,20},{20,16},{24,28},{28,24},{1,5},{5... | collective-permute-start | bytes 245768 | tf_op jit(solution)/shard_map/ppermute | solution.py:71
  16.7 5.0 %collective-permute-start.3 = (f32[16,1280]{1,0:T(8,128)S(1)}, f32[16,1280]{1,0:T(8,128)S(1)}, u32[]{:S(2)}, u32[]{:S(2)}) collective-permute-start(f32[16,1280]{1,0:T(8,128)S(1)} %add.43), channel_id=1, source_target_pairs={{0,8},{4,12},{8,0},{12,4},{16,24},{20,28},{24,16},{28,20},{1,9},{5... | collective-permute-start | bytes 245768 | tf_op jit(solution)/shard_map/ppermute | solution.py:71
  18.6 24.9 %collective-permute-start.11 = (f32[144,576]{1,0:T(8,128)S(1)}, f32[144,576]{1,0:T(8,128)S(1)}, u32[]{:S(2)}, u32[]{:S(2)}) collective-permute-start(f32[144,576]{1,0:T(8,128)S(1)} %get-tuple-element.147.refs_0_), channel_id=1, source_target_pairs={{0,4},{4,0},{8,12},{12,8},{16,20},{20,16},{24,28},{28,24},{1,5},{5... | collective-permute-start | bytes 995336 | tf_op jit(solution)/shard_map/ppermute | solution.py:71
  21.7 5.6 %collective-permute-start.4 = (f32[16,1280]{1,0:T(8,128)S(1)}, f32[16,1280]{1,0:T(8,128)S(1)}, u32[]{:S(2)}, u32[]{:S(2)}) collective-permute-start(f32[16,1280]{1,0:T(8,128)S(1)} %add.44), channel_id=1, source_target_pairs={{0,16},{4,20},{8,24},{12,28},{16,0},{20,4},{24,8},{28,12},{1,17},{... | collective-permute-start | bytes 245768 | tf_op jit(solution)/shard_map/ppermute | solution.py:71
  27.3 4.5 %collective-permute-start.5 = (f32[16,1280]{1,0:T(8,128)S(1)}, f32[16,1280]{1,0:T(8,128)S(1)}, u32[]{:S(2)}, u32[]{:S(2)}) collective-permute-start(f32[16,1280]{1,0:T(8,128)S(1)} %add.45.ours), channel_id=1, source_target_pairs={{0,2},{1,3},{2,0},{3,1},{4,6},{5,7},{6,4},{7,5},{8,10},{9,11},{10,... | collective-permute-start | bytes 245768 | tf_op jit(solution)/shard_map/ppermute | solution.py:71
  28.4 15.0 %collective-permute-start.10 = (f32[72,576]{1,0:T(8,128)S(1)}, f32[72,576]{1,0:T(8,128)S(1)}, u32[]{:S(2)}, u32[]{:S(2)}) collective-permute-start(f32[72,576]{1,0:T(8,128)S(1)} %get-tuple-element.151), channel_id=1, source_target_pairs={{0,16},{4,20},{8,24},{12,28},{16,0},{20,4},{24,8},{28,12},{1,17},{... | collective-permute-start | bytes 497672 | tf_op jit(solution)/shard_map/ppermute | solution.py:71
  33.2 4.5 %collective-permute-start.8 = (f32[32,576]{1,0:T(8,128)S(1)}, f32[32,576]{1,0:T(8,128)S(1)}, u32[]{:S(2)}, u32[]{:S(2)}) collective-permute-start(f32[32,576]{1,0:T(8,128)S(1)} %get-tuple-element.143), channel_id=1, source_target_pairs={{0,4},{4,0},{8,12},{12,8},{16,20},{20,16},{24,28},{28,24},{1,5},{5... | collective-permute-start | bytes 221192 | tf_op jit(solution)/shard_map/ppermute | solution.py:71
  37.7 5.7 %collective-permute-start.9 = (f32[32,576]{1,0:T(8,128)S(1)}, f32[32,576]{1,0:T(8,128)S(1)}, u32[]{:S(2)}, u32[]{:S(2)}) collective-permute-start(f32[32,576]{1,0:T(8,128)S(1)} %add.46), channel_id=1, source_target_pairs={{0,8},{4,12},{8,0},{12,4},{16,24},{20,28},{24,16},{28,20},{1,9},{5... | collective-permute-start | bytes 221192 | tf_op jit(solution)/shard_map/ppermute | solution.py:71
  40.2 27.9 %collective-permute-start.19 = (f32[144,576]{1,0:T(8,128)S(1)}, f32[144,576]{1,0:T(8,128)S(1)}, u32[]{:S(2)}, u32[]{:S(2)}) collective-permute-start(f32[144,576]{1,0:T(8,128)S(1)} %collective-permute-done.6.refs_0_), channel_id=1, source_target_pairs={{0,4},{4,0},{8,12},{12,8},{16,20},{20,16},{24,28},{28,24},{1,5},{5... | collective-permute-start | bytes 995336 | tf_op jit(solution)/shard_map/ppermute | solution.py:71
  43.4 9.3 %collective-permute-start.12 = (f32[32,576]{1,0:T(8,128)S(1)}, f32[32,576]{1,0:T(8,128)S(1)}, u32[]{:S(2)}, u32[]{:S(2)}) collective-permute-start(f32[32,576]{1,0:T(8,128)S(1)} %add.47), channel_id=1, source_target_pairs={{0,16},{4,20},{8,24},{12,28},{16,0},{20,4},{24,8},{28,12},{1,17},{... | collective-permute-start | bytes 221192 | tf_op jit(solution)/shard_map/ppermute | solution.py:71
  46.9 15.9 %collective-permute-start.15 = (f32[72,576]{1,0:T(8,128)S(1)}, f32[72,576]{1,0:T(8,128)S(1)}, u32[]{:S(2)}, u32[]{:S(2)}) collective-permute-start(f32[72,576]{1,0:T(8,128)S(1)} %collective-permute-done.10.refs_0_), channel_id=1, source_target_pairs={{0,8},{4,12},{8,0},{12,4},{16,24},{20,28},{24,16},{28,20},{1,9},{5... | collective-permute-start | bytes 497672 | tf_op jit(solution)/shard_map/ppermute | solution.py:71
  48.8 14.0 %collective-permute-start.16 = (f32[72,576]{1,0:T(8,128)S(1)}, f32[72,576]{1,0:T(8,128)S(1)}, u32[]{:S(2)}, u32[]{:S(2)}) collective-permute-start(f32[72,576]{1,0:T(8,128)S(1)} %collective-permute-done.10.refs_0_), channel_id=1, source_target_pairs={{0,4},{4,0},{8,12},{12,8},{16,20},{20,16},{24,28},{28,24},{1,5},{5... | collective-permute-start | bytes 497672 | tf_op jit(solution)/shard_map/ppermute | solution.py:71
  53.9 4.4 %collective-permute-start.13 = (f32[16,1152]{1,0:T(8,128)S(1)}, f32[16,1152]{1,0:T(8,128)S(1)}, u32[]{:S(2)}, u32[]{:S(2)}) collective-permute-start(f32[16,1152]{1,0:T(8,128)S(1)} %get-tuple-element.160), channel_id=1, source_target_pairs={{0,2},{1,3},{2,0},{3,1},{4,6},{5,7},{6,4},{7,5},{8,10},{9,11},{10,... | collective-permute-start | bytes 221192 | tf_op jit(solution)/shard_map/ppermute | solution.py:71
  55.6 12.4 %collective-permute-start.18 = (f32[72,576]{1,0:T(8,128)S(1)}, f32[72,576]{1,0:T(8,128)S(1)}, u32[]{:S(2)}, u32[]{:S(2)}) collective-permute-start(f32[72,576]{1,0:T(8,128)S(1)} %get-tuple-element.177), channel_id=1, source_target_pairs={{0,16},{4,20},{8,24},{12,28},{16,0},{20,4},{24,8},{28,12},{1,17},{... | collective-permute-start | bytes 497672 | tf_op jit(solution)/shard_map/ppermute | solution.py:71
  58.4 4.4 %collective-permute-start.14 = (f32[16,1152]{1,0:T(8,128)S(1)}, f32[16,1152]{1,0:T(8,128)S(1)}, u32[]{:S(2)}, u32[]{:S(2)}) collective-permute-start(f32[16,1152]{1,0:T(8,128)S(1)} %add.49), channel_id=1, source_target_pairs={{0,4},{4,0},{8,12},{12,8},{16,20},{20,16},{24,28},{28,24},{1,5},{5... | collective-permute-start | bytes 221192 | tf_op jit(solution)/shard_map/ppermute | solution.py:71
  62.8 5.2 %collective-permute-start.17 = (f32[16,1152]{1,0:T(8,128)S(1)}, f32[16,1152]{1,0:T(8,128)S(1)}, u32[]{:S(2)}, u32[]{:S(2)}) collective-permute-start(f32[16,1152]{1,0:T(8,128)S(1)} %add.50), channel_id=1, source_target_pairs={{0,8},{4,12},{8,0},{12,4},{16,24},{20,28},{24,16},{28,20},{1,9},{5... | collective-permute-start | bytes 221192 | tf_op jit(solution)/shard_map/ppermute | solution.py:71
  63.4 15.1 %collective-permute-start.22 = (f32[72,576]{1,0:T(8,128)S(1)}, f32[72,576]{1,0:T(8,128)S(1)}, u32[]{:S(2)}, u32[]{:S(2)}) collective-permute-start(f32[72,576]{1,0:T(8,128)S(1)} %collective-permute-done.15.refs_1_), channel_id=1, source_target_pairs={{0,4},{4,0},{8,12},{12,8},{16,20},{20,16},{24,28},{28,24},{1,5},{5... | collective-permute-start | bytes 497672 | tf_op jit(solution)/shard_map/ppermute | solution.py:71
  68.0 6.0 %collective-permute-start.20 = (f32[16,1152]{1,0:T(8,128)S(1)}, f32[16,1152]{1,0:T(8,128)S(1)}, u32[]{:S(2)}, u32[]{:S(2)}) collective-permute-start(f32[16,1152]{1,0:T(8,128)S(1)} %add.51), channel_id=1, source_target_pairs={{0,16},{4,20},{8,24},{12,28},{16,0},{20,4},{24,8},{28,12},{1,17},{... | collective-permute-start | bytes 221192 | tf_op jit(solution)/shard_map/ppermute | solution.py:71
  74.0 4.4 %collective-permute-start.21 = (f32[16,1152]{1,0:T(8,128)S(1)}, f32[16,1152]{1,0:T(8,128)S(1)}, u32[]{:S(2)}, u32[]{:S(2)}) collective-permute-start(f32[16,1152]{1,0:T(8,128)S(1)} %add.52.ours), channel_id=1, source_target_pairs={{0,2},{1,3},{2,0},{3,1},{4,6},{5,7},{6,4},{7,5},{8,10},{9,11},{10,... | collective-permute-start | bytes 221192 | tf_op jit(solution)/shard_map/ppermute | solution.py:71
  75.6 9.2 %collective-permute-start.24 = (f32[72,576]{1,0:T(8,128)S(1)}, f32[72,576]{1,0:T(8,128)S(1)}, u32[]{:S(2)}, u32[]{:S(2)}) collective-permute-start(f32[72,576]{1,0:T(8,128)S(1)} %collective-permute-done.18.refs_0_), channel_id=1, source_target_pairs={{0,8},{4,12},{8,0},{12,4},{16,24},{20,28},{24,16},{28,20},{1,9},{5... | collective-permute-start | bytes 497672 | tf_op jit(solution)/shard_map/ppermute | solution.py:71
  75.6 9.2 %collective-permute-start.25 = (f32[72,576]{1,0:T(8,128)S(1)}, f32[72,576]{1,0:T(8,128)S(1)}, u32[]{:S(2)}, u32[]{:S(2)}) collective-permute-start(f32[72,576]{1,0:T(8,128)S(1)} %collective-permute-done.18.refs_0_), channel_id=1, source_target_pairs={{0,4},{4,0},{8,12},{12,8},{16,20},{20,16},{24,28},{28,24},{1,5},{5... | collective-permute-start | bytes 497672 | tf_op jit(solution)/shard_map/ppermute | solution.py:71
  79.8 5.0 %collective-permute-start.26 = (f32[32,1280]{1,0:T(8,128)S(1)}, f32[32,1280]{1,0:T(8,128)S(1)}, u32[]{:S(2)}, u32[]{:S(2)}) collective-permute-start(f32[32,1280]{1,0:T(8,128)S(1)} %get-tuple-element.217.ours), channel_id=1, source_target_pairs={{0,1},{1,0},{2,3},{3,2},{4,5},{5,4},{6,7},{7,6},{8,9},{9,8},{10,11... | collective-permute-start | bytes 491528 | tf_op jit(solution)/shard_map/ppermute | solution.py:71
  79.9 6.6 %copy-start.4 = (f32[72]{0:T(128)S(1)}, f32[72]{0:T(128)}, u32[]{:S(2)}) copy-start(f32[72]{0:T(128)} %param.24) | copy-start | bytes 868
  79.9 4.8 %collective-permute-start.23 = (f32[32,576]{1,0:T(8,128)S(1)}, f32[32,576]{1,0:T(8,128)S(1)}, u32[]{:S(2)}, u32[]{:S(2)}) collective-permute-start(f32[32,576]{1,0:T(8,128)S(1)} %get-tuple-element.197), channel_id=1, source_target_pairs={{0,4},{4,0},{8,12},{12,8},{16,20},{20,16},{24,28},{28,24},{1,5},{5... | collective-permute-start | bytes 221192 | tf_op jit(solution)/shard_map/ppermute | solution.py:71
  84.8 4.5 %collective-permute-start.27 = (f32[32,576]{1,0:T(8,128)S(1)}, f32[32,576]{1,0:T(8,128)S(1)}, u32[]{:S(2)}, u32[]{:S(2)}) collective-permute-start(f32[32,576]{1,0:T(8,128)S(1)} %add.53), channel_id=1, source_target_pairs={{0,8},{4,12},{8,0},{12,4},{16,24},{20,28},{24,16},{28,20},{1,9},{5... | collective-permute-start | bytes 221192 | tf_op jit(solution)/shard_map/ppermute | solution.py:71
  85.4 10.3 %collective-permute-start.30 = (f32[72,576]{1,0:T(8,128)S(1)}, f32[72,576]{1,0:T(8,128)S(1)}, u32[]{:S(2)}, u32[]{:S(2)}) collective-permute-start(f32[72,576]{1,0:T(8,128)S(1)} %collective-permute-done.24.refs_1_), channel_id=1, source_target_pairs={{0,4},{4,0},{8,12},{12,8},{16,20},{20,16},{24,28},{28,24},{1,5},{5... | collective-permute-start | bytes 497672 | tf_op jit(solution)/shard_map/ppermute | solution.py:71
  89.3 6.3 %collective-permute-start.28 = (f32[32,576]{1,0:T(8,128)S(1)}, f32[32,576]{1,0:T(8,128)S(1)}, u32[]{:S(2)}, u32[]{:S(2)}) collective-permute-start(f32[32,576]{1,0:T(8,128)S(1)} %add.54), channel_id=1, source_target_pairs={{0,16},{4,20},{8,24},{12,28},{16,0},{20,4},{24,8},{28,12},{1,17},{... | collective-permute-start | bytes 221192 | tf_op jit(solution)/shard_map/ppermute | solution.py:71
  95.6 1.3 %collective-permute-start.29 = (f32[32,576]{1,0:T(8,128)S(1)}, f32[32,576]{1,0:T(8,128)S(1)}, u32[]{:S(2)}, u32[]{:S(2)}) collective-permute-start(f32[32,576]{1,0:T(8,128)S(1)} %add.55.right), channel_id=1, source_target_pairs={{0,1},{1,0},{2,3},{3,2},{4,5},{5,4},{6,7},{7,6},{8,9},{9,8},{10,11... | collective-permute-start | bytes 221192 | tf_op jit(solution)/shard_map/ppermute | solution.py:71

commit v10 on v9

--- a/solution.py
+++ b/solution.py
@@ -10,6 +10,7 @@
 ROUNDS = 2
 GROUP = 8
 LANES = 128
+MEETINGS = (1, 2)
 
 highest = lax.Precision.HIGHEST
 decay_rate = 0.9
@@ -91,6 +92,8 @@
                 give, along = lax.optimization_barrier((give, along))
                 partner = swap(along, "shard", mask, n_shard)
             keep = gather.after(gather.before(keep, stage, "core"), stage, "core")
+    if stage in MEETINGS:
+        gather.meet(stage, keep)
     part = sum_over(keep + got, n_rep, gather, stage)
     for mask in reversed(halves(n_shard)[1:]):
         part = gather.start_tasks(part, stage, "x")
@@ -149,8 +152,8 @@
     PLAN = (
         ("near", "own", 2, (0, "core"), (0, "joined")),
         ("turned", "own", 1, (0, 1), (1, 4)),
-        ("far_a", "own_a", 4, (0, 4), (1, 4)),
-        ("turned_near", "near", 1, (1, 1), (2, 4)),
+        ("far_a", "own_a", 4, (0, 4), (1, 2)),
+        ("turned_near", "near", 1, (1, 1), (2, 2)),
         ("last_a", "far_a", 2, (1, 2), (2, 2)),
         ("turned_far_a", "far_a", 1, (1, 2), (2, 2)),
         ("far_b", "own_b", 4, (2, "begin"), (2, 4)),
@@ -175,8 +178,9 @@
         skipped = self.blocks["own"].shape[0] - self.blocks[name].shape[0]
         return self.PLACES[whole], skipped if name.endswith("_b") else 0
 
-    def __init__(self, own, own_a, own_b, place, count):
+    def __init__(self, own, own_a, own_b, place, count, n_shard):
         self.count = count
+        self.n_shard = n_shard
         self.place = place
         self.blocks = {"own": own, "own_a": own_a, "own_b": own_b}
         self.paired = count == 8 and own.shape[0] % 16 == 0
@@ -190,6 +194,12 @@
             for name, source, mask, after, _ in self.PLAN:
                 if after == point:
                     self.blocks[name] = swap(self.blocks[source], "rep", mask, self.count)
+
+    def meet(self, stage, array):
+        self.tasks[stage, 4] = (functools.partial(swap, axis="shard", mask=1, count=self.n_shard), array)
+
+    def met(self, stage):
+        return [self.results[stage, 4]] if stage in MEETINGS else []
 
     def start_tasks(self, value, stage, mask):
         point = (stage, mask)
@@ -391,9 +401,9 @@
     return jnp.concatenate([corr[shard_ref[0] & 1], other[...]], axis=0)
 
 
-def right_kernel(count, shard_ref, whole, corr, other, *refs):
+def right_kernel(count, waits, shard_ref, whole, corr, other, *refs):
     size = corr.shape[2]
-    right, left, *extra = refs[count:]
+    right, left, *extra = refs[count + waits :]
     left[:, :size] = whole[:, :size]
     if count:
         left[:, size:] = refs[0][...]
@@ -402,23 +412,24 @@
     right[...] = stacked(whole[:, :size], both_shares(shard_ref, corr, other), NT)
 
 
-def right_of(whole, shard, corr, other, *more):
+def right_of(whole, shard, corr, other, more, waits):
     rank = whole.shape[0]
     width, size = other.shape
     beside = whole.shape[1] - size
     shapes = [(rank, 2 * width), (rank, size + sum(array.shape[1] for array in more))] + ([(rank, beside)] if beside else [])
     return pl.pallas_call(
-        functools.partial(right_kernel, len(more)),
-        in_specs=[IN_SMEM] + [IN_VMEM] * (3 + len(more)),
+        functools.partial(right_kernel, len(more), len(waits)),
+        in_specs=[IN_SMEM] + [IN_VMEM] * (3 + len(more) + len(waits)),
         out_specs=[IN_VMEM] * len(shapes),
         out_shape=[pltpu.VMEM(shape, f32) for shape in shapes],
         compiler_params=SMALL,
         cost_estimate=QUICK,
         name="right",
-    )(shard, whole, *hold(pltpu.VMEM, corr, other), *more)
-
-
-def left_kernel(mask, shard_ref, right, inverse, corr, other, keep, give):
+    )(shard, whole, *hold(pltpu.VMEM, corr, other), *more, *waits)
+
+
+def left_kernel(mask, shard_ref, right, inverse, corr, other, *refs):
+    keep, give = refs[-2:]
     basis = exact(inverse[0], right[...], NN)
     part = stacked(basis, both_shares(shard_ref, corr, other), NN)
     half = part.shape[0] // 2
@@ -427,17 +438,17 @@
     give[...] = jnp.where(high, part[:half], part[half:])
 
 
-def left_of(right, inverse, shard, mask, corr, other):
+def left_of(right, inverse, shard, mask, corr, other, waits):
     half = pltpu.VMEM((right.shape[0] // 2, other.shape[1]), f32)
     return pl.pallas_call(
         functools.partial(left_kernel, mask),
-        in_specs=[IN_SMEM] + [IN_VMEM] * 4,
+        in_specs=[IN_SMEM] + [IN_VMEM] * (4 + len(waits)),
         out_specs=[IN_VMEM] * 2,
         out_shape=[half, half],
         compiler_params=SMALL,
         cost_estimate=QUICK,
         name="left",
-    )(shard, right, inverse, *hold(pltpu.VMEM, corr, other))
+    )(shard, right, inverse, *hold(pltpu.VMEM, corr, other), *waits)
 
 
 def eliminate(gram_q, gram_o, rank):
@@ -586,7 +597,7 @@
     place = lax.axis_index("rep").astype(jnp.int32).reshape(1)
     shard = lax.axis_index("shard").astype(jnp.int32).reshape(1)
 
-    gather = Gather(*base_of(q_weight, q_moment, o_weight, o_moment), place, n_rep)
+    gather = Gather(*base_of(q_weight, q_moment, o_weight, o_moment), place, n_rep, n_shard)
     norm_moment, norm_weight = norm_moment.reshape(1, -1), norm_weight.reshape(1, -1)
     norms = (norm_grads[0], norm_moment, norm_weight)
     corr, give_corr, keep, give = first((q_grad[0].T, o_grad[0].T), (q_error[0].T, o_error[0].T), (q_basis.T, o_basis.T), norms, place, shard, n_shard)
@@ -602,17 +613,19 @@
             whole, other_corr = sum_over_all(keep, give, shard, masks, n_rep, n_shard, gather, 0, give_corr)
         else:
             whole, _ = sum_over_all(keep, give, shard, masks[1:], n_rep, n_shard, gather, 2 * sweep)
-        right, left, *beside = right_of(whole, shard, corr, other_corr, *([norms] if last else []))
+        right, left, *beside = right_of(whole, shard, corr, other_corr, [norms] if last else [], gather.met(2 * sweep))
         if sweep == 0:
             (norms,) = beside
-        theirs = swap(left, "shard", masks[0], n_shard) if last else left
-        gather.tasks[2 * sweep + 1, 4 if last else 1] = (functools.partial(inverse_of, size=size), left, theirs)
+        theirs = swap(left, "shard", masks[0], n_shard)
+        gather.tasks[2 * sweep + 1, 4 if last else 2] = (functools.partial(inverse_of, size=size), left, theirs)
         if last:
             gather.tasks[3, 2] = (ending, left, theirs)
+        if 2 * sweep + 1 in MEETINGS:
+            gather.meet(2 * sweep + 1, keep)
         right = sum_over(right, n_rep, gather, 2 * sweep + 1)
-        inverse = gather.results[2 * sweep + 1, 4 if last else 1]
+        inverse = gather.results[2 * sweep + 1, 4 if last else 2]
         if not last:
-            keep, give = left_of(right, inverse, shard, masks[1], corr, other_corr)
+            keep, give = left_of(right, inverse, shard, masks[1], corr, other_corr, gather.met(1))
     their_right = swap(right, "shard", masks[0], n_shard)
     (norm_moment_new, norm_weight_new), *terms = gather.results[3, 2]
     if gather.paired:

time: 101 us -> 98.5 us (0.975)
  starting transfers between devices: 44.4 us -> 41.4 us
    ppermute x31 -> x34, starting transfers between devices: 44.4 us -> 41.4 us  [swap(): return lax.ppermute(block, axis, pairs)]
    ppermute x31 -> x34, waiting for transfers between devices: 36.4 us -> 37 us  [swap(): return lax.ppermute(block, axis, pairs)]
  transfers between devices with their start and end apart: 31 -> 34, of which waited for: 18 -> 18; matrix products, arithmetic and copies ran while one was open for 0% -> 0% of each run, Pallas kernels for 11% -> 11%
where the time goes in v10:
time: 98.5 us; the launch traced here: 98.4 us
  starting transfers between devices  41.4 us (42%)
  waiting for transfers between devices  37 us (38%)
  Pallas kernels  18.7 us (19%)
  between operations  1.02 us (1%)
    ppermute x34, starting transfers between devices, swap(): return lax.ppermute(block, axis, pairs)  41.4 us
    ppermute x34, waiting for transfers between devices, swap(): return lax.ppermute(block, axis, pairs)  37 us
    pallas_call x8, Pallas kernels, insert(): pl.pallas_call(functools.partial(insert_kernel, masks, rows_each), in_spe...  4.11 us
    pallas_call x1, Pallas kernels, first(): pl.pallas_call(functools.partial(first_kernel, n_shard), in_specs=[IN_SME...  3.85 us
    pallas_call x1, Pallas kernels, finish(): pl.pallas_call(functools.partial(finish_kernel, chunks), in_specs=[IN_SME...  3.46 us
    pallas_call x2, Pallas kernels, right_of(): pl.pallas_call(functools.partial(right_kernel, len(more), len(waits)), in...  2.62 us
    pallas_call x2, Pallas kernels, inverse_of(): pl.pallas_call(functools.partial(inverse_kernel, size), out_shape=pltpu.V...  2.6 us
  transfers between devices with their start and end apart: 34, of which 18 were waited for; matrix products, arithmetic and copies ran while one was open for 0% of the time, Pallas kernels for 11%

profile of v10, /device:TPU:0, one launch (start us, length us, event | category | flops | bytes accessed | tf_op | source)
XLA Modules:
  0.0 98.4 jit_solution(221739795945572669)
XLA Ops:
  0.7 3.9 %first.1 = (f32[2,288,1152]{2,1,0:T(8,128)S(1)}, f32[288,1152]{1,0:T(8,128)S(1)}, f32[32,1280]{1,0:T(8,128)S(1)}, f32[32,1280]{1,0:T(8,128)S(1)}) custom-call(s32[1]{0:T(128)} %bitcast.1.place_ref, s32[1]{0:T(128)} %bitcast.shard_ref, f32[288,1152]{1,0:T(8,128)} %bitcast.31, f32[288,1152]{1,0:T(8,128)} %bitcast.32, f32[288,1152]{1,0:T(8,128)} %bitcast.33, ...), custom_call_target="tpu_custom_call" | custom-call | tf_op jit(solution)/shard_map/first/pallas_call | solution.py:383
  5.1 1.0 %collective-permute-done.got = f32[32,1280]{1,0:T(8,128)S(1)} collective-permute-done((f32[32,1280]{1,0:T(8,128)S(1)}, f32[32,1280]{1,0:T(8,128)S(1)}, u32[]{:S(2)}, u32[]{:S(2)}) %collective-permute-start) | collective-permute-done | bytes 163872 | tf_op jit(solution)/shard_map/ppermute | solution.py:72
  6.5 2.6 %collective-permute-start.1 = (f32[16,1280]{1,0:T(8,128)S(1)}, f32[16,1280]{1,0:T(8,128)S(1)}, u32[]{:S(2)}, u32[]{:S(2)}) collective-permute-start(f32[16,1280]{1,0:T(8,128)S(1)} %get-tuple-element.140), channel_id=1, source_target_pairs={{0,2},{1,3},{2,0},{3,1},{4,6},{5,7},{6,4},{7,5},{8,10},{9,11},{10,... | collective-permute-start | bytes 245768 | tf_op jit(solution)/shard_map/ppermute | solution.py:72
  9.3 1.6 %collective-permute-start.6 = (f32[144,576]{1,0:T(8,128)S(1)}, f32[144,576]{1,0:T(8,128)S(1)}, u32[]{:S(2)}, u32[]{:S(2)}) collective-permute-start(f32[144,576]{1,0:T(8,128)S(1)} %get-tuple-element.150.refs_0_), channel_id=1, source_target_pairs={{0,8},{4,12},{8,0},{12,4},{16,24},{20,28},{24,16},{28,20},{1,9},{5... | collective-permute-start | bytes 995336 | tf_op jit(solution)/shard_map/ppermute | solution.py:72
  11.0 1.2 %collective-permute-done.1 = f32[16,1280]{1,0:T(8,128)S(1)} collective-permute-done((f32[16,1280]{1,0:T(8,128)S(1)}, f32[16,1280]{1,0:T(8,128)S(1)}, u32[]{:S(2)}, u32[]{:S(2)}) %collective-permute-start.1) | collective-permute-done | bytes 81952 | tf_op jit(solution)/shard_map/ppermute | solution.py:72
  12.2 1.8 %collective-permute-start.2 = (f32[16,1280]{1,0:T(8,128)S(1)}, f32[16,1280]{1,0:T(8,128)S(1)}, u32[]{:S(2)}, u32[]{:S(2)}) collective-permute-start(f32[16,1280]{1,0:T(8,128)S(1)} %add.42), channel_id=1, source_target_pairs={{0,4},{4,0},{8,12},{12,8},{16,20},{20,16},{24,28},{28,24},{1,5},{5... | collective-permute-start | bytes 245768 | tf_op jit(solution)/shard_map/ppermute | solution.py:72
  14.0 2.7 %collective-permute-done.2 = f32[16,1280]{1,0:T(8,128)S(1)} collective-permute-done((f32[16,1280]{1,0:T(8,128)S(1)}, f32[16,1280]{1,0:T(8,128)S(1)}, u32[]{:S(2)}, u32[]{:S(2)}) %collective-permute-start.2) | collective-permute-done | bytes 81952 | tf_op jit(solution)/shard_map/ppermute | solution.py:72
  16.7 1.9 %collective-permute-start.3 = (f32[16,1280]{1,0:T(8,128)S(1)}, f32[16,1280]{1,0:T(8,128)S(1)}, u32[]{:S(2)}, u32[]{:S(2)}) collective-permute-start(f32[16,1280]{1,0:T(8,128)S(1)} %add.43), channel_id=1, source_target_pairs={{0,8},{4,12},{8,0},{12,4},{16,24},{20,28},{24,16},{28,20},{1,9},{5... | collective-permute-start | bytes 245768 | tf_op jit(solution)/shard_map/ppermute | solution.py:72
  18.6 3.2 %collective-permute-done.3 = f32[16,1280]{1,0:T(8,128)S(1)} collective-permute-done((f32[16,1280]{1,0:T(8,128)S(1)}, f32[16,1280]{1,0:T(8,128)S(1)}, u32[]{:S(2)}, u32[]{:S(2)}) %collective-permute-start.3) | collective-permute-done | bytes 81952 | tf_op jit(solution)/shard_map/ppermute | solution.py:72
  21.7 2.7 %collective-permute-start.4 = (f32[16,1280]{1,0:T(8,128)S(1)}, f32[16,1280]{1,0:T(8,128)S(1)}, u32[]{:S(2)}, u32[]{:S(2)}) collective-permute-start(f32[16,1280]{1,0:T(8,128)S(1)} %add.44), channel_id=1, source_target_pairs={{0,16},{4,20},{8,24},{12,28},{16,0},{20,4},{24,8},{28,12},{1,17},{... | collective-permute-start | bytes 245768 | tf_op jit(solution)/shard_map/ppermute | solution.py:72
  24.4 1.5 %collective-permute-start.12 = (f32[144,576]{1,0:T(8,128)S(1)}, f32[144,576]{1,0:T(8,128)S(1)}, u32[]{:S(2)}, u32[]{:S(2)}) collective-permute-start(f32[144,576]{1,0:T(8,128)S(1)} %get-tuple-element.150.refs_0_), channel_id=1, source_target_pairs={{0,4},{4,0},{8,12},{12,8},{16,20},{20,16},{24,28},{28,24},{1,5},{5... | collective-permute-start | bytes 995336 | tf_op jit(solution)/shard_map/ppermute | solution.py:72
  25.9 1.4 %collective-permute-done.4 = f32[16,1280]{1,0:T(8,128)S(1)} collective-permute-done((f32[16,1280]{1,0:T(8,128)S(1)}, f32[16,1280]{1,0:T(8,128)S(1)}, u32[]{:S(2)}, u32[]{:S(2)}) %collective-permute-start.4) | collective-permute-done | bytes 81952 | tf_op jit(solution)/shard_map/ppermute | solution.py:72
  27.3 1.1 %collective-permute-start.5 = (f32[16,1280]{1,0:T(8,128)S(1)}, f32[16,1280]{1,0:T(8,128)S(1)}, u32[]{:S(2)}, u32[]{:S(2)}) collective-permute-start(f32[16,1280]{1,0:T(8,128)S(1)} %add.45.ours), channel_id=1, source_target_pairs={{0,2},{1,3},{2,0},{3,1},{4,6},{5,7},{6,4},{7,5},{8,10},{9,11},{10,... | collective-permute-start | bytes 245768 | tf_op jit(solution)/shard_map/ppermute | solution.py:72
  28.4 2.7 %collective-permute-start.9 = (f32[72,576]{1,0:T(8,128)S(1)}, f32[72,576]{1,0:T(8,128)S(1)}, u32[]{:S(2)}, u32[]{:S(2)}) collective-permute-start(f32[72,576]{1,0:T(8,128)S(1)} %get-tuple-element.154), channel_id=1, source_target_pairs={{0,16},{4,20},{8,24},{12,28},{16,0},{20,4},{24,8},{28,12},{1,17},{... | collective-permute-start | bytes 497672 | tf_op jit(solution)/shard_map/ppermute | solution.py:72
  31.9 1.3 %right.2 = (f32[32,576]{1,0:T(8,128)S(1)}, f32[32,1152]{1,0:T(8,128)S(1)}, f32[32,128]{1,0:T(8,128)S(1)}) custom-call(s32[1]{0:T(128)} %bitcast.shard_ref, f32[32,1280]{1,0:T(8,128)S(1)} %join.2.whole, f32[2,288,1152]{2,1,0:T(8,128)S(1)} %get-tuple-element.132.corr, f32[288,1152]{1,0:T(8,128)S(1)} %collective-permute-done.7.other), custom_call_target="tpu_custom_call" | custom-call | flops 1000 | bytes 1000 | tf_op jit(solution)/shard_map/right/pallas_call | solution.py:420
  33.3 1.6 %collective-permute-start.8 = (f32[32,576]{1,0:T(8,128)S(1)}, f32[32,576]{1,0:T(8,128)S(1)}, u32[]{:S(2)}, u32[]{:S(2)}) collective-permute-start(f32[32,576]{1,0:T(8,128)S(1)} %get-tuple-element.149), channel_id=1, source_target_pairs={{0,4},{4,0},{8,12},{12,8},{16,20},{20,16},{24,28},{28,24},{1,5},{5... | collective-permute-start | bytes 221192 | tf_op jit(solution)/shard_map/ppermute | solution.py:72
  35.4 2.7 %collective-permute-done.8 = f32[32,576]{1,0:T(8,128)S(1)} collective-permute-done((f32[32,576]{1,0:T(8,128)S(1)}, f32[32,576]{1,0:T(8,128)S(1)}, u32[]{:S(2)}, u32[]{:S(2)}) %collective-permute-start.8) | collective-permute-done | bytes 73760 | tf_op jit(solution)/shard_map/ppermute | solution.py:72
  38.2 1.6 %collective-permute-start.11 = (f32[32,576]{1,0:T(8,128)S(1)}, f32[32,576]{1,0:T(8,128)S(1)}, u32[]{:S(2)}, u32[]{:S(2)}) collective-permute-start(f32[32,576]{1,0:T(8,128)S(1)} %add.46), channel_id=1, source_target_pairs={{0,8},{4,12},{8,0},{12,4},{16,24},{20,28},{24,16},{28,20},{1,9},{5... | collective-permute-start | bytes 221192 | tf_op jit(solution)/shard_map/ppermute | solution.py:72
  39.8 1.5 %collective-permute-start.18 = (f32[144,576]{1,0:T(8,128)S(1)}, f32[144,576]{1,0:T(8,128)S(1)}, u32[]{:S(2)}, u32[]{:S(2)}) collective-permute-start(f32[144,576]{1,0:T(8,128)S(1)} %collective-permute-done.6.refs_0_), channel_id=1, source_target_pairs={{0,4},{4,0},{8,12},{12,8},{16,20},{20,16},{24,28},{28,24},{1,5},{5... | collective-permute-start | bytes 995336 | tf_op jit(solution)/shard_map/ppermute | solution.py:72
  41.3 1.3 %inverse.2 = f32[2,32,32]{2,1,0:T(8,128)S(1)} custom-call(f32[32,1152]{1,0:T(8,128)S(1)} %get-tuple-element.158.ours, f32[32,1152]{1,0:T(8,128)S(1)} %collective-permute-done.10.theirs), custom_call_target="tpu_custom_call" | custom-call | flops 1000 | bytes 6000000 | tf_op jit(solution)/shard_map/inverse/pallas_call | solution.py:489
  42.8 3.2 %collective-permute-start.13 = (f32[32,576]{1,0:T(8,128)S(1)}, f32[32,576]{1,0:T(8,128)S(1)}, u32[]{:S(2)}, u32[]{:S(2)}) collective-permute-start(f32[32,576]{1,0:T(8,128)S(1)} %add.47), channel_id=1, source_target_pairs={{0,16},{4,20},{8,24},{12,28},{16,0},{20,4},{24,8},{28,12},{1,17},{... | collective-permute-start | bytes 221192 | tf_op jit(solution)/shard_map/ppermute | solution.py:72
  46.0 1.6 %collective-permute-start.17 = (f32[72,576]{1,0:T(8,128)S(1)}, f32[72,576]{1,0:T(8,128)S(1)}, u32[]{:S(2)}, u32[]{:S(2)}) collective-permute-start(f32[72,576]{1,0:T(8,128)S(1)} %collective-permute-done.9.refs_0_), channel_id=1, source_target_pairs={{0,8},{4,12},{8,0},{12,4},{16,24},{20,28},{24,16},{28,20},{1,9},{5... | collective-permute-start | bytes 497672 | tf_op jit(solution)/shard_map/ppermute | solution.py:72
  47.6 1.5 %collective-permute-start.19 = (f32[72,576]{1,0:T(8,128)S(1)}, f32[72,576]{1,0:T(8,128)S(1)}, u32[]{:S(2)}, u32[]{:S(2)}) collective-permute-start(f32[72,576]{1,0:T(8,128)S(1)} %collective-permute-done.9.refs_0_), channel_id=1, source_target_pairs={{0,4},{4,0},{8,12},{12,8},{16,20},{20,16},{24,28},{28,24},{1,5},{5... | collective-permute-start | bytes 497672 | tf_op jit(solution)/shard_map/ppermute | solution.py:72
  49.1 1.8 %collective-permute-done.13 = f32[32,576]{1,0:T(8,128)S(1)} collective-permute-done((f32[32,576]{1,0:T(8,128)S(1)}, f32[32,576]{1,0:T(8,128)S(1)}, u32[]{:S(2)}, u32[]{:S(2)}) %collective-permute-start.13) | collective-permute-done | bytes 73760 | tf_op jit(solution)/shard_map/ppermute | solution.py:72
  50.9 1.2 %left.1 = (f32[16,1152]{1,0:T(8,128)S(1)}, f32[16,1152]{1,0:T(8,128)S(1)}) custom-call(s32[1]{0:T(128)} %bitcast.shard_ref, f32[32,576]{1,0:T(8,128)S(1)} %add.48.right, f32[2,32,32]{2,1,0:T(8,128)S(1)} %inverse.2, f32[2,288,1152]{2,1,0:T(8,128)S(1)} %get-tuple-element.132.corr, f32[288,1152]{1,0:T(8,128)S(1)} %collective-permute-done.7.other, ...), custom_call_target="tpu_custom_call" | custom-call | flops 1000 | bytes 1000 | tf_op jit(solution)/shard_map/left/pallas_call | solution.py:443
  52.1 1.3 %collective-permute-start.15 = (f32[16,1152]{1,0:T(8,128)S(1)}, f32[16,1152]{1,0:T(8,128)S(1)}, u32[]{:S(2)}, u32[]{:S(2)}) collective-permute-start(f32[16,1152]{1,0:T(8,128)S(1)} %get-tuple-element.172), channel_id=1, source_target_pairs={{0,2},{1,3},{2,0},{3,1},{4,6},{5,7},{6,4},{7,5},{8,10},{9,11},{10,... | collective-permute-start | bytes 221192 | tf_op jit(solution)/shard_map/ppermute | solution.py:72
  53.4 1.3 %collective-permute-start.21 = (f32[72,576]{1,0:T(8,128)S(1)}, f32[72,576]{1,0:T(8,128)S(1)}, u32[]{:S(2)}, u32[]{:S(2)}) collective-permute-start(f32[72,576]{1,0:T(8,128)S(1)} %get-tuple-element.192), channel_id=1, source_target_pairs={{0,16},{4,20},{8,24},{12,28},{16,0},{20,4},{24,8},{28,12},{1,17},{... | collective-permute-start | bytes 497672 | tf_op jit(solution)/shard_map/ppermute | solution.py:72
  54.6 1.9 %collective-permute-done.15 = f32[16,1152]{1,0:T(8,128)S(1)} collective-permute-done((f32[16,1152]{1,0:T(8,128)S(1)}, f32[16,1152]{1,0:T(8,128)S(1)}, u32[]{:S(2)}, u32[]{:S(2)}) %collective-permute-start.15) | collective-permute-done | bytes 73760 | tf_op jit(solution)/shard_map/ppermute | solution.py:72
  56.5 1.1 %collective-permute-start.16 = (f32[16,1152]{1,0:T(8,128)S(1)}, f32[16,1152]{1,0:T(8,128)S(1)}, u32[]{:S(2)}, u32[]{:S(2)}) collective-permute-start(f32[16,1152]{1,0:T(8,128)S(1)} %add.49), channel_id=1, source_target_pairs={{0,4},{4,0},{8,12},{12,8},{16,20},{20,16},{24,28},{28,24},{1,5},{5... | collective-permute-start | bytes 221192 | tf_op jit(solution)/shard_map/ppermute | solution.py:72
  58.3 2.6 %collective-permute-done.16 = f32[16,1152]{1,0:T(8,128)S(1)} collective-permute-done((f32[16,1152]{1,0:T(8,128)S(1)}, f32[16,1152]{1,0:T(8,128)S(1)}, u32[]{:S(2)}, u32[]{:S(2)}) %collective-permute-start.16) | collective-permute-done | bytes 73760 | tf_op jit(solution)/shard_map/ppermute | solution.py:72
  61.0 1.0 %collective-permute-start.20 = (f32[16,1152]{1,0:T(8,128)S(1)}, f32[16,1152]{1,0:T(8,128)S(1)}, u32[]{:S(2)}, u32[]{:S(2)}) collective-permute-start(f32[16,1152]{1,0:T(8,128)S(1)} %add.50), channel_id=1, source_target_pairs={{0,8},{4,12},{8,0},{12,4},{16,24},{20,28},{24,16},{28,20},{1,9},{5... | collective-permute-start | bytes 221192 | tf_op jit(solution)/shard_map/ppermute | solution.py:72
  62.0 1.1 %collective-permute-start.25 = (f32[72,576]{1,0:T(8,128)S(1)}, f32[72,576]{1,0:T(8,128)S(1)}, u32[]{:S(2)}, u32[]{:S(2)}) collective-permute-start(f32[72,576]{1,0:T(8,128)S(1)} %collective-permute-done.17.refs_1_), channel_id=1, source_target_pairs={{0,4},{4,0},{8,12},{12,8},{16,20},{20,16},{24,28},{28,24},{1,5},{5... | collective-permute-start | bytes 497672 | tf_op jit(solution)/shard_map/ppermute | solution.py:72
  63.7 2.0 %collective-permute-done.20 = f32[16,1152]{1,0:T(8,128)S(1)} collective-permute-done((f32[16,1152]{1,0:T(8,128)S(1)}, f32[16,1152]{1,0:T(8,128)S(1)}, u32[]{:S(2)}, u32[]{:S(2)}) %collective-permute-start.20) | collective-permute-done | bytes 73760 | tf_op jit(solution)/shard_map/ppermute | solution.py:72
  65.8 1.9 %collective-permute-start.22 = (f32[16,1152]{1,0:T(8,128)S(1)}, f32[16,1152]{1,0:T(8,128)S(1)}, u32[]{:S(2)}, u32[]{:S(2)}) collective-permute-start(f32[16,1152]{1,0:T(8,128)S(1)} %add.51), channel_id=1, source_target_pairs={{0,16},{4,20},{8,24},{12,28},{16,0},{20,4},{24,8},{28,12},{1,17},{... | collective-permute-start | bytes 221192 | tf_op jit(solution)/shard_map/ppermute | solution.py:72
  68.0 3.8 %collective-permute-done.22 = f32[16,1152]{1,0:T(8,128)S(1)} collective-permute-done((f32[16,1152]{1,0:T(8,128)S(1)}, f32[16,1152]{1,0:T(8,128)S(1)}, u32[]{:S(2)}, u32[]{:S(2)}) %collective-permute-start.22) | collective-permute-done | bytes 73760 | tf_op jit(solution)/shard_map/ppermute | solution.py:72
  71.9 0.9 collective-permute-start.24
  73.4 1.0 %collective-permute-start.28 = (f32[72,576]{1,0:T(8,128)S(1)}, f32[72,576]{1,0:T(8,128)S(1)}, u32[]{:S(2)}, u32[]{:S(2)}) collective-permute-start(f32[72,576]{1,0:T(8,128)S(1)} %collective-permute-done.21.refs_0_), channel_id=1, source_target_pairs={{0,4},{4,0},{8,12},{12,8},{16,20},{20,16},{24,28},{28,24},{1,5},{5... | collective-permute-start | bytes 497672 | tf_op jit(solution)/shard_map/ppermute | solution.py:72
  74.8 1.5 %collective-permute-done.24.got = f32[16,1152]{1,0:T(8,128)S(1)} collective-permute-done((f32[16,1152]{1,0:T(8,128)S(1)}, f32[16,1152]{1,0:T(8,128)S(1)}, u32[]{:S(2)}, u32[]{:S(2)}) %collective-permute-start.24) | collective-permute-done | bytes 73760 | tf_op jit(solution)/shard_map/ppermute | solution.py:72
  76.3 1.3 %right.3 = (f32[32,576]{1,0:T(8,128)S(1)}, f32[32,1280]{1,0:T(8,128)S(1)}) custom-call(s32[1]{0:T(128)} %bitcast.shard_ref, f32[32,1152]{1,0:T(8,128)S(1)} %join.3.whole, f32[2,288,1152]{2,1,0:T(8,128)S(1)} %get-tuple-element.132.corr, f32[288,1152]{1,0:T(8,128)S(1)} %collective-permute-done.7.other, f32[32,128]{1,0:T(8,128)S(1)} %get-tuple-element.208.refs_0_, ...), custom_call_target="tpu_custom_call" | custom-call | flops 1000 | bytes 1000 | tf_op jit(solution)/shard_map/right/pallas_call | solution.py:420
  78.2 4.4 %collective-permute-done.26 = f32[32,576]{1,0:T(8,128)S(1)} collective-permute-done((f32[32,576]{1,0:T(8,128)S(1)}, f32[32,576]{1,0:T(8,128)S(1)}, u32[]{:S(2)}, u32[]{:S(2)}) %collective-permute-start.26) | collective-permute-done | bytes 73760 | tf_op jit(solution)/shard_map/ppermute | solution.py:72
  82.9 1.0 %collective-permute-start.33 = (f32[72,576]{1,0:T(8,128)S(1)}, f32[72,576]{1,0:T(8,128)S(1)}, u32[]{:S(2)}, u32[]{:S(2)}) collective-permute-start(f32[72,576]{1,0:T(8,128)S(1)} %collective-permute-done.27.refs_1_), channel_id=1, source_target_pairs={{0,4},{4,0},{8,12},{12,8},{16,20},{20,16},{24,28},{28,24},{1,5},{5... | collective-permute-start | bytes 497672 | tf_op jit(solution)/shard_map/ppermute | solution.py:72
  84.7 2.4 %collective-permute-done.30 = f32[32,576]{1,0:T(8,128)S(1)} collective-permute-done((f32[32,576]{1,0:T(8,128)S(1)}, f32[32,576]{1,0:T(8,128)S(1)}, u32[]{:S(2)}, u32[]{:S(2)}) %collective-permute-start.30) | collective-permute-done | bytes 73760 | tf_op jit(solution)/shard_map/ppermute | solution.py:72
  87.2 1.7 %collective-permute-start.31 = (f32[32,576]{1,0:T(8,128)S(1)}, f32[32,576]{1,0:T(8,128)S(1)}, u32[]{:S(2)}, u32[]{:S(2)}) collective-permute-start(f32[32,576]{1,0:T(8,128)S(1)} %add.54), channel_id=1, source_target_pairs={{0,16},{4,20},{8,24},{12,28},{16,0},{20,4},{24,8},{28,12},{1,17},{... | collective-permute-start | bytes 221192 | tf_op jit(solution)/shard_map/ppermute | solution.py:72
  88.9 1.3 %inverse.3 = f32[2,32,32]{2,1,0:T(8,128)S(1)} custom-call(f32[32,1280]{1,0:T(8,128)S(1)} %get-tuple-element.233.ours, f32[32,1280]{1,0:T(8,128)S(1)} %collective-permute-done.29.got.theirs), custom_call_target="tpu_custom_call" | custom-call | flops 1000 | bytes 6000000 | tf_op jit(solution)/shard_map/inverse/pallas_call | solution.py:489
  90.2 0.8 insert.14.refs_1_
  91.0 2.2 %collective-permute-done.31 = f32[32,576]{1,0:T(8,128)S(1)} collective-permute-done((f32[32,576]{1,0:T(8,128)S(1)}, f32[32,576]{1,0:T(8,128)S(1)}, u32[]{:S(2)}, u32[]{:S(2)}) %collective-permute-start.31) | collective-permute-done | bytes 73760 | tf_op jit(solution)/shard_map/ppermute | solution.py:72
  93.3 1.3 %collective-permute-done.32.their_right = f32[32,576]{1,0:T(8,128)S(1)} collective-permute-done((f32[32,576]{1,0:T(8,128)S(1)}, f32[32,576]{1,0:T(8,128)S(1)}, u32[]{:S(2)}, u32[]{:S(2)}) %collective-permute-start.32) | collective-permute-done | bytes 73760 | tf_op jit(solution)/shard_map/ppermute | solution.py:72
  94.9 3.5 %finish.1 = (f32[288,1152]{1,0:T(8,128)}, f32[288,1152]{1,0:T(8,128)}, f32[288,1152]{1,0:T(8,128)}, f32[288,1152]{1,0:T(8,128)}, f32[144,288]{1,0:T(8,128)}, /*index=5*/f32[144,288]{1,0:T(8,128)}) custom-call(s32[1]{0:T(128)} %bitcast.shard_ref, f32[2,288,1152]{2,1,0:T(8,128)S(1)} %get-tuple-element.132.corr, f32[576,1152]{1,0:T(8,128)S(1)} %insert.15.rows, ...), custom_call_target="tpu_custom_call" | custom-call | tf_op jit(solution)/shard_map/finish/pallas_call | solution.py:559
  (65 shorter events, 7.4 us)
Async XLA Ops:
  0.6 8.5 %copy-start = (f32[144,288]{1,0:T(8,128)S(1)}, f32[144,288]{1,0:T(8,128)}, u32[]{:S(2)}) copy-start(f32[144,288]{1,0:T(8,128)} %moment_q.3) | copy-start | bytes 497668
  0.7 8.5 %copy-start.1 = (f32[144,288]{1,0:T(8,128)S(1)}, f32[144,288]{1,0:T(8,128)}, u32[]{:S(2)}) copy-start(f32[144,288]{1,0:T(8,128)} %moment_o.3) | copy-start | bytes 497668
  0.7 8.5 %copy-start.2 = (f32[144,288]{1,0:T(8,128)S(1)}, f32[144,288]{1,0:T(8,128)}, u32[]{:S(2)}) copy-start(f32[144,288]{1,0:T(8,128)} %weight_q.1) | copy-start | bytes 497668
  0.7 8.5 %copy-start.3 = (f32[144,288]{1,0:T(8,128)S(1)}, f32[144,288]{1,0:T(8,128)}, u32[]{:S(2)}) copy-start(f32[144,288]{1,0:T(8,128)} %weight_o.1) | copy-start | bytes 497668
  4.5 1.5 %collective-permute-start = (f32[32,1280]{1,0:T(8,128)S(1)}, f32[32,1280]{1,0:T(8,128)S(1)}, u32[]{:S(2)}, u32[]{:S(2)}) collective-permute-start(f32[32,1280]{1,0:T(8,128)S(1)} %get-tuple-element.134), channel_id=1, source_target_pairs={{0,1},{1,0},{2,3},{3,2},{4,5},{5,4},{6,7},{7,6},{8,9},{9,8},{10,11... | collective-permute-start | bytes 491528 | tf_op jit(solution)/shard_map/ppermute | solution.py:72
  6.1 25.8 %collective-permute-start.7 = (f32[288,1152]{1,0:T(8,128)S(1)}, f32[288,1152]{1,0:T(8,128)S(1)}, u32[]{:S(2)}, u32[]{:S(2)}) collective-permute-start(f32[288,1152]{1,0:T(8,128)S(1)} %get-tuple-element.146), channel_id=1, source_target_pairs={{0,1},{1,0},{2,3},{3,2},{4,5},{5,4},{6,7},{7,6},{8,9},{9,8},{10,11... | collective-permute-start | bytes 3981320 | tf_op jit(solution)/shard_map/ppermute | solution.py:72
  6.5 5.6 %collective-permute-start.1 = (f32[16,1280]{1,0:T(8,128)S(1)}, f32[16,1280]{1,0:T(8,128)S(1)}, u32[]{:S(2)}, u32[]{:S(2)}) collective-permute-start(f32[16,1280]{1,0:T(8,128)S(1)} %get-tuple-element.140), channel_id=1, source_target_pairs={{0,2},{1,3},{2,0},{3,1},{4,6},{5,7},{6,4},{7,5},{8,10},{9,11},{10,... | collective-permute-start | bytes 245768 | tf_op jit(solution)/shard_map/ppermute | solution.py:72
  9.3 22.5 %collective-permute-start.6 = (f32[144,576]{1,0:T(8,128)S(1)}, f32[144,576]{1,0:T(8,128)S(1)}, u32[]{:S(2)}, u32[]{:S(2)}) collective-permute-start(f32[144,576]{1,0:T(8,128)S(1)} %get-tuple-element.150.refs_0_), channel_id=1, source_target_pairs={{0,8},{4,12},{8,0},{12,4},{16,24},{20,28},{24,16},{28,20},{1,9},{5... | collective-permute-start | bytes 995336 | tf_op jit(solution)/shard_map/ppermute | solution.py:72
  12.2 4.5 %collective-permute-start.2 = (f32[16,1280]{1,0:T(8,128)S(1)}, f32[16,1280]{1,0:T(8,128)S(1)}, u32[]{:S(2)}, u32[]{:S(2)}) collective-permute-start(f32[16,1280]{1,0:T(8,128)S(1)} %add.42), channel_id=1, source_target_pairs={{0,4},{4,0},{8,12},{12,8},{16,20},{20,16},{24,28},{28,24},{1,5},{5... | collective-permute-start | bytes 245768 | tf_op jit(solution)/shard_map/ppermute | solution.py:72
  16.7 5.0 %collective-permute-start.3 = (f32[16,1280]{1,0:T(8,128)S(1)}, f32[16,1280]{1,0:T(8,128)S(1)}, u32[]{:S(2)}, u32[]{:S(2)}) collective-permute-start(f32[16,1280]{1,0:T(8,128)S(1)} %add.43), channel_id=1, source_target_pairs={{0,8},{4,12},{8,0},{12,4},{16,24},{20,28},{24,16},{28,20},{1,9},{5... | collective-permute-start | bytes 245768 | tf_op jit(solution)/shard_map/ppermute | solution.py:72
  21.7 5.6 %collective-permute-start.4 = (f32[16,1280]{1,0:T(8,128)S(1)}, f32[16,1280]{1,0:T(8,128)S(1)}, u32[]{:S(2)}, u32[]{:S(2)}) collective-permute-start(f32[16,1280]{1,0:T(8,128)S(1)} %add.44), channel_id=1, source_target_pairs={{0,16},{4,20},{8,24},{12,28},{16,0},{20,4},{24,8},{28,12},{1,17},{... | collective-permute-start | bytes 245768 | tf_op jit(solution)/shard_map/ppermute | solution.py:72
  24.4 18.3 %collective-permute-start.12 = (f32[144,576]{1,0:T(8,128)S(1)}, f32[144,576]{1,0:T(8,128)S(1)}, u32[]{:S(2)}, u32[]{:S(2)}) collective-permute-start(f32[144,576]{1,0:T(8,128)S(1)} %get-tuple-element.150.refs_0_), channel_id=1, source_target_pairs={{0,4},{4,0},{8,12},{12,8},{16,20},{20,16},{24,28},{28,24},{1,5},{5... | collective-permute-start | bytes 995336 | tf_op jit(solution)/shard_map/ppermute | solution.py:72
  27.3 4.5 %collective-permute-start.5 = (f32[16,1280]{1,0:T(8,128)S(1)}, f32[16,1280]{1,0:T(8,128)S(1)}, u32[]{:S(2)}, u32[]{:S(2)}) collective-permute-start(f32[16,1280]{1,0:T(8,128)S(1)} %add.45.ours), channel_id=1, source_target_pairs={{0,2},{1,3},{2,0},{3,1},{4,6},{5,7},{6,4},{7,5},{8,10},{9,11},{10,... | collective-permute-start | bytes 245768 | tf_op jit(solution)/shard_map/ppermute | solution.py:72
  28.4 9.7 %collective-permute-start.9 = (f32[72,576]{1,0:T(8,128)S(1)}, f32[72,576]{1,0:T(8,128)S(1)}, u32[]{:S(2)}, u32[]{:S(2)}) collective-permute-start(f32[72,576]{1,0:T(8,128)S(1)} %get-tuple-element.154), channel_id=1, source_target_pairs={{0,16},{4,20},{8,24},{12,28},{16,0},{20,4},{24,8},{28,12},{1,17},{... | collective-permute-start | bytes 497672 | tf_op jit(solution)/shard_map/ppermute | solution.py:72
  33.2 5.0 %collective-permute-start.10 = (f32[32,1152]{1,0:T(8,128)S(1)}, f32[32,1152]{1,0:T(8,128)S(1)}, u32[]{:S(2)}, u32[]{:S(2)}) collective-permute-start(f32[32,1152]{1,0:T(8,128)S(1)} %get-tuple-element.158.ours), channel_id=1, source_target_pairs={{0,1},{1,0},{2,3},{3,2},{4,5},{5,4},{6,7},{7,6},{8,9},{9,8},{10,11... | collective-permute-start | bytes 442376 | tf_op jit(solution)/shard_map/ppermute | solution.py:72
  33.3 4.9 %collective-permute-start.8 = (f32[32,576]{1,0:T(8,128)S(1)}, f32[32,576]{1,0:T(8,128)S(1)}, u32[]{:S(2)}, u32[]{:S(2)}) collective-permute-start(f32[32,576]{1,0:T(8,128)S(1)} %get-tuple-element.149), channel_id=1, source_target_pairs={{0,4},{4,0},{8,12},{12,8},{16,20},{20,16},{24,28},{28,24},{1,5},{5... | collective-permute-start | bytes 221192 | tf_op jit(solution)/shard_map/ppermute | solution.py:72
  38.2 4.5 %collective-permute-start.11 = (f32[32,576]{1,0:T(8,128)S(1)}, f32[32,576]{1,0:T(8,128)S(1)}, u32[]{:S(2)}, u32[]{:S(2)}) collective-permute-start(f32[32,576]{1,0:T(8,128)S(1)} %add.46), channel_id=1, source_target_pairs={{0,8},{4,12},{8,0},{12,4},{16,24},{20,28},{24,16},{28,20},{1,9},{5... | collective-permute-start | bytes 221192 | tf_op jit(solution)/shard_map/ppermute | solution.py:72
  39.8 21.2 %collective-permute-start.18 = (f32[144,576]{1,0:T(8,128)S(1)}, f32[144,576]{1,0:T(8,128)S(1)}, u32[]{:S(2)}, u32[]{:S(2)}) collective-permute-start(f32[144,576]{1,0:T(8,128)S(1)} %collective-permute-done.6.refs_0_), channel_id=1, source_target_pairs={{0,4},{4,0},{8,12},{12,8},{16,20},{20,16},{24,28},{28,24},{1,5},{5... | collective-permute-start | bytes 995336 | tf_op jit(solution)/shard_map/ppermute | solution.py:72
  42.7 8.2 %collective-permute-start.14 = (f32[32,1280]{1,0:T(8,128)S(1)}, f32[32,1280]{1,0:T(8,128)S(1)}, u32[]{:S(2)}, u32[]{:S(2)}) collective-permute-start(f32[32,1280]{1,0:T(8,128)S(1)} %get-tuple-element.165.ours), channel_id=1, source_target_pairs={{0,1},{1,0},{2,3},{3,2},{4,5},{5,4},{6,7},{7,6},{8,9},{9,8},{10,11... | collective-permute-start | bytes 491528 | tf_op jit(solution)/shard_map/ppermute | solution.py:72
  42.8 8.1 %collective-permute-start.13 = (f32[32,576]{1,0:T(8,128)S(1)}, f32[32,576]{1,0:T(8,128)S(1)}, u32[]{:S(2)}, u32[]{:S(2)}) collective-permute-start(f32[32,576]{1,0:T(8,128)S(1)} %add.47), channel_id=1, source_target_pairs={{0,16},{4,20},{8,24},{12,28},{16,0},{20,4},{24,8},{28,12},{1,17},{... | collective-permute-start | bytes 221192 | tf_op jit(solution)/shard_map/ppermute | solution.py:72
  46.0 15.0 %collective-permute-start.17 = (f32[72,576]{1,0:T(8,128)S(1)}, f32[72,576]{1,0:T(8,128)S(1)}, u32[]{:S(2)}, u32[]{:S(2)}) collective-permute-start(f32[72,576]{1,0:T(8,128)S(1)} %collective-permute-done.9.refs_0_), channel_id=1, source_target_pairs={{0,8},{4,12},{8,0},{12,4},{16,24},{20,28},{24,16},{28,20},{1,9},{5... | collective-permute-start | bytes 497672 | tf_op jit(solution)/shard_map/ppermute | solution.py:72
  47.6 13.4 %collective-permute-start.19 = (f32[72,576]{1,0:T(8,128)S(1)}, f32[72,576]{1,0:T(8,128)S(1)}, u32[]{:S(2)}, u32[]{:S(2)}) collective-permute-start(f32[72,576]{1,0:T(8,128)S(1)} %collective-permute-done.9.refs_0_), channel_id=1, source_target_pairs={{0,4},{4,0},{8,12},{12,8},{16,20},{20,16},{24,28},{28,24},{1,5},{5... | collective-permute-start | bytes 497672 | tf_op jit(solution)/shard_map/ppermute | solution.py:72
  52.1 4.4 %collective-permute-start.15 = (f32[16,1152]{1,0:T(8,128)S(1)}, f32[16,1152]{1,0:T(8,128)S(1)}, u32[]{:S(2)}, u32[]{:S(2)}) collective-permute-start(f32[16,1152]{1,0:T(8,128)S(1)} %get-tuple-element.172), channel_id=1, source_target_pairs={{0,2},{1,3},{2,0},{3,1},{4,6},{5,7},{6,4},{7,5},{8,10},{9,11},{10,... | collective-permute-start | bytes 221192 | tf_op jit(solution)/shard_map/ppermute | solution.py:72
  53.4 12.4 %collective-permute-start.21 = (f32[72,576]{1,0:T(8,128)S(1)}, f32[72,576]{1,0:T(8,128)S(1)}, u32[]{:S(2)}, u32[]{:S(2)}) collective-permute-start(f32[72,576]{1,0:T(8,128)S(1)} %get-tuple-element.192), channel_id=1, source_target_pairs={{0,16},{4,20},{8,24},{12,28},{16,0},{20,4},{24,8},{28,12},{1,17},{... | collective-permute-start | bytes 497672 | tf_op jit(solution)/shard_map/ppermute | solution.py:72
  56.5 4.4 %collective-permute-start.16 = (f32[16,1152]{1,0:T(8,128)S(1)}, f32[16,1152]{1,0:T(8,128)S(1)}, u32[]{:S(2)}, u32[]{:S(2)}) collective-permute-start(f32[16,1152]{1,0:T(8,128)S(1)} %add.49), channel_id=1, source_target_pairs={{0,4},{4,0},{8,12},{12,8},{16,20},{20,16},{24,28},{28,24},{1,5},{5... | collective-permute-start | bytes 221192 | tf_op jit(solution)/shard_map/ppermute | solution.py:72
  61.0 4.7 %collective-permute-start.20 = (f32[16,1152]{1,0:T(8,128)S(1)}, f32[16,1152]{1,0:T(8,128)S(1)}, u32[]{:S(2)}, u32[]{:S(2)}) collective-permute-start(f32[16,1152]{1,0:T(8,128)S(1)} %add.50), channel_id=1, source_target_pairs={{0,8},{4,12},{8,0},{12,4},{16,24},{20,28},{24,16},{28,20},{1,9},{5... | collective-permute-start | bytes 221192 | tf_op jit(solution)/shard_map/ppermute | solution.py:72
  62.0 14.3 %collective-permute-start.25 = (f32[72,576]{1,0:T(8,128)S(1)}, f32[72,576]{1,0:T(8,128)S(1)}, u32[]{:S(2)}, u32[]{:S(2)}) collective-permute-start(f32[72,576]{1,0:T(8,128)S(1)} %collective-permute-done.17.refs_1_), channel_id=1, source_target_pairs={{0,4},{4,0},{8,12},{12,8},{16,20},{20,16},{24,28},{28,24},{1,5},{5... | collective-permute-start | bytes 497672 | tf_op jit(solution)/shard_map/ppermute | solution.py:72
  65.8 6.1 %collective-permute-start.22 = (f32[16,1152]{1,0:T(8,128)S(1)}, f32[16,1152]{1,0:T(8,128)S(1)}, u32[]{:S(2)}, u32[]{:S(2)}) collective-permute-start(f32[16,1152]{1,0:T(8,128)S(1)} %add.51), channel_id=1, source_target_pairs={{0,16},{4,20},{8,24},{12,28},{16,0},{20,4},{24,8},{28,12},{1,17},{... | collective-permute-start | bytes 221192 | tf_op jit(solution)/shard_map/ppermute | solution.py:72
  67.6 4.3 %collective-permute-start.23 = (f32[16,1152]{1,0:T(8,128)S(1)}, f32[16,1152]{1,0:T(8,128)S(1)}, u32[]{:S(2)}, u32[]{:S(2)}) collective-permute-start(f32[16,1152]{1,0:T(8,128)S(1)} %get-tuple-element.197), channel_id=1, source_target_pairs={{0,1},{1,0},{2,3},{3,2},{4,5},{5,4},{6,7},{7,6},{8,9},{9,8},{10,11... | collective-permute-start | bytes 221192 | tf_op jit(solution)/shard_map/ppermute | solution.py:72
  71.9 4.4 %collective-permute-start.24 = (f32[16,1152]{1,0:T(8,128)S(1)}, f32[16,1152]{1,0:T(8,128)S(1)}, u32[]{:S(2)}, u32[]{:S(2)}) collective-permute-start(f32[16,1152]{1,0:T(8,128)S(1)} %add.52.ours), channel_id=1, source_target_pairs={{0,2},{1,3},{2,0},{3,1},{4,6},{5,7},{6,4},{7,5},{8,10},{9,11},{10,... | collective-permute-start | bytes 221192 | tf_op jit(solution)/shard_map/ppermute | solution.py:72
  72.8 9.8 %collective-permute-start.27 = (f32[72,576]{1,0:T(8,128)S(1)}, f32[72,576]{1,0:T(8,128)S(1)}, u32[]{:S(2)}, u32[]{:S(2)}) collective-permute-start(f32[72,576]{1,0:T(8,128)S(1)} %collective-permute-done.21.refs_0_), channel_id=1, source_target_pairs={{0,8},{4,12},{8,0},{12,4},{16,24},{20,28},{24,16},{28,20},{1,9},{5... | collective-permute-start | bytes 497672 | tf_op jit(solution)/shard_map/ppermute | solution.py:72
  73.4 9.3 %collective-permute-start.28 = (f32[72,576]{1,0:T(8,128)S(1)}, f32[72,576]{1,0:T(8,128)S(1)}, u32[]{:S(2)}, u32[]{:S(2)}) collective-permute-start(f32[72,576]{1,0:T(8,128)S(1)} %collective-permute-done.21.refs_0_), channel_id=1, source_target_pairs={{0,4},{4,0},{8,12},{12,8},{16,20},{20,16},{24,28},{28,24},{1,5},{5... | collective-permute-start | bytes 497672 | tf_op jit(solution)/shard_map/ppermute | solution.py:72
  77.6 5.0 %collective-permute-start.29 = (f32[32,1280]{1,0:T(8,128)S(1)}, f32[32,1280]{1,0:T(8,128)S(1)}, u32[]{:S(2)}, u32[]{:S(2)}) collective-permute-start(f32[32,1280]{1,0:T(8,128)S(1)} %get-tuple-element.233.ours), channel_id=1, source_target_pairs={{0,1},{1,0},{2,3},{3,2},{4,5},{5,4},{6,7},{7,6},{8,9},{9,8},{10,11... | collective-permute-start | bytes 491528 | tf_op jit(solution)/shard_map/ppermute | solution.py:72
  77.7 6.2 %copy-start.4 = (f32[72]{0:T(128)S(1)}, f32[72]{0:T(128)}, u32[]{:S(2)}) copy-start(f32[72]{0:T(128)} %param.24) | copy-start | bytes 868
  77.7 4.8 %collective-permute-start.26 = (f32[32,576]{1,0:T(8,128)S(1)}, f32[32,576]{1,0:T(8,128)S(1)}, u32[]{:S(2)}, u32[]{:S(2)}) collective-permute-start(f32[32,576]{1,0:T(8,128)S(1)} %get-tuple-element.212), channel_id=1, source_target_pairs={{0,4},{4,0},{8,12},{12,8},{16,20},{20,16},{24,28},{28,24},{1,5},{5... | collective-permute-start | bytes 221192 | tf_op jit(solution)/shard_map/ppermute | solution.py:72
  82.6 4.5 %collective-permute-start.30 = (f32[32,576]{1,0:T(8,128)S(1)}, f32[32,576]{1,0:T(8,128)S(1)}, u32[]{:S(2)}, u32[]{:S(2)}) collective-permute-start(f32[32,576]{1,0:T(8,128)S(1)} %add.53), channel_id=1, source_target_pairs={{0,8},{4,12},{8,0},{12,4},{16,24},{20,28},{24,16},{28,20},{1,9},{5... | collective-permute-start | bytes 221192 | tf_op jit(solution)/shard_map/ppermute | solution.py:72
  82.9 10.4 %collective-permute-start.33 = (f32[72,576]{1,0:T(8,128)S(1)}, f32[72,576]{1,0:T(8,128)S(1)}, u32[]{:S(2)}, u32[]{:S(2)}) collective-permute-start(f32[72,576]{1,0:T(8,128)S(1)} %collective-permute-done.27.refs_1_), channel_id=1, source_target_pairs={{0,4},{4,0},{8,12},{12,8},{16,20},{20,16},{24,28},{28,24},{1,5},{5... | collective-permute-start | bytes 497672 | tf_op jit(solution)/shard_map/ppermute | solution.py:72
  87.2 6.1 %collective-permute-start.31 = (f32[32,576]{1,0:T(8,128)S(1)}, f32[32,576]{1,0:T(8,128)S(1)}, u32[]{:S(2)}, u32[]{:S(2)}) collective-permute-start(f32[32,576]{1,0:T(8,128)S(1)} %add.54), channel_id=1, source_target_pairs={{0,16},{4,20},{8,24},{12,28},{16,0},{20,4},{24,8},{28,12},{1,17},{... | collective-permute-start | bytes 221192 | tf_op jit(solution)/shard_map/ppermute | solution.py:72
  93.3 1.3 %collective-permute-start.32 = (f32[32,576]{1,0:T(8,128)S(1)}, f32[32,576]{1,0:T(8,128)S(1)}, u32[]{:S(2)}, u32[]{:S(2)}) collective-permute-start(f32[32,576]{1,0:T(8,128)S(1)} %add.55.right), channel_id=1, source_target_pairs={{0,1},{1,0},{2,3},{3,2},{4,5},{5,4},{6,7},{7,6},{8,9},{9,8},{10,11... | collective-permute-start | bytes 221192 | tf_op jit(solution)/shard_map/ppermute | solution.py:72

commit v11 on v10

--- a/solution.py
+++ b/solution.py
@@ -153,7 +153,7 @@
         ("near", "own", 2, (0, "core"), (0, "joined")),
         ("turned", "own", 1, (0, 1), (1, 4)),
         ("far_a", "own_a", 4, (0, 4), (1, 2)),
-        ("turned_near", "near", 1, (1, 1), (2, 2)),
+        ("turned_near", "near", 1, (1, 1), (2, 4)),
         ("last_a", "far_a", 2, (1, 2), (2, 2)),
         ("turned_far_a", "far_a", 1, (1, 2), (2, 2)),
         ("far_b", "own_b", 4, (2, "begin"), (2, 4)),

time: 98.5 us -> 97.3 us (0.988)
  waiting for transfers between devices: 37 us -> 33.8 us
  starting transfers between devices: 41.4 us -> 43.4 us
    ppermute x34, waiting for transfers between devices: 37 us -> 33.8 us  [swap(): return lax.ppermute(block, axis, pairs)]
    ppermute x34, starting transfers between devices: 41.4 us -> 43.4 us  [swap(): return lax.ppermute(block, axis, pairs)]
where the time goes in v11:
time: 97.3 us; the launch traced here: 97.1 us
  starting transfers between devices  43.4 us (45%)
  waiting for transfers between devices  33.8 us (35%)
  Pallas kernels  18.7 us (19%)
  between operations  1.01 us (1%)
    ppermute x34, starting transfers between devices, swap(): return lax.ppermute(block, axis, pairs)  43.4 us
    ppermute x34, waiting for transfers between devices, swap(): return lax.ppermute(block, axis, pairs)  33.8 us
    pallas_call x8, Pallas kernels, insert(): pl.pallas_call(functools.partial(insert_kernel, masks, rows_each), in_spe...  4.1 us
    pallas_call x1, Pallas kernels, first(): pl.pallas_call(functools.partial(first_kernel, n_shard), in_specs=[IN_SME...  3.85 us
    pallas_call x1, Pallas kernels, finish(): pl.pallas_call(functools.partial(finish_kernel, chunks), in_specs=[IN_SME...  3.45 us
    pallas_call x2, Pallas kernels, right_of(): pl.pallas_call(functools.partial(right_kernel, len(more), len(waits)), in...  2.62 us
    pallas_call x2, Pallas kernels, inverse_of(): pl.pallas_call(functools.partial(inverse_kernel, size), out_shape=pltpu.V...  2.6 us
  transfers between devices with their start and end apart: 34, of which 18 were waited for; matrix products, arithmetic and copies ran while one was open for 0% of the time, Pallas kernels for 11%

profile of v11, /device:TPU:0, one launch (start us, length us, event | category | flops | bytes accessed | tf_op | source)
XLA Modules:
  0.0 97.1 jit_solution(14085497558291465707)
XLA Ops:
  0.7 3.9 %first.1 = (f32[2,288,1152]{2,1,0:T(8,128)S(1)}, f32[288,1152]{1,0:T(8,128)S(1)}, f32[32,1280]{1,0:T(8,128)S(1)}, f32[32,1280]{1,0:T(8,128)S(1)}) custom-call(s32[1]{0:T(128)} %bitcast.1.place_ref, s32[1]{0:T(128)} %bitcast.shard_ref, f32[288,1152]{1,0:T(8,128)} %bitcast.31, f32[288,1152]{1,0:T(8,128)} %bitcast.32, f32[288,1152]{1,0:T(8,128)} %bitcast.33, ...), custom_call_target="tpu_custom_call" | custom-call | tf_op jit(solution)/shard_map/first/pallas_call | solution.py:383
  5.1 1.0 %collective-permute-done.got = f32[32,1280]{1,0:T(8,128)S(1)} collective-permute-done((f32[32,1280]{1,0:T(8,128)S(1)}, f32[32,1280]{1,0:T(8,128)S(1)}, u32[]{:S(2)}, u32[]{:S(2)}) %collective-permute-start) | collective-permute-done | bytes 163872 | tf_op jit(solution)/shard_map/ppermute | solution.py:72
  6.5 2.6 %collective-permute-start.1 = (f32[16,1280]{1,0:T(8,128)S(1)}, f32[16,1280]{1,0:T(8,128)S(1)}, u32[]{:S(2)}, u32[]{:S(2)}) collective-permute-start(f32[16,1280]{1,0:T(8,128)S(1)} %get-tuple-element.140), channel_id=1, source_target_pairs={{0,2},{1,3},{2,0},{3,1},{4,6},{5,7},{6,4},{7,5},{8,10},{9,11},{10,... | collective-permute-start | bytes 245768 | tf_op jit(solution)/shard_map/ppermute | solution.py:72
  9.3 1.6 %collective-permute-start.6 = (f32[144,576]{1,0:T(8,128)S(1)}, f32[144,576]{1,0:T(8,128)S(1)}, u32[]{:S(2)}, u32[]{:S(2)}) collective-permute-start(f32[144,576]{1,0:T(8,128)S(1)} %get-tuple-element.150.refs_0_), channel_id=1, source_target_pairs={{0,8},{4,12},{8,0},{12,4},{16,24},{20,28},{24,16},{28,20},{1,9},{5... | collective-permute-start | bytes 995336 | tf_op jit(solution)/shard_map/ppermute | solution.py:72
  11.0 1.2 %collective-permute-done.1 = f32[16,1280]{1,0:T(8,128)S(1)} collective-permute-done((f32[16,1280]{1,0:T(8,128)S(1)}, f32[16,1280]{1,0:T(8,128)S(1)}, u32[]{:S(2)}, u32[]{:S(2)}) %collective-permute-start.1) | collective-permute-done | bytes 81952 | tf_op jit(solution)/shard_map/ppermute | solution.py:72
  12.2 1.8 %collective-permute-start.2 = (f32[16,1280]{1,0:T(8,128)S(1)}, f32[16,1280]{1,0:T(8,128)S(1)}, u32[]{:S(2)}, u32[]{:S(2)}) collective-permute-start(f32[16,1280]{1,0:T(8,128)S(1)} %add.42), channel_id=1, source_target_pairs={{0,4},{4,0},{8,12},{12,8},{16,20},{20,16},{24,28},{28,24},{1,5},{5... | collective-permute-start | bytes 245768 | tf_op jit(solution)/shard_map/ppermute | solution.py:72
  14.0 2.7 %collective-permute-done.2 = f32[16,1280]{1,0:T(8,128)S(1)} collective-permute-done((f32[16,1280]{1,0:T(8,128)S(1)}, f32[16,1280]{1,0:T(8,128)S(1)}, u32[]{:S(2)}, u32[]{:S(2)}) %collective-permute-start.2) | collective-permute-done | bytes 81952 | tf_op jit(solution)/shard_map/ppermute | solution.py:72
  16.7 1.9 %collective-permute-start.3 = (f32[16,1280]{1,0:T(8,128)S(1)}, f32[16,1280]{1,0:T(8,128)S(1)}, u32[]{:S(2)}, u32[]{:S(2)}) collective-permute-start(f32[16,1280]{1,0:T(8,128)S(1)} %add.43), channel_id=1, source_target_pairs={{0,8},{4,12},{8,0},{12,4},{16,24},{20,28},{24,16},{28,20},{1,9},{5... | collective-permute-start | bytes 245768 | tf_op jit(solution)/shard_map/ppermute | solution.py:72
  18.6 3.2 %collective-permute-done.3 = f32[16,1280]{1,0:T(8,128)S(1)} collective-permute-done((f32[16,1280]{1,0:T(8,128)S(1)}, f32[16,1280]{1,0:T(8,128)S(1)}, u32[]{:S(2)}, u32[]{:S(2)}) %collective-permute-start.3) | collective-permute-done | bytes 81952 | tf_op jit(solution)/shard_map/ppermute | solution.py:72
  21.7 2.7 %collective-permute-start.4 = (f32[16,1280]{1,0:T(8,128)S(1)}, f32[16,1280]{1,0:T(8,128)S(1)}, u32[]{:S(2)}, u32[]{:S(2)}) collective-permute-start(f32[16,1280]{1,0:T(8,128)S(1)} %add.44), channel_id=1, source_target_pairs={{0,16},{4,20},{8,24},{12,28},{16,0},{20,4},{24,8},{28,12},{1,17},{... | collective-permute-start | bytes 245768 | tf_op jit(solution)/shard_map/ppermute | solution.py:72
  24.4 1.5 %collective-permute-start.12 = (f32[144,576]{1,0:T(8,128)S(1)}, f32[144,576]{1,0:T(8,128)S(1)}, u32[]{:S(2)}, u32[]{:S(2)}) collective-permute-start(f32[144,576]{1,0:T(8,128)S(1)} %get-tuple-element.150.refs_0_), channel_id=1, source_target_pairs={{0,4},{4,0},{8,12},{12,8},{16,20},{20,16},{24,28},{28,24},{1,5},{5... | collective-permute-start | bytes 995336 | tf_op jit(solution)/shard_map/ppermute | solution.py:72
  25.9 1.4 %collective-permute-done.4 = f32[16,1280]{1,0:T(8,128)S(1)} collective-permute-done((f32[16,1280]{1,0:T(8,128)S(1)}, f32[16,1280]{1,0:T(8,128)S(1)}, u32[]{:S(2)}, u32[]{:S(2)}) %collective-permute-start.4) | collective-permute-done | bytes 81952 | tf_op jit(solution)/shard_map/ppermute | solution.py:72
  27.3 1.1 %collective-permute-start.5 = (f32[16,1280]{1,0:T(8,128)S(1)}, f32[16,1280]{1,0:T(8,128)S(1)}, u32[]{:S(2)}, u32[]{:S(2)}) collective-permute-start(f32[16,1280]{1,0:T(8,128)S(1)} %add.45.ours), channel_id=1, source_target_pairs={{0,2},{1,3},{2,0},{3,1},{4,6},{5,7},{6,4},{7,5},{8,10},{9,11},{10,... | collective-permute-start | bytes 245768 | tf_op jit(solution)/shard_map/ppermute | solution.py:72
  28.4 2.7 %collective-permute-start.9 = (f32[72,576]{1,0:T(8,128)S(1)}, f32[72,576]{1,0:T(8,128)S(1)}, u32[]{:S(2)}, u32[]{:S(2)}) collective-permute-start(f32[72,576]{1,0:T(8,128)S(1)} %get-tuple-element.154), channel_id=1, source_target_pairs={{0,16},{4,20},{8,24},{12,28},{16,0},{20,4},{24,8},{28,12},{1,17},{... | collective-permute-start | bytes 497672 | tf_op jit(solution)/shard_map/ppermute | solution.py:72
  31.1 0.7 collective-permute-done.5.got
  31.9 1.3 %right.2 = (f32[32,576]{1,0:T(8,128)S(1)}, f32[32,1152]{1,0:T(8,128)S(1)}, f32[32,128]{1,0:T(8,128)S(1)}) custom-call(s32[1]{0:T(128)} %bitcast.shard_ref, f32[32,1280]{1,0:T(8,128)S(1)} %join.2.whole, f32[2,288,1152]{2,1,0:T(8,128)S(1)} %get-tuple-element.132.corr, f32[288,1152]{1,0:T(8,128)S(1)} %collective-permute-done.7.other), custom_call_target="tpu_custom_call" | custom-call | flops 1000 | bytes 1000 | tf_op jit(solution)/shard_map/right/pallas_call | solution.py:420
  33.3 1.6 %collective-permute-start.8 = (f32[32,576]{1,0:T(8,128)S(1)}, f32[32,576]{1,0:T(8,128)S(1)}, u32[]{:S(2)}, u32[]{:S(2)}) collective-permute-start(f32[32,576]{1,0:T(8,128)S(1)} %get-tuple-element.149), channel_id=1, source_target_pairs={{0,4},{4,0},{8,12},{12,8},{16,20},{20,16},{24,28},{28,24},{1,5},{5... | collective-permute-start | bytes 221192 | tf_op jit(solution)/shard_map/ppermute | solution.py:72
  35.4 2.7 %collective-permute-done.8 = f32[32,576]{1,0:T(8,128)S(1)} collective-permute-done((f32[32,576]{1,0:T(8,128)S(1)}, f32[32,576]{1,0:T(8,128)S(1)}, u32[]{:S(2)}, u32[]{:S(2)}) %collective-permute-start.8) | collective-permute-done | bytes 73760 | tf_op jit(solution)/shard_map/ppermute | solution.py:72
  38.2 1.6 %collective-permute-start.11 = (f32[32,576]{1,0:T(8,128)S(1)}, f32[32,576]{1,0:T(8,128)S(1)}, u32[]{:S(2)}, u32[]{:S(2)}) collective-permute-start(f32[32,576]{1,0:T(8,128)S(1)} %add.46), channel_id=1, source_target_pairs={{0,8},{4,12},{8,0},{12,4},{16,24},{20,28},{24,16},{28,20},{1,9},{5... | collective-permute-start | bytes 221192 | tf_op jit(solution)/shard_map/ppermute | solution.py:72
  39.8 1.3 %inverse.2 = f32[2,32,32]{2,1,0:T(8,128)S(1)} custom-call(f32[32,1152]{1,0:T(8,128)S(1)} %get-tuple-element.158.ours, f32[32,1152]{1,0:T(8,128)S(1)} %collective-permute-done.10.theirs), custom_call_target="tpu_custom_call" | custom-call | flops 1000 | bytes 6000000 | tf_op jit(solution)/shard_map/inverse/pallas_call | solution.py:489
  41.1 1.6 %collective-permute-done.11 = f32[32,576]{1,0:T(8,128)S(1)} collective-permute-done((f32[32,576]{1,0:T(8,128)S(1)}, f32[32,576]{1,0:T(8,128)S(1)}, u32[]{:S(2)}, u32[]{:S(2)}) %collective-permute-start.11) | collective-permute-done | bytes 73760 | tf_op jit(solution)/shard_map/ppermute | solution.py:72
  42.8 1.6 %collective-permute-start.21 = (f32[144,576]{1,0:T(8,128)S(1)}, f32[144,576]{1,0:T(8,128)S(1)}, u32[]{:S(2)}, u32[]{:S(2)}) collective-permute-start(f32[144,576]{1,0:T(8,128)S(1)} %collective-permute-done.6.refs_0_), channel_id=1, source_target_pairs={{0,4},{4,0},{8,12},{12,8},{16,20},{20,16},{24,28},{28,24},{1,5},{5... | collective-permute-start | bytes 995336 | tf_op jit(solution)/shard_map/ppermute | solution.py:72
  44.4 2.8 %collective-permute-start.13 = (f32[32,576]{1,0:T(8,128)S(1)}, f32[32,576]{1,0:T(8,128)S(1)}, u32[]{:S(2)}, u32[]{:S(2)}) collective-permute-start(f32[32,576]{1,0:T(8,128)S(1)} %add.47), channel_id=1, source_target_pairs={{0,16},{4,20},{8,24},{12,28},{16,0},{20,4},{24,8},{28,12},{1,17},{... | collective-permute-start | bytes 221192 | tf_op jit(solution)/shard_map/ppermute | solution.py:72
  47.1 2.0 %collective-permute-start.17 = (f32[72,576]{1,0:T(8,128)S(1)}, f32[72,576]{1,0:T(8,128)S(1)}, u32[]{:S(2)}, u32[]{:S(2)}) collective-permute-start(f32[72,576]{1,0:T(8,128)S(1)} %collective-permute-done.9.refs_0_), channel_id=1, source_target_pairs={{0,8},{4,12},{8,0},{12,4},{16,24},{20,28},{24,16},{28,20},{1,9},{5... | collective-permute-start | bytes 497672 | tf_op jit(solution)/shard_map/ppermute | solution.py:72
  49.7 1.8 %collective-permute-done.13 = f32[32,576]{1,0:T(8,128)S(1)} collective-permute-done((f32[32,576]{1,0:T(8,128)S(1)}, f32[32,576]{1,0:T(8,128)S(1)}, u32[]{:S(2)}, u32[]{:S(2)}) %collective-permute-start.13) | collective-permute-done | bytes 73760 | tf_op jit(solution)/shard_map/ppermute | solution.py:72
  51.5 1.2 %left.1 = (f32[16,1152]{1,0:T(8,128)S(1)}, f32[16,1152]{1,0:T(8,128)S(1)}) custom-call(s32[1]{0:T(128)} %bitcast.shard_ref, f32[32,576]{1,0:T(8,128)S(1)} %add.48.right, f32[2,32,32]{2,1,0:T(8,128)S(1)} %inverse.2, f32[2,288,1152]{2,1,0:T(8,128)S(1)} %get-tuple-element.132.corr, f32[288,1152]{1,0:T(8,128)S(1)} %collective-permute-done.7.other, ...), custom_call_target="tpu_custom_call" | custom-call | flops 1000 | bytes 1000 | tf_op jit(solution)/shard_map/left/pallas_call | solution.py:443
  52.6 1.2 %collective-permute-start.15 = (f32[16,1152]{1,0:T(8,128)S(1)}, f32[16,1152]{1,0:T(8,128)S(1)}, u32[]{:S(2)}, u32[]{:S(2)}) collective-permute-start(f32[16,1152]{1,0:T(8,128)S(1)} %get-tuple-element.172), channel_id=1, source_target_pairs={{0,2},{1,3},{2,0},{3,1},{4,6},{5,7},{6,4},{7,5},{8,10},{9,11},{10,... | collective-permute-start | bytes 221192 | tf_op jit(solution)/shard_map/ppermute | solution.py:72
  53.9 1.2 %collective-permute-start.20 = (f32[72,576]{1,0:T(8,128)S(1)}, f32[72,576]{1,0:T(8,128)S(1)}, u32[]{:S(2)}, u32[]{:S(2)}) collective-permute-start(f32[72,576]{1,0:T(8,128)S(1)} %get-tuple-element.189), channel_id=1, source_target_pairs={{0,16},{4,20},{8,24},{12,28},{16,0},{20,4},{24,8},{28,12},{1,17},{... | collective-permute-start | bytes 497672 | tf_op jit(solution)/shard_map/ppermute | solution.py:72
  55.1 2.0 %collective-permute-done.15 = f32[16,1152]{1,0:T(8,128)S(1)} collective-permute-done((f32[16,1152]{1,0:T(8,128)S(1)}, f32[16,1152]{1,0:T(8,128)S(1)}, u32[]{:S(2)}, u32[]{:S(2)}) %collective-permute-start.15) | collective-permute-done | bytes 73760 | tf_op jit(solution)/shard_map/ppermute | solution.py:72
  57.7 0.7 insert.9.refs_2_
  58.4 3.1 %collective-permute-done.16 = f32[16,1152]{1,0:T(8,128)S(1)} collective-permute-done((f32[16,1152]{1,0:T(8,128)S(1)}, f32[16,1152]{1,0:T(8,128)S(1)}, u32[]{:S(2)}, u32[]{:S(2)}) %collective-permute-start.16) | collective-permute-done | bytes 73760 | tf_op jit(solution)/shard_map/ppermute | solution.py:72
  61.5 1.3 %collective-permute-start.19 = (f32[16,1152]{1,0:T(8,128)S(1)}, f32[16,1152]{1,0:T(8,128)S(1)}, u32[]{:S(2)}, u32[]{:S(2)}) collective-permute-start(f32[16,1152]{1,0:T(8,128)S(1)} %add.50), channel_id=1, source_target_pairs={{0,8},{4,12},{8,0},{12,4},{16,24},{20,28},{24,16},{28,20},{1,9},{5... | collective-permute-start | bytes 221192 | tf_op jit(solution)/shard_map/ppermute | solution.py:72
  64.0 2.0 %collective-permute-done.19 = f32[16,1152]{1,0:T(8,128)S(1)} collective-permute-done((f32[16,1152]{1,0:T(8,128)S(1)}, f32[16,1152]{1,0:T(8,128)S(1)}, u32[]{:S(2)}, u32[]{:S(2)}) %collective-permute-start.19) | collective-permute-done | bytes 73760 | tf_op jit(solution)/shard_map/ppermute | solution.py:72
  66.0 2.5 %collective-permute-start.22 = (f32[16,1152]{1,0:T(8,128)S(1)}, f32[16,1152]{1,0:T(8,128)S(1)}, u32[]{:S(2)}, u32[]{:S(2)}) collective-permute-start(f32[16,1152]{1,0:T(8,128)S(1)} %add.51), channel_id=1, source_target_pairs={{0,16},{4,20},{8,24},{12,28},{16,0},{20,4},{24,8},{28,12},{1,17},{... | collective-permute-start | bytes 221192 | tf_op jit(solution)/shard_map/ppermute | solution.py:72
  68.9 2.5 %collective-permute-done.22 = f32[16,1152]{1,0:T(8,128)S(1)} collective-permute-done((f32[16,1152]{1,0:T(8,128)S(1)}, f32[16,1152]{1,0:T(8,128)S(1)}, u32[]{:S(2)}, u32[]{:S(2)}) %collective-permute-start.22) | collective-permute-done | bytes 73760 | tf_op jit(solution)/shard_map/ppermute | solution.py:72
  71.3 1.2 %collective-permute-start.24 = (f32[16,1152]{1,0:T(8,128)S(1)}, f32[16,1152]{1,0:T(8,128)S(1)}, u32[]{:S(2)}, u32[]{:S(2)}) collective-permute-start(f32[16,1152]{1,0:T(8,128)S(1)} %add.52.ours), channel_id=1, source_target_pairs={{0,2},{1,3},{2,0},{3,1},{4,6},{5,7},{6,4},{7,5},{8,10},{9,11},{10,... | collective-permute-start | bytes 221192 | tf_op jit(solution)/shard_map/ppermute | solution.py:72
  72.6 1.5 %collective-permute-start.27 = (f32[72,576]{1,0:T(8,128)S(1)}, f32[72,576]{1,0:T(8,128)S(1)}, u32[]{:S(2)}, u32[]{:S(2)}) collective-permute-start(f32[72,576]{1,0:T(8,128)S(1)} %collective-permute-done.20.refs_0_), channel_id=1, source_target_pairs={{0,8},{4,12},{8,0},{12,4},{16,24},{20,28},{24,16},{28,20},{1,9},{5... | collective-permute-start | bytes 497672 | tf_op jit(solution)/shard_map/ppermute | solution.py:72
  75.0 0.8 collective-permute-done.24.got
  75.8 1.3 %right.3 = (f32[32,576]{1,0:T(8,128)S(1)}, f32[32,1280]{1,0:T(8,128)S(1)}) custom-call(s32[1]{0:T(128)} %bitcast.shard_ref, f32[32,1152]{1,0:T(8,128)S(1)} %join.3.whole, f32[2,288,1152]{2,1,0:T(8,128)S(1)} %get-tuple-element.132.corr, f32[288,1152]{1,0:T(8,128)S(1)} %collective-permute-done.7.other, f32[32,128]{1,0:T(8,128)S(1)} %get-tuple-element.209.refs_0_, ...), custom_call_target="tpu_custom_call" | custom-call | flops 1000 | bytes 1000 | tf_op jit(solution)/shard_map/right/pallas_call | solution.py:420
  77.2 0.8 collective-permute-start.26
  78.3 3.7 %collective-permute-done.26 = f32[32,576]{1,0:T(8,128)S(1)} collective-permute-done((f32[32,576]{1,0:T(8,128)S(1)}, f32[32,576]{1,0:T(8,128)S(1)}, u32[]{:S(2)}, u32[]{:S(2)}) %collective-permute-start.26) | collective-permute-done | bytes 73760 | tf_op jit(solution)/shard_map/ppermute | solution.py:72
  82.1 1.6 %collective-permute-start.30 = (f32[32,576]{1,0:T(8,128)S(1)}, f32[32,576]{1,0:T(8,128)S(1)}, u32[]{:S(2)}, u32[]{:S(2)}) collective-permute-start(f32[32,576]{1,0:T(8,128)S(1)} %add.53), channel_id=1, source_target_pairs={{0,8},{4,12},{8,0},{12,4},{16,24},{20,28},{24,16},{28,20},{1,9},{5... | collective-permute-start | bytes 221192 | tf_op jit(solution)/shard_map/ppermute | solution.py:72
  84.9 1.7 %collective-permute-done.30 = f32[32,576]{1,0:T(8,128)S(1)} collective-permute-done((f32[32,576]{1,0:T(8,128)S(1)}, f32[32,576]{1,0:T(8,128)S(1)}, u32[]{:S(2)}, u32[]{:S(2)}) %collective-permute-start.30) | collective-permute-done | bytes 73760 | tf_op jit(solution)/shard_map/ppermute | solution.py:72
  86.6 2.7 %collective-permute-start.31 = (f32[32,576]{1,0:T(8,128)S(1)}, f32[32,576]{1,0:T(8,128)S(1)}, u32[]{:S(2)}, u32[]{:S(2)}) collective-permute-start(f32[32,576]{1,0:T(8,128)S(1)} %add.54), channel_id=1, source_target_pairs={{0,16},{4,20},{8,24},{12,28},{16,0},{20,4},{24,8},{28,12},{1,17},{... | collective-permute-start | bytes 221192 | tf_op jit(solution)/shard_map/ppermute | solution.py:72
  89.3 1.3 %inverse.3 = f32[2,32,32]{2,1,0:T(8,128)S(1)} custom-call(f32[32,1280]{1,0:T(8,128)S(1)} %get-tuple-element.233.ours, f32[32,1280]{1,0:T(8,128)S(1)} %collective-permute-done.29.got.theirs), custom_call_target="tpu_custom_call" | custom-call | flops 1000 | bytes 6000000 | tf_op jit(solution)/shard_map/inverse/pallas_call | solution.py:489
  90.6 0.8 insert.14.refs_1_
  92.1 1.3 %collective-permute-done.32.their_right = f32[32,576]{1,0:T(8,128)S(1)} collective-permute-done((f32[32,576]{1,0:T(8,128)S(1)}, f32[32,576]{1,0:T(8,128)S(1)}, u32[]{:S(2)}, u32[]{:S(2)}) %collective-permute-start.32) | collective-permute-done | bytes 73760 | tf_op jit(solution)/shard_map/ppermute | solution.py:72
  93.7 3.5 %finish.1 = (f32[288,1152]{1,0:T(8,128)}, f32[288,1152]{1,0:T(8,128)}, f32[288,1152]{1,0:T(8,128)}, f32[288,1152]{1,0:T(8,128)}, f32[144,288]{1,0:T(8,128)}, /*index=5*/f32[144,288]{1,0:T(8,128)}) custom-call(s32[1]{0:T(128)} %bitcast.shard_ref, f32[2,288,1152]{2,1,0:T(8,128)S(1)} %get-tuple-element.132.corr, f32[576,1152]{1,0:T(8,128)S(1)} %insert.15.rows, ...), custom_call_target="tpu_custom_call" | custom-call | tf_op jit(solution)/shard_map/finish/pallas_call | solution.py:559
  (65 shorter events, 8.1 us)
Async XLA Ops:
  0.6 8.5 %copy-start = (f32[144,288]{1,0:T(8,128)S(1)}, f32[144,288]{1,0:T(8,128)}, u32[]{:S(2)}) copy-start(f32[144,288]{1,0:T(8,128)} %moment_q.3) | copy-start | bytes 497668
  0.7 8.5 %copy-start.1 = (f32[144,288]{1,0:T(8,128)S(1)}, f32[144,288]{1,0:T(8,128)}, u32[]{:S(2)}) copy-start(f32[144,288]{1,0:T(8,128)} %moment_o.3) | copy-start | bytes 497668
  0.7 8.5 %copy-start.2 = (f32[144,288]{1,0:T(8,128)S(1)}, f32[144,288]{1,0:T(8,128)}, u32[]{:S(2)}) copy-start(f32[144,288]{1,0:T(8,128)} %weight_q.1) | copy-start | bytes 497668
  0.7 8.5 %copy-start.3 = (f32[144,288]{1,0:T(8,128)S(1)}, f32[144,288]{1,0:T(8,128)}, u32[]{:S(2)}) copy-start(f32[144,288]{1,0:T(8,128)} %weight_o.1) | copy-start | bytes 497668
  4.5 1.5 %collective-permute-start = (f32[32,1280]{1,0:T(8,128)S(1)}, f32[32,1280]{1,0:T(8,128)S(1)}, u32[]{:S(2)}, u32[]{:S(2)}) collective-permute-start(f32[32,1280]{1,0:T(8,128)S(1)} %get-tuple-element.134), channel_id=1, source_target_pairs={{0,1},{1,0},{2,3},{3,2},{4,5},{5,4},{6,7},{7,6},{8,9},{9,8},{10,11... | collective-permute-start | bytes 491528 | tf_op jit(solution)/shard_map/ppermute | solution.py:72
  6.1 25.8 %collective-permute-start.7 = (f32[288,1152]{1,0:T(8,128)S(1)}, f32[288,1152]{1,0:T(8,128)S(1)}, u32[]{:S(2)}, u32[]{:S(2)}) collective-permute-start(f32[288,1152]{1,0:T(8,128)S(1)} %get-tuple-element.146), channel_id=1, source_target_pairs={{0,1},{1,0},{2,3},{3,2},{4,5},{5,4},{6,7},{7,6},{8,9},{9,8},{10,11... | collective-permute-start | bytes 3981320 | tf_op jit(solution)/shard_map/ppermute | solution.py:72
  6.5 5.6 %collective-permute-start.1 = (f32[16,1280]{1,0:T(8,128)S(1)}, f32[16,1280]{1,0:T(8,128)S(1)}, u32[]{:S(2)}, u32[]{:S(2)}) collective-permute-start(f32[16,1280]{1,0:T(8,128)S(1)} %get-tuple-element.140), channel_id=1, source_target_pairs={{0,2},{1,3},{2,0},{3,1},{4,6},{5,7},{6,4},{7,5},{8,10},{9,11},{10,... | collective-permute-start | bytes 245768 | tf_op jit(solution)/shard_map/ppermute | solution.py:72
  9.3 22.5 %collective-permute-start.6 = (f32[144,576]{1,0:T(8,128)S(1)}, f32[144,576]{1,0:T(8,128)S(1)}, u32[]{:S(2)}, u32[]{:S(2)}) collective-permute-start(f32[144,576]{1,0:T(8,128)S(1)} %get-tuple-element.150.refs_0_), channel_id=1, source_target_pairs={{0,8},{4,12},{8,0},{12,4},{16,24},{20,28},{24,16},{28,20},{1,9},{5... | collective-permute-start | bytes 995336 | tf_op jit(solution)/shard_map/ppermute | solution.py:72
  12.2 4.5 %collective-permute-start.2 = (f32[16,1280]{1,0:T(8,128)S(1)}, f32[16,1280]{1,0:T(8,128)S(1)}, u32[]{:S(2)}, u32[]{:S(2)}) collective-permute-start(f32[16,1280]{1,0:T(8,128)S(1)} %add.42), channel_id=1, source_target_pairs={{0,4},{4,0},{8,12},{12,8},{16,20},{20,16},{24,28},{28,24},{1,5},{5... | collective-permute-start | bytes 245768 | tf_op jit(solution)/shard_map/ppermute | solution.py:72
  16.7 5.0 %collective-permute-start.3 = (f32[16,1280]{1,0:T(8,128)S(1)}, f32[16,1280]{1,0:T(8,128)S(1)}, u32[]{:S(2)}, u32[]{:S(2)}) collective-permute-start(f32[16,1280]{1,0:T(8,128)S(1)} %add.43), channel_id=1, source_target_pairs={{0,8},{4,12},{8,0},{12,4},{16,24},{20,28},{24,16},{28,20},{1,9},{5... | collective-permute-start | bytes 245768 | tf_op jit(solution)/shard_map/ppermute | solution.py:72
  21.7 5.6 %collective-permute-start.4 = (f32[16,1280]{1,0:T(8,128)S(1)}, f32[16,1280]{1,0:T(8,128)S(1)}, u32[]{:S(2)}, u32[]{:S(2)}) collective-permute-start(f32[16,1280]{1,0:T(8,128)S(1)} %add.44), channel_id=1, source_target_pairs={{0,16},{4,20},{8,24},{12,28},{16,0},{20,4},{24,8},{28,12},{1,17},{... | collective-permute-start | bytes 245768 | tf_op jit(solution)/shard_map/ppermute | solution.py:72
  24.4 18.3 %collective-permute-start.12 = (f32[144,576]{1,0:T(8,128)S(1)}, f32[144,576]{1,0:T(8,128)S(1)}, u32[]{:S(2)}, u32[]{:S(2)}) collective-permute-start(f32[144,576]{1,0:T(8,128)S(1)} %get-tuple-element.150.refs_0_), channel_id=1, source_target_pairs={{0,4},{4,0},{8,12},{12,8},{16,20},{20,16},{24,28},{28,24},{1,5},{5... | collective-permute-start | bytes 995336 | tf_op jit(solution)/shard_map/ppermute | solution.py:72
  27.3 4.5 %collective-permute-start.5 = (f32[16,1280]{1,0:T(8,128)S(1)}, f32[16,1280]{1,0:T(8,128)S(1)}, u32[]{:S(2)}, u32[]{:S(2)}) collective-permute-start(f32[16,1280]{1,0:T(8,128)S(1)} %add.45.ours), channel_id=1, source_target_pairs={{0,2},{1,3},{2,0},{3,1},{4,6},{5,7},{6,4},{7,5},{8,10},{9,11},{10,... | collective-permute-start | bytes 245768 | tf_op jit(solution)/shard_map/ppermute | solution.py:72
  28.4 9.7 %collective-permute-start.9 = (f32[72,576]{1,0:T(8,128)S(1)}, f32[72,576]{1,0:T(8,128)S(1)}, u32[]{:S(2)}, u32[]{:S(2)}) collective-permute-start(f32[72,576]{1,0:T(8,128)S(1)} %get-tuple-element.154), channel_id=1, source_target_pairs={{0,16},{4,20},{8,24},{12,28},{16,0},{20,4},{24,8},{28,12},{1,17},{... | collective-permute-start | bytes 497672 | tf_op jit(solution)/shard_map/ppermute | solution.py:72
  33.2 5.0 %collective-permute-start.10 = (f32[32,1152]{1,0:T(8,128)S(1)}, f32[32,1152]{1,0:T(8,128)S(1)}, u32[]{:S(2)}, u32[]{:S(2)}) collective-permute-start(f32[32,1152]{1,0:T(8,128)S(1)} %get-tuple-element.158.ours), channel_id=1, source_target_pairs={{0,1},{1,0},{2,3},{3,2},{4,5},{5,4},{6,7},{7,6},{8,9},{9,8},{10,11... | collective-permute-start | bytes 442376 | tf_op jit(solution)/shard_map/ppermute | solution.py:72
  33.3 4.9 %collective-permute-start.8 = (f32[32,576]{1,0:T(8,128)S(1)}, f32[32,576]{1,0:T(8,128)S(1)}, u32[]{:S(2)}, u32[]{:S(2)}) collective-permute-start(f32[32,576]{1,0:T(8,128)S(1)} %get-tuple-element.149), channel_id=1, source_target_pairs={{0,4},{4,0},{8,12},{12,8},{16,20},{20,16},{24,28},{28,24},{1,5},{5... | collective-permute-start | bytes 221192 | tf_op jit(solution)/shard_map/ppermute | solution.py:72
  38.2 4.5 %collective-permute-start.11 = (f32[32,576]{1,0:T(8,128)S(1)}, f32[32,576]{1,0:T(8,128)S(1)}, u32[]{:S(2)}, u32[]{:S(2)}) collective-permute-start(f32[32,576]{1,0:T(8,128)S(1)} %add.46), channel_id=1, source_target_pairs={{0,8},{4,12},{8,0},{12,4},{16,24},{20,28},{24,16},{28,20},{1,9},{5... | collective-permute-start | bytes 221192 | tf_op jit(solution)/shard_map/ppermute | solution.py:72
  42.7 8.8 %collective-permute-start.14 = (f32[32,1280]{1,0:T(8,128)S(1)}, f32[32,1280]{1,0:T(8,128)S(1)}, u32[]{:S(2)}, u32[]{:S(2)}) collective-permute-start(f32[32,1280]{1,0:T(8,128)S(1)} %get-tuple-element.165.ours), channel_id=1, source_target_pairs={{0,1},{1,0},{2,3},{3,2},{4,5},{5,4},{6,7},{7,6},{8,9},{9,8},{10,11... | collective-permute-start | bytes 491528 | tf_op jit(solution)/shard_map/ppermute | solution.py:72
  42.8 23.2 %collective-permute-start.21 = (f32[144,576]{1,0:T(8,128)S(1)}, f32[144,576]{1,0:T(8,128)S(1)}, u32[]{:S(2)}, u32[]{:S(2)}) collective-permute-start(f32[144,576]{1,0:T(8,128)S(1)} %collective-permute-done.6.refs_0_), channel_id=1, source_target_pairs={{0,4},{4,0},{8,12},{12,8},{16,20},{20,16},{24,28},{28,24},{1,5},{5... | collective-permute-start | bytes 995336 | tf_op jit(solution)/shard_map/ppermute | solution.py:72
  44.4 7.1 %collective-permute-start.13 = (f32[32,576]{1,0:T(8,128)S(1)}, f32[32,576]{1,0:T(8,128)S(1)}, u32[]{:S(2)}, u32[]{:S(2)}) collective-permute-start(f32[32,576]{1,0:T(8,128)S(1)} %add.47), channel_id=1, source_target_pairs={{0,16},{4,20},{8,24},{12,28},{16,0},{20,4},{24,8},{28,12},{1,17},{... | collective-permute-start | bytes 221192 | tf_op jit(solution)/shard_map/ppermute | solution.py:72
  47.1 14.4 %collective-permute-start.17 = (f32[72,576]{1,0:T(8,128)S(1)}, f32[72,576]{1,0:T(8,128)S(1)}, u32[]{:S(2)}, u32[]{:S(2)}) collective-permute-start(f32[72,576]{1,0:T(8,128)S(1)} %collective-permute-done.9.refs_0_), channel_id=1, source_target_pairs={{0,8},{4,12},{8,0},{12,4},{16,24},{20,28},{24,16},{28,20},{1,9},{5... | collective-permute-start | bytes 497672 | tf_op jit(solution)/shard_map/ppermute | solution.py:72
  49.2 12.4 %collective-permute-start.18 = (f32[72,576]{1,0:T(8,128)S(1)}, f32[72,576]{1,0:T(8,128)S(1)}, u32[]{:S(2)}, u32[]{:S(2)}) collective-permute-start(f32[72,576]{1,0:T(8,128)S(1)} %collective-permute-done.9.refs_0_), channel_id=1, source_target_pairs={{0,4},{4,0},{8,12},{12,8},{16,20},{20,16},{24,28},{28,24},{1,5},{5... | collective-permute-start | bytes 497672 | tf_op jit(solution)/shard_map/ppermute | solution.py:72
  52.6 4.4 %collective-permute-start.15 = (f32[16,1152]{1,0:T(8,128)S(1)}, f32[16,1152]{1,0:T(8,128)S(1)}, u32[]{:S(2)}, u32[]{:S(2)}) collective-permute-start(f32[16,1152]{1,0:T(8,128)S(1)} %get-tuple-element.172), channel_id=1, source_target_pairs={{0,2},{1,3},{2,0},{3,1},{4,6},{5,7},{6,4},{7,5},{8,10},{9,11},{10,... | collective-permute-start | bytes 221192 | tf_op jit(solution)/shard_map/ppermute | solution.py:72
  53.9 12.1 %collective-permute-start.20 = (f32[72,576]{1,0:T(8,128)S(1)}, f32[72,576]{1,0:T(8,128)S(1)}, u32[]{:S(2)}, u32[]{:S(2)}) collective-permute-start(f32[72,576]{1,0:T(8,128)S(1)} %get-tuple-element.189), channel_id=1, source_target_pairs={{0,16},{4,20},{8,24},{12,28},{16,0},{20,4},{24,8},{28,12},{1,17},{... | collective-permute-start | bytes 497672 | tf_op jit(solution)/shard_map/ppermute | solution.py:72
  57.1 4.4 %collective-permute-start.16 = (f32[16,1152]{1,0:T(8,128)S(1)}, f32[16,1152]{1,0:T(8,128)S(1)}, u32[]{:S(2)}, u32[]{:S(2)}) collective-permute-start(f32[16,1152]{1,0:T(8,128)S(1)} %add.49), channel_id=1, source_target_pairs={{0,4},{4,0},{8,12},{12,8},{16,20},{20,16},{24,28},{28,24},{1,5},{5... | collective-permute-start | bytes 221192 | tf_op jit(solution)/shard_map/ppermute | solution.py:72
  61.5 4.4 %collective-permute-start.19 = (f32[16,1152]{1,0:T(8,128)S(1)}, f32[16,1152]{1,0:T(8,128)S(1)}, u32[]{:S(2)}, u32[]{:S(2)}) collective-permute-start(f32[16,1152]{1,0:T(8,128)S(1)} %add.50), channel_id=1, source_target_pairs={{0,8},{4,12},{8,0},{12,4},{16,24},{20,28},{24,16},{28,20},{1,9},{5... | collective-permute-start | bytes 221192 | tf_op jit(solution)/shard_map/ppermute | solution.py:72
  62.9 12.9 %collective-permute-start.25 = (f32[72,576]{1,0:T(8,128)S(1)}, f32[72,576]{1,0:T(8,128)S(1)}, u32[]{:S(2)}, u32[]{:S(2)}) collective-permute-start(f32[72,576]{1,0:T(8,128)S(1)} %collective-permute-done.17.refs_1_), channel_id=1, source_target_pairs={{0,4},{4,0},{8,12},{12,8},{16,20},{20,16},{24,28},{28,24},{1,5},{5... | collective-permute-start | bytes 497672 | tf_op jit(solution)/shard_map/ppermute | solution.py:72
  66.0 5.3 %collective-permute-start.22 = (f32[16,1152]{1,0:T(8,128)S(1)}, f32[16,1152]{1,0:T(8,128)S(1)}, u32[]{:S(2)}, u32[]{:S(2)}) collective-permute-start(f32[16,1152]{1,0:T(8,128)S(1)} %add.51), channel_id=1, source_target_pairs={{0,16},{4,20},{8,24},{12,28},{16,0},{20,4},{24,8},{28,12},{1,17},{... | collective-permute-start | bytes 221192 | tf_op jit(solution)/shard_map/ppermute | solution.py:72
  68.4 2.9 %collective-permute-start.23 = (f32[16,1152]{1,0:T(8,128)S(1)}, f32[16,1152]{1,0:T(8,128)S(1)}, u32[]{:S(2)}, u32[]{:S(2)}) collective-permute-start(f32[16,1152]{1,0:T(8,128)S(1)} %get-tuple-element.197), channel_id=1, source_target_pairs={{0,1},{1,0},{2,3},{3,2},{4,5},{5,4},{6,7},{7,6},{8,9},{9,8},{10,11... | collective-permute-start | bytes 221192 | tf_op jit(solution)/shard_map/ppermute | solution.py:72
  71.3 4.4 %collective-permute-start.24 = (f32[16,1152]{1,0:T(8,128)S(1)}, f32[16,1152]{1,0:T(8,128)S(1)}, u32[]{:S(2)}, u32[]{:S(2)}) collective-permute-start(f32[16,1152]{1,0:T(8,128)S(1)} %add.52.ours), channel_id=1, source_target_pairs={{0,2},{1,3},{2,0},{3,1},{4,6},{5,7},{6,4},{7,5},{8,10},{9,11},{10,... | collective-permute-start | bytes 221192 | tf_op jit(solution)/shard_map/ppermute | solution.py:72
  72.6 9.5 %collective-permute-start.27 = (f32[72,576]{1,0:T(8,128)S(1)}, f32[72,576]{1,0:T(8,128)S(1)}, u32[]{:S(2)}, u32[]{:S(2)}) collective-permute-start(f32[72,576]{1,0:T(8,128)S(1)} %collective-permute-done.20.refs_0_), channel_id=1, source_target_pairs={{0,8},{4,12},{8,0},{12,4},{16,24},{20,28},{24,16},{28,20},{1,9},{5... | collective-permute-start | bytes 497672 | tf_op jit(solution)/shard_map/ppermute | solution.py:72
  74.1 8.0 %collective-permute-start.28 = (f32[72,576]{1,0:T(8,128)S(1)}, f32[72,576]{1,0:T(8,128)S(1)}, u32[]{:S(2)}, u32[]{:S(2)}) collective-permute-start(f32[72,576]{1,0:T(8,128)S(1)} %collective-permute-done.20.refs_0_), channel_id=1, source_target_pairs={{0,4},{4,0},{8,12},{12,8},{16,20},{20,16},{24,28},{28,24},{1,5},{5... | collective-permute-start | bytes 497672 | tf_op jit(solution)/shard_map/ppermute | solution.py:72
  77.1 5.0 %collective-permute-start.29 = (f32[32,1280]{1,0:T(8,128)S(1)}, f32[32,1280]{1,0:T(8,128)S(1)}, u32[]{:S(2)}, u32[]{:S(2)}) collective-permute-start(f32[32,1280]{1,0:T(8,128)S(1)} %get-tuple-element.233.ours), channel_id=1, source_target_pairs={{0,1},{1,0},{2,3},{3,2},{4,5},{5,4},{6,7},{7,6},{8,9},{9,8},{10,11... | collective-permute-start | bytes 491528 | tf_op jit(solution)/shard_map/ppermute | solution.py:72
  77.2 7.0 %copy-start.4 = (f32[72]{0:T(128)S(1)}, f32[72]{0:T(128)}, u32[]{:S(2)}) copy-start(f32[72]{0:T(128)} %param.24) | copy-start | bytes 868
  77.2 4.8 %collective-permute-start.26 = (f32[32,576]{1,0:T(8,128)S(1)}, f32[32,576]{1,0:T(8,128)S(1)}, u32[]{:S(2)}, u32[]{:S(2)}) collective-permute-start(f32[32,576]{1,0:T(8,128)S(1)} %get-tuple-element.213), channel_id=1, source_target_pairs={{0,4},{4,0},{8,12},{12,8},{16,20},{20,16},{24,28},{28,24},{1,5},{5... | collective-permute-start | bytes 221192 | tf_op jit(solution)/shard_map/ppermute | solution.py:72
  82.1 4.5 %collective-permute-start.30 = (f32[32,576]{1,0:T(8,128)S(1)}, f32[32,576]{1,0:T(8,128)S(1)}, u32[]{:S(2)}, u32[]{:S(2)}) collective-permute-start(f32[32,576]{1,0:T(8,128)S(1)} %add.53), channel_id=1, source_target_pairs={{0,8},{4,12},{8,0},{12,4},{16,24},{20,28},{24,16},{28,20},{1,9},{5... | collective-permute-start | bytes 221192 | tf_op jit(solution)/shard_map/ppermute | solution.py:72
  83.6 8.5 %collective-permute-start.33 = (f32[72,576]{1,0:T(8,128)S(1)}, f32[72,576]{1,0:T(8,128)S(1)}, u32[]{:S(2)}, u32[]{:S(2)}) collective-permute-start(f32[72,576]{1,0:T(8,128)S(1)} %collective-permute-done.27.refs_1_), channel_id=1, source_target_pairs={{0,4},{4,0},{8,12},{12,8},{16,20},{20,16},{24,28},{28,24},{1,5},{5... | collective-permute-start | bytes 497672 | tf_op jit(solution)/shard_map/ppermute | solution.py:72
  86.6 5.4 %collective-permute-start.31 = (f32[32,576]{1,0:T(8,128)S(1)}, f32[32,576]{1,0:T(8,128)S(1)}, u32[]{:S(2)}, u32[]{:S(2)}) collective-permute-start(f32[32,576]{1,0:T(8,128)S(1)} %add.54), channel_id=1, source_target_pairs={{0,16},{4,20},{8,24},{12,28},{16,0},{20,4},{24,8},{28,12},{1,17},{... | collective-permute-start | bytes 221192 | tf_op jit(solution)/shard_map/ppermute | solution.py:72
  92.0 1.3 %collective-permute-start.32 = (f32[32,576]{1,0:T(8,128)S(1)}, f32[32,576]{1,0:T(8,128)S(1)}, u32[]{:S(2)}, u32[]{:S(2)}) collective-permute-start(f32[32,576]{1,0:T(8,128)S(1)} %add.55.right), channel_id=1, source_target_pairs={{0,1},{1,0},{2,3},{3,2},{4,5},{5,4},{6,7},{7,6},{8,9},{9,8},{10,11... | collective-permute-start | bytes 221192 | tf_op jit(solution)/shard_map/ppermute | solution.py:72

commit v12 on v11

--- a/solution.py
+++ b/solution.py
@@ -630,7 +630,7 @@
     (norm_moment_new, norm_weight_new), *terms = gather.results[3, 2]
     if gather.paired:
         stack, own = terms
-        their_right, turned = lax.optimization_barrier((their_right, gather.blocks["turned_last_b"]))
+        right, turned = lax.optimization_barrier((right, gather.blocks["turned_last_b"]))
         gather.insert([turned], ["turned_last_b"])
         outs = finish(shard, corr, gather.rows, stack, inverse, right, their_right, own, q_moment, o_moment)
     else:

time: 97.3 us -> 96.9 us (level)
  transfers between devices with their start and end apart: 34 -> 34, of which waited for: 18 -> 18; matrix products, arithmetic and copies ran while one was open for 0% -> 0% of each run, Pallas kernels for 11% -> 12%
where the time goes in v12:
time: 96.9 us; the launch traced here: 96.8 us
  starting transfers between devices  43.4 us (45%)
  waiting for transfers between devices  33.5 us (35%)
  Pallas kernels  18.7 us (19%)
  between operations  1.01 us (1%)
    ppermute x34, starting transfers between devices, swap(): return lax.ppermute(block, axis, pairs)  43.4 us
    ppermute x34, waiting for transfers between devices, swap(): return lax.ppermute(block, axis, pairs)  33.5 us
    pallas_call x8, Pallas kernels, insert(): pl.pallas_call(functools.partial(insert_kernel, masks, rows_each), in_spe...  4.11 us
    pallas_call x1, Pallas kernels, first(): pl.pallas_call(functools.partial(first_kernel, n_shard), in_specs=[IN_SME...  3.85 us
    pallas_call x1, Pallas kernels, finish(): pl.pallas_call(functools.partial(finish_kernel, chunks), in_specs=[IN_SME...  3.45 us
    pallas_call x2, Pallas kernels, right_of(): pl.pallas_call(functools.partial(right_kernel, len(more), len(waits)), in...  2.62 us
    pallas_call x2, Pallas kernels, inverse_of(): pl.pallas_call(functools.partial(inverse_kernel, size), out_shape=pltpu.V...  2.6 us
  transfers between devices with their start and end apart: 34, of which 18 were waited for; matrix products, arithmetic and copies ran while one was open for 0% of the time, Pallas kernels for 12%

profile of v12, /device:TPU:0, one launch (start us, length us, event | category | flops | bytes accessed | tf_op | source)
XLA Modules:
  0.0 96.8 jit_solution(55509712576946041)
XLA Ops:
  0.7 3.9 %first.1 = (f32[2,288,1152]{2,1,0:T(8,128)S(1)}, f32[288,1152]{1,0:T(8,128)S(1)}, f32[32,1280]{1,0:T(8,128)S(1)}, f32[32,1280]{1,0:T(8,128)S(1)}) custom-call(s32[1]{0:T(128)} %bitcast.1.place_ref, s32[1]{0:T(128)} %bitcast.shard_ref, f32[288,1152]{1,0:T(8,128)} %bitcast.31, f32[288,1152]{1,0:T(8,128)} %bitcast.32, f32[288,1152]{1,0:T(8,128)} %bitcast.33, ...), custom_call_target="tpu_custom_call" | custom-call | tf_op jit(solution)/shard_map/first/pallas_call | solution.py:383
  5.1 1.0 %collective-permute-done.got = f32[32,1280]{1,0:T(8,128)S(1)} collective-permute-done((f32[32,1280]{1,0:T(8,128)S(1)}, f32[32,1280]{1,0:T(8,128)S(1)}, u32[]{:S(2)}, u32[]{:S(2)}) %collective-permute-start) | collective-permute-done | bytes 163872 | tf_op jit(solution)/shard_map/ppermute | solution.py:72
  6.5 2.6 %collective-permute-start.1 = (f32[16,1280]{1,0:T(8,128)S(1)}, f32[16,1280]{1,0:T(8,128)S(1)}, u32[]{:S(2)}, u32[]{:S(2)}) collective-permute-start(f32[16,1280]{1,0:T(8,128)S(1)} %get-tuple-element.140), channel_id=1, source_target_pairs={{0,2},{1,3},{2,0},{3,1},{4,6},{5,7},{6,4},{7,5},{8,10},{9,11},{10,... | collective-permute-start | bytes 245768 | tf_op jit(solution)/shard_map/ppermute | solution.py:72
  9.3 1.6 %collective-permute-start.6 = (f32[144,576]{1,0:T(8,128)S(1)}, f32[144,576]{1,0:T(8,128)S(1)}, u32[]{:S(2)}, u32[]{:S(2)}) collective-permute-start(f32[144,576]{1,0:T(8,128)S(1)} %get-tuple-element.150.refs_0_), channel_id=1, source_target_pairs={{0,8},{4,12},{8,0},{12,4},{16,24},{20,28},{24,16},{28,20},{1,9},{5... | collective-permute-start | bytes 995336 | tf_op jit(solution)/shard_map/ppermute | solution.py:72
  11.0 1.2 %collective-permute-done.1 = f32[16,1280]{1,0:T(8,128)S(1)} collective-permute-done((f32[16,1280]{1,0:T(8,128)S(1)}, f32[16,1280]{1,0:T(8,128)S(1)}, u32[]{:S(2)}, u32[]{:S(2)}) %collective-permute-start.1) | collective-permute-done | bytes 81952 | tf_op jit(solution)/shard_map/ppermute | solution.py:72
  12.2 1.8 %collective-permute-start.2 = (f32[16,1280]{1,0:T(8,128)S(1)}, f32[16,1280]{1,0:T(8,128)S(1)}, u32[]{:S(2)}, u32[]{:S(2)}) collective-permute-start(f32[16,1280]{1,0:T(8,128)S(1)} %add.42), channel_id=1, source_target_pairs={{0,4},{4,0},{8,12},{12,8},{16,20},{20,16},{24,28},{28,24},{1,5},{5... | collective-permute-start | bytes 245768 | tf_op jit(solution)/shard_map/ppermute | solution.py:72
  14.0 2.7 %collective-permute-done.2 = f32[16,1280]{1,0:T(8,128)S(1)} collective-permute-done((f32[16,1280]{1,0:T(8,128)S(1)}, f32[16,1280]{1,0:T(8,128)S(1)}, u32[]{:S(2)}, u32[]{:S(2)}) %collective-permute-start.2) | collective-permute-done | bytes 81952 | tf_op jit(solution)/shard_map/ppermute | solution.py:72
  16.7 1.9 %collective-permute-start.3 = (f32[16,1280]{1,0:T(8,128)S(1)}, f32[16,1280]{1,0:T(8,128)S(1)}, u32[]{:S(2)}, u32[]{:S(2)}) collective-permute-start(f32[16,1280]{1,0:T(8,128)S(1)} %add.43), channel_id=1, source_target_pairs={{0,8},{4,12},{8,0},{12,4},{16,24},{20,28},{24,16},{28,20},{1,9},{5... | collective-permute-start | bytes 245768 | tf_op jit(solution)/shard_map/ppermute | solution.py:72
  18.6 3.2 %collective-permute-done.3 = f32[16,1280]{1,0:T(8,128)S(1)} collective-permute-done((f32[16,1280]{1,0:T(8,128)S(1)}, f32[16,1280]{1,0:T(8,128)S(1)}, u32[]{:S(2)}, u32[]{:S(2)}) %collective-permute-start.3) | collective-permute-done | bytes 81952 | tf_op jit(solution)/shard_map/ppermute | solution.py:72
  21.7 2.7 %collective-permute-start.4 = (f32[16,1280]{1,0:T(8,128)S(1)}, f32[16,1280]{1,0:T(8,128)S(1)}, u32[]{:S(2)}, u32[]{:S(2)}) collective-permute-start(f32[16,1280]{1,0:T(8,128)S(1)} %add.44), channel_id=1, source_target_pairs={{0,16},{4,20},{8,24},{12,28},{16,0},{20,4},{24,8},{28,12},{1,17},{... | collective-permute-start | bytes 245768 | tf_op jit(solution)/shard_map/ppermute | solution.py:72
  24.4 1.5 %collective-permute-start.12 = (f32[144,576]{1,0:T(8,128)S(1)}, f32[144,576]{1,0:T(8,128)S(1)}, u32[]{:S(2)}, u32[]{:S(2)}) collective-permute-start(f32[144,576]{1,0:T(8,128)S(1)} %get-tuple-element.150.refs_0_), channel_id=1, source_target_pairs={{0,4},{4,0},{8,12},{12,8},{16,20},{20,16},{24,28},{28,24},{1,5},{5... | collective-permute-start | bytes 995336 | tf_op jit(solution)/shard_map/ppermute | solution.py:72
  25.9 1.4 %collective-permute-done.4 = f32[16,1280]{1,0:T(8,128)S(1)} collective-permute-done((f32[16,1280]{1,0:T(8,128)S(1)}, f32[16,1280]{1,0:T(8,128)S(1)}, u32[]{:S(2)}, u32[]{:S(2)}) %collective-permute-start.4) | collective-permute-done | bytes 81952 | tf_op jit(solution)/shard_map/ppermute | solution.py:72
  27.3 1.1 %collective-permute-start.5 = (f32[16,1280]{1,0:T(8,128)S(1)}, f32[16,1280]{1,0:T(8,128)S(1)}, u32[]{:S(2)}, u32[]{:S(2)}) collective-permute-start(f32[16,1280]{1,0:T(8,128)S(1)} %add.45.ours), channel_id=1, source_target_pairs={{0,2},{1,3},{2,0},{3,1},{4,6},{5,7},{6,4},{7,5},{8,10},{9,11},{10,... | collective-permute-start | bytes 245768 | tf_op jit(solution)/shard_map/ppermute | solution.py:72
  28.4 2.7 %collective-permute-start.9 = (f32[72,576]{1,0:T(8,128)S(1)}, f32[72,576]{1,0:T(8,128)S(1)}, u32[]{:S(2)}, u32[]{:S(2)}) collective-permute-start(f32[72,576]{1,0:T(8,128)S(1)} %get-tuple-element.154), channel_id=1, source_target_pairs={{0,16},{4,20},{8,24},{12,28},{16,0},{20,4},{24,8},{28,12},{1,17},{... | collective-permute-start | bytes 497672 | tf_op jit(solution)/shard_map/ppermute | solution.py:72
  31.1 0.7 collective-permute-done.5.got
  31.9 1.3 %right.2 = (f32[32,576]{1,0:T(8,128)S(1)}, f32[32,1152]{1,0:T(8,128)S(1)}, f32[32,128]{1,0:T(8,128)S(1)}) custom-call(s32[1]{0:T(128)} %bitcast.shard_ref, f32[32,1280]{1,0:T(8,128)S(1)} %join.2.whole, f32[2,288,1152]{2,1,0:T(8,128)S(1)} %get-tuple-element.132.corr, f32[288,1152]{1,0:T(8,128)S(1)} %collective-permute-done.7.other), custom_call_target="tpu_custom_call" | custom-call | flops 1000 | bytes 1000 | tf_op jit(solution)/shard_map/right/pallas_call | solution.py:420
  33.3 1.6 %collective-permute-start.8 = (f32[32,576]{1,0:T(8,128)S(1)}, f32[32,576]{1,0:T(8,128)S(1)}, u32[]{:S(2)}, u32[]{:S(2)}) collective-permute-start(f32[32,576]{1,0:T(8,128)S(1)} %get-tuple-element.149), channel_id=1, source_target_pairs={{0,4},{4,0},{8,12},{12,8},{16,20},{20,16},{24,28},{28,24},{1,5},{5... | collective-permute-start | bytes 221192 | tf_op jit(solution)/shard_map/ppermute | solution.py:72
  35.4 2.7 %collective-permute-done.8 = f32[32,576]{1,0:T(8,128)S(1)} collective-permute-done((f32[32,576]{1,0:T(8,128)S(1)}, f32[32,576]{1,0:T(8,128)S(1)}, u32[]{:S(2)}, u32[]{:S(2)}) %collective-permute-start.8) | collective-permute-done | bytes 73760 | tf_op jit(solution)/shard_map/ppermute | solution.py:72
  38.2 1.6 %collective-permute-start.11 = (f32[32,576]{1,0:T(8,128)S(1)}, f32[32,576]{1,0:T(8,128)S(1)}, u32[]{:S(2)}, u32[]{:S(2)}) collective-permute-start(f32[32,576]{1,0:T(8,128)S(1)} %add.46), channel_id=1, source_target_pairs={{0,8},{4,12},{8,0},{12,4},{16,24},{20,28},{24,16},{28,20},{1,9},{5... | collective-permute-start | bytes 221192 | tf_op jit(solution)/shard_map/ppermute | solution.py:72
  39.8 1.3 %inverse.2 = f32[2,32,32]{2,1,0:T(8,128)S(1)} custom-call(f32[32,1152]{1,0:T(8,128)S(1)} %get-tuple-element.158.ours, f32[32,1152]{1,0:T(8,128)S(1)} %collective-permute-done.10.theirs), custom_call_target="tpu_custom_call" | custom-call | flops 1000 | bytes 6000000 | tf_op jit(solution)/shard_map/inverse/pallas_call | solution.py:489
  41.1 1.6 %collective-permute-done.11 = f32[32,576]{1,0:T(8,128)S(1)} collective-permute-done((f32[32,576]{1,0:T(8,128)S(1)}, f32[32,576]{1,0:T(8,128)S(1)}, u32[]{:S(2)}, u32[]{:S(2)}) %collective-permute-start.11) | collective-permute-done | bytes 73760 | tf_op jit(solution)/shard_map/ppermute | solution.py:72
  42.8 1.6 %collective-permute-start.21 = (f32[144,576]{1,0:T(8,128)S(1)}, f32[144,576]{1,0:T(8,128)S(1)}, u32[]{:S(2)}, u32[]{:S(2)}) collective-permute-start(f32[144,576]{1,0:T(8,128)S(1)} %collective-permute-done.6.refs_0_), channel_id=1, source_target_pairs={{0,4},{4,0},{8,12},{12,8},{16,20},{20,16},{24,28},{28,24},{1,5},{5... | collective-permute-start | bytes 995336 | tf_op jit(solution)/shard_map/ppermute | solution.py:72
  44.4 2.8 %collective-permute-start.13 = (f32[32,576]{1,0:T(8,128)S(1)}, f32[32,576]{1,0:T(8,128)S(1)}, u32[]{:S(2)}, u32[]{:S(2)}) collective-permute-start(f32[32,576]{1,0:T(8,128)S(1)} %add.47), channel_id=1, source_target_pairs={{0,16},{4,20},{8,24},{12,28},{16,0},{20,4},{24,8},{28,12},{1,17},{... | collective-permute-start | bytes 221192 | tf_op jit(solution)/shard_map/ppermute | solution.py:72
  47.1 2.0 %collective-permute-start.17 = (f32[72,576]{1,0:T(8,128)S(1)}, f32[72,576]{1,0:T(8,128)S(1)}, u32[]{:S(2)}, u32[]{:S(2)}) collective-permute-start(f32[72,576]{1,0:T(8,128)S(1)} %collective-permute-done.9.refs_0_), channel_id=1, source_target_pairs={{0,8},{4,12},{8,0},{12,4},{16,24},{20,28},{24,16},{28,20},{1,9},{5... | collective-permute-start | bytes 497672 | tf_op jit(solution)/shard_map/ppermute | solution.py:72
  49.7 1.8 %collective-permute-done.13 = f32[32,576]{1,0:T(8,128)S(1)} collective-permute-done((f32[32,576]{1,0:T(8,128)S(1)}, f32[32,576]{1,0:T(8,128)S(1)}, u32[]{:S(2)}, u32[]{:S(2)}) %collective-permute-start.13) | collective-permute-done | bytes 73760 | tf_op jit(solution)/shard_map/ppermute | solution.py:72
  51.5 1.2 %left.1 = (f32[16,1152]{1,0:T(8,128)S(1)}, f32[16,1152]{1,0:T(8,128)S(1)}) custom-call(s32[1]{0:T(128)} %bitcast.shard_ref, f32[32,576]{1,0:T(8,128)S(1)} %add.48.right, f32[2,32,32]{2,1,0:T(8,128)S(1)} %inverse.2, f32[2,288,1152]{2,1,0:T(8,128)S(1)} %get-tuple-element.132.corr, f32[288,1152]{1,0:T(8,128)S(1)} %collective-permute-done.7.other, ...), custom_call_target="tpu_custom_call" | custom-call | flops 1000 | bytes 1000 | tf_op jit(solution)/shard_map/left/pallas_call | solution.py:443
  52.6 1.2 %collective-permute-start.15 = (f32[16,1152]{1,0:T(8,128)S(1)}, f32[16,1152]{1,0:T(8,128)S(1)}, u32[]{:S(2)}, u32[]{:S(2)}) collective-permute-start(f32[16,1152]{1,0:T(8,128)S(1)} %get-tuple-element.172), channel_id=1, source_target_pairs={{0,2},{1,3},{2,0},{3,1},{4,6},{5,7},{6,4},{7,5},{8,10},{9,11},{10,... | collective-permute-start | bytes 221192 | tf_op jit(solution)/shard_map/ppermute | solution.py:72
  53.9 1.2 %collective-permute-start.20 = (f32[72,576]{1,0:T(8,128)S(1)}, f32[72,576]{1,0:T(8,128)S(1)}, u32[]{:S(2)}, u32[]{:S(2)}) collective-permute-start(f32[72,576]{1,0:T(8,128)S(1)} %get-tuple-element.189), channel_id=1, source_target_pairs={{0,16},{4,20},{8,24},{12,28},{16,0},{20,4},{24,8},{28,12},{1,17},{... | collective-permute-start | bytes 497672 | tf_op jit(solution)/shard_map/ppermute | solution.py:72
  55.1 2.0 %collective-permute-done.15 = f32[16,1152]{1,0:T(8,128)S(1)} collective-permute-done((f32[16,1152]{1,0:T(8,128)S(1)}, f32[16,1152]{1,0:T(8,128)S(1)}, u32[]{:S(2)}, u32[]{:S(2)}) %collective-permute-start.15) | collective-permute-done | bytes 73760 | tf_op jit(solution)/shard_map/ppermute | solution.py:72
  57.7 0.7 insert.9.refs_2_
  58.4 3.1 %collective-permute-done.16 = f32[16,1152]{1,0:T(8,128)S(1)} collective-permute-done((f32[16,1152]{1,0:T(8,128)S(1)}, f32[16,1152]{1,0:T(8,128)S(1)}, u32[]{:S(2)}, u32[]{:S(2)}) %collective-permute-start.16) | collective-permute-done | bytes 73760 | tf_op jit(solution)/shard_map/ppermute | solution.py:72
  61.5 1.3 %collective-permute-start.19 = (f32[16,1152]{1,0:T(8,128)S(1)}, f32[16,1152]{1,0:T(8,128)S(1)}, u32[]{:S(2)}, u32[]{:S(2)}) collective-permute-start(f32[16,1152]{1,0:T(8,128)S(1)} %add.50), channel_id=1, source_target_pairs={{0,8},{4,12},{8,0},{12,4},{16,24},{20,28},{24,16},{28,20},{1,9},{5... | collective-permute-start | bytes 221192 | tf_op jit(solution)/shard_map/ppermute | solution.py:72
  64.0 2.0 %collective-permute-done.19 = f32[16,1152]{1,0:T(8,128)S(1)} collective-permute-done((f32[16,1152]{1,0:T(8,128)S(1)}, f32[16,1152]{1,0:T(8,128)S(1)}, u32[]{:S(2)}, u32[]{:S(2)}) %collective-permute-start.19) | collective-permute-done | bytes 73760 | tf_op jit(solution)/shard_map/ppermute | solution.py:72
  66.0 2.5 %collective-permute-start.22 = (f32[16,1152]{1,0:T(8,128)S(1)}, f32[16,1152]{1,0:T(8,128)S(1)}, u32[]{:S(2)}, u32[]{:S(2)}) collective-permute-start(f32[16,1152]{1,0:T(8,128)S(1)} %add.51), channel_id=1, source_target_pairs={{0,16},{4,20},{8,24},{12,28},{16,0},{20,4},{24,8},{28,12},{1,17},{... | collective-permute-start | bytes 221192 | tf_op jit(solution)/shard_map/ppermute | solution.py:72
  68.9 2.5 %collective-permute-done.22 = f32[16,1152]{1,0:T(8,128)S(1)} collective-permute-done((f32[16,1152]{1,0:T(8,128)S(1)}, f32[16,1152]{1,0:T(8,128)S(1)}, u32[]{:S(2)}, u32[]{:S(2)}) %collective-permute-start.22) | collective-permute-done | bytes 73760 | tf_op jit(solution)/shard_map/ppermute | solution.py:72
  71.3 1.2 %collective-permute-start.24 = (f32[16,1152]{1,0:T(8,128)S(1)}, f32[16,1152]{1,0:T(8,128)S(1)}, u32[]{:S(2)}, u32[]{:S(2)}) collective-permute-start(f32[16,1152]{1,0:T(8,128)S(1)} %add.52.ours), channel_id=1, source_target_pairs={{0,2},{1,3},{2,0},{3,1},{4,6},{5,7},{6,4},{7,5},{8,10},{9,11},{10,... | collective-permute-start | bytes 221192 | tf_op jit(solution)/shard_map/ppermute | solution.py:72
  72.6 1.5 %collective-permute-start.27 = (f32[72,576]{1,0:T(8,128)S(1)}, f32[72,576]{1,0:T(8,128)S(1)}, u32[]{:S(2)}, u32[]{:S(2)}) collective-permute-start(f32[72,576]{1,0:T(8,128)S(1)} %collective-permute-done.20.refs_0_), channel_id=1, source_target_pairs={{0,8},{4,12},{8,0},{12,4},{16,24},{20,28},{24,16},{28,20},{1,9},{5... | collective-permute-start | bytes 497672 | tf_op jit(solution)/shard_map/ppermute | solution.py:72
  75.0 0.8 collective-permute-done.24.got
  75.8 1.3 %right.3 = (f32[32,576]{1,0:T(8,128)S(1)}, f32[32,1280]{1,0:T(8,128)S(1)}) custom-call(s32[1]{0:T(128)} %bitcast.shard_ref, f32[32,1152]{1,0:T(8,128)S(1)} %join.3.whole, f32[2,288,1152]{2,1,0:T(8,128)S(1)} %get-tuple-element.132.corr, f32[288,1152]{1,0:T(8,128)S(1)} %collective-permute-done.7.other, f32[32,128]{1,0:T(8,128)S(1)} %get-tuple-element.209.refs_0_, ...), custom_call_target="tpu_custom_call" | custom-call | flops 1000 | bytes 1000 | tf_op jit(solution)/shard_map/right/pallas_call | solution.py:420
  77.2 0.8 collective-permute-start.26
  78.3 3.7 %collective-permute-done.26 = f32[32,576]{1,0:T(8,128)S(1)} collective-permute-done((f32[32,576]{1,0:T(8,128)S(1)}, f32[32,576]{1,0:T(8,128)S(1)}, u32[]{:S(2)}, u32[]{:S(2)}) %collective-permute-start.26) | collective-permute-done | bytes 73760 | tf_op jit(solution)/shard_map/ppermute | solution.py:72
  82.1 1.6 %collective-permute-start.30 = (f32[32,576]{1,0:T(8,128)S(1)}, f32[32,576]{1,0:T(8,128)S(1)}, u32[]{:S(2)}, u32[]{:S(2)}) collective-permute-start(f32[32,576]{1,0:T(8,128)S(1)} %add.53), channel_id=1, source_target_pairs={{0,8},{4,12},{8,0},{12,4},{16,24},{20,28},{24,16},{28,20},{1,9},{5... | collective-permute-start | bytes 221192 | tf_op jit(solution)/shard_map/ppermute | solution.py:72
  84.9 1.7 %collective-permute-done.30 = f32[32,576]{1,0:T(8,128)S(1)} collective-permute-done((f32[32,576]{1,0:T(8,128)S(1)}, f32[32,576]{1,0:T(8,128)S(1)}, u32[]{:S(2)}, u32[]{:S(2)}) %collective-permute-start.30) | collective-permute-done | bytes 73760 | tf_op jit(solution)/shard_map/ppermute | solution.py:72
  86.6 2.7 %collective-permute-start.31 = (f32[32,576]{1,0:T(8,128)S(1)}, f32[32,576]{1,0:T(8,128)S(1)}, u32[]{:S(2)}, u32[]{:S(2)}) collective-permute-start(f32[32,576]{1,0:T(8,128)S(1)} %add.54), channel_id=1, source_target_pairs={{0,16},{4,20},{8,24},{12,28},{16,0},{20,4},{24,8},{28,12},{1,17},{... | collective-permute-start | bytes 221192 | tf_op jit(solution)/shard_map/ppermute | solution.py:72
  89.3 1.3 %inverse.3 = f32[2,32,32]{2,1,0:T(8,128)S(1)} custom-call(f32[32,1280]{1,0:T(8,128)S(1)} %get-tuple-element.233.ours, f32[32,1280]{1,0:T(8,128)S(1)} %collective-permute-done.29.got.theirs), custom_call_target="tpu_custom_call" | custom-call | flops 1000 | bytes 6000000 | tf_op jit(solution)/shard_map/inverse/pallas_call | solution.py:489
  90.6 0.8 insert.14.refs_1_
  92.4 0.9 collective-permute-done.33.their_right
  93.4 3.4 %finish.1 = (f32[288,1152]{1,0:T(8,128)}, f32[288,1152]{1,0:T(8,128)}, f32[288,1152]{1,0:T(8,128)}, f32[288,1152]{1,0:T(8,128)}, f32[144,288]{1,0:T(8,128)}, /*index=5*/f32[144,288]{1,0:T(8,128)}) custom-call(s32[1]{0:T(128)} %bitcast.shard_ref, f32[2,288,1152]{2,1,0:T(8,128)S(1)} %get-tuple-element.132.corr, f32[576,1152]{1,0:T(8,128)S(1)} %insert.15.rows, ...), custom_call_target="tpu_custom_call" | custom-call | tf_op jit(solution)/shard_map/finish/pallas_call | solution.py:559
  (65 shorter events, 8.1 us)
Async XLA Ops:
  0.6 8.5 %copy-start = (f32[144,288]{1,0:T(8,128)S(1)}, f32[144,288]{1,0:T(8,128)}, u32[]{:S(2)}) copy-start(f32[144,288]{1,0:T(8,128)} %moment_q.3) | copy-start | bytes 497668
  0.7 8.5 %copy-start.1 = (f32[144,288]{1,0:T(8,128)S(1)}, f32[144,288]{1,0:T(8,128)}, u32[]{:S(2)}) copy-start(f32[144,288]{1,0:T(8,128)} %moment_o.3) | copy-start | bytes 497668
  0.7 8.5 %copy-start.2 = (f32[144,288]{1,0:T(8,128)S(1)}, f32[144,288]{1,0:T(8,128)}, u32[]{:S(2)}) copy-start(f32[144,288]{1,0:T(8,128)} %weight_q.1) | copy-start | bytes 497668
  0.7 8.5 %copy-start.3 = (f32[144,288]{1,0:T(8,128)S(1)}, f32[144,288]{1,0:T(8,128)}, u32[]{:S(2)}) copy-start(f32[144,288]{1,0:T(8,128)} %weight_o.1) | copy-start | bytes 497668
  4.5 1.5 %collective-permute-start = (f32[32,1280]{1,0:T(8,128)S(1)}, f32[32,1280]{1,0:T(8,128)S(1)}, u32[]{:S(2)}, u32[]{:S(2)}) collective-permute-start(f32[32,1280]{1,0:T(8,128)S(1)} %get-tuple-element.134), channel_id=1, source_target_pairs={{0,1},{1,0},{2,3},{3,2},{4,5},{5,4},{6,7},{7,6},{8,9},{9,8},{10,11... | collective-permute-start | bytes 491528 | tf_op jit(solution)/shard_map/ppermute | solution.py:72
  6.1 25.8 %collective-permute-start.7 = (f32[288,1152]{1,0:T(8,128)S(1)}, f32[288,1152]{1,0:T(8,128)S(1)}, u32[]{:S(2)}, u32[]{:S(2)}) collective-permute-start(f32[288,1152]{1,0:T(8,128)S(1)} %get-tuple-element.146), channel_id=1, source_target_pairs={{0,1},{1,0},{2,3},{3,2},{4,5},{5,4},{6,7},{7,6},{8,9},{9,8},{10,11... | collective-permute-start | bytes 3981320 | tf_op jit(solution)/shard_map/ppermute | solution.py:72
  6.5 5.6 %collective-permute-start.1 = (f32[16,1280]{1,0:T(8,128)S(1)}, f32[16,1280]{1,0:T(8,128)S(1)}, u32[]{:S(2)}, u32[]{:S(2)}) collective-permute-start(f32[16,1280]{1,0:T(8,128)S(1)} %get-tuple-element.140), channel_id=1, source_target_pairs={{0,2},{1,3},{2,0},{3,1},{4,6},{5,7},{6,4},{7,5},{8,10},{9,11},{10,... | collective-permute-start | bytes 245768 | tf_op jit(solution)/shard_map/ppermute | solution.py:72
  9.3 22.5 %collective-permute-start.6 = (f32[144,576]{1,0:T(8,128)S(1)}, f32[144,576]{1,0:T(8,128)S(1)}, u32[]{:S(2)}, u32[]{:S(2)}) collective-permute-start(f32[144,576]{1,0:T(8,128)S(1)} %get-tuple-element.150.refs_0_), channel_id=1, source_target_pairs={{0,8},{4,12},{8,0},{12,4},{16,24},{20,28},{24,16},{28,20},{1,9},{5... | collective-permute-start | bytes 995336 | tf_op jit(solution)/shard_map/ppermute | solution.py:72
  12.2 4.5 %collective-permute-start.2 = (f32[16,1280]{1,0:T(8,128)S(1)}, f32[16,1280]{1,0:T(8,128)S(1)}, u32[]{:S(2)}, u32[]{:S(2)}) collective-permute-start(f32[16,1280]{1,0:T(8,128)S(1)} %add.42), channel_id=1, source_target_pairs={{0,4},{4,0},{8,12},{12,8},{16,20},{20,16},{24,28},{28,24},{1,5},{5... | collective-permute-start | bytes 245768 | tf_op jit(solution)/shard_map/ppermute | solution.py:72
  16.7 5.0 %collective-permute-start.3 = (f32[16,1280]{1,0:T(8,128)S(1)}, f32[16,1280]{1,0:T(8,128)S(1)}, u32[]{:S(2)}, u32[]{:S(2)}) collective-permute-start(f32[16,1280]{1,0:T(8,128)S(1)} %add.43), channel_id=1, source_target_pairs={{0,8},{4,12},{8,0},{12,4},{16,24},{20,28},{24,16},{28,20},{1,9},{5... | collective-permute-start | bytes 245768 | tf_op jit(solution)/shard_map/ppermute | solution.py:72
  21.7 5.6 %collective-permute-start.4 = (f32[16,1280]{1,0:T(8,128)S(1)}, f32[16,1280]{1,0:T(8,128)S(1)}, u32[]{:S(2)}, u32[]{:S(2)}) collective-permute-start(f32[16,1280]{1,0:T(8,128)S(1)} %add.44), channel_id=1, source_target_pairs={{0,16},{4,20},{8,24},{12,28},{16,0},{20,4},{24,8},{28,12},{1,17},{... | collective-permute-start | bytes 245768 | tf_op jit(solution)/shard_map/ppermute | solution.py:72
  24.4 18.3 %collective-permute-start.12 = (f32[144,576]{1,0:T(8,128)S(1)}, f32[144,576]{1,0:T(8,128)S(1)}, u32[]{:S(2)}, u32[]{:S(2)}) collective-permute-start(f32[144,576]{1,0:T(8,128)S(1)} %get-tuple-element.150.refs_0_), channel_id=1, source_target_pairs={{0,4},{4,0},{8,12},{12,8},{16,20},{20,16},{24,28},{28,24},{1,5},{5... | collective-permute-start | bytes 995336 | tf_op jit(solution)/shard_map/ppermute | solution.py:72
  27.3 4.5 %collective-permute-start.5 = (f32[16,1280]{1,0:T(8,128)S(1)}, f32[16,1280]{1,0:T(8,128)S(1)}, u32[]{:S(2)}, u32[]{:S(2)}) collective-permute-start(f32[16,1280]{1,0:T(8,128)S(1)} %add.45.ours), channel_id=1, source_target_pairs={{0,2},{1,3},{2,0},{3,1},{4,6},{5,7},{6,4},{7,5},{8,10},{9,11},{10,... | collective-permute-start | bytes 245768 | tf_op jit(solution)/shard_map/ppermute | solution.py:72
  28.4 9.7 %collective-permute-start.9 = (f32[72,576]{1,0:T(8,128)S(1)}, f32[72,576]{1,0:T(8,128)S(1)}, u32[]{:S(2)}, u32[]{:S(2)}) collective-permute-start(f32[72,576]{1,0:T(8,128)S(1)} %get-tuple-element.154), channel_id=1, source_target_pairs={{0,16},{4,20},{8,24},{12,28},{16,0},{20,4},{24,8},{28,12},{1,17},{... | collective-permute-start | bytes 497672 | tf_op jit(solution)/shard_map/ppermute | solution.py:72
  33.2 5.0 %collective-permute-start.10 = (f32[32,1152]{1,0:T(8,128)S(1)}, f32[32,1152]{1,0:T(8,128)S(1)}, u32[]{:S(2)}, u32[]{:S(2)}) collective-permute-start(f32[32,1152]{1,0:T(8,128)S(1)} %get-tuple-element.158.ours), channel_id=1, source_target_pairs={{0,1},{1,0},{2,3},{3,2},{4,5},{5,4},{6,7},{7,6},{8,9},{9,8},{10,11... | collective-permute-start | bytes 442376 | tf_op jit(solution)/shard_map/ppermute | solution.py:72
  33.3 4.9 %collective-permute-start.8 = (f32[32,576]{1,0:T(8,128)S(1)}, f32[32,576]{1,0:T(8,128)S(1)}, u32[]{:S(2)}, u32[]{:S(2)}) collective-permute-start(f32[32,576]{1,0:T(8,128)S(1)} %get-tuple-element.149), channel_id=1, source_target_pairs={{0,4},{4,0},{8,12},{12,8},{16,20},{20,16},{24,28},{28,24},{1,5},{5... | collective-permute-start | bytes 221192 | tf_op jit(solution)/shard_map/ppermute | solution.py:72
  38.2 4.5 %collective-permute-start.11 = (f32[32,576]{1,0:T(8,128)S(1)}, f32[32,576]{1,0:T(8,128)S(1)}, u32[]{:S(2)}, u32[]{:S(2)}) collective-permute-start(f32[32,576]{1,0:T(8,128)S(1)} %add.46), channel_id=1, source_target_pairs={{0,8},{4,12},{8,0},{12,4},{16,24},{20,28},{24,16},{28,20},{1,9},{5... | collective-permute-start | bytes 221192 | tf_op jit(solution)/shard_map/ppermute | solution.py:72
  42.7 8.8 %collective-permute-start.14 = (f32[32,1280]{1,0:T(8,128)S(1)}, f32[32,1280]{1,0:T(8,128)S(1)}, u32[]{:S(2)}, u32[]{:S(2)}) collective-permute-start(f32[32,1280]{1,0:T(8,128)S(1)} %get-tuple-element.165.ours), channel_id=1, source_target_pairs={{0,1},{1,0},{2,3},{3,2},{4,5},{5,4},{6,7},{7,6},{8,9},{9,8},{10,11... | collective-permute-start | bytes 491528 | tf_op jit(solution)/shard_map/ppermute | solution.py:72
  42.8 23.2 %collective-permute-start.21 = (f32[144,576]{1,0:T(8,128)S(1)}, f32[144,576]{1,0:T(8,128)S(1)}, u32[]{:S(2)}, u32[]{:S(2)}) collective-permute-start(f32[144,576]{1,0:T(8,128)S(1)} %collective-permute-done.6.refs_0_), channel_id=1, source_target_pairs={{0,4},{4,0},{8,12},{12,8},{16,20},{20,16},{24,28},{28,24},{1,5},{5... | collective-permute-start | bytes 995336 | tf_op jit(solution)/shard_map/ppermute | solution.py:72
  44.4 7.1 %collective-permute-start.13 = (f32[32,576]{1,0:T(8,128)S(1)}, f32[32,576]{1,0:T(8,128)S(1)}, u32[]{:S(2)}, u32[]{:S(2)}) collective-permute-start(f32[32,576]{1,0:T(8,128)S(1)} %add.47), channel_id=1, source_target_pairs={{0,16},{4,20},{8,24},{12,28},{16,0},{20,4},{24,8},{28,12},{1,17},{... | collective-permute-start | bytes 221192 | tf_op jit(solution)/shard_map/ppermute | solution.py:72
  47.1 14.4 %collective-permute-start.17 = (f32[72,576]{1,0:T(8,128)S(1)}, f32[72,576]{1,0:T(8,128)S(1)}, u32[]{:S(2)}, u32[]{:S(2)}) collective-permute-start(f32[72,576]{1,0:T(8,128)S(1)} %collective-permute-done.9.refs_0_), channel_id=1, source_target_pairs={{0,8},{4,12},{8,0},{12,4},{16,24},{20,28},{24,16},{28,20},{1,9},{5... | collective-permute-start | bytes 497672 | tf_op jit(solution)/shard_map/ppermute | solution.py:72
  49.2 12.4 %collective-permute-start.18 = (f32[72,576]{1,0:T(8,128)S(1)}, f32[72,576]{1,0:T(8,128)S(1)}, u32[]{:S(2)}, u32[]{:S(2)}) collective-permute-start(f32[72,576]{1,0:T(8,128)S(1)} %collective-permute-done.9.refs_0_), channel_id=1, source_target_pairs={{0,4},{4,0},{8,12},{12,8},{16,20},{20,16},{24,28},{28,24},{1,5},{5... | collective-permute-start | bytes 497672 | tf_op jit(solution)/shard_map/ppermute | solution.py:72
  52.6 4.4 %collective-permute-start.15 = (f32[16,1152]{1,0:T(8,128)S(1)}, f32[16,1152]{1,0:T(8,128)S(1)}, u32[]{:S(2)}, u32[]{:S(2)}) collective-permute-start(f32[16,1152]{1,0:T(8,128)S(1)} %get-tuple-element.172), channel_id=1, source_target_pairs={{0,2},{1,3},{2,0},{3,1},{4,6},{5,7},{6,4},{7,5},{8,10},{9,11},{10,... | collective-permute-start | bytes 221192 | tf_op jit(solution)/shard_map/ppermute | solution.py:72
  53.9 12.1 %collective-permute-start.20 = (f32[72,576]{1,0:T(8,128)S(1)}, f32[72,576]{1,0:T(8,128)S(1)}, u32[]{:S(2)}, u32[]{:S(2)}) collective-permute-start(f32[72,576]{1,0:T(8,128)S(1)} %get-tuple-element.189), channel_id=1, source_target_pairs={{0,16},{4,20},{8,24},{12,28},{16,0},{20,4},{24,8},{28,12},{1,17},{... | collective-permute-start | bytes 497672 | tf_op jit(solution)/shard_map/ppermute | solution.py:72
  57.1 4.4 %collective-permute-start.16 = (f32[16,1152]{1,0:T(8,128)S(1)}, f32[16,1152]{1,0:T(8,128)S(1)}, u32[]{:S(2)}, u32[]{:S(2)}) collective-permute-start(f32[16,1152]{1,0:T(8,128)S(1)} %add.49), channel_id=1, source_target_pairs={{0,4},{4,0},{8,12},{12,8},{16,20},{20,16},{24,28},{28,24},{1,5},{5... | collective-permute-start | bytes 221192 | tf_op jit(solution)/shard_map/ppermute | solution.py:72
  61.5 4.4 %collective-permute-start.19 = (f32[16,1152]{1,0:T(8,128)S(1)}, f32[16,1152]{1,0:T(8,128)S(1)}, u32[]{:S(2)}, u32[]{:S(2)}) collective-permute-start(f32[16,1152]{1,0:T(8,128)S(1)} %add.50), channel_id=1, source_target_pairs={{0,8},{4,12},{8,0},{12,4},{16,24},{20,28},{24,16},{28,20},{1,9},{5... | collective-permute-start | bytes 221192 | tf_op jit(solution)/shard_map/ppermute | solution.py:72
  62.9 12.9 %collective-permute-start.25 = (f32[72,576]{1,0:T(8,128)S(1)}, f32[72,576]{1,0:T(8,128)S(1)}, u32[]{:S(2)}, u32[]{:S(2)}) collective-permute-start(f32[72,576]{1,0:T(8,128)S(1)} %collective-permute-done.17.refs_1_), channel_id=1, source_target_pairs={{0,4},{4,0},{8,12},{12,8},{16,20},{20,16},{24,28},{28,24},{1,5},{5... | collective-permute-start | bytes 497672 | tf_op jit(solution)/shard_map/ppermute | solution.py:72
  66.0 5.3 %collective-permute-start.22 = (f32[16,1152]{1,0:T(8,128)S(1)}, f32[16,1152]{1,0:T(8,128)S(1)}, u32[]{:S(2)}, u32[]{:S(2)}) collective-permute-start(f32[16,1152]{1,0:T(8,128)S(1)} %add.51), channel_id=1, source_target_pairs={{0,16},{4,20},{8,24},{12,28},{16,0},{20,4},{24,8},{28,12},{1,17},{... | collective-permute-start | bytes 221192 | tf_op jit(solution)/shard_map/ppermute | solution.py:72
  68.4 2.9 %collective-permute-start.23 = (f32[16,1152]{1,0:T(8,128)S(1)}, f32[16,1152]{1,0:T(8,128)S(1)}, u32[]{:S(2)}, u32[]{:S(2)}) collective-permute-start(f32[16,1152]{1,0:T(8,128)S(1)} %get-tuple-element.197), channel_id=1, source_target_pairs={{0,1},{1,0},{2,3},{3,2},{4,5},{5,4},{6,7},{7,6},{8,9},{9,8},{10,11... | collective-permute-start | bytes 221192 | tf_op jit(solution)/shard_map/ppermute | solution.py:72
  71.3 4.4 %collective-permute-start.24 = (f32[16,1152]{1,0:T(8,128)S(1)}, f32[16,1152]{1,0:T(8,128)S(1)}, u32[]{:S(2)}, u32[]{:S(2)}) collective-permute-start(f32[16,1152]{1,0:T(8,128)S(1)} %add.52.ours), channel_id=1, source_target_pairs={{0,2},{1,3},{2,0},{3,1},{4,6},{5,7},{6,4},{7,5},{8,10},{9,11},{10,... | collective-permute-start | bytes 221192 | tf_op jit(solution)/shard_map/ppermute | solution.py:72
  72.6 9.5 %collective-permute-start.27 = (f32[72,576]{1,0:T(8,128)S(1)}, f32[72,576]{1,0:T(8,128)S(1)}, u32[]{:S(2)}, u32[]{:S(2)}) collective-permute-start(f32[72,576]{1,0:T(8,128)S(1)} %collective-permute-done.20.refs_0_), channel_id=1, source_target_pairs={{0,8},{4,12},{8,0},{12,4},{16,24},{20,28},{24,16},{28,20},{1,9},{5... | collective-permute-start | bytes 497672 | tf_op jit(solution)/shard_map/ppermute | solution.py:72
  74.1 8.0 %collective-permute-start.28 = (f32[72,576]{1,0:T(8,128)S(1)}, f32[72,576]{1,0:T(8,128)S(1)}, u32[]{:S(2)}, u32[]{:S(2)}) collective-permute-start(f32[72,576]{1,0:T(8,128)S(1)} %collective-permute-done.20.refs_0_), channel_id=1, source_target_pairs={{0,4},{4,0},{8,12},{12,8},{16,20},{20,16},{24,28},{28,24},{1,5},{5... | collective-permute-start | bytes 497672 | tf_op jit(solution)/shard_map/ppermute | solution.py:72
  77.1 5.0 %collective-permute-start.29 = (f32[32,1280]{1,0:T(8,128)S(1)}, f32[32,1280]{1,0:T(8,128)S(1)}, u32[]{:S(2)}, u32[]{:S(2)}) collective-permute-start(f32[32,1280]{1,0:T(8,128)S(1)} %get-tuple-element.233.ours), channel_id=1, source_target_pairs={{0,1},{1,0},{2,3},{3,2},{4,5},{5,4},{6,7},{7,6},{8,9},{9,8},{10,11... | collective-permute-start | bytes 491528 | tf_op jit(solution)/shard_map/ppermute | solution.py:72
  77.2 7.0 %copy-start.4 = (f32[72]{0:T(128)S(1)}, f32[72]{0:T(128)}, u32[]{:S(2)}) copy-start(f32[72]{0:T(128)} %param.24) | copy-start | bytes 868
  77.2 4.8 %collective-permute-start.26 = (f32[32,576]{1,0:T(8,128)S(1)}, f32[32,576]{1,0:T(8,128)S(1)}, u32[]{:S(2)}, u32[]{:S(2)}) collective-permute-start(f32[32,576]{1,0:T(8,128)S(1)} %get-tuple-element.213), channel_id=1, source_target_pairs={{0,4},{4,0},{8,12},{12,8},{16,20},{20,16},{24,28},{28,24},{1,5},{5... | collective-permute-start | bytes 221192 | tf_op jit(solution)/shard_map/ppermute | solution.py:72
  82.1 4.5 %collective-permute-start.30 = (f32[32,576]{1,0:T(8,128)S(1)}, f32[32,576]{1,0:T(8,128)S(1)}, u32[]{:S(2)}, u32[]{:S(2)}) collective-permute-start(f32[32,576]{1,0:T(8,128)S(1)} %add.53), channel_id=1, source_target_pairs={{0,8},{4,12},{8,0},{12,4},{16,24},{20,28},{24,16},{28,20},{1,9},{5... | collective-permute-start | bytes 221192 | tf_op jit(solution)/shard_map/ppermute | solution.py:72
  83.6 8.5 %collective-permute-start.32 = (f32[72,576]{1,0:T(8,128)S(1)}, f32[72,576]{1,0:T(8,128)S(1)}, u32[]{:S(2)}, u32[]{:S(2)}) collective-permute-start(f32[72,576]{1,0:T(8,128)S(1)} %collective-permute-done.27.refs_1_), channel_id=1, source_target_pairs={{0,4},{4,0},{8,12},{12,8},{16,20},{20,16},{24,28},{28,24},{1,5},{5... | collective-permute-start | bytes 497672 | tf_op jit(solution)/shard_map/ppermute | solution.py:72
  86.6 5.4 %collective-permute-start.31 = (f32[32,576]{1,0:T(8,128)S(1)}, f32[32,576]{1,0:T(8,128)S(1)}, u32[]{:S(2)}, u32[]{:S(2)}) collective-permute-start(f32[32,576]{1,0:T(8,128)S(1)} %add.54), channel_id=1, source_target_pairs={{0,16},{4,20},{8,24},{12,28},{16,0},{20,4},{24,8},{28,12},{1,17},{... | collective-permute-start | bytes 221192 | tf_op jit(solution)/shard_map/ppermute | solution.py:72
  92.0 1.3 %collective-permute-start.33 = (f32[32,576]{1,0:T(8,128)S(1)}, f32[32,576]{1,0:T(8,128)S(1)}, u32[]{:S(2)}, u32[]{:S(2)}) collective-permute-start(f32[32,576]{1,0:T(8,128)S(1)} %add.55.right), channel_id=1, source_target_pairs={{0,1},{1,0},{2,3},{3,2},{4,5},{5,4},{6,7},{7,6},{8,9},{9,8},{10,11... | collective-permute-start | bytes 221192 | tf_op jit(solution)/shard_map/ppermute | solution.py:72
